TPU v7x, 512 devices: a whole 4x8x8 slice. The times are simulated.
512 devices in a mesh: lat: 16 (over y, core), lon: 32 (over z, x).
Axes of the slice: x: 4, y: 8, z: 8, core: 2. Of those that a mesh axis runs over, the one named last changes fastest.
Arguments:
- base_state: float32 [16, 48, 128, 128], P(None, 'lat', 'lon'), may hold values from -6 to 6
- tangent: float32 [16, 48, 128, 128], P(None, 'lat', 'lon'), may hold values from -6 to 6
- blocks: bfloat16 [48, 128, 9, 128, 128], P('lat', 'lon'), may hold values from -0.26516504 to 1.26516504
- pattern: int32 [48, 128, 9], P('lat', 'lon'), may hold values from 0 to 6143, as said below
- live: int32 [48, 128, 9], P('lat', 'lon'), may hold values from 0 to 1, as said below
- column_inverse: float32 [48, 128, 8, 16, 16], P('lat', 'lon'), may hold values from -0.4 to 1
- col_depth: int32 [48, 128, 8], P('lat', 'lon'), may hold values from 1 to 16
- uptake_rate: float32 [48, 128, 128], P('lat', 'lon'), may hold values from 0.3 to 3
- stoich: float32 [16], replicated, may hold values from -4 to 4
- basis: float32 [4, 16, 48, 128, 128], P(None, None, 'lat', 'lon'), may hold values from -0.00169145587 to 0.00169145587
Outputs:
- product: float32 [16, 48, 128, 128], P(None, 'lat', 'lon')
- next_basis: float32 [16, 48, 128, 128], P(None, 'lat', 'lon')
- coeffs: float32 [5], replicated
Inputs may be any that keep to these rules, and one draw needn't show every extreme that they name: pattern[i, j, s] is the flat index i2 * 128 + j2 of a block with |i2 - i| <= 1 and |j2 - j| <= 1; slot 0 names the block itself; the live slots of a row block name different blocks. Slot 0 is always live.
All inputs are finite; a program needn't handle non-finite values.
Results may differ from a plain program's by a relative error of at most 0.0046.
Values may be sent and summed in bfloat16 or wider, within the bound.
No kernel may reach another device: no remote copies, remote signals or barrier semaphores. Data moves between devices by JAX's collectives and lax.ppermute only.
A program may use at most 64 MiB of HBM per device.

v0:
```python
import jax
import jax.numpy as jnp
from jax import lax
from jax.sharding import PartitionSpec as P


def padded_2(x, sides, width):
    for axis, dim in sides:
        size, length = (lax.axis_size(axis), x.shape[dim])
        up = [(i, (i + 1) % size) for i in range(size - 1)]
        down = [(j, i) for i, j in up]
        last = lax.slice_in_dim(x, length - width, length, axis=dim)
        first = lax.slice_in_dim(x, 0, width, axis=dim)
        before = lax.ppermute(last, axis, up)
        after = lax.ppermute(first, axis, down)
        x = jnp.concatenate([before, x, after], axis=dim)
    return x


def extend(stacked):
    return padded_2(stacked, (("lat", 1), ("lon", 2)), 1)


def body(
    base_state,
    tangent,
    blocks,
    pattern,
    live,
    column_inverse,
    col_depth,
    uptake_rate,
    stoich,
    basis,
):
    tracers = base_state.shape[0]
    lat_blocks = base_state.shape[1]
    lon_blocks = base_state.shape[2]
    points = base_state.shape[3]
    columns = column_inverse.shape[2]
    levels = column_inverse.shape[3]
    total_lon = lon_blocks * lax.axis_size("lon")
    lat_first = lax.axis_index("lat") * lat_blocks
    lon_first = lax.axis_index("lon") * lon_blocks
    row_lat = pattern // total_lon - lat_first + 1
    row_lon = pattern % total_lon - lon_first + 1
    local_index = row_lat * (lon_blocks + 2) + row_lon
    live_weight = live.astype(jnp.bfloat16)[None, :, :, :, None]
    wet = (jnp.arange(levels)[None, None, None, :] < col_depth[..., None]).astype(jnp.float32)
    scaled = stoich[:, None, None, None]
    state = base_state
    along = tangent
    for turn in range(2):
        stacked = jnp.concatenate([state, along], 0).astype(jnp.bfloat16)
        padded = extend(stacked)
        flat = padded.reshape(2 * tracers, (lat_blocks + 2) * (lon_blocks + 2), points)
        gathered = jnp.take(flat, local_index, axis=1) * live_weight
        moved = jnp.einsum(
            "abspq,tabsq->tabp", blocks, gathered, preferred_element_type=jnp.float32
        )
        nutrient = state[0]
        denom = nutrient * nutrient + 1.0
        uptake = uptake_rate * nutrient * nutrient / denom
        slope = uptake_rate * 2.0 * nutrient / (denom * denom)
        source = jnp.concatenate([scaled * uptake[None], scaled * (slope * along[0])[None]], 0)
        mixed = (moved + source).reshape(2 * tracers, lat_blocks, lon_blocks, columns, levels) * wet
        result = (
            jnp.einsum("abclm,tabcm->tabcl", column_inverse, mixed, precision=lax.Precision.HIGHEST)
            * wet
        )
        result = result.reshape(2 * tracers, lat_blocks, lon_blocks, points)
        state = result[:tracers]
        along = result[tracers:]
    local_heights = jnp.einsum("ktabp,tabp->k", basis, along, precision=lax.Precision.HIGHEST)
    heights = lax.psum(local_heights, ("lat", "lon"))
    rest = along - jnp.einsum("k,ktabp->tabp", heights, basis, precision=lax.Precision.HIGHEST)
    squared = lax.psum(jnp.sum(rest * rest), ("lat", "lon"))
    beta = jnp.sqrt(squared + 1e-06)
    next_basis = rest / beta
    coeffs = jnp.concatenate([heights, beta[None]])
    return (along, next_basis, coeffs)


def solution(mesh):
    placed = (
        P(None, "lat", "lon", None),
        P(None, "lat", "lon", None),
        P("lat", "lon", None, None, None),
        P("lat", "lon", None),
        P("lat", "lon", None),
        P("lat", "lon", None, None, None),
        P("lat", "lon", None),
        P("lat", "lon", None),
        P(),
        P(None, None, "lat", "lon", None),
    )
    return jax.shard_map(
        body,
        mesh=mesh,
        in_specs=placed,
        out_specs=(P(None, "lat", "lon", None), P(None, "lat", "lon", None), P()),
        check_vma=False,
    )
```

profile of v0, /device:TPU:1, one launch (start us, length us, event | category | flops | bytes accessed | tf_op | source)
XLA Modules:
  0.0 296.3 jit_solution(17240382466065508070)
XLA Ops:
  0.6 0.0 copy-start
  0.6 1.1 copy.48
  1.7 0.0 copy-start.1
  1.7 1.0 copy.47
  2.7 0.0 copy-done.1
  2.7 0.0 copy-start.2
  2.7 0.6 pad_maximum_fusion.13
  3.3 0.0 copy-done.2
  3.3 4.6 %collective-permute-start = (bf16[32,1,4,128]{3,0,2,1:T(8,128)(2,1)}, bf16[32,1,4,128]{3,0,2,1:T(8,128)(2,1)}, u32[]{:S(2)}, u32[]{:S(2)}) collective-permute-start(bf16[32,1,4,128]{3,0,2,1:T(8,128)(2,1)} %get-tuple-element.29), channel_id=1, source_target_pairs={{0,32},{32,64},{64,96},{96,128},{128,160},{160,192},{192,224},{224... | collective-permute-start | bytes 98312 | tf_op jit(solution)/shard_map/ppermute | solution.py:14
  7.9 6.1 %collective-permute-start.1 = (bf16[32,1,4,128]{3,0,2,1:T(8,128)(2,1)}, bf16[32,1,4,128]{3,0,2,1:T(8,128)(2,1)}, u32[]{:S(2)}, u32[]{:S(2)}) collective-permute-start(bf16[32,1,4,128]{3,0,2,1:T(8,128)(2,1)} %get-tuple-element.30), channel_id=1, source_target_pairs={{32,0},{64,32},{96,64},{128,96},{160,128},{192,160},{224,192},{256... | collective-permute-start | bytes 98312 | tf_op jit(solution)/shard_map/ppermute | solution.py:15
  14.0 0.7 fusion.26
  14.7 1.4 fusion.19
  16.1 1.4 broadcast_multiply_fusion.3
  17.5 1.3 compare_and_fusion
  18.8 0.1 reshape.69
  18.9 0.0 copy-start.3
  18.9 0.0 collective-permute-done
  19.0 0.0 collective-permute-done.1
  19.0 0.8 pad_maximum_fusion.9
  19.8 1.3 collective-permute-start.2
  21.1 1.3 collective-permute-start.3
  22.4 0.7 convert_element_type.12
  23.1 0.0 collective-permute-done.2
  23.1 3.1 %collective-permute-done.3 = bf16[32,5,1,128]{3,0,2,1:T(8,128)(2,1)S(1)} collective-permute-done((bf16[32,5,1,128]{3,0,2,1:T(8,128)(2,1)S(1)}, bf16[32,5,1,128]{3,0,2,1:T(8,128)(2,1)S(1)}, u32[]{:S(2)}, u32[]{:S(2)}) %collective-permute-start.3) | collective-permute-done | bytes 40992 | tf_op jit(solution)/shard_map/ppermute | solution.py:15
  26.3 1.6 pad_maximum_fusion
  27.8 2.6 gather_fusion
  30.4 0.0 copy-done
  30.4 0.0 copy-done.3
  30.4 3.2 %fusion.3 = f32[32,3,4,128]{3,0,2,1:T(8,128)} fusion(bf16[3,4,9,128,128]{4,3,2,1,0:T(8,128)(2,1)S(1)} %copy-done, bf16[3,4,9,32,128]{4,3,2,1,0:T(8,128)(2,1)} %bitcast.81, pred[3,4,9]{2,1,0:T(4,128)(4,1)S(1)} %copy-done.3, bf16[3,4,9]{2,1,0:T(4,128)(2,1)S(1)} %convert_element_type.12, f32[16,3,4,128]{3,0,2,1:T(8,128)} %get-tuple-element.36, ...), kind=kOutput, calls=%fused_computation.9 | convolution fusion | flops 114229248 | bytes 4817220 | tf_op jit(solution)/shard_map/abspq,tabsq->tabp/dot_general | solution.py:58
  33.6 2.1 copy.27
  35.7 3.2 %fusion.37 = (bf16[32,3,4,8,16]{0,4,3,2,1:T(8,128)(2,1)}, f32[32,3,4,8,16]{0,4,3,2,1:T(8,128)S(1)}) fusion(f32[3,4,8,16]{3,2,1,0:T(8,128)} %fusion.19, f32[3,4,8,16,16]{4,3,2,1,0:T(8,128)} %param.17, f32[32,3,4,8,16]{0,4,3,2,1:T(8,128)} %bitcast.78), kind=kOutput, calls=%fused_computation.88 | convolution fusion | flops 9584640 | bytes 595968 | tf_op jit(solution)/shard_map/abclm,tabcm->tabcl/dot_general | solution.py:68
  38.9 1.3 slice_reduce_fusion.1
  40.2 0.9 squeeze.14
  41.1 1.5 squeeze.15
  42.5 2.1 fusion.36
  44.7 1.7 copy.28
  46.4 1.8 copy.29
  48.2 0.8 pad_maximum_fusion.11
  48.9 2.3 collective-permute-start.4
  51.3 2.0 collective-permute-start.5
  53.3 0.7 fusion.27
  54.0 0.0 collective-permute-done.4
  54.0 2.5 collective-permute-done.5
  56.5 0.8 pad_maximum_fusion.5
  57.3 3.1 %collective-permute-start.6 = (bf16[32,5,1,128]{3,0,2,1:T(8,128)(2,1)S(1)}, bf16[32,5,1,128]{3,0,2,1:T(8,128)(2,1)S(1)}, u32[]{:S(2)}, u32[]{:S(2)}) collective-permute-start(bf16[32,5,1,128]{3,0,2,1:T(8,128)(2,1)S(1)} %get-tuple-element.21), channel_id=1, source_target_pairs={{0,1},{1,2},{2,3},{3,4},{4,5},{5,6},{6,7},{7,8},{8,9},{9,10},{10,1... | collective-permute-start | bytes 122888 | tf_op jit(solution)/shard_map/ppermute | solution.py:14
  60.4 1.3 collective-permute-start.7
  61.7 1.4 broadcast_multiply_fusion.1
  63.1 0.0 collective-permute-done.6
  63.1 2.0 collective-permute-done.7
  65.1 1.5 pad_maximum_fusion.1
  66.7 2.6 gather_fusion.1
  69.3 3.2 %fusion.2 = f32[32,3,4,128]{3,0,2,1:T(8,128)} fusion(bf16[3,4,9,128,128]{4,3,2,1,0:T(8,128)(2,1)S(1)} %copy-done, bf16[3,4,9,32,128]{4,3,2,1,0:T(8,128)(2,1)} %bitcast.80, pred[3,4,9]{2,1,0:T(4,128)(4,1)} %get-tuple-element.17, bf16[3,4,9]{2,1,0:T(4,128)(2,1)S(1)} %convert_element_type.12, f32[16,3,4,128]{3,0,2,1:T(8,128)} %get-tuple-element.34, ...), kind=kOutput, calls=%fused_computation.7 | convolution fusion | flops 114229248 | bytes 4817220 | tf_op jit(solution)/shard_map/abspq,tabsq->tabp/dot_general | solution.py:58
  72.5 2.1 copy.30
  74.6 2.4 fusion
  76.9 1.1 slice.86
  78.1 2.0 copy.35
  80.1 2.9 convolution_bitcast_fusion.2
  83.0 2.0 copy.32
  85.0 109.9 %psum.14 = f32[4]{0:T(128)S(1)} all-reduce(f32[4]{0:T(128)S(1)} %convolution_bitcast_fusion.2), channel_id=1, replica_groups=mesh['lat'=16,'lon'=32] {'lat','lon'}, use_global_device_ids=true, to_apply=%region_0.2 | all-reduce | flops 4 | bytes 32 | tf_op jit(solution)/shard_map/psum | solution.py:75
  195.0 1.9 fusion.14
  196.9 2.2 multiply_reduce_fusion
  199.1 94.4 %psum.15 = f32[]{:T(128)} all-reduce(f32[]{:T(128)} %get-tuple-element.15), channel_id=1, replica_groups=mesh['lat'=16,'lon'=32] {'lat','lon'}, use_global_device_ids=true, to_apply=%region_2.4 | all-reduce | flops 1 | bytes 8 | tf_op jit(solution)/shard_map/psum | solution.py:77
  294.2 1.6 broadcast_divide_fusion
  295.8 0.6 pad_maximum_fusion.14
  (1 shorter events, 0.0 us)
Async XLA Ops:
  0.6 29.8 %copy-start = (bf16[3,4,9,128,128]{4,3,2,1,0:T(8,128)(2,1)S(1)}, bf16[3,4,9,128,128]{4,3,2,1,0:T(8,128)(2,1)}, u32[]{:S(2)}) copy-start(bf16[3,4,9,128,128]{4,3,2,1,0:T(8,128)(2,1)} %param.14) | copy-start | bytes 10616836
  1.7 1.0 copy-start.1
  2.7 0.6 copy-start.2
  3.3 15.6 %collective-permute-start = (bf16[32,1,4,128]{3,0,2,1:T(8,128)(2,1)}, bf16[32,1,4,128]{3,0,2,1:T(8,128)(2,1)}, u32[]{:S(2)}, u32[]{:S(2)}) collective-permute-start(bf16[32,1,4,128]{3,0,2,1:T(8,128)(2,1)} %get-tuple-element.29), channel_id=1, source_target_pairs={{0,32},{32,64},{64,96},{96,128},{128,160},{160,192},{192,224},{224... | collective-permute-start | bytes 98312 | tf_op jit(solution)/shard_map/ppermute | solution.py:14
  7.9 11.0 %collective-permute-start.1 = (bf16[32,1,4,128]{3,0,2,1:T(8,128)(2,1)}, bf16[32,1,4,128]{3,0,2,1:T(8,128)(2,1)}, u32[]{:S(2)}, u32[]{:S(2)}) collective-permute-start(bf16[32,1,4,128]{3,0,2,1:T(8,128)(2,1)} %get-tuple-element.30), channel_id=1, source_target_pairs={{32,0},{64,32},{96,64},{128,96},{160,128},{192,160},{224,192},{256... | collective-permute-start | bytes 98312 | tf_op jit(solution)/shard_map/ppermute | solution.py:15
  18.9 11.5 %copy-start.3 = (pred[3,4,9]{2,1,0:T(4,128)(4,1)S(1)}, pred[3,4,9]{2,1,0:T(4,128)(4,1)}, u32[]{:S(2)}) copy-start(pred[3,4,9]{2,1,0:T(4,128)(4,1)} %get-tuple-element.17) | copy-start | bytes 328
  19.8 3.3 %collective-permute-start.2 = (bf16[32,5,1,128]{3,0,2,1:T(8,128)(2,1)S(1)}, bf16[32,5,1,128]{3,0,2,1:T(8,128)(2,1)S(1)}, u32[]{:S(2)}, u32[]{:S(2)}) collective-permute-start(bf16[32,5,1,128]{3,0,2,1:T(8,128)(2,1)S(1)} %get-tuple-element.23), channel_id=1, source_target_pairs={{0,1},{1,2},{2,3},{3,4},{4,5},{5,6},{6,7},{7,8},{8,9},{9,10},{10,1... | collective-permute-start | bytes 122888 | tf_op jit(solution)/shard_map/ppermute | solution.py:14
  21.1 5.2 %collective-permute-start.3 = (bf16[32,5,1,128]{3,0,2,1:T(8,128)(2,1)S(1)}, bf16[32,5,1,128]{3,0,2,1:T(8,128)(2,1)S(1)}, u32[]{:S(2)}, u32[]{:S(2)}) collective-permute-start(bf16[32,5,1,128]{3,0,2,1:T(8,128)(2,1)S(1)} %get-tuple-element.24), channel_id=1, source_target_pairs={{1,0},{2,1},{3,2},{4,3},{5,4},{6,5},{7,6},{8,7},{9,8},{10,9},{11,1... | collective-permute-start | bytes 122888 | tf_op jit(solution)/shard_map/ppermute | solution.py:15
  48.9 5.1 %collective-permute-start.4 = (bf16[32,1,4,128]{3,0,2,1:T(8,128)(2,1)S(1)}, bf16[32,1,4,128]{3,0,2,1:T(8,128)(2,1)S(1)}, u32[]{:S(2)}, u32[]{:S(2)}) collective-permute-start(bf16[32,1,4,128]{3,0,2,1:T(8,128)(2,1)S(1)} %get-tuple-element.27), channel_id=1, source_target_pairs={{0,32},{32,64},{64,96},{96,128},{128,160},{160,192},{192,224},{224... | collective-permute-start | bytes 98312 | tf_op jit(solution)/shard_map/ppermute | solution.py:14
  51.3 5.2 %collective-permute-start.5 = (bf16[32,1,4,128]{3,0,2,1:T(8,128)(2,1)S(1)}, bf16[32,1,4,128]{3,0,2,1:T(8,128)(2,1)S(1)}, u32[]{:S(2)}, u32[]{:S(2)}) collective-permute-start(bf16[32,1,4,128]{3,0,2,1:T(8,128)(2,1)S(1)} %get-tuple-element.28), channel_id=1, source_target_pairs={{32,0},{64,32},{96,64},{128,96},{160,128},{192,160},{224,192},{256... | collective-permute-start | bytes 98312 | tf_op jit(solution)/shard_map/ppermute | solution.py:15
  57.3 5.8 %collective-permute-start.6 = (bf16[32,5,1,128]{3,0,2,1:T(8,128)(2,1)S(1)}, bf16[32,5,1,128]{3,0,2,1:T(8,128)(2,1)S(1)}, u32[]{:S(2)}, u32[]{:S(2)}) collective-permute-start(bf16[32,5,1,128]{3,0,2,1:T(8,128)(2,1)S(1)} %get-tuple-element.21), channel_id=1, source_target_pairs={{0,1},{1,2},{2,3},{3,4},{4,5},{5,6},{6,7},{7,8},{8,9},{9,10},{10,1... | collective-permute-start | bytes 122888 | tf_op jit(solution)/shard_map/ppermute | solution.py:14
  60.4 4.7 %collective-permute-start.7 = (bf16[32,5,1,128]{3,0,2,1:T(8,128)(2,1)S(1)}, bf16[32,5,1,128]{3,0,2,1:T(8,128)(2,1)S(1)}, u32[]{:S(2)}, u32[]{:S(2)}) collective-permute-start(bf16[32,5,1,128]{3,0,2,1:T(8,128)(2,1)S(1)} %get-tuple-element.22), channel_id=1, source_target_pairs={{1,0},{2,1},{3,2},{4,3},{5,4},{6,5},{7,6},{8,7},{9,8},{10,9},{11,1... | collective-permute-start | bytes 122888 | tf_op jit(solution)/shard_map/ppermute | solution.py:15
where the time goes:
time: 298 us; the launch traced here: 296 us
  blocking collectives  204 us (68%)
  local copies, waits for them, and re-layouts  25.9 us (9%)
  starting transfers between devices  21.9 us (7%)
  other arithmetic  18.1 us (6%)
  matrix products  16.8 us (6%)
  waiting for transfers between devices  7.69 us (3%)
    psum x1, blocking collectives, body(): heights = lax.psum(local_heights, ('lat', 'lon'))  110 us
    psum x1, blocking collectives, body(): squared = lax.psum(jnp.sum(rest * rest), ('lat', 'lon'))  94.4 us
    ppermute x4, starting transfers between devices, padded_2(): before = lax.ppermute(last, axis, up)  11.3 us
    ppermute x4, starting transfers between devices, padded_2(): after = lax.ppermute(first, axis, down)  10.6 us
    ppermute x4, waiting for transfers between devices, padded_2(): after = lax.ppermute(first, axis, down)  7.68 us
    dot_general x2, matrix products, body(): jnp.einsum('abspq,tabsq->tabp', blocks, gathered, preferred_element_type=...  6.44 us
  transfers between devices with their start and end apart: 8, of which 3 were waited for; matrix products, arithmetic and copies ran while one was open for 3% of the time, Pallas kernels for 0%

commit v1 on v0

--- a/solution.py
+++ b/solution.py
@@ -19,6 +19,15 @@
 
 def extend(stacked):
     return padded_2(stacked, (("lat", 1), ("lon", 2)), 1)
+
+
+def summed(part):
+    length = part.shape[0]
+    row = jnp.pad(part, (0, 128 - length))
+    for axis in ("lat", "lon"):
+        copies = jnp.broadcast_to(row[None], (lax.axis_size(axis), 128))
+        row = jnp.sum(lax.all_to_all(copies, axis, 0, 0), 0)
+    return row[:length]
 
 
 def body(
@@ -71,10 +80,21 @@
         result = result.reshape(2 * tracers, lat_blocks, lon_blocks, points)
         state = result[:tracers]
         along = result[tracers:]
-    local_heights = jnp.einsum("ktabp,tabp->k", basis, along, precision=lax.Precision.HIGHEST)
-    heights = lax.psum(local_heights, ("lat", "lon"))
+    vectors = jnp.concatenate([basis, along[None]], 0)
+    gram = jnp.einsum("ktabp,jtabp->kj", vectors, vectors, precision=lax.Precision.HIGHEST)
+    total = summed(gram.reshape(25)).reshape(5, 5)
+    heights = total[:4, 4]
     rest = along - jnp.einsum("k,ktabp->tabp", heights, basis, precision=lax.Precision.HIGHEST)
-    squared = lax.psum(jnp.sum(rest * rest), ("lat", "lon"))
+    cross = jnp.sum(heights[:, None] * heights[None, :] * total[:4, :4])
+    squares = jnp.sum(heights * heights)
+    short = total[4, 4] - 2.0 * squares + cross
+    size = total[4, 4] + 2.0 * squares + cross
+    squared = lax.cond(
+        short < 0.01 * size,
+        lambda r: summed(jnp.sum(r * r).reshape(1))[0],
+        lambda r: short,
+        rest,
+    )
     beta = jnp.sqrt(squared + 1e-06)
     next_basis = rest / beta
     coeffs = jnp.concatenate([heights, beta[None]])

time: 298 us -> 142 us (0.48)
  blocking collectives: 204 us -> 16.6 us
  starting transfers between devices: 21.9 us -> 39.4 us
  waiting for transfers between devices: 7.69 us -> 12.2 us
  local copies, waits for them, and re-layouts: 25.9 us -> 30.1 us
    psum x2 -> x0, blocking collectives: 204 us -> none  [the longest x1 110 us: body(): heights = lax.psum(local_heights, ('lat', 'lon'))]
    all_to_all x0 -> x1, starting transfers between devices: none -> 17.5 us  [summed(): row = jnp.sum(lax.all_to_all(copies, axis, 0, 0), 0)]
    all_to_all x0 -> x1, blocking collectives: none -> 16.6 us  [summed(): row = jnp.sum(lax.all_to_all(copies, axis, 0, 0), 0)]
    all_to_all x0 -> x1, waiting for transfers between devices: none -> 6.49 us  [summed(): row = jnp.sum(lax.all_to_all(copies, axis, 0, 0), 0)]
    unnamed x11 -> x14, local copies, waits for them, and re-layouts: 4.06 us -> 6.05 us
  transfers between devices with their start and end apart: 8 -> 9, of which waited for: 3 -> 4; matrix products, arithmetic and copies ran while one was open for 3% -> 8% of each run, Pallas kernels for 0% -> 0%
where the time goes in v1:
time: 142 us; the launch traced here: 140 us
  starting transfers between devices  39.4 us (28%)
  local copies, waits for them, and re-layouts  30.1 us (21%)
  other arithmetic  20.1 us (14%)
  matrix products  17.8 us (13%)
  blocking collectives  16.6 us (12%)
  waiting for transfers between devices  12.2 us (9%)
  between operations  3.92 us (3%)
    all_to_all x1, starting transfers between devices, summed(): row = jnp.sum(lax.all_to_all(copies, axis, 0, 0), 0)  17.5 us
    all_to_all x1, blocking collectives, summed(): row = jnp.sum(lax.all_to_all(copies, axis, 0, 0), 0)  16.6 us
    ppermute x4, starting transfers between devices, padded_2(): before = lax.ppermute(last, axis, up)  11.3 us
    ppermute x4, starting transfers between devices, padded_2(): after = lax.ppermute(first, axis, down)  10.6 us
    all_to_all x1, waiting for transfers between devices, summed(): row = jnp.sum(lax.all_to_all(copies, axis, 0, 0), 0)  6.49 us
    dot_general x2, matrix products, body(): jnp.einsum('abspq,tabsq->tabp', blocks, gathered, preferred_element_type=...  6.43 us
    unnamed x14, local copies, waits for them, and re-layouts  6.05 us
    ppermute x4, waiting for transfers between devices, padded_2(): after = lax.ppermute(first, axis, down)  5.68 us
  transfers between devices with their start and end apart: 9, of which 4 were waited for; matrix products, arithmetic and copies ran while one was open for 8% of the time, Pallas kernels for 0%

profile of v1, /device:TPU:1, one launch (start us, length us, event | category | flops | bytes accessed | tf_op | source)
XLA Modules:
  0.0 140.1 jit_solution(27740394038157380)
XLA Ops:
  0.6 0.0 copy-start
  0.6 1.1 copy.73
  1.7 1.0 copy.74
  2.7 0.6 pad_maximum_fusion.13
  3.3 4.6 %collective-permute-start = (bf16[32,1,4,128]{3,0,2,1:T(8,128)(2,1)}, bf16[32,1,4,128]{3,0,2,1:T(8,128)(2,1)}, u32[]{:S(2)}, u32[]{:S(2)}) collective-permute-start(bf16[32,1,4,128]{3,0,2,1:T(8,128)(2,1)} %get-tuple-element.47), channel_id=1, source_target_pairs={{0,32},{32,64},{64,96},{96,128},{128,160},{160,192},{192,224},{224... | collective-permute-start | bytes 98312 | tf_op jit(solution)/shard_map/ppermute | solution.py:14
  7.9 6.1 %collective-permute-start.1 = (bf16[32,1,4,128]{3,0,2,1:T(8,128)(2,1)}, bf16[32,1,4,128]{3,0,2,1:T(8,128)(2,1)}, u32[]{:S(2)}, u32[]{:S(2)}) collective-permute-start(bf16[32,1,4,128]{3,0,2,1:T(8,128)(2,1)} %get-tuple-element.48), channel_id=1, source_target_pairs={{32,0},{64,32},{96,64},{128,96},{160,128},{192,160},{224,192},{256... | collective-permute-start | bytes 98312 | tf_op jit(solution)/shard_map/ppermute | solution.py:15
  14.0 0.7 fusion.28
  14.7 1.4 fusion.21
  16.1 1.4 %broadcast_multiply_fusion.3 = (f32[16,3,4,128]{3,0,2,1:T(8,128)}, f32[16,3,4,128]{3,0,2,1:T(8,128)}) fusion(f32[3,4,128]{2,1,0:T(4,128)S(1)} %get-tuple-element.43, f32[16]{0:T(128)} %param.22, f32[3,4,128]{2,1,0:T(4,128)S(1)} %get-tuple-element.44), kind=kLoop, calls=%fused_computation.42 | loop fusion | flops 49152 | bytes 208960 | tf_op jit(solution)/shard_map/mul | solution.py:74
  17.5 1.3 compare_and_fusion
  18.8 0.1 reshape.110
  18.9 0.0 collective-permute-done
  18.9 0.0 collective-permute-done.1
  18.9 0.8 pad_maximum_fusion.9
  19.8 1.3 collective-permute-start.2
  21.1 1.3 collective-permute-start.3
  22.4 0.7 convert_element_type.19
  23.1 2.0 %copy.57 = f32[4,16,3,4,128]{4,0,1,3,2:T(4,128)} copy(f32[4,16,3,4,128]{4,3,2,1,0:T(4,128)} %param.23) | data formatting | bytes 786432 | tf_op args[9]
  25.1 1.1 collective-permute-done.3
  26.2 1.6 %pad_maximum_fusion = bf16[32,5,6,128]{3,0,2,1:T(8,128)(2,1)} fusion(bf16[32,5,1,128]{3,0,2,1:T(8,128)(2,1)S(1)} %collective-permute-done.3, bf16[32,1,4,128]{3,0,2,1:T(8,128)(2,1)} %collective-permute-done.1, bf16[16,3,4,128]{3,0,2,1:T(8,128)(2,1)} %copy-done.1, bf16[16,3,4,128]{3,0,2,1:T(8,128)(2,1)} %copy-done.2, ...), kind=kLoop, calls=%fused_computation.33 | loop fusion | flops 1474560 | bytes 491520 | tf_op jit(solution)/shard_map/concatenate | solution.py:16
  27.8 2.6 %gather_fusion = bf16[108,32,128]{2,1,0:T(8,128)(2,1)} fusion(bf16[32,30,128]{2,0,1:T(8,128)(2,1)} %bitcast.82, s32[1024]{0:T(1024)S(1)} %pad_clamp_fusion), kind=kCustom, calls=%fused_computation.clone | custom fusion | bytes 1769904 | tf_op jit(solution)/shard_map/jit(_take)/gather | solution.py:66
  30.4 3.2 %fusion.3 = f32[32,3,4,128]{3,0,2,1:T(8,128)} fusion(bf16[3,4,9,128,128]{4,3,2,1,0:T(8,128)(2,1)S(1)} %copy-done, bf16[3,4,9,32,128]{4,3,2,1,0:T(8,128)(2,1)} %bitcast.88, pred[3,4,9]{2,1,0:T(4,128)(4,1)S(1)} %copy-done.4, bf16[3,4,9]{2,1,0:T(4,128)(2,1)S(1)} %convert_element_type.19, f32[16,3,4,128]{3,0,2,1:T(8,128)} %get-tuple-element.54, ...), kind=kOutput, calls=%fused_computation.10 | convolution fusion | flops 114229248 | bytes 4817220 | tf_op jit(solution)/shard_map/abspq,tabsq->tabp/dot_general | solution.py:67
  33.6 2.1 %copy.53 = f32[32,3,4,128]{0,3,2,1:T(8,128)} copy(f32[32,3,4,128]{3,0,2,1:T(8,128)} %fusion.3) | data formatting | bytes 393216 | tf_op jit(solution)/shard_map/add | solution.py:75
  35.7 3.1 %fusion.40 = (bf16[32,3,4,8,16]{0,4,3,2,1:T(8,128)(2,1)}, f32[32,3,4,8,16]{0,4,3,2,1:T(8,128)S(1)}) fusion(f32[3,4,8,16]{3,2,1,0:T(8,128)} %fusion.21, f32[3,4,8,16,16]{4,3,2,1,0:T(8,128)} %param.19, f32[32,3,4,8,16]{0,4,3,2,1:T(8,128)} %bitcast.85), kind=kOutput, calls=%fused_computation.94 | convolution fusion | flops 9584640 | bytes 595968 | tf_op jit(solution)/shard_map/abclm,tabcm->tabcl/dot_general | solution.py:77
  38.8 1.3 slice_reduce_fusion.1
  40.2 0.9 squeeze.22
  41.0 1.5 %squeeze.23 = f32[3,4,128]{2,1,0:T(4,128)} reshape(f32[3,4,8,16]{3,2,1,0:T(8,128)} %get-tuple-element.34) | data formatting | bytes 12288 | tf_op jit(solution)/shard_map/squeeze | solution.py:74
  42.5 2.1 %fusion.39 = (bf16[16,3,4,8,16]{0,4,3,2,1:T(8,128)(2,1)}, bf16[16,3,4,8,16]{0,4,3,2,1:T(8,128)(2,1)}) fusion(bf16[32,3,4,8,16]{0,4,3,2,1:T(8,128)(2,1)} %get-tuple-element.55), kind=kLoop, calls=%fused_computation.93 | loop fusion | bytes 196608 | tf_op jit(solution)/shard_map/slice | solution.py:81
  44.7 1.8 %copy.54 = bf16[16,3,4,128]{3,0,2,1:T(8,128)(2,1)} copy(bf16[16,3,4,128]{0,3,2,1:T(8,128)(2,1)} %bitcast.90) | data formatting | bytes 98304 | tf_op jit(solution)/shard_map/slice | solution.py:81
  46.4 1.8 %copy.55 = bf16[16,3,4,128]{3,0,2,1:T(8,128)(2,1)} copy(bf16[16,3,4,128]{0,3,2,1:T(8,128)(2,1)} %bitcast.89) | data formatting | bytes 98304 | tf_op jit(solution)/shard_map/slice | solution.py:82
  48.2 0.8 pad_maximum_fusion.11
  48.9 2.3 %collective-permute-start.4 = (bf16[32,1,4,128]{3,0,2,1:T(8,128)(2,1)S(1)}, bf16[32,1,4,128]{3,0,2,1:T(8,128)(2,1)S(1)}, u32[]{:S(2)}, u32[]{:S(2)}) collective-permute-start(bf16[32,1,4,128]{3,0,2,1:T(8,128)(2,1)S(1)} %get-tuple-element.45), channel_id=1, source_target_pairs={{0,32},{32,64},{64,96},{96,128},{128,160},{160,192},{192,224},{224... | collective-permute-start | bytes 98312 | tf_op jit(solution)/shard_map/ppermute | solution.py:14
  51.3 2.0 %collective-permute-start.5 = (bf16[32,1,4,128]{3,0,2,1:T(8,128)(2,1)S(1)}, bf16[32,1,4,128]{3,0,2,1:T(8,128)(2,1)S(1)}, u32[]{:S(2)}, u32[]{:S(2)}) collective-permute-start(bf16[32,1,4,128]{3,0,2,1:T(8,128)(2,1)S(1)} %get-tuple-element.46), channel_id=1, source_target_pairs={{32,0},{64,32},{96,64},{128,96},{160,128},{192,160},{224,192},{256... | collective-permute-start | bytes 98312 | tf_op jit(solution)/shard_map/ppermute | solution.py:15
  53.3 0.7 fusion.29
  54.0 2.5 %collective-permute-done.5 = bf16[32,1,4,128]{3,0,2,1:T(8,128)(2,1)S(1)} collective-permute-done((bf16[32,1,4,128]{3,0,2,1:T(8,128)(2,1)S(1)}, bf16[32,1,4,128]{3,0,2,1:T(8,128)(2,1)S(1)}, u32[]{:S(2)}, u32[]{:S(2)}) %collective-permute-start.5) | collective-permute-done | bytes 32800 | tf_op jit(solution)/shard_map/ppermute | solution.py:15
  56.5 0.8 pad_maximum_fusion.5
  57.3 3.1 %collective-permute-start.6 = (bf16[32,5,1,128]{3,0,2,1:T(8,128)(2,1)S(1)}, bf16[32,5,1,128]{3,0,2,1:T(8,128)(2,1)S(1)}, u32[]{:S(2)}, u32[]{:S(2)}) collective-permute-start(bf16[32,5,1,128]{3,0,2,1:T(8,128)(2,1)S(1)} %get-tuple-element.39), channel_id=1, source_target_pairs={{0,1},{1,2},{2,3},{3,4},{4,5},{5,6},{6,7},{7,8},{8,9},{9,10},{10,1... | collective-permute-start | bytes 122888 | tf_op jit(solution)/shard_map/ppermute | solution.py:14
  60.4 1.3 collective-permute-start.7
  61.7 1.4 %broadcast_multiply_fusion.1 = (f32[16,3,4,128]{3,0,2,1:T(8,128)}, f32[16,3,4,128]{3,0,2,1:T(8,128)}) fusion(f32[3,4,128]{2,1,0:T(4,128)S(1)} %get-tuple-element.49, f32[16]{0:T(128)} %param.22, f32[3,4,128]{2,1,0:T(4,128)S(1)} %get-tuple-element.50), kind=kLoop, calls=%fused_computation.39 | loop fusion | flops 49152 | bytes 208960 | tf_op jit(solution)/shard_map/mul | solution.py:74
  63.1 2.0 %collective-permute-done.7 = bf16[32,5,1,128]{3,0,2,1:T(8,128)(2,1)S(1)} collective-permute-done((bf16[32,5,1,128]{3,0,2,1:T(8,128)(2,1)S(1)}, bf16[32,5,1,128]{3,0,2,1:T(8,128)(2,1)S(1)}, u32[]{:S(2)}, u32[]{:S(2)}) %collective-permute-start.7) | collective-permute-done | bytes 40992 | tf_op jit(solution)/shard_map/ppermute | solution.py:15
  65.1 1.6 %pad_maximum_fusion.1 = bf16[32,5,6,128]{3,0,2,1:T(8,128)(2,1)} fusion(bf16[32,5,1,128]{3,0,2,1:T(8,128)(2,1)S(1)} %collective-permute-done.7, bf16[32,1,4,128]{3,0,2,1:T(8,128)(2,1)S(1)} %collective-permute-done.5, bf16[16,3,4,128]{3,0,2,1:T(8,128)(2,1)} %copy.55, bf16[16,3,4,128]{3,0,2,1:T(8,128)(2,1)} %copy.54, ...), kind=kLoop, calls=%fused_computation.34 | loop fusion | flops 1474560 | bytes 491520 | tf_op jit(solution)/shard_map/concatenate | solution.py:16
  66.7 2.6 %gather_fusion.1 = bf16[108,32,128]{2,1,0:T(8,128)(2,1)} fusion(bf16[32,30,128]{2,0,1:T(8,128)(2,1)} %bitcast.81, s32[1024]{0:T(1024)S(1)} %pad_clamp_fusion), kind=kCustom, calls=%fused_computation.1.clone | custom fusion | bytes 1769904 | tf_op jit(solution)/shard_map/jit(_take)/gather | solution.py:66
  69.3 3.2 %fusion.2 = f32[32,3,4,128]{3,0,2,1:T(8,128)} fusion(bf16[3,4,9,128,128]{4,3,2,1,0:T(8,128)(2,1)S(1)} %copy-done, bf16[3,4,9,32,128]{4,3,2,1,0:T(8,128)(2,1)} %bitcast.87, pred[3,4,9]{2,1,0:T(4,128)(4,1)} %get-tuple-element.35, bf16[3,4,9]{2,1,0:T(4,128)(2,1)S(1)} %convert_element_type.19, f32[16,3,4,128]{3,0,2,1:T(8,128)} %get-tuple-element.52, ...), kind=kOutput, calls=%fused_computation.8 | convolution fusion | flops 114229248 | bytes 4817220 | tf_op jit(solution)/shard_map/abspq,tabsq->tabp/dot_general | solution.py:67
  72.5 2.1 %copy.56 = f32[32,3,4,128]{0,3,2,1:T(8,128)} copy(f32[32,3,4,128]{3,0,2,1:T(8,128)} %fusion.2) | data formatting | bytes 393216 | tf_op jit(solution)/shard_map/add | solution.py:75
  74.6 2.4 %fusion = f32[32,3,4,8,16]{0,4,3,2,1:T(8,128)S(1)} fusion(f32[3,4,8,16,16]{4,3,2,1,0:T(8,128)} %param.19, f32[32,3,4,8,16]{0,4,3,2,1:T(8,128)} %bitcast.86, f32[3,4,8,16]{3,2,1,0:T(8,128)} %fusion.21), kind=kOutput, calls=%fused_computation.4 | convolution fusion | flops 9535488 | bytes 497664 | tf_op jit(solution)/shard_map/abclm,tabcm->tabcl/dot_general | solution.py:77
  76.9 1.1 slice.106
  78.1 2.0 %copy.58 = f32[1,16,3,4,128]{4,0,1,3,2:T(1,128)} copy(f32[1,16,3,4,128]{1,4,3,2,0:T(8,128)} %bitcast.83) | data formatting | bytes 196608 | tf_op jit(solution)/shard_map/broadcast_in_dim | solution.py:83
  80.1 3.2 %convolution_bitcast_fusion.2 = f32[5,5]{1,0:T(8,128)S(1)} fusion(f32[1,16,3,4,128]{4,0,1,3,2:T(1,128)} %copy.58, f32[4,16,3,4,128]{4,0,1,3,2:T(4,128)} %copy.57), kind=kOutput, calls=%fused_computation.11 | convolution fusion | flops 7495680 | bytes 491620 | tf_op jit(solution)/shard_map/ktabp,jtabp->kj/dot_general | solution.py:84
  83.3 0.1 reshape.87
  83.4 16.6 %all_to_all.24 = f32[16,1,128]{2,1,0:T(1,128)S(1)} all-to-all(f32[16,1,128]{2,1,0:T(1,128)S(1)} %broadcast_in_dim.28), channel_id=1, replica_groups=mesh['lat'=16,'lon'=32] {'lat'}, dimensions={0} | all-to-all | bytes 16384 | tf_op jit(solution)/shard_map/all_to_all | solution.py:29
  100.0 0.6 broadcast_in_dim.29
  100.7 17.5 %all-to-all-start.3 = ((f32[32,1,128]{2,1,0:T(1,128)}), f32[32,1,128]{2,1,0:T(1,128)S(1)}, u32[]{:S(2)}, u32[]{:S(2)}) async-start(f32[32,1,128]{2,1,0:T(1,128)} %broadcast_in_dim.29), calls=%async_computation.3 | async-start | bytes 32768 | tf_op jit(solution)/shard_map/all_to_all | solution.py:29
  118.2 2.0 %copy.62 = f32[16,3,4,128]{3,2,1,0:T(4,128)} copy(f32[16,3,4,128]{0,3,2,1:T(8,128)} %bitcast.84) | data formatting | bytes 196608
  120.2 6.5 %all-to-all-done.3 = f32[32,1,128]{2,1,0:T(1,128)S(1)} async-done(((f32[32,1,128]{2,1,0:T(1,128)}), f32[32,1,128]{2,1,0:T(1,128)S(1)}, u32[]{:S(2)}, u32[]{:S(2)}) %all-to-all-start.3) | async-done | bytes 16416 | tf_op jit(solution)/shard_map/all_to_all | solution.py:29
  126.7 0.5 reduce_sum.64
  127.2 0.7 reshape.88
  127.9 0.2 slice_reduce_fusion.2
  128.1 0.6 slice.96
  128.7 0.6 multiply_reduce_fusion.2
  129.3 0.7 multiply_reduce_fusion.1
  131.9 2.6 %fusion.17 = f32[1,16,3,4,128]{4,0,3,2,1:T(1,128)} fusion(f32[4,16,3,4,128]{4,3,2,1,0:T(4,128)} %param.23, f32[4]{0:T(128)S(1)} %slice_reduce_fusion.2), kind=kOutput, calls=%fused_computation.29 | convolution fusion | flops 1179648 | bytes 491536 | tf_op jit(solution)/shard_map/k,ktabp->tabp/dot_general | solution.py:87
  135.6 1.6 %sub.32 = f32[16,3,4,128]{3,2,1,0:T(4,128)} subtract(f32[16,3,4,128]{3,2,1,0:T(4,128)} %copy.62, f32[16,3,4,128]{3,2,1,0:T(4,128)} %bitcast.91) | non-fusion elementwise | flops 24576 | bytes 294912 | tf_op jit(solution)/shard_map/sub | solution.py:87
  137.3 1.3 pad_maximum_fusion.14
  138.6 1.6 %broadcast_divide_fusion = f32[16,3,4,128]{3,2,1,0:T(4,128)} fusion(f32[16,3,4,128]{3,2,1,0:T(4,128)} %sub.32, f32[]{:T(128)} %get-tuple-element.16), kind=kLoop, calls=%fused_computation.37 | loop fusion | flops 24576 | bytes 196612 | tf_op jit(solution)/shard_map/div | solution.py:99
  (17 shorter events, 0.1 us)
Async XLA Ops:
  0.6 29.8 %copy-start = (bf16[3,4,9,128,128]{4,3,2,1,0:T(8,128)(2,1)S(1)}, bf16[3,4,9,128,128]{4,3,2,1,0:T(8,128)(2,1)}, u32[]{:S(2)}) copy-start(bf16[3,4,9,128,128]{4,3,2,1,0:T(8,128)(2,1)} %param.16) | copy-start | bytes 10616836
  1.7 1.0 copy-start.1
  2.7 0.6 copy-start.2
  3.3 15.6 %collective-permute-start = (bf16[32,1,4,128]{3,0,2,1:T(8,128)(2,1)}, bf16[32,1,4,128]{3,0,2,1:T(8,128)(2,1)}, u32[]{:S(2)}, u32[]{:S(2)}) collective-permute-start(bf16[32,1,4,128]{3,0,2,1:T(8,128)(2,1)} %get-tuple-element.47), channel_id=1, source_target_pairs={{0,32},{32,64},{64,96},{96,128},{128,160},{160,192},{192,224},{224... | collective-permute-start | bytes 98312 | tf_op jit(solution)/shard_map/ppermute | solution.py:14
  7.9 11.0 %collective-permute-start.1 = (bf16[32,1,4,128]{3,0,2,1:T(8,128)(2,1)}, bf16[32,1,4,128]{3,0,2,1:T(8,128)(2,1)}, u32[]{:S(2)}, u32[]{:S(2)}) collective-permute-start(bf16[32,1,4,128]{3,0,2,1:T(8,128)(2,1)} %get-tuple-element.48), channel_id=1, source_target_pairs={{32,0},{64,32},{96,64},{128,96},{160,128},{192,160},{224,192},{256... | collective-permute-start | bytes 98312 | tf_op jit(solution)/shard_map/ppermute | solution.py:15
  18.9 11.5 %copy-start.4 = (pred[3,4,9]{2,1,0:T(4,128)(4,1)S(1)}, pred[3,4,9]{2,1,0:T(4,128)(4,1)}, u32[]{:S(2)}) copy-start(pred[3,4,9]{2,1,0:T(4,128)(4,1)} %get-tuple-element.35) | copy-start | bytes 328
  19.8 5.3 %collective-permute-start.2 = (bf16[32,5,1,128]{3,0,2,1:T(8,128)(2,1)S(1)}, bf16[32,5,1,128]{3,0,2,1:T(8,128)(2,1)S(1)}, u32[]{:S(2)}, u32[]{:S(2)}) collective-permute-start(bf16[32,5,1,128]{3,0,2,1:T(8,128)(2,1)S(1)} %get-tuple-element.41), channel_id=1, source_target_pairs={{0,1},{1,2},{2,3},{3,4},{4,5},{5,6},{6,7},{7,8},{8,9},{9,10},{10,1... | collective-permute-start | bytes 122888 | tf_op jit(solution)/shard_map/ppermute | solution.py:14
  21.1 5.2 %collective-permute-start.3 = (bf16[32,5,1,128]{3,0,2,1:T(8,128)(2,1)S(1)}, bf16[32,5,1,128]{3,0,2,1:T(8,128)(2,1)S(1)}, u32[]{:S(2)}, u32[]{:S(2)}) collective-permute-start(bf16[32,5,1,128]{3,0,2,1:T(8,128)(2,1)S(1)} %get-tuple-element.42), channel_id=1, source_target_pairs={{1,0},{2,1},{3,2},{4,3},{5,4},{6,5},{7,6},{8,7},{9,8},{10,9},{11,1... | collective-permute-start | bytes 122888 | tf_op jit(solution)/shard_map/ppermute | solution.py:15
  48.9 5.1 %collective-permute-start.4 = (bf16[32,1,4,128]{3,0,2,1:T(8,128)(2,1)S(1)}, bf16[32,1,4,128]{3,0,2,1:T(8,128)(2,1)S(1)}, u32[]{:S(2)}, u32[]{:S(2)}) collective-permute-start(bf16[32,1,4,128]{3,0,2,1:T(8,128)(2,1)S(1)} %get-tuple-element.45), channel_id=1, source_target_pairs={{0,32},{32,64},{64,96},{96,128},{128,160},{160,192},{192,224},{224... | collective-permute-start | bytes 98312 | tf_op jit(solution)/shard_map/ppermute | solution.py:14
  51.3 5.2 %collective-permute-start.5 = (bf16[32,1,4,128]{3,0,2,1:T(8,128)(2,1)S(1)}, bf16[32,1,4,128]{3,0,2,1:T(8,128)(2,1)S(1)}, u32[]{:S(2)}, u32[]{:S(2)}) collective-permute-start(bf16[32,1,4,128]{3,0,2,1:T(8,128)(2,1)S(1)} %get-tuple-element.46), channel_id=1, source_target_pairs={{32,0},{64,32},{96,64},{128,96},{160,128},{192,160},{224,192},{256... | collective-permute-start | bytes 98312 | tf_op jit(solution)/shard_map/ppermute | solution.py:15
  57.3 5.8 %collective-permute-start.6 = (bf16[32,5,1,128]{3,0,2,1:T(8,128)(2,1)S(1)}, bf16[32,5,1,128]{3,0,2,1:T(8,128)(2,1)S(1)}, u32[]{:S(2)}, u32[]{:S(2)}) collective-permute-start(bf16[32,5,1,128]{3,0,2,1:T(8,128)(2,1)S(1)} %get-tuple-element.39), channel_id=1, source_target_pairs={{0,1},{1,2},{2,3},{3,4},{4,5},{5,6},{6,7},{7,8},{8,9},{9,10},{10,1... | collective-permute-start | bytes 122888 | tf_op jit(solution)/shard_map/ppermute | solution.py:14
  60.4 4.7 %collective-permute-start.7 = (bf16[32,5,1,128]{3,0,2,1:T(8,128)(2,1)S(1)}, bf16[32,5,1,128]{3,0,2,1:T(8,128)(2,1)S(1)}, u32[]{:S(2)}, u32[]{:S(2)}) collective-permute-start(bf16[32,5,1,128]{3,0,2,1:T(8,128)(2,1)S(1)} %get-tuple-element.40), channel_id=1, source_target_pairs={{1,0},{2,1},{3,2},{4,3},{5,4},{6,5},{7,6},{8,7},{9,8},{10,9},{11,1... | collective-permute-start | bytes 122888 | tf_op jit(solution)/shard_map/ppermute | solution.py:15
  100.7 26.0 %all-to-all-start.3 = ((f32[32,1,128]{2,1,0:T(1,128)}), f32[32,1,128]{2,1,0:T(1,128)S(1)}, u32[]{:S(2)}, u32[]{:S(2)}) async-start(f32[32,1,128]{2,1,0:T(1,128)} %broadcast_in_dim.29), calls=%async_computation.3 | async-start | bytes 32768 | tf_op jit(solution)/shard_map/all_to_all | solution.py:29
  128.1 9.1 %copy-start.3 = (f32[4]{0:T(128)}, f32[4]{0:T(128)S(1)}, u32[]{:S(2)}) copy-start(f32[4]{0:T(128)S(1)} %slice_reduce_fusion.2) | copy-start | bytes 52

commit v2 on v0

v2 whole, which is shorter than its diff:
```python
import functools

import jax
import jax.numpy as jnp
from jax import lax
from jax.experimental import pallas as pl
from jax.experimental.pallas import tpu as pltpu
from jax.sharding import PartitionSpec as P

F32 = jnp.float32
BF16 = jnp.bfloat16
VMEM = pl.BlockSpec(memory_space=pltpu.VMEM)
SMEM = pl.BlockSpec(memory_space=pltpu.SMEM)
ANY = pl.BlockSpec(memory_space=pl.ANY)
NT = (((1,), (1,)), ((), ()))


def call(kernel, outs, ins, out_specs, scratch=(), flops=0, size=0, limit=16):
    return pl.pallas_call(
        kernel,
        out_shape=outs,
        in_specs=ins,
        out_specs=out_specs,
        scratch_shapes=list(scratch),
        compiler_params=pltpu.CompilerParams(vmem_limit_bytes=limit * 2**20),
        cost_estimate=pl.CostEstimate(flops=flops, bytes_accessed=size, transcendentals=0),
    )


def like(shape, dtype=F32):
    return jax.ShapeDtypeStruct(shape, dtype)


def iota(shape, dim):
    return lax.broadcasted_iota(jnp.int32, shape, dim)


def pack_kernel(lon, c_ref, v_ref, x_ref, first_ref, last_ref, own_ref):
    rows = x_ref.shape[0]
    tracers = c_ref.shape[0] // rows
    for r in range(rows):
        at = pl.ds(r, tracers, stride=rows)
        x = jnp.concatenate([c_ref[at, :], v_ref[at, :]], 0).astype(BF16)
        x_ref[r] = x
        if r < lon:
            first_ref[r] = x
        if r >= rows - lon:
            last_ref[r - (rows - lon)] = x
    own_ref[0] = c_ref[:rows, :]
    own_ref[1] = v_ref[:rows, :]


def sources(own_c, own_v, rate):
    denom = own_c * own_c + 1.0
    uptake = rate * own_c * own_c / denom
    slope = rate * 2.0 * own_c / (denom * denom)
    return uptake, slope * own_v


def prep_kernel(
    total_lon,
    pattern_ref,
    live_ref,
    inverse_ref,
    depth_ref,
    rate_ref,
    own_ref,
    stoich_ref,
    basis_ref,
    index_ref,
    high_ref,
    low_ref,
    wet_ref,
    source_ref,
    share_ref,
    gram_ref,
):
    lat, lon, slots = pattern_ref.shape
    rows, points, levels = inverse_ref.shape
    pattern = pattern_ref[...]
    itself = pattern[:, :, :1]
    far_lat = pattern // total_lon - itself // total_lon
    far_lon = pattern % total_lon - itself % total_lon
    shape = pattern.shape
    place = (iota(shape, 0) + 1 + far_lat) * (lon + 2) + iota(shape, 1) + 1 + far_lon
    index_ref[...] = jnp.where(live_ref[...] > 0, place, (lat + 2) * (lon + 2))

    lane = iota((rows, points), 1)
    depth = depth_ref[...]
    below = jnp.zeros((rows, points), jnp.int32)
    for k in range(points // levels):
        below = jnp.where(lane // levels == k, depth[:, k : k + 1], below)
    wet = (lane % levels < below).astype(F32)
    wet_ref[...] = wet

    uptake, pull = sources(own_ref[0], own_ref[1], rate_ref[...])
    source_ref[0] = uptake
    source_ref[1] = pull

    tracers = share_ref.shape[0]
    square = (tracers, tracers)
    stoich = jnp.broadcast_to(stoich_ref[...], square)
    column = jnp.sum(jnp.where(iota(square, 0) == iota(square, 1), stoich, 0.0), 1, keepdims=True)
    share_ref[...] = jnp.broadcast_to(column, share_ref.shape)

    spread = (iota((levels, points), 1) % levels == iota((levels, points), 0)).astype(BF16)
    full = (points, points)
    same = iota(full, 0) // levels == iota(full, 1) // levels
    for r in range(rows):
        inverse = inverse_ref[r]
        high = inverse.astype(BF16)
        low = (inverse - high.astype(F32)).astype(BF16)
        keep = jnp.where(same, wet[r : r + 1, :], 0.0)
        for ref, part in ((high_ref, high), (low_ref, low)):
            tiled = jnp.dot(part, spread, preferred_element_type=F32)
            ref[r] = (tiled * keep).astype(BF16)

    gram_ref[...] = jnp.zeros(gram_ref.shape, F32)
    count = basis_ref.shape[0]
    row = 0
    for k in range(count):
        for j in range(k, count):
            gram_ref[row : row + 1, :] = jnp.sum(basis_ref[k] * basis_ref[j], 0, keepdims=True)
            row += 1


def fill(pad_ref, x_ref, north_ref, south_ref, west_ref, east_ref, lat, lon):
    wide = lon + 2
    for j in range(lon):
        pad_ref[1 + j] = north_ref[j]
        pad_ref[(lat + 1) * wide + 1 + j] = south_ref[j]
        for i in range(lat):
            pad_ref[(i + 1) * wide + 1 + j] = x_ref[i * lon + j]
    for i in range(lat + 2):
        pad_ref[i * wide] = west_ref[i]
        pad_ref[i * wide + lon + 1] = east_ref[i]
    pad_ref[(lat + 2) * wide] = jnp.zeros(pad_ref.shape[1:], BF16)


def transport(r, index_ref, pad_ref, held_ref, lon, slots):
    total = None
    for s in range(slots):
        x = pad_ref[index_ref[r // lon, r % lon, s]]
        term = lax.dot_general(x, held_ref[r * slots + s], NT, preferred_element_type=F32)
        total = term if total is None else total + term
    return total


def mix(z, high, low, wet):
    z_high = z.astype(BF16)
    z_low = (z - z_high.astype(F32)).astype(BF16)
    dot = functools.partial(lax.dot_general, dimension_numbers=NT, preferred_element_type=F32)
    return (dot(z_high, high) + (dot(z_high, low) + dot(z_low, high))) * wet


def fetches(blocks_ref, held_ref, sems, slots, rows):
    copies = []
    for r in range(rows):
        part = pl.ds(r * slots, slots)
        copies.append(pltpu.make_async_copy(blocks_ref.at[part], held_ref.at[part], sems.at[r]))
        copies[-1].start()
    return copies


def first_kernel(
    lat,
    lon,
    slots,
    index_ref,
    x_ref,
    north_ref,
    south_ref,
    west_ref,
    east_ref,
    high_ref,
    low_ref,
    wet_ref,
    source_ref,
    share_ref,
    rate_ref,
    blocks_ref,
    y_ref,
    first_ref,
    last_ref,
    pull_ref,
    pad_ref,
    held_ref,
    own_ref,
    sems,
):
    rows = lat * lon
    copies = fetches(blocks_ref, held_ref, sems, slots, rows)
    fill(pad_ref, x_ref, north_ref, south_ref, west_ref, east_ref, lat, lon)
    share = share_ref[...]
    tracers = share.shape[0]
    for r in range(rows):
        copies[r].wait()
        at = slice(r, r + 1)
        added = jnp.concatenate([share * source_ref[0, at, :], share * source_ref[1, at, :]], 0)
        z = transport(r, index_ref, pad_ref, held_ref, lon, slots) + added
        out = mix(z, high_ref[r], low_ref[r], wet_ref[at, :])
        own_ref[0, at, :] = out[:1]
        own_ref[1, at, :] = out[tracers : tracers + 1]
        y = out[tracers:].astype(BF16)
        y_ref[r] = y
        if r < lon:
            first_ref[r] = y
        if r >= rows - lon:
            last_ref[r - (rows - lon)] = y
    pull_ref[...] = sources(own_ref[0], own_ref[1], rate_ref[...])[1]


def second_kernel(
    lat,
    lon,
    slots,
    index_ref,
    x_ref,
    north_ref,
    south_ref,
    west_ref,
    east_ref,
    high_ref,
    low_ref,
    wet_ref,
    pull_ref,
    share_ref,
    gram_ref,
    basis_ref,
    blocks_ref,
    product_ref,
    sums_ref,
    pad_ref,
    held_ref,
    sems,
):
    rows = lat * lon
    copies = fetches(blocks_ref, held_ref, sems, slots, rows)
    fill(pad_ref, x_ref, north_ref, south_ref, west_ref, east_ref, lat, lon)
    share = share_ref[...]
    tracers = share.shape[0]
    for r in range(rows):
        copies[r].wait()
        at = slice(r, r + 1)
        z = transport(r, index_ref, pad_ref, held_ref, lon, slots) + share * pull_ref[at, :]
        out = mix(z, high_ref[r], low_ref[r], wet_ref[at, :])
        product_ref[pl.ds(r, tracers, stride=rows), :] = out
    product = product_ref[...]
    parts = [gram_ref[...]]
    count = basis_ref.shape[0]
    pairs = count * (count + 1) // 2
    height = gram_ref.shape[0]
    spot = iota(gram_ref.shape, 0)
    all_sums = gram_ref[...]
    for k in range(count + 1):
        other = basis_ref[k] if k < count else product
        part = jnp.sum(product * other, 0, keepdims=True)
        all_sums = jnp.where(spot == pairs + k, part, all_sums)
    column = jnp.sum(all_sums, 1, keepdims=True)
    row = jnp.sum(jnp.where(spot == iota(spot.shape, 1), column, 0.0), 0, keepdims=True)
    sums_ref[...] = jnp.broadcast_to(row, sums_ref.shape)


def last_kernel(parts_ref, product_ref, basis_ref, next_ref, coeffs_ref, flag_ref):
    count = basis_ref.shape[0]
    row = jnp.sum(parts_ref[...], 0, keepdims=True)
    lane = iota(row.shape, 1)

    def pick(at):
        return jnp.sum(jnp.where(lane == at, row, 0.0), 1, keepdims=True)

    pairs = count * (count + 1) // 2
    heights = [pick(pairs + k) for k in range(count)]
    whole = pick(pairs + count)
    cross = jnp.zeros((1, 1), F32)
    at = 0
    for k in range(count):
        for j in range(k, count):
            twice = 1.0 if k == j else 2.0
            cross = cross + twice * (heights[k] * heights[j] * pick(at))
            at += 1
    squares = sum(h * h for h in heights)
    short = whole - 2.0 * squares + cross
    size = whole + 2.0 * squares + cross
    beta = jnp.sqrt(jnp.maximum(short, 0.0) + 1e-06)
    rest = product_ref[...]
    for k in range(count):
        rest = rest - heights[k] * basis_ref[k]
    next_ref[...] = rest / beta
    for k in range(count):
        coeffs_ref[k] = heights[k][0, 0]
    coeffs_ref[count] = beta[0, 0]
    flag_ref[0] = jnp.where(short < 0.01 * size, 1, 0)[0, 0]


def summed(rows):
    row = jnp.sum(lax.all_to_all(rows, "lat", 0, 0), 0, keepdims=True)
    rows = jnp.broadcast_to(row, (lax.axis_size("lon"), row.shape[1]))
    return lax.all_to_all(rows, "lon", 0, 0)


def halo(x, first, last, lat, lon):
    def moved(a, axis, step):
        size = lax.axis_size(axis)
        pairs = [(i, i + step) for i in range(size) if 0 <= i + step < size]
        return lax.ppermute(a, axis, pairs)

    north = moved(last, "lat", 1)
    south = moved(first, "lat", -1)
    grid = x.reshape((lat, lon) + x.shape[1:])
    right = jnp.concatenate([north[None, lon - 1], grid[:, lon - 1], south[None, lon - 1]], 0)
    left = jnp.concatenate([north[None, 0], grid[:, 0], south[None, 0]], 0)
    west = moved(right, "lon", 1)
    east = moved(left, "lon", -1)
    return north, south, west, east


def body(
    base_state,
    tangent,
    blocks,
    pattern,
    live,
    column_inverse,
    col_depth,
    uptake_rate,
    stoich,
    basis,
):
    tracers, lat, lon, points = base_state.shape
    columns, levels = column_inverse.shape[2:4]
    slots = pattern.shape[2]
    count = basis.shape[0]
    rows = lat * lon
    total_lon = lon * lax.axis_size("lon")
    size = tracers * rows
    places = (lat + 2) * (lon + 2) + 1
    flat_basis = basis.reshape(count, size, points)
    rate = uptake_rate.reshape(rows, points)
    matrices = blocks.reshape(rows * slots, points, points)

    x, first, last, own = call(
        functools.partial(pack_kernel, lon),
        (
            like((rows, 2 * tracers, points), BF16),
            like((lon, 2 * tracers, points), BF16),
            like((lon, 2 * tracers, points), BF16),
            like((2, rows, points)),
        ),
        [VMEM] * 2,
        [VMEM] * 4,
        size=400000,
    )(base_state.reshape(size, points), tangent.reshape(size, points))

    index, high, low, wet, source, share, gram = call(
        functools.partial(prep_kernel, total_lon),
        (
            like((lat, lon, slots), jnp.int32),
            like((rows, points, points), BF16),
            like((rows, points, points), BF16),
            like((rows, points)),
            like((2, rows, points)),
            like((tracers, points)),
            like((16, points)),
        ),
        [VMEM] * 8,
        [VMEM] * 7,
        size=2500000,
    )(
        pattern,
        live,
        column_inverse.reshape(rows, points, levels),
        col_depth.reshape(rows, columns),
        rate,
        own,
        stoich.reshape(1, tracers),
        flat_basis,
    )

    north, south, west, east = halo(x, first, last, lat, lon)
    held = pltpu.VMEM((rows * slots, points, points), BF16)
    work = 2 * 2 * tracers * rows * slots * points * points
    x, first, last, pull = call(
        functools.partial(first_kernel, lat, lon, slots),
        (
            like((rows, tracers, points), BF16),
            like((lon, tracers, points), BF16),
            like((lon, tracers, points), BF16),
            like((rows, points)),
        ),
        [SMEM] + [VMEM] * 11 + [ANY],
        [VMEM] * 4,
        scratch=[
            pltpu.VMEM((places, 2 * tracers, points), BF16),
            held,
            pltpu.VMEM((2, rows, points), F32),
            pltpu.SemaphoreType.DMA((rows,)),
        ],
        flops=work,
        size=5000000,
    )(index, x, north, south, west, east, high, low, wet, source, share, rate, matrices)

    north, south, west, east = halo(x, first, last, lat, lon)
    product, sums = call(
        functools.partial(second_kernel, lat, lon, slots),
        (like((size, points)), like((lax.axis_size("lat"), points))),
        [SMEM] + [VMEM] * 12 + [ANY],
        [VMEM] * 2,
        scratch=[
            pltpu.VMEM((places, tracers, points), BF16),
            held,
            pltpu.SemaphoreType.DMA((rows,)),
        ],
        flops=work // 2,
        size=5000000,
    )(index, x, north, south, west, east, high, low, wet, pull, share, gram, flat_basis, matrices)

    parts = summed(sums)
    following, coeffs, flag = call(
        last_kernel,
        (like((size, points)), like((count + 1,)), like((1,), jnp.int32)),
        [VMEM] * 3,
        [VMEM, SMEM, SMEM],
        size=700000,
    )(parts, product, flat_basis)

    def again(carry):
        following, coeffs, flag = carry
        rest = product - jnp.einsum(
            "k,ksp->sp", coeffs[:count], flat_basis, precision=lax.Precision.HIGHEST
        )
        part = jnp.pad(jnp.sum(rest * rest).reshape(1, 1), ((0, 0), (0, points - 1)))
        squared = jnp.sum(summed(jnp.broadcast_to(part, (lax.axis_size("lat"), points))), 0)[0]
        beta = jnp.sqrt(squared + 1e-06)
        return rest / beta, jnp.concatenate([coeffs[:count], beta[None]]), flag * 0

    following, coeffs, flag = lax.while_loop(
        lambda carry: carry[2][0] > 0, again, (following, coeffs, flag)
    )
    shape = base_state.shape
    return product.reshape(shape), following.reshape(shape), coeffs


def solution(mesh):
    placed = (
        P(None, "lat", "lon", None),
        P(None, "lat", "lon", None),
        P("lat", "lon", None, None, None),
        P("lat", "lon", None),
        P("lat", "lon", None),
        P("lat", "lon", None, None, None),
        P("lat", "lon", None),
        P("lat", "lon", None),
        P(),
        P(None, None, "lat", "lon", None),
    )
    return jax.shard_map(
        body,
        mesh=mesh,
        in_specs=placed,
        out_specs=(P(None, "lat", "lon", None), P(None, "lat", "lon", None), P()),
        check_vma=False,
    )
```

time: 298 us -> 104 us (0.35)
  blocking collectives: 204 us -> 43.2 us
  Pallas kernels: 0 us -> 18.8 us
  other arithmetic: 18.1 us -> 0.07 us
  local copies, waits for them, and re-layouts: 25.9 us -> 9.01 us
  matrix products: 16.8 us -> 0 us
    psum x2 -> x0, blocking collectives: 204 us -> none  [the longest x1 110 us: body(): heights = lax.psum(local_heights, ('lat', 'lon'))]
    all_to_all x0 -> x2, blocking collectives: none -> 43.2 us  [the longest x1 26.6 us: summed(): return lax.all_to_all(rows, 'lon', 0, 0)]
    pallas_call x0 -> x5, Pallas kernels: none -> 18.8 us  [the longest x1 8.82 us: body(): call(functools.partial(first_kernel, lat, lon, slots), (like((rows, trace...]
    dot_general x6 -> x0, matrix products: 16.8 us -> none  [the longest x2 6.44 us: body(): jnp.einsum('abspq,tabsq->tabp', blocks, gathered, preferred_element_type=...]
    slice x6 -> x4, local copies, waits for them, and re-layouts: 10.1 us -> 0.01 us  [halo(): left = jnp.concatenate([north[None, 0], grid[:, 0], south[None, 0]], 0)]
    gather x2 -> x0, local copies, waits for them, and re-layouts: 5.14 us -> none  [body(): gathered = jnp.take(flat, local_index, axis=1) * live_weight]
    add x2 -> x0, local copies, waits for them, and re-layouts: 4.15 us -> none  [body(): moved + source]
    concatenate x3 -> x4, other arithmetic: 3.7 us -> 0.03 us  [the longest x2 0.02 us: halo(): left = jnp.concatenate([north[None, 0], grid[:, 0], south[None, 0]], 0)]
  transfers between devices with their start and end apart: 8 -> 8, of which waited for: 3 -> 3; matrix products, arithmetic and copies ran while one was open for 3% -> 1% of each run, Pallas kernels for 0% -> 1%
where the time goes in v2:
time: 104 us; the launch traced here: 103 us
  blocking collectives  43.2 us (42%)
  starting transfers between devices  23.4 us (22%)
  Pallas kernels  18.8 us (18%)
  local copies, waits for them, and re-layouts  9.01 us (9%)
  waiting for transfers between devices  6.93 us (7%)
    all_to_all x1, blocking collectives, summed(): return lax.all_to_all(rows, 'lon', 0, 0)  26.6 us
    ppermute x8, starting transfers between devices, moved(): return lax.ppermute(a, axis, pairs)  23.4 us
    all_to_all x1, blocking collectives, summed(): row = jnp.sum(lax.all_to_all(rows, 'lat', 0, 0), 0, keepdims=True)  16.6 us
    pallas_call x1, Pallas kernels, body(): call(functools.partial(first_kernel, lat, lon, slots), (like((rows, trace...  8.82 us
    pallas_call x1, Pallas kernels, body(): call(functools.partial(second_kernel, lat, lon, slots), (like((size, poin...  7.72 us
    unnamed x22, local copies, waits for them, and re-layouts  7.58 us
    ppermute x8, waiting for transfers between devices, moved(): return lax.ppermute(a, axis, pairs)  6.93 us
  transfers between devices with their start and end apart: 8, of which 3 were waited for; matrix products, arithmetic and copies ran while one was open for 1% of the time, Pallas kernels for 1%

profile of v2, /device:TPU:1, one launch (start us, length us, event | category | flops | bytes accessed | tf_op | source)
XLA Modules:
  0.0 102.9 jit_solution(13724066660166432631)
XLA Ops:
  0.6 0.0 copy-start.3
  0.6 0.9 copy-done.3
  1.5 0.0 copy-start.4
  1.5 0.9 copy-done.4
  2.4 0.0 copy-start.8
  2.4 4.7 %collective-permute-start = (bf16[4,32,128]{2,1,0:T(8,128)(2,1)S(1)}, bf16[4,32,128]{2,1,0:T(8,128)(2,1)S(1)}, u32[]{:S(2)}, u32[]{:S(2)}) collective-permute-start(bf16[4,32,128]{2,1,0:T(8,128)(2,1)S(1)} %get-tuple-element.52), channel_id=1, source_target_pairs={{0,32},{32,64},{64,96},{96,128},{128,160},{160,192},{192,224},{224... | collective-permute-start | bytes 98312 | tf_op jit(solution)/shard_map/ppermute | solution.py:306
  7.2 5.5 %collective-permute-start.1 = (bf16[4,32,128]{2,1,0:T(8,128)(2,1)S(1)}, bf16[4,32,128]{2,1,0:T(8,128)(2,1)S(1)}, u32[]{:S(2)}, u32[]{:S(2)}) collective-permute-start(bf16[4,32,128]{2,1,0:T(8,128)(2,1)S(1)} %get-tuple-element.53), channel_id=1, source_target_pairs={{32,0},{64,32},{96,64},{128,96},{160,128},{192,160},{224,192},{256... | collective-permute-start | bytes 98312 | tf_op jit(solution)/shard_map/ppermute | solution.py:306
  12.7 0.0 collective-permute-done.north_ref
  12.7 0.8 collective-permute-done.1.south_ref
  13.5 2.0 %collective-permute-start.2 = (bf16[5,32,128]{2,1,0:T(8,128)(2,1)S(1)}, bf16[5,32,128]{2,1,0:T(8,128)(2,1)S(1)}, u32[]{:S(2)}, u32[]{:S(2)}) collective-permute-start(bf16[5,32,128]{2,1,0:T(8,128)(2,1)S(1)} %pad_maximum_fusion.1), channel_id=1, source_target_pairs={{0,1},{1,2},{2,3},{3,4},{4,5},{5,6},{6,7},{7,8},{8,9},{9,10},{10,1... | collective-permute-start | bytes 122888 | tf_op jit(solution)/shard_map/ppermute | solution.py:306
  15.6 1.3 %collective-permute-start.3 = (bf16[5,32,128]{2,1,0:T(8,128)(2,1)S(1)}, bf16[5,32,128]{2,1,0:T(8,128)(2,1)S(1)}, u32[]{:S(2)}, u32[]{:S(2)}) collective-permute-start(bf16[5,32,128]{2,1,0:T(8,128)(2,1)S(1)} %pad_maximum_fusion.2), channel_id=1, source_target_pairs={{1,0},{2,1},{3,2},{4,3},{5,4},{6,5},{7,6},{8,7},{9,8},{10,9},{11,1... | collective-permute-start | bytes 122888 | tf_op jit(solution)/shard_map/ppermute | solution.py:306
  16.9 0.7 reshape.73.rate_ref
  17.6 0.7 reshape.72.depth_ref
  18.3 0.0 copy-start.2
  18.3 1.1 %copy-done.2 = f32[3,4,8,16,16]{4,3,2,1,0:T(8,128)S(1)} copy-done((f32[3,4,8,16,16]{4,3,2,1,0:T(8,128)S(1)}, f32[3,4,8,16,16]{4,3,2,1,0:T(8,128)}, u32[]{:S(2)}) %copy-start.2) | copy-done | bytes 98328
  19.4 0.0 copy-start.5
  19.4 0.7 copy-done.5
  20.1 0.0 copy-start.6
  20.1 0.7 copy-done.6
  20.8 0.0 copy-start.7
  20.8 0.7 copy-done.7
  21.4 1.4 %shard_map.122 = (s32[3,4,9]{2,1,0:T(4,128)S(1)}, bf16[12,128,128]{2,1,0:T(8,128)(2,1)S(1)}, bf16[12,128,128]{2,1,0:T(8,128)(2,1)S(1)}, f32[12,128]{1,0:T(8,128)...) custom-call(s32[3,4,9]{2,1,0:T(4,128)S(1)} %copy-done.5, s32[3,4,9]{2,1,0:T(4,128)S(1)} %copy-done.6, ...), custom_call_target="tpu_custom_call" | custom-call | bytes 2500000 | tf_op jit(solution)/shard_map/pallas_call | solution.py:355
  22.9 0.0 collective-permute-done.2.west_ref
  22.9 0.0 collective-permute-done.3.east_ref
  22.9 0.0 copy-start
  22.9 2.0 %copy-done = bf16[3,4,9,128,128]{4,3,2,1,0:T(8,128)(2,1)S(1)} copy-done((bf16[3,4,9,128,128]{4,3,2,1,0:T(8,128)(2,1)S(1)}, bf16[3,4,9,128,128]{4,3,2,1,0:T(8,128)(2,1)}, u32[]{:S(2)}) %copy-start) | copy-done | bytes 3538968
  24.9 0.0 copy-start.1
  24.9 8.8 %shard_map.123 = (bf16[12,16,128]{2,1,0:T(8,128)(2,1)S(1)}, bf16[4,16,128]{2,1,0:T(8,128)(2,1)S(1)}, bf16[4,16,128]{2,1,0:T(8,128)(2,1)S(1)}, f32[12,128]{1,0:T(8,128)S(1)}) custom-call(s32[3,4,9]{2,1,0:T(4,128)S(1)} %get-tuple-element.50.index_ref, bf16[12,32,128]{2,1,0:T(8,128)(2,1)S(1)} %get-tuple-element.51.x_ref, ...), custom_call_target="tpu_custom_call" | custom-call | flops 113246208 | bytes 5000000 | tf_op jit(solution)/shard_map/pallas_call | solution.py:383
  33.7 2.2 %collective-permute-start.4 = (bf16[4,16,128]{2,1,0:T(8,128)(2,1)S(1)}, bf16[4,16,128]{2,1,0:T(8,128)(2,1)S(1)}, u32[]{:S(2)}, u32[]{:S(2)}) collective-permute-start(bf16[4,16,128]{2,1,0:T(8,128)(2,1)S(1)} %get-tuple-element.60), channel_id=1, source_target_pairs={{0,32},{32,64},{64,96},{96,128},{128,160},{160,192},{192,224},{224... | collective-permute-start | bytes 49160 | tf_op jit(solution)/shard_map/ppermute | solution.py:306
  35.9 2.1 %collective-permute-start.5 = (bf16[4,16,128]{2,1,0:T(8,128)(2,1)S(1)}, bf16[4,16,128]{2,1,0:T(8,128)(2,1)S(1)}, u32[]{:S(2)}, u32[]{:S(2)}) collective-permute-start(bf16[4,16,128]{2,1,0:T(8,128)(2,1)S(1)} %get-tuple-element.61), channel_id=1, source_target_pairs={{32,0},{64,32},{96,64},{128,96},{160,128},{192,160},{224,192},{256... | collective-permute-start | bytes 49160 | tf_op jit(solution)/shard_map/ppermute | solution.py:306
  38.1 0.0 collective-permute-done.4.north_ref
  38.1 2.9 %collective-permute-done.5.south_ref = bf16[4,16,128]{2,1,0:T(8,128)(2,1)S(1)} collective-permute-done((bf16[4,16,128]{2,1,0:T(8,128)(2,1)S(1)}, bf16[4,16,128]{2,1,0:T(8,128)(2,1)S(1)}, u32[]{:S(2)}, u32[]{:S(2)}) %collective-permute-start.5) | collective-permute-done | bytes 16416 | tf_op jit(solution)/shard_map/ppermute | solution.py:306
  41.0 4.3 %collective-permute-start.6 = (bf16[5,16,128]{2,1,0:T(8,128)(2,1)S(1)}, bf16[5,16,128]{2,1,0:T(8,128)(2,1)S(1)}, u32[]{:S(2)}, u32[]{:S(2)}) collective-permute-start(bf16[5,16,128]{2,1,0:T(8,128)(2,1)S(1)} %pad_maximum_fusion.3), channel_id=1, source_target_pairs={{0,1},{1,2},{2,3},{3,4},{4,5},{5,6},{6,7},{7,8},{8,9},{9,10},{10,1... | collective-permute-start | bytes 61448 | tf_op jit(solution)/shard_map/ppermute | solution.py:306
  45.3 1.3 %collective-permute-start.7 = (bf16[5,16,128]{2,1,0:T(8,128)(2,1)S(1)}, bf16[5,16,128]{2,1,0:T(8,128)(2,1)S(1)}, u32[]{:S(2)}, u32[]{:S(2)}) collective-permute-start(bf16[5,16,128]{2,1,0:T(8,128)(2,1)S(1)} %pad_maximum_fusion.4), channel_id=1, source_target_pairs={{1,0},{2,1},{3,2},{4,3},{5,4},{6,5},{7,6},{8,7},{9,8},{10,9},{11,1... | collective-permute-start | bytes 61448 | tf_op jit(solution)/shard_map/ppermute | solution.py:306
  46.6 0.0 collective-permute-done.6.west_ref
  46.6 3.2 %collective-permute-done.7.east_ref = bf16[5,16,128]{2,1,0:T(8,128)(2,1)S(1)} collective-permute-done((bf16[5,16,128]{2,1,0:T(8,128)(2,1)S(1)}, bf16[5,16,128]{2,1,0:T(8,128)(2,1)S(1)}, u32[]{:S(2)}, u32[]{:S(2)}) %collective-permute-start.7) | collective-permute-done | bytes 20512 | tf_op jit(solution)/shard_map/ppermute | solution.py:306
  49.8 0.0 copy-done.8
  49.8 0.0 copy-done.1
  49.8 7.7 %shard_map.124 = (f32[192,128]{1,0:T(8,128)S(1)}, f32[16,128]{1,0:T(8,128)S(1)}) custom-call(s32[3,4,9]{2,1,0:T(4,128)S(1)} %get-tuple-element.50.index_ref, bf16[12,16,128]{2,1,0:T(8,128)(2,1)S(1)} %get-tuple-element.59.x_ref, bf16[4,16,128]{2,1,0:T(8,128)(2,1)S(1)} %collective-permute-done.4.north_ref, ...), custom_call_target="tpu_custom_call" | custom-call | flops 56623104 | bytes 5000000 | tf_op jit(solution)/shard_map/pallas_call | solution.py:404
  57.6 16.6 %all_to_all.28 = f32[16,1,128]{2,1,0:T(1,128)S(1)} all-to-all(f32[16,1,128]{2,1,0:T(1,128)S(1)} %bitcast.52), channel_id=1, replica_groups=mesh['lat'=16,'lon'=32] {'lat'}, dimensions={0} | all-to-all | bytes 16384 | tf_op jit(solution)/shard_map/all_to_all | solution.py:297
  74.2 26.6 %all_to_all.29 = f32[32,1,128]{2,1,0:T(1,128)S(1)} all-to-all(f32[32,1,128]{2,1,0:T(1,128)S(1)} %broadcast_in_dim.6), channel_id=1, replica_groups=mesh['lat'=16,'lon'=32] {'lon'}, dimensions={0} | all-to-all | bytes 32768 | tf_op jit(solution)/shard_map/all_to_all | solution.py:299
  100.8 0.8 shard_map.125
  101.6 0.7 while.11
  102.3 0.0 copy-start.9
  102.3 0.0 copy-start.10
  102.3 0.6 copy-done.9
  102.9 0.0 copy-done.10
  (13 shorter events, 0.1 us)
Async XLA Ops:
  0.6 0.9 copy-start.3
  1.5 0.9 copy-start.4
  2.4 47.4 %copy-start.8 = (f32[4,16,3,4,128]{4,3,2,1,0:T(4,128)S(1)}, f32[4,16,3,4,128]{4,3,2,1,0:T(4,128)}, u32[]{:S(2)}) copy-start(f32[4,16,3,4,128]{4,3,2,1,0:T(4,128)} %param.21) | copy-start | bytes 1179652
  2.4 10.2 %collective-permute-start = (bf16[4,32,128]{2,1,0:T(8,128)(2,1)S(1)}, bf16[4,32,128]{2,1,0:T(8,128)(2,1)S(1)}, u32[]{:S(2)}, u32[]{:S(2)}) collective-permute-start(bf16[4,32,128]{2,1,0:T(8,128)(2,1)S(1)} %get-tuple-element.52), channel_id=1, source_target_pairs={{0,32},{32,64},{64,96},{96,128},{128,160},{160,192},{192,224},{224... | collective-permute-start | bytes 98312 | tf_op jit(solution)/shard_map/ppermute | solution.py:306
  7.2 6.3 %collective-permute-start.1 = (bf16[4,32,128]{2,1,0:T(8,128)(2,1)S(1)}, bf16[4,32,128]{2,1,0:T(8,128)(2,1)S(1)}, u32[]{:S(2)}, u32[]{:S(2)}) collective-permute-start(bf16[4,32,128]{2,1,0:T(8,128)(2,1)S(1)} %get-tuple-element.53), channel_id=1, source_target_pairs={{32,0},{64,32},{96,64},{128,96},{160,128},{192,160},{224,192},{256... | collective-permute-start | bytes 98312 | tf_op jit(solution)/shard_map/ppermute | solution.py:306
  13.5 9.4 %collective-permute-start.2 = (bf16[5,32,128]{2,1,0:T(8,128)(2,1)S(1)}, bf16[5,32,128]{2,1,0:T(8,128)(2,1)S(1)}, u32[]{:S(2)}, u32[]{:S(2)}) collective-permute-start(bf16[5,32,128]{2,1,0:T(8,128)(2,1)S(1)} %pad_maximum_fusion.1), channel_id=1, source_target_pairs={{0,1},{1,2},{2,3},{3,4},{4,5},{5,6},{6,7},{7,8},{8,9},{9,10},{10,1... | collective-permute-start | bytes 122888 | tf_op jit(solution)/shard_map/ppermute | solution.py:306
  15.6 7.3 %collective-permute-start.3 = (bf16[5,32,128]{2,1,0:T(8,128)(2,1)S(1)}, bf16[5,32,128]{2,1,0:T(8,128)(2,1)S(1)}, u32[]{:S(2)}, u32[]{:S(2)}) collective-permute-start(bf16[5,32,128]{2,1,0:T(8,128)(2,1)S(1)} %pad_maximum_fusion.2), channel_id=1, source_target_pairs={{1,0},{2,1},{3,2},{4,3},{5,4},{6,5},{7,6},{8,7},{9,8},{10,9},{11,1... | collective-permute-start | bytes 122888 | tf_op jit(solution)/shard_map/ppermute | solution.py:306
  18.3 1.1 %copy-start.2 = (f32[3,4,8,16,16]{4,3,2,1,0:T(8,128)S(1)}, f32[3,4,8,16,16]{4,3,2,1,0:T(8,128)}, u32[]{:S(2)}) copy-start(f32[3,4,8,16,16]{4,3,2,1,0:T(8,128)} %param.17) | copy-start | bytes 294916
  19.4 0.7 copy-start.5
  20.1 0.7 copy-start.6
  20.8 0.7 copy-start.7
  22.9 2.0 %copy-start = (bf16[3,4,9,128,128]{4,3,2,1,0:T(8,128)(2,1)S(1)}, bf16[3,4,9,128,128]{4,3,2,1,0:T(8,128)(2,1)}, u32[]{:S(2)}) copy-start(bf16[3,4,9,128,128]{4,3,2,1,0:T(8,128)(2,1)} %param.14) | copy-start | bytes 10616836
  24.9 24.9 %copy-start.1 = (bf16[3,4,9,128,128]{4,3,2,1,0:T(8,128)(2,1)S(1)}, bf16[3,4,9,128,128]{4,3,2,1,0:T(8,128)(2,1)}, u32[]{:S(2)}) copy-start(bf16[3,4,9,128,128]{4,3,2,1,0:T(8,128)(2,1)} %param.14) | copy-start | bytes 10616836
  33.7 4.4 %collective-permute-start.4 = (bf16[4,16,128]{2,1,0:T(8,128)(2,1)S(1)}, bf16[4,16,128]{2,1,0:T(8,128)(2,1)S(1)}, u32[]{:S(2)}, u32[]{:S(2)}) collective-permute-start(bf16[4,16,128]{2,1,0:T(8,128)(2,1)S(1)} %get-tuple-element.60), channel_id=1, source_target_pairs={{0,32},{32,64},{64,96},{96,128},{128,160},{160,192},{192,224},{224... | collective-permute-start | bytes 49160 | tf_op jit(solution)/shard_map/ppermute | solution.py:306
  35.9 5.1 %collective-permute-start.5 = (bf16[4,16,128]{2,1,0:T(8,128)(2,1)S(1)}, bf16[4,16,128]{2,1,0:T(8,128)(2,1)S(1)}, u32[]{:S(2)}, u32[]{:S(2)}) collective-permute-start(bf16[4,16,128]{2,1,0:T(8,128)(2,1)S(1)} %get-tuple-element.61), channel_id=1, source_target_pairs={{32,0},{64,32},{96,64},{128,96},{160,128},{192,160},{224,192},{256... | collective-permute-start | bytes 49160 | tf_op jit(solution)/shard_map/ppermute | solution.py:306
  41.0 5.6 %collective-permute-start.6 = (bf16[5,16,128]{2,1,0:T(8,128)(2,1)S(1)}, bf16[5,16,128]{2,1,0:T(8,128)(2,1)S(1)}, u32[]{:S(2)}, u32[]{:S(2)}) collective-permute-start(bf16[5,16,128]{2,1,0:T(8,128)(2,1)S(1)} %pad_maximum_fusion.3), channel_id=1, source_target_pairs={{0,1},{1,2},{2,3},{3,4},{4,5},{5,6},{6,7},{7,8},{8,9},{9,10},{10,1... | collective-permute-start | bytes 61448 | tf_op jit(solution)/shard_map/ppermute | solution.py:306
  45.3 4.5 %collective-permute-start.7 = (bf16[5,16,128]{2,1,0:T(8,128)(2,1)S(1)}, bf16[5,16,128]{2,1,0:T(8,128)(2,1)S(1)}, u32[]{:S(2)}, u32[]{:S(2)}) collective-permute-start(bf16[5,16,128]{2,1,0:T(8,128)(2,1)S(1)} %pad_maximum_fusion.4), channel_id=1, source_target_pairs={{1,0},{2,1},{3,2},{4,3},{5,4},{6,5},{7,6},{8,7},{9,8},{10,9},{11,1... | collective-permute-start | bytes 61448 | tf_op jit(solution)/shard_map/ppermute | solution.py:306
  102.3 0.6 copy-start.9
  102.3 0.6 copy-start.10

commit v3 on v2

v3 whole, which is shorter than its diff:
```python
import functools

import jax
import jax.numpy as jnp
from jax import lax
from jax.experimental import pallas as pl
from jax.experimental.pallas import tpu as pltpu
from jax.sharding import PartitionSpec as P

F32 = jnp.float32
BF16 = jnp.bfloat16
VMEM = pl.BlockSpec(memory_space=pltpu.VMEM)
SMEM = pl.BlockSpec(memory_space=pltpu.SMEM)
HBM = pl.BlockSpec(memory_space=pltpu.HBM)
NT = (((1,), (1,)), ((), ()))


def call(kernel, outs, ins, out_specs, scratch=(), flops=0, size=0, limit=16):
    return pl.pallas_call(
        kernel,
        out_shape=outs,
        in_specs=ins,
        out_specs=out_specs,
        scratch_shapes=list(scratch),
        compiler_params=pltpu.CompilerParams(vmem_limit_bytes=limit * 2**20),
        cost_estimate=pl.CostEstimate(flops=flops, bytes_accessed=size, transcendentals=0),
    )


def like(shape, dtype=F32):
    return jax.ShapeDtypeStruct(shape, dtype)


def iota(shape, dim):
    return lax.broadcasted_iota(jnp.int32, shape, dim)


def pack_kernel(lon, c_hbm, v_hbm, x_ref, first_ref, last_ref, own_ref, c_ref, v_ref, sems):
    copies = [
        pltpu.make_async_copy(c_hbm, c_ref, sems.at[0]),
        pltpu.make_async_copy(v_hbm, v_ref, sems.at[1]),
    ]
    for copy in copies:
        copy.start()
    for copy in copies:
        copy.wait()
    rows = x_ref.shape[0]
    tracers = c_ref.shape[0] // rows
    for r in range(rows):
        at = pl.ds(r, tracers, stride=rows)
        x = jnp.concatenate([c_ref[at, :], v_ref[at, :]], 0).astype(BF16)
        x_ref[r] = x
        if r < lon:
            first_ref[r] = x
        if r >= rows - lon:
            last_ref[r - (rows - lon)] = x
    own_ref[0] = c_ref[:rows, :]
    own_ref[1] = v_ref[:rows, :]


def prep_kernel(
    total_lon,
    pattern_hbm,
    live_hbm,
    inverse_hbm,
    depth_hbm,
    rate_hbm,
    stoich_hbm,
    basis_hbm,
    blocks_hbm,
    own_ref,
    index_ref,
    high_ref,
    low_ref,
    source_ref,
    rate_column_ref,
    gram_ref,
    basis_ref,
    held_ref,
    pattern_ref,
    live_ref,
    inverse_ref,
    depth_ref,
    rate_ref,
    stoich_ref,
    sems,
):
    pairs = [
        (pattern_hbm, pattern_ref),
        (live_hbm, live_ref),
        (depth_hbm, depth_ref),
        (rate_hbm, rate_ref),
        (stoich_hbm, stoich_ref),
        (inverse_hbm, inverse_ref),
        (basis_hbm, basis_ref),
        (blocks_hbm, held_ref),
    ]
    copies = [pltpu.make_async_copy(a, b, sems.at[i]) for i, (a, b) in enumerate(pairs)]
    for copy in copies:
        copy.start()
    for copy in copies[:5]:
        copy.wait()
    lat, lon, slots = pattern_ref.shape
    rows = lat * lon
    columns, levels = inverse_ref.shape[2:4]
    points = columns * levels
    pattern = pattern_ref[...]
    itself = pattern[:, :, :1]
    far_lat = pattern // total_lon - itself // total_lon
    far_lon = pattern % total_lon - itself % total_lon
    shape = pattern.shape
    place = (iota(shape, 0) + 1 + far_lat) * (lon + 2) + iota(shape, 1) + 1 + far_lon
    index_ref[...] = jnp.where(live_ref[...] > 0, place, (lat + 2) * (lon + 2))

    lane = iota((rows, points), 1)
    depth = jnp.concatenate([depth_ref[i] for i in range(lat)], 0)
    below = jnp.zeros((rows, points), jnp.int32)
    for k in range(columns):
        below = jnp.where(lane // levels == k, depth[:, k : k + 1], below)
    wet = (lane % levels < below).astype(F32)

    rate = jnp.concatenate([rate_ref[i] for i in range(lat)], 0)
    uptake, pull = sources(own_ref[0], own_ref[1], rate)
    spare = 8 - rows % 8 if rows % 8 else 0
    blank = [jnp.zeros((spare, points), F32)] if spare else []
    columns_of = [
        jnp.transpose(jnp.concatenate([part] + blank, 0)) for part in (uptake, pull, rate, wet)
    ]
    rate_column_ref[...] = columns_of[2]
    tracers = source_ref.shape[2] // 2
    share = stoich_ref[...]
    nothing = jnp.zeros((1, tracers), F32)
    share_c = jnp.concatenate([share, nothing], 1)
    share_v = jnp.concatenate([nothing, share], 1)
    for r in range(rows):
        at = slice(r, r + 1)
        source_ref[r] = columns_of[0][:, at] * share_c + columns_of[1][:, at] * share_v

    copies[5].wait()
    spread = (iota((levels, points), 1) % levels == iota((levels, points), 0)).astype(BF16)
    full = (points, points)
    same = iota(full, 0) // levels == iota(full, 1) // levels
    for r in range(rows):
        at = slice(r, r + 1)
        inverse = inverse_ref[r // lon, r % lon].reshape(points, levels)
        high = inverse.astype(BF16)
        low = (inverse - high.astype(F32)).astype(BF16)
        keep = jnp.where(same, wet[at, :] * columns_of[3][:, at], 0.0)
        for ref, part in ((high_ref, high), (low_ref, low)):
            tiled = jnp.dot(part, spread, preferred_element_type=F32)
            ref[r] = (tiled * keep).astype(BF16)

    copies[6].wait()
    gram_ref[...] = jnp.zeros(gram_ref.shape, F32)
    count = basis_ref.shape[0]
    row = 0
    for k in range(count):
        for j in range(k, count):
            gram_ref[row : row + 1, :] = jnp.sum(basis_ref[k] * basis_ref[j], 0, keepdims=True)
            row += 1
    copies[7].wait()


def sources(own_c, own_v, rate):
    denom = own_c * own_c + 1.0
    uptake = rate * own_c * own_c / denom
    slope = rate * 2.0 * own_c / (denom * denom)
    return uptake, slope * own_v


def pull_kernel(state_ref, rate_column_ref, stoich_ref, source_ref):
    rows, _, tracers = source_ref.shape
    share = stoich_ref[...]
    for r in range(rows):
        own_c = state_ref[r, :, 0:1]
        own_v = state_ref[r, :, tracers : tracers + 1]
        source_ref[r] = sources(own_c, own_v, rate_column_ref[:, r : r + 1])[1] * share


def fill(pad_ref, x_ref, north_ref, south_ref, west_ref, east_ref, lat, lon):
    wide = lon + 2
    for j in range(lon):
        pad_ref[1 + j] = north_ref[j]
        pad_ref[(lat + 1) * wide + 1 + j] = south_ref[j]
        for i in range(lat):
            pad_ref[(i + 1) * wide + 1 + j] = x_ref[i * lon + j]
    for i in range(lat + 2):
        pad_ref[i * wide] = west_ref[i]
        pad_ref[i * wide + lon + 1] = east_ref[i]
    pad_ref[(lat + 2) * wide] = jnp.zeros(pad_ref.shape[1:], BF16)


def advance(r, index_ref, pad_ref, held_ref, high_ref, low_ref, source_ref):
    slots = index_ref.shape[2]
    lon = index_ref.shape[1]
    z = source_ref[r]
    for s in range(slots):
        x = pad_ref[index_ref[r // lon, r % lon, s]]
        z = z + lax.dot_general(held_ref[r * slots + s], x, NT, preferred_element_type=F32)
    z_high = z.astype(BF16)
    z_low = (z - z_high.astype(F32)).astype(BF16)
    dot = functools.partial(jnp.dot, preferred_element_type=F32)
    return dot(high_ref[r], z_high) + (dot(low_ref[r], z_high) + dot(high_ref[r], z_low))


def first_kernel(
    lat,
    lon,
    index_ref,
    x_ref,
    north_ref,
    south_ref,
    west_ref,
    east_ref,
    held_ref,
    high_ref,
    low_ref,
    source_ref,
    y_ref,
    first_ref,
    last_ref,
    state_ref,
    pad_ref,
):
    rows = lat * lon
    fill(pad_ref, x_ref, north_ref, south_ref, west_ref, east_ref, lat, lon)
    tracers = y_ref.shape[1]
    for r in range(rows):
        out = advance(r, index_ref, pad_ref, held_ref, high_ref, low_ref, source_ref)
        state_ref[r] = out
        y = jnp.transpose(out)[tracers:].astype(BF16)
        y_ref[r] = y
        if r < lon:
            first_ref[r] = y
        if r >= rows - lon:
            last_ref[r - (rows - lon)] = y


def second_kernel(
    lat,
    lon,
    index_ref,
    x_ref,
    north_ref,
    south_ref,
    west_ref,
    east_ref,
    held_ref,
    high_ref,
    low_ref,
    source_ref,
    gram_ref,
    basis_ref,
    product_ref,
    sums_ref,
    pad_ref,
):
    rows = lat * lon
    fill(pad_ref, x_ref, north_ref, south_ref, west_ref, east_ref, lat, lon)
    tracers = x_ref.shape[1]
    for r in range(rows):
        out = advance(r, index_ref, pad_ref, held_ref, high_ref, low_ref, source_ref)
        product_ref[pl.ds(r, tracers, stride=rows), :] = jnp.transpose(out)
    product = product_ref[...]
    count = basis_ref.shape[0]
    pairs = count * (count + 1) // 2
    all_sums = gram_ref[...]
    spot = iota(all_sums.shape, 0)
    for k in range(count + 1):
        other = basis_ref[k] if k < count else product
        part = jnp.sum(product * other, 0, keepdims=True)
        all_sums = jnp.where(spot == pairs + k, part, all_sums)
    column = jnp.sum(all_sums, 1, keepdims=True)
    row = jnp.sum(jnp.where(spot == iota(spot.shape, 1), column, 0.0), 0, keepdims=True)
    sums_ref[...] = jnp.broadcast_to(row, sums_ref.shape)


def last_kernel(
    parts_ref, product_ref, basis_ref, next_ref, out_hbm, coeffs_ref, flag_ref, sem
):
    copy = pltpu.make_async_copy(product_ref, out_hbm, sem)
    copy.start()
    count = basis_ref.shape[0]
    row = jnp.sum(parts_ref[...], 0, keepdims=True)
    lane = iota(row.shape, 1)

    def pick(at):
        return jnp.sum(jnp.where(lane == at, row, 0.0), 1, keepdims=True)

    pairs = count * (count + 1) // 2
    heights = [pick(pairs + k) for k in range(count)]
    whole = pick(pairs + count)
    cross = jnp.zeros((1, 1), F32)
    at = 0
    for k in range(count):
        for j in range(k, count):
            twice = 1.0 if k == j else 2.0
            cross = cross + twice * (heights[k] * heights[j] * pick(at))
            at += 1
    squares = sum(h * h for h in heights)
    short = whole - 2.0 * squares + cross
    size = whole + 2.0 * squares + cross
    beta = jnp.sqrt(jnp.maximum(short, 0.0) + 1e-06)
    rest = product_ref[...]
    for k in range(count):
        rest = rest - heights[k] * basis_ref[k]
    next_ref[...] = rest / beta
    for k in range(count):
        coeffs_ref[k] = heights[k][0, 0]
    coeffs_ref[count] = beta[0, 0]
    flag_ref[0] = jnp.where(short < 0.01 * size, 1, 0)[0, 0]
    copy.wait()


def summed(rows):
    row = jnp.sum(lax.all_to_all(rows, "lat", 0, 0), 0, keepdims=True)
    rows = jnp.broadcast_to(row, (lax.axis_size("lon"), row.shape[1]))
    return lax.all_to_all(rows, "lon", 0, 0)


def halo(x, first, last, lat, lon):
    def moved(a, axis, step):
        size = lax.axis_size(axis)
        pairs = [(i, i + step) for i in range(size) if 0 <= i + step < size]
        return lax.ppermute(a, axis, pairs)

    north = moved(last, "lat", 1)
    south = moved(first, "lat", -1)
    grid = x.reshape((lat, lon) + x.shape[1:])
    right = jnp.concatenate([north[None, lon - 1], grid[:, lon - 1], south[None, lon - 1]], 0)
    left = jnp.concatenate([north[None, 0], grid[:, 0], south[None, 0]], 0)
    west = moved(right, "lon", 1)
    east = moved(left, "lon", -1)
    return north, south, west, east


def body(
    base_state,
    tangent,
    blocks,
    pattern,
    live,
    column_inverse,
    col_depth,
    uptake_rate,
    stoich,
    basis,
):
    tracers, lat, lon, points = base_state.shape
    slots = pattern.shape[2]
    count = basis.shape[0]
    rows = lat * lon
    total_lon = lon * lax.axis_size("lon")
    size = tracers * rows
    places = (lat + 2) * (lon + 2) + 1
    share = stoich.reshape(1, tracers)

    x, first, last, own = call(
        functools.partial(pack_kernel, lon),
        (
            like((rows, 2 * tracers, points), BF16),
            like((lon, 2 * tracers, points), BF16),
            like((lon, 2 * tracers, points), BF16),
            like((2, rows, points)),
        ),
        [HBM] * 2,
        [VMEM] * 4,
        scratch=[pltpu.VMEM((size, points), F32)] * 2 + [pltpu.SemaphoreType.DMA((2,))],
        size=400000,
    )(base_state.reshape(size, points), tangent.reshape(size, points))

    index, high, low, source, rate_column, gram, flat_basis, held = call(
        functools.partial(prep_kernel, total_lon),
        (
            like((lat, lon, slots), jnp.int32),
            like((rows, points, points), BF16),
            like((rows, points, points), BF16),
            like((rows, points, 2 * tracers)),
            like((points, (rows + 7) // 8 * 8)),
            like((16, points)),
            like((count, size, points)),
            like((rows * slots, points, points), BF16),
        ),
        [HBM] * 8 + [VMEM],
        [VMEM] * 8,
        scratch=[
            pltpu.VMEM(pattern.shape, jnp.int32),
            pltpu.VMEM(live.shape, jnp.int32),
            pltpu.VMEM(column_inverse.shape, F32),
            pltpu.VMEM(col_depth.shape, jnp.int32),
            pltpu.VMEM(uptake_rate.shape, F32),
            pltpu.VMEM(share.shape, F32),
            pltpu.SemaphoreType.DMA((8,)),
        ],
        flops=20000000,
        size=8000000,
    )(
        pattern,
        live,
        column_inverse,
        col_depth,
        uptake_rate,
        share,
        basis.reshape(count, size, points),
        blocks.reshape(rows * slots, points, points),
        own,
    )

    north, south, west, east = halo(x, first, last, lat, lon)
    work = 2 * 2 * tracers * rows * slots * points * points
    x, first, last, state = call(
        functools.partial(first_kernel, lat, lon),
        (
            like((rows, tracers, points), BF16),
            like((lon, tracers, points), BF16),
            like((lon, tracers, points), BF16),
            like((rows, points, 2 * tracers)),
        ),
        [SMEM] + [VMEM] * 9,
        [VMEM] * 4,
        scratch=[pltpu.VMEM((places, 2 * tracers, points), BF16)],
        flops=work,
        size=5000000,
    )(index, x, north, south, west, east, held, high, low, source)

    source = call(
        pull_kernel, like((rows, points, tracers)), [VMEM] * 3, VMEM, flops=100000, size=2000000
    )(state, rate_column, share)

    north, south, west, east = halo(x, first, last, lat, lon)
    product, sums = call(
        functools.partial(second_kernel, lat, lon),
        (like((size, points)), like((lax.axis_size("lat"), points))),
        [SMEM] + [VMEM] * 11,
        [VMEM] * 2,
        scratch=[pltpu.VMEM((places, tracers, points), BF16)],
        flops=work // 2,
        size=5000000,
    )(index, x, north, south, west, east, held, high, low, source, gram, flat_basis)

    parts = summed(sums)
    following, written, coeffs, flag = call(
        last_kernel,
        (like((size, points)), like((size, points)), like((count + 1,)), like((1,), jnp.int32)),
        [VMEM] * 3,
        [VMEM, HBM, SMEM, SMEM],
        scratch=[pltpu.SemaphoreType.DMA],
        size=700000,
    )(parts, product, flat_basis)

    def again(carry):
        following, coeffs, flag = carry
        rest = product - jnp.einsum(
            "k,ksp->sp", coeffs[:count], flat_basis, precision=lax.Precision.HIGHEST
        )
        part = jnp.pad(jnp.sum(rest * rest).reshape(1, 1), ((0, 0), (0, points - 1)))
        squared = jnp.sum(summed(jnp.broadcast_to(part, (lax.axis_size("lat"), points))), 0)[0]
        beta = jnp.sqrt(squared + 1e-06)
        return rest / beta, jnp.concatenate([coeffs[:count], beta[None]]), flag * 0

    following, coeffs, flag = lax.while_loop(
        lambda carry: carry[2][0] > 0, again, (following, coeffs, flag)
    )
    shape = base_state.shape
    return written.reshape(shape), following.reshape(shape), coeffs


def solution(mesh):
    placed = (
        P(None, "lat", "lon", None),
        P(None, "lat", "lon", None),
        P("lat", "lon", None, None, None),
        P("lat", "lon", None),
        P("lat", "lon", None),
        P("lat", "lon", None, None, None),
        P("lat", "lon", None),
        P("lat", "lon", None),
        P(),
        P(None, None, "lat", "lon", None),
    )
    return jax.shard_map(
        body,
        mesh=mesh,
        in_specs=placed,
        out_specs=(P(None, "lat", "lon", None), P(None, "lat", "lon", None), P()),
        check_vma=False,
    )
```

time: 104 us -> 98.8 us (0.950)
  Pallas kernels: 18.8 us -> 14.6 us
  waiting for transfers between devices: 6.93 us -> 5.48 us
    pallas_call x3 -> x4, Pallas kernels: 17.3 us -> 12.4 us  [the longest x1 4.88 us: body(): call(functools.partial(second_kernel, lat, lon), (like((size, points)), l...]
    unnamed x22 -> x24, local copies, waits for them, and re-layouts: 7.58 us -> 9.83 us
    ppermute x8, waiting for transfers between devices: 6.93 us -> 5.48 us  [moved(): return lax.ppermute(a, axis, pairs)]
    reshape x2 -> x0, local copies, waits for them, and re-layouts: 1.4 us -> none  [the longest x1 0.7 us: body(): rate = uptake_rate.reshape(rows, points)]
  transfers between devices with their start and end apart: 8 -> 8, of which waited for: 3 -> 3; matrix products, arithmetic and copies ran while one was open for 1% -> 0% of each run, Pallas kernels for 1% -> 3%
where the time goes in v3:
time: 98.8 us; the launch traced here: 98.1 us
  blocking collectives  43.2 us (44%)
  starting transfers between devices  23.3 us (24%)
  Pallas kernels  14.6 us (15%)
  local copies, waits for them, and re-layouts  9.87 us (10%)
  waiting for transfers between devices  5.48 us (6%)
    all_to_all x1, blocking collectives, summed(): return lax.all_to_all(rows, 'lon', 0, 0)  26.6 us
    ppermute x8, starting transfers between devices, moved(): return lax.ppermute(a, axis, pairs)  23.3 us
    all_to_all x1, blocking collectives, summed(): row = jnp.sum(lax.all_to_all(rows, 'lat', 0, 0), 0, keepdims=True)  16.6 us
    unnamed x24, local copies, waits for them, and re-layouts  9.83 us
    ppermute x8, waiting for transfers between devices, moved(): return lax.ppermute(a, axis, pairs)  5.48 us
    pallas_call x1, Pallas kernels, body(): call(functools.partial(second_kernel, lat, lon), (like((size, points)), l...  4.88 us
    pallas_call x1, Pallas kernels, body(): call(functools.partial(first_kernel, lat, lon), (like((rows, tracers, poi...  4.73 us
  transfers between devices with their start and end apart: 8, of which 3 were waited for; matrix products, arithmetic and copies ran while one was open for 0% of the time, Pallas kernels for 3%

profile of v3, /device:TPU:1, one launch (start us, length us, event | category | flops | bytes accessed | tf_op | source)
XLA Modules:
  0.0 98.1 jit_solution(9994290273954614875)
XLA Ops:
  0.6 0.0 copy-start.3
  0.6 0.9 copy-done.3
  1.5 0.0 copy-start.4
  1.5 0.9 copy-done.4
  2.4 0.3 shard_map.121
  2.7 4.6 %collective-permute-start = (bf16[4,32,128]{2,1,0:T(8,128)(2,1)S(1)}, bf16[4,32,128]{2,1,0:T(8,128)(2,1)S(1)}, u32[]{:S(2)}, u32[]{:S(2)}) collective-permute-start(bf16[4,32,128]{2,1,0:T(8,128)(2,1)S(1)} %get-tuple-element.54), channel_id=1, source_target_pairs={{0,32},{32,64},{64,96},{96,128},{128,160},{160,192},{192,224},{224... | collective-permute-start | bytes 98312 | tf_op jit(solution)/shard_map/ppermute | solution.py:325
  7.3 5.5 %collective-permute-start.1 = (bf16[4,32,128]{2,1,0:T(8,128)(2,1)S(1)}, bf16[4,32,128]{2,1,0:T(8,128)(2,1)S(1)}, u32[]{:S(2)}, u32[]{:S(2)}) collective-permute-start(bf16[4,32,128]{2,1,0:T(8,128)(2,1)S(1)} %get-tuple-element.55), channel_id=1, source_target_pairs={{32,0},{64,32},{96,64},{128,96},{160,128},{192,160},{224,192},{256... | collective-permute-start | bytes 98312 | tf_op jit(solution)/shard_map/ppermute | solution.py:325
  12.8 0.0 collective-permute-done.north_ref
  12.8 0.8 collective-permute-done.1.south_ref
  13.6 2.0 %collective-permute-start.2 = (bf16[5,32,128]{2,1,0:T(8,128)(2,1)S(1)}, bf16[5,32,128]{2,1,0:T(8,128)(2,1)S(1)}, u32[]{:S(2)}, u32[]{:S(2)}) collective-permute-start(bf16[5,32,128]{2,1,0:T(8,128)(2,1)S(1)} %pad_maximum_fusion.1), channel_id=1, source_target_pairs={{0,1},{1,2},{2,3},{3,4},{4,5},{5,6},{6,7},{7,8},{8,9},{9,10},{10,1... | collective-permute-start | bytes 122888 | tf_op jit(solution)/shard_map/ppermute | solution.py:325
  15.7 1.3 %collective-permute-start.3 = (bf16[5,32,128]{2,1,0:T(8,128)(2,1)S(1)}, bf16[5,32,128]{2,1,0:T(8,128)(2,1)S(1)}, u32[]{:S(2)}, u32[]{:S(2)}) collective-permute-start(bf16[5,32,128]{2,1,0:T(8,128)(2,1)S(1)} %pad_maximum_fusion.2), channel_id=1, source_target_pairs={{1,0},{2,1},{3,2},{4,3},{5,4},{6,5},{7,6},{8,7},{9,8},{10,9},{11,1... | collective-permute-start | bytes 122888 | tf_op jit(solution)/shard_map/ppermute | solution.py:325
  17.0 0.0 copy-start
  17.0 2.0 %copy-done = bf16[3,4,9,128,128]{4,3,2,1,0:T(8,128)(2,1)S(1)} copy-done((bf16[3,4,9,128,128]{4,3,2,1,0:T(8,128)(2,1)S(1)}, bf16[3,4,9,128,128]{4,3,2,1,0:T(8,128)(2,1)}, u32[]{:S(2)}) %copy-start) | copy-done | bytes 3538968
  19.0 0.0 copy-start.1
  19.0 1.1 %copy-done.1 = f32[3,4,8,16,16]{4,3,2,1,0:T(8,128)S(1)} copy-done((f32[3,4,8,16,16]{4,3,2,1,0:T(8,128)S(1)}, f32[3,4,8,16,16]{4,3,2,1,0:T(8,128)}, u32[]{:S(2)}) %copy-start.1) | copy-done | bytes 98328
  20.1 0.0 copy-start.2
  20.1 1.0 %copy-done.2 = f32[4,16,3,4,128]{4,3,2,1,0:T(4,128)S(1)} copy-done((f32[4,16,3,4,128]{4,3,2,1,0:T(4,128)S(1)}, f32[4,16,3,4,128]{4,3,2,1,0:T(4,128)}, u32[]{:S(2)}) %copy-start.2) | copy-done | bytes 393240
  21.1 0.0 copy-start.5
  21.1 0.7 copy-done.5
  21.8 0.0 copy-start.6
  21.8 0.7 copy-done.6
  22.5 0.0 copy-start.7
  22.5 0.7 copy-done.7
  23.2 0.0 copy-start.8
  23.2 0.7 copy-done.8
  23.9 0.0 copy-start.9
  23.9 0.7 copy-done.9
  24.5 2.0 %shard_map.122 = (s32[3,4,9]{2,1,0:T(4,128)S(1)}, bf16[12,128,128]{2,1,0:T(8,128)(2,1)S(1)}, bf16[12,128,128]{2,1,0:T(8,128)(2,1)S(1)}, f32[12,128,32]{2,1,0:T(8...) custom-call(s32[3,4,9]{2,1,0:T(4,128)S(1)} %copy-done.5, ...), custom_call_target="tpu_custom_call" | custom-call | flops 20000000 | bytes 8000000 | tf_op jit(solution)/shard_map/pallas_call | solution.py:372
  26.5 0.0 copy-start.10
  26.5 0.0 collective-permute-done.2.west_ref
  26.5 0.0 collective-permute-done.3.east_ref
  26.5 4.7 %shard_map.123 = (bf16[12,16,128]{2,1,0:T(8,128)(2,1)S(1)}, bf16[4,16,128]{2,1,0:T(8,128)(2,1)S(1)}, bf16[4,16,128]{2,1,0:T(8,128)(2,1)S(1)}, f32[12,128,32]{2,1,0:T(8,128)S(1)}) custom-call(s32[3,4,9]{2,1,0:T(4,128)S(1)} %get-tuple-element.52.index_ref, bf16[12,32,128]{2,1,0:T(8,128)(2,1)S(1)} %get-tuple-element.53.x_ref, ...), custom_call_target="tpu_custom_call" | custom-call | flops 113246208 | bytes 5000000 | tf_op jit(solution)/shard_map/pallas_call | solution.py:411
  31.3 2.2 %collective-permute-start.4 = (bf16[4,16,128]{2,1,0:T(8,128)(2,1)S(1)}, bf16[4,16,128]{2,1,0:T(8,128)(2,1)S(1)}, u32[]{:S(2)}, u32[]{:S(2)}) collective-permute-start(bf16[4,16,128]{2,1,0:T(8,128)(2,1)S(1)} %get-tuple-element.61), channel_id=1, source_target_pairs={{0,32},{32,64},{64,96},{96,128},{128,160},{160,192},{192,224},{224... | collective-permute-start | bytes 49160 | tf_op jit(solution)/shard_map/ppermute | solution.py:325
  33.5 2.1 %collective-permute-start.5 = (bf16[4,16,128]{2,1,0:T(8,128)(2,1)S(1)}, bf16[4,16,128]{2,1,0:T(8,128)(2,1)S(1)}, u32[]{:S(2)}, u32[]{:S(2)}) collective-permute-start(bf16[4,16,128]{2,1,0:T(8,128)(2,1)S(1)} %get-tuple-element.62), channel_id=1, source_target_pairs={{32,0},{64,32},{96,64},{128,96},{160,128},{192,160},{224,192},{256... | collective-permute-start | bytes 49160 | tf_op jit(solution)/shard_map/ppermute | solution.py:325
  35.7 0.0 collective-permute-done.4.north_ref
  35.7 2.9 %collective-permute-done.5.south_ref = bf16[4,16,128]{2,1,0:T(8,128)(2,1)S(1)} collective-permute-done((bf16[4,16,128]{2,1,0:T(8,128)(2,1)S(1)}, bf16[4,16,128]{2,1,0:T(8,128)(2,1)S(1)}, u32[]{:S(2)}, u32[]{:S(2)}) %collective-permute-start.5) | collective-permute-done | bytes 16416 | tf_op jit(solution)/shard_map/ppermute | solution.py:325
  38.6 4.3 %collective-permute-start.6 = (bf16[5,16,128]{2,1,0:T(8,128)(2,1)S(1)}, bf16[5,16,128]{2,1,0:T(8,128)(2,1)S(1)}, u32[]{:S(2)}, u32[]{:S(2)}) collective-permute-start(bf16[5,16,128]{2,1,0:T(8,128)(2,1)S(1)} %pad_maximum_fusion.3), channel_id=1, source_target_pairs={{0,1},{1,2},{2,3},{3,4},{4,5},{5,6},{6,7},{7,8},{8,9},{9,10},{10,1... | collective-permute-start | bytes 61448 | tf_op jit(solution)/shard_map/ppermute | solution.py:325
  42.9 1.3 %collective-permute-start.7 = (bf16[5,16,128]{2,1,0:T(8,128)(2,1)S(1)}, bf16[5,16,128]{2,1,0:T(8,128)(2,1)S(1)}, u32[]{:S(2)}, u32[]{:S(2)}) collective-permute-start(bf16[5,16,128]{2,1,0:T(8,128)(2,1)S(1)} %pad_maximum_fusion.4), channel_id=1, source_target_pairs={{1,0},{2,1},{3,2},{4,3},{5,4},{6,5},{7,6},{8,7},{9,8},{10,9},{11,1... | collective-permute-start | bytes 61448 | tf_op jit(solution)/shard_map/ppermute | solution.py:325
  44.2 0.0 copy-done.10
  44.2 1.4 %shard_map.124.source_ref = f32[12,128,16]{2,1,0:T(8,128)S(1)} custom-call(f32[12,128,32]{2,1,0:T(8,128)S(1)} %get-tuple-element.63.state_ref, f32[128,16]{1,0:T(8,128)S(1)} %get-tuple-element.64.rate_column_ref, f32[1,16]{1,0:T(1,128)S(1)} %bitcast.52), custom_call_target="tpu_custom_call" | custom-call | flops 100000 | bytes 2000000 | tf_op jit(solution)/shard_map/pallas_call | solution.py:426
  45.7 0.0 collective-permute-done.6.west_ref
  45.7 1.8 %collective-permute-done.7.east_ref = bf16[5,16,128]{2,1,0:T(8,128)(2,1)S(1)} collective-permute-done((bf16[5,16,128]{2,1,0:T(8,128)(2,1)S(1)}, bf16[5,16,128]{2,1,0:T(8,128)(2,1)S(1)}, u32[]{:S(2)}, u32[]{:S(2)}) %collective-permute-start.7) | collective-permute-done | bytes 20512 | tf_op jit(solution)/shard_map/ppermute | solution.py:325
  47.4 4.9 %shard_map.125 = (f32[192,128]{1,0:T(8,128)S(1)}, f32[16,128]{1,0:T(8,128)S(1)}) custom-call(s32[3,4,9]{2,1,0:T(4,128)S(1)} %get-tuple-element.52.index_ref, bf16[12,16,128]{2,1,0:T(8,128)(2,1)S(1)} %get-tuple-element.60.x_ref, bf16[4,16,128]{2,1,0:T(8,128)(2,1)S(1)} %collective-permute-done.4.north_ref, ...), custom_call_target="tpu_custom_call" | custom-call | flops 56623104 | bytes 5000000 | tf_op jit(solution)/shard_map/pallas_call | solution.py:431
  52.3 16.6 %all_to_all.28 = f32[16,1,128]{2,1,0:T(1,128)S(1)} all-to-all(f32[16,1,128]{2,1,0:T(1,128)S(1)} %bitcast.50), channel_id=1, replica_groups=mesh['lat'=16,'lon'=32] {'lat'}, dimensions={0} | all-to-all | bytes 16384 | tf_op jit(solution)/shard_map/all_to_all | solution.py:316
  69.0 26.6 %all_to_all.29 = f32[32,1,128]{2,1,0:T(1,128)S(1)} all-to-all(f32[32,1,128]{2,1,0:T(1,128)S(1)} %broadcast_in_dim.6), channel_id=1, replica_groups=mesh['lat'=16,'lon'=32] {'lon'}, dimensions={0} | all-to-all | bytes 32768 | tf_op jit(solution)/shard_map/all_to_all | solution.py:318
  95.6 1.3 %shard_map.126 = (f32[192,128]{1,0:T(8,128)}, f32[192,128]{1,0:T(8,128)}, f32[5]{0:T(128)S(1)}, s32[1]{0:T(128)}) custom-call(f32[32,128]{1,0:T(8,128)S(1)} %bitcast.49, f32[192,128]{1,0:T(8,128)S(1)} %get-tuple-element.108.product_ref, f32[4,192,128]{2,1,0:T(8,128)S(1)} %get-tuple-element.107.basis_ref), custom_call_target="tpu_custom_call" | custom-call | bytes 700000 | tf_op jit(solution)/shard_map/pallas_call | solution.py:442
  96.9 0.7 while.11
  97.5 0.0 copy-start.11
  97.6 0.5 copy-done.11
  (12 shorter events, 0.1 us)
Async XLA Ops:
  0.6 0.9 copy-start.3
  1.5 0.9 copy-start.4
  2.7 10.1 %collective-permute-start = (bf16[4,32,128]{2,1,0:T(8,128)(2,1)S(1)}, bf16[4,32,128]{2,1,0:T(8,128)(2,1)S(1)}, u32[]{:S(2)}, u32[]{:S(2)}) collective-permute-start(bf16[4,32,128]{2,1,0:T(8,128)(2,1)S(1)} %get-tuple-element.54), channel_id=1, source_target_pairs={{0,32},{32,64},{64,96},{96,128},{128,160},{160,192},{192,224},{224... | collective-permute-start | bytes 98312 | tf_op jit(solution)/shard_map/ppermute | solution.py:325
  7.3 6.3 %collective-permute-start.1 = (bf16[4,32,128]{2,1,0:T(8,128)(2,1)S(1)}, bf16[4,32,128]{2,1,0:T(8,128)(2,1)S(1)}, u32[]{:S(2)}, u32[]{:S(2)}) collective-permute-start(bf16[4,32,128]{2,1,0:T(8,128)(2,1)S(1)} %get-tuple-element.55), channel_id=1, source_target_pairs={{32,0},{64,32},{96,64},{128,96},{160,128},{192,160},{224,192},{256... | collective-permute-start | bytes 98312 | tf_op jit(solution)/shard_map/ppermute | solution.py:325
  13.6 12.9 %collective-permute-start.2 = (bf16[5,32,128]{2,1,0:T(8,128)(2,1)S(1)}, bf16[5,32,128]{2,1,0:T(8,128)(2,1)S(1)}, u32[]{:S(2)}, u32[]{:S(2)}) collective-permute-start(bf16[5,32,128]{2,1,0:T(8,128)(2,1)S(1)} %pad_maximum_fusion.1), channel_id=1, source_target_pairs={{0,1},{1,2},{2,3},{3,4},{4,5},{5,6},{6,7},{7,8},{8,9},{9,10},{10,1... | collective-permute-start | bytes 122888 | tf_op jit(solution)/shard_map/ppermute | solution.py:325
  15.7 10.9 %collective-permute-start.3 = (bf16[5,32,128]{2,1,0:T(8,128)(2,1)S(1)}, bf16[5,32,128]{2,1,0:T(8,128)(2,1)S(1)}, u32[]{:S(2)}, u32[]{:S(2)}) collective-permute-start(bf16[5,32,128]{2,1,0:T(8,128)(2,1)S(1)} %pad_maximum_fusion.2), channel_id=1, source_target_pairs={{1,0},{2,1},{3,2},{4,3},{5,4},{6,5},{7,6},{8,7},{9,8},{10,9},{11,1... | collective-permute-start | bytes 122888 | tf_op jit(solution)/shard_map/ppermute | solution.py:325
  17.0 2.0 %copy-start = (bf16[3,4,9,128,128]{4,3,2,1,0:T(8,128)(2,1)S(1)}, bf16[3,4,9,128,128]{4,3,2,1,0:T(8,128)(2,1)}, u32[]{:S(2)}) copy-start(bf16[3,4,9,128,128]{4,3,2,1,0:T(8,128)(2,1)} %param.14) | copy-start | bytes 10616836
  19.0 1.1 %copy-start.1 = (f32[3,4,8,16,16]{4,3,2,1,0:T(8,128)S(1)}, f32[3,4,8,16,16]{4,3,2,1,0:T(8,128)}, u32[]{:S(2)}) copy-start(f32[3,4,8,16,16]{4,3,2,1,0:T(8,128)} %inverse_hbm.1) | copy-start | bytes 294916
  20.1 1.0 %copy-start.2 = (f32[4,16,3,4,128]{4,3,2,1,0:T(4,128)S(1)}, f32[4,16,3,4,128]{4,3,2,1,0:T(4,128)}, u32[]{:S(2)}) copy-start(f32[4,16,3,4,128]{4,3,2,1,0:T(4,128)} %param.21) | copy-start | bytes 1179652
  21.1 0.7 copy-start.5
  21.8 0.7 copy-start.6
  22.5 0.7 copy-start.7
  23.2 0.7 copy-start.8
  23.9 0.7 copy-start.9
  26.5 17.7 %copy-start.10 = (f32[16]{0:T(128)S(1)}, f32[16]{0:T(128)}, u32[]{:S(2)}) copy-start(f32[16]{0:T(128)} %param.20) | copy-start | bytes 196
  31.3 4.4 %collective-permute-start.4 = (bf16[4,16,128]{2,1,0:T(8,128)(2,1)S(1)}, bf16[4,16,128]{2,1,0:T(8,128)(2,1)S(1)}, u32[]{:S(2)}, u32[]{:S(2)}) collective-permute-start(bf16[4,16,128]{2,1,0:T(8,128)(2,1)S(1)} %get-tuple-element.61), channel_id=1, source_target_pairs={{0,32},{32,64},{64,96},{96,128},{128,160},{160,192},{192,224},{224... | collective-permute-start | bytes 49160 | tf_op jit(solution)/shard_map/ppermute | solution.py:325
  33.5 5.1 %collective-permute-start.5 = (bf16[4,16,128]{2,1,0:T(8,128)(2,1)S(1)}, bf16[4,16,128]{2,1,0:T(8,128)(2,1)S(1)}, u32[]{:S(2)}, u32[]{:S(2)}) collective-permute-start(bf16[4,16,128]{2,1,0:T(8,128)(2,1)S(1)} %get-tuple-element.62), channel_id=1, source_target_pairs={{32,0},{64,32},{96,64},{128,96},{160,128},{192,160},{224,192},{256... | collective-permute-start | bytes 49160 | tf_op jit(solution)/shard_map/ppermute | solution.py:325
  38.6 7.1 %collective-permute-start.6 = (bf16[5,16,128]{2,1,0:T(8,128)(2,1)S(1)}, bf16[5,16,128]{2,1,0:T(8,128)(2,1)S(1)}, u32[]{:S(2)}, u32[]{:S(2)}) collective-permute-start(bf16[5,16,128]{2,1,0:T(8,128)(2,1)S(1)} %pad_maximum_fusion.3), channel_id=1, source_target_pairs={{0,1},{1,2},{2,3},{3,4},{4,5},{5,6},{6,7},{7,8},{8,9},{9,10},{10,1... | collective-permute-start | bytes 61448 | tf_op jit(solution)/shard_map/ppermute | solution.py:325
  42.9 4.5 %collective-permute-start.7 = (bf16[5,16,128]{2,1,0:T(8,128)(2,1)S(1)}, bf16[5,16,128]{2,1,0:T(8,128)(2,1)S(1)}, u32[]{:S(2)}, u32[]{:S(2)}) collective-permute-start(bf16[5,16,128]{2,1,0:T(8,128)(2,1)S(1)} %pad_maximum_fusion.4), channel_id=1, source_target_pairs={{1,0},{2,1},{3,2},{4,3},{5,4},{6,5},{7,6},{8,7},{9,8},{10,9},{11,1... | collective-permute-start | bytes 61448 | tf_op jit(solution)/shard_map/ppermute | solution.py:325
  97.5 0.5 copy-start.11

commit v4 on v3

--- a/solution.py
+++ b/solution.py
@@ -12,6 +12,8 @@
 VMEM = pl.BlockSpec(memory_space=pltpu.VMEM)
 SMEM = pl.BlockSpec(memory_space=pltpu.SMEM)
 HBM = pl.BlockSpec(memory_space=pltpu.HBM)
+PACK = 20000000000
+PREP = 10000000000
 NT = (((1,), (1,)), ((), ()))
 
 
@@ -35,7 +37,7 @@
     return lax.broadcasted_iota(jnp.int32, shape, dim)
 
 
-def pack_kernel(lon, c_hbm, v_hbm, x_ref, first_ref, last_ref, own_ref, c_ref, v_ref, sems):
+def pack_kernel(lon, c_hbm, v_hbm, x_ref, first_ref, last_ref, c_ref, v_ref, sems):
     copies = [
         pltpu.make_async_copy(c_hbm, c_ref, sems.at[0]),
         pltpu.make_async_copy(v_hbm, v_ref, sems.at[1]),
@@ -54,52 +56,26 @@
             first_ref[r] = x
         if r >= rows - lon:
             last_ref[r - (rows - lon)] = x
-    own_ref[0] = c_ref[:rows, :]
-    own_ref[1] = v_ref[:rows, :]
 
 
 def prep_kernel(
     total_lon,
-    pattern_hbm,
-    live_hbm,
-    inverse_hbm,
-    depth_hbm,
-    rate_hbm,
-    stoich_hbm,
-    basis_hbm,
-    blocks_hbm,
-    own_ref,
+    pattern_ref,
+    live_ref,
+    inverse_ref,
+    depth_ref,
+    rate_ref,
+    stoich_ref,
+    basis_ref,
+    c_ref,
+    v_ref,
     index_ref,
     high_ref,
     low_ref,
     source_ref,
     rate_column_ref,
     gram_ref,
-    basis_ref,
-    held_ref,
-    pattern_ref,
-    live_ref,
-    inverse_ref,
-    depth_ref,
-    rate_ref,
-    stoich_ref,
-    sems,
 ):
-    pairs = [
-        (pattern_hbm, pattern_ref),
-        (live_hbm, live_ref),
-        (depth_hbm, depth_ref),
-        (rate_hbm, rate_ref),
-        (stoich_hbm, stoich_ref),
-        (inverse_hbm, inverse_ref),
-        (basis_hbm, basis_ref),
-        (blocks_hbm, held_ref),
-    ]
-    copies = [pltpu.make_async_copy(a, b, sems.at[i]) for i, (a, b) in enumerate(pairs)]
-    for copy in copies:
-        copy.start()
-    for copy in copies[:5]:
-        copy.wait()
     lat, lon, slots = pattern_ref.shape
     rows = lat * lon
     columns, levels = inverse_ref.shape[2:4]
@@ -120,7 +96,7 @@
     wet = (lane % levels < below).astype(F32)
 
     rate = jnp.concatenate([rate_ref[i] for i in range(lat)], 0)
-    uptake, pull = sources(own_ref[0], own_ref[1], rate)
+    uptake, pull = sources(c_ref[:rows, :], v_ref[:rows, :], rate)
     spare = 8 - rows % 8 if rows % 8 else 0
     blank = [jnp.zeros((spare, points), F32)] if spare else []
     columns_of = [
@@ -136,7 +112,6 @@
         at = slice(r, r + 1)
         source_ref[r] = columns_of[0][:, at] * share_c + columns_of[1][:, at] * share_v
 
-    copies[5].wait()
     spread = (iota((levels, points), 1) % levels == iota((levels, points), 0)).astype(BF16)
     full = (points, points)
     same = iota(full, 0) // levels == iota(full, 1) // levels
@@ -150,7 +125,6 @@
             tiled = jnp.dot(part, spread, preferred_element_type=F32)
             ref[r] = (tiled * keep).astype(BF16)
 
-    copies[6].wait()
     gram_ref[...] = jnp.zeros(gram_ref.shape, F32)
     count = basis_ref.shape[0]
     row = 0
@@ -158,7 +132,6 @@
         for j in range(k, count):
             gram_ref[row : row + 1, :] = jnp.sum(basis_ref[k] * basis_ref[j], 0, keepdims=True)
             row += 1
-    copies[7].wait()
 
 
 def sources(own_c, own_v, rate):
@@ -190,17 +163,20 @@
     pad_ref[(lat + 2) * wide] = jnp.zeros(pad_ref.shape[1:], BF16)
 
 
-def advance(r, index_ref, pad_ref, held_ref, high_ref, low_ref, source_ref):
-    slots = index_ref.shape[2]
-    lon = index_ref.shape[1]
+def transport(r, index_ref, pad_ref, held_ref, source_ref):
+    lon, slots = index_ref.shape[1:]
     z = source_ref[r]
     for s in range(slots):
         x = pad_ref[index_ref[r // lon, r % lon, s]]
         z = z + lax.dot_general(held_ref[r * slots + s], x, NT, preferred_element_type=F32)
+    return z
+
+
+def mix(z, high, low):
     z_high = z.astype(BF16)
     z_low = (z - z_high.astype(F32)).astype(BF16)
     dot = functools.partial(jnp.dot, preferred_element_type=F32)
-    return dot(high_ref[r], z_high) + (dot(low_ref[r], z_high) + dot(high_ref[r], z_low))
+    return dot(high, z_high) + (dot(low, z_high) + dot(high, z_low))
 
 
 def first_kernel(
@@ -226,9 +202,11 @@
     fill(pad_ref, x_ref, north_ref, south_ref, west_ref, east_ref, lat, lon)
     tracers = y_ref.shape[1]
     for r in range(rows):
-        out = advance(r, index_ref, pad_ref, held_ref, high_ref, low_ref, source_ref)
-        state_ref[r] = out
-        y = jnp.transpose(out)[tracers:].astype(BF16)
+        state_ref[r] = transport(r, index_ref, pad_ref, held_ref, source_ref)
+    for r in range(rows):
+        state_ref[r] = mix(state_ref[r], high_ref[r], low_ref[r])
+    for r in range(rows):
+        y = jnp.transpose(state_ref[r])[tracers:].astype(BF16)
         y_ref[r] = y
         if r < lon:
             first_ref[r] = y
@@ -254,13 +232,17 @@
     product_ref,
     sums_ref,
     pad_ref,
+    state_ref,
 ):
     rows = lat * lon
     fill(pad_ref, x_ref, north_ref, south_ref, west_ref, east_ref, lat, lon)
     tracers = x_ref.shape[1]
     for r in range(rows):
-        out = advance(r, index_ref, pad_ref, held_ref, high_ref, low_ref, source_ref)
-        product_ref[pl.ds(r, tracers, stride=rows), :] = jnp.transpose(out)
+        state_ref[r] = transport(r, index_ref, pad_ref, held_ref, source_ref)
+    for r in range(rows):
+        state_ref[r] = mix(state_ref[r], high_ref[r], low_ref[r])
+    for r in range(rows):
+        product_ref[pl.ds(r, tracers, stride=rows), :] = jnp.transpose(state_ref[r])
     product = product_ref[...]
     count = basis_ref.shape[0]
     pairs = count * (count + 1) // 2
@@ -355,21 +337,26 @@
     places = (lat + 2) * (lon + 2) + 1
     share = stoich.reshape(1, tracers)
 
-    x, first, last, own = call(
+    flat_c = base_state.reshape(size, points)
+    flat_v = tangent.reshape(size, points)
+    x, first, last = call(
         functools.partial(pack_kernel, lon),
         (
             like((rows, 2 * tracers, points), BF16),
             like((lon, 2 * tracers, points), BF16),
             like((lon, 2 * tracers, points), BF16),
-            like((2, rows, points)),
         ),
         [HBM] * 2,
-        [VMEM] * 4,
+        [VMEM] * 3,
         scratch=[pltpu.VMEM((size, points), F32)] * 2 + [pltpu.SemaphoreType.DMA((2,))],
         size=400000,
-    )(base_state.reshape(size, points), tangent.reshape(size, points))
-
-    index, high, low, source, rate_column, gram, flat_basis, held = call(
+        flops=PACK,
+        limit=59,
+    )(flat_c, flat_v)
+
+    flat_basis = basis.reshape(count, size, points)
+    held = blocks.reshape(rows * slots, points, points)
+    index, high, low, source, rate_column, gram = call(
         functools.partial(prep_kernel, total_lon),
         (
             like((lat, lon, slots), jnp.int32),
@@ -378,21 +365,10 @@
             like((rows, points, 2 * tracers)),
             like((points, (rows + 7) // 8 * 8)),
             like((16, points)),
-            like((count, size, points)),
-            like((rows * slots, points, points), BF16),
         ),
-        [HBM] * 8 + [VMEM],
-        [VMEM] * 8,
-        scratch=[
-            pltpu.VMEM(pattern.shape, jnp.int32),
-            pltpu.VMEM(live.shape, jnp.int32),
-            pltpu.VMEM(column_inverse.shape, F32),
-            pltpu.VMEM(col_depth.shape, jnp.int32),
-            pltpu.VMEM(uptake_rate.shape, F32),
-            pltpu.VMEM(share.shape, F32),
-            pltpu.SemaphoreType.DMA((8,)),
-        ],
-        flops=20000000,
+        [VMEM] * 9,
+        [VMEM] * 6,
+        flops=PREP,
         size=8000000,
     )(
         pattern,
@@ -401,9 +377,9 @@
         col_depth,
         uptake_rate,
         share,
-        basis.reshape(count, size, points),
-        blocks.reshape(rows * slots, points, points),
-        own,
+        flat_basis,
+        flat_c,
+        flat_v,
     )
 
     north, south, west, east = halo(x, first, last, lat, lon)
@@ -433,7 +409,10 @@
         (like((size, points)), like((lax.axis_size("lat"), points))),
         [SMEM] + [VMEM] * 11,
         [VMEM] * 2,
-        scratch=[pltpu.VMEM((places, tracers, points), BF16)],
+        scratch=[
+            pltpu.VMEM((places, tracers, points), BF16),
+            pltpu.VMEM((rows, points, tracers), F32),
+        ],
         flops=work // 2,
         size=5000000,
     )(index, x, north, south, west, east, held, high, low, source, gram, flat_basis)

time: 98.8 us -> 85.8 us (0.87)
  local copies, waits for them, and re-layouts: 9.87 us -> 1.35 us
  Pallas kernels: 14.6 us -> 9.81 us
  waiting for transfers between devices: 5.48 us -> 8.09 us
  blocking collectives: 43.2 us -> 41.7 us
    unnamed x24, local copies, waits for them, and re-layouts: 9.83 us -> 0.56 us
    pallas_call x1, Pallas kernels: 4.88 us -> 2.23 us  [body(): call(functools.partial(second_kernel, lat, lon), (like((size, points)), l...]
    pallas_call x1, Pallas kernels: 4.73 us -> 2.08 us  [body(): call(functools.partial(first_kernel, lat, lon), (like((rows, tracers, poi...]
    ppermute x8, waiting for transfers between devices: 5.48 us -> 8.09 us  [moved(): return lax.ppermute(a, axis, pairs)]
    pallas_call x1, Pallas kernels: 0.25 us -> 1.72 us  [body(): call(functools.partial(pack_kernel, lon), (like((rows, 2 * tracers, point...]
    all_to_all x1, blocking collectives: 26.6 us -> 25.3 us  [summed(): return lax.all_to_all(rows, 'lon', 0, 0)]
  transfers between devices with their start and end apart: 8 -> 8, of which waited for: 3 -> 4; matrix products, arithmetic and copies ran while one was open for 0% -> 1% of each run, Pallas kernels for 3% -> 3%
where the time goes in v4:
time: 85.8 us; the launch traced here: 85.3 us
  blocking collectives  41.7 us (49%)
  starting transfers between devices  22.7 us (26%)
  Pallas kernels  9.81 us (11%)
  waiting for transfers between devices  8.09 us (9%)
  local copies, waits for them, and re-layouts  1.35 us (2%)
  between operations  0.98 us (1%)
    all_to_all x1, blocking collectives, summed(): return lax.all_to_all(rows, 'lon', 0, 0)  25.3 us
    ppermute x8, starting transfers between devices, moved(): return lax.ppermute(a, axis, pairs)  22.7 us
    all_to_all x1, blocking collectives, summed(): row = jnp.sum(lax.all_to_all(rows, 'lat', 0, 0), 0, keepdims=True)  16.5 us
    ppermute x8, waiting for transfers between devices, moved(): return lax.ppermute(a, axis, pairs)  8.09 us
    pallas_call x1, Pallas kernels, body(): call(functools.partial(second_kernel, lat, lon), (like((size, points)), l...  2.23 us
    pallas_call x1, Pallas kernels, body(): call(functools.partial(first_kernel, lat, lon), (like((rows, tracers, poi...  2.08 us
    pallas_call x1, Pallas kernels, body(): call(functools.partial(pack_kernel, lon), (like((rows, 2 * tracers, point...  1.72 us
  transfers between devices with their start and end apart: 8, of which 4 were waited for; matrix products, arithmetic and copies ran while one was open for 1% of the time, Pallas kernels for 3%

profile of v4, /device:TPU:1, one launch (start us, length us, event | category | flops | bytes accessed | tf_op | source)
XLA Modules:
  0.0 85.3 jit_solution(11999376893860179312)
XLA Ops:
  0.6 0.0 copy-start.2
  0.6 0.0 copy-start.3
  0.7 0.0 copy-start.4
  0.7 0.0 copy-start.5
  0.7 0.0 copy-start.6
  0.7 0.0 copy-start.7
  0.7 0.0 copy-start.8
  0.7 0.0 copy-start.9
  0.7 0.0 copy-start.10
  0.7 1.7 %shard_map.122 = (bf16[12,32,128]{2,1,0:T(8,128)(2,1)}, bf16[4,32,128]{2,1,0:T(8,128)(2,1)}, bf16[4,32,128]{2,1,0:T(8,128)(2,1)}) custom-call(f32[192,128]{1,0:T(8,128)} %bitcast.51, f32[192,128]{1,0:T(8,128)} %bitcast.53), custom_call_target="tpu_custom_call" | custom-call | flops 20000000000 | bytes 400000 | tf_op jit(solution)/shard_map/pallas_call | solution.py:342
  2.4 4.6 %collective-permute-start = (bf16[4,32,128]{2,1,0:T(8,128)(2,1)}, bf16[4,32,128]{2,1,0:T(8,128)(2,1)S(1)}, u32[]{:S(2)}, u32[]{:S(2)}) collective-permute-start(bf16[4,32,128]{2,1,0:T(8,128)(2,1)} %get-tuple-element.50), channel_id=1, source_target_pairs={{0,32},{32,64},{64,96},{96,128},{128,160},{160,192},{192,224},{224... | collective-permute-start | bytes 98312 | tf_op jit(solution)/shard_map/ppermute | solution.py:307
  7.0 5.5 %collective-permute-start.1 = (bf16[4,32,128]{2,1,0:T(8,128)(2,1)}, bf16[4,32,128]{2,1,0:T(8,128)(2,1)S(1)}, u32[]{:S(2)}, u32[]{:S(2)}) collective-permute-start(bf16[4,32,128]{2,1,0:T(8,128)(2,1)} %get-tuple-element.51), channel_id=1, source_target_pairs={{32,0},{64,32},{96,64},{128,96},{160,128},{192,160},{224,192},{256... | collective-permute-start | bytes 98312 | tf_op jit(solution)/shard_map/ppermute | solution.py:307
  12.5 0.8 slice_bitcast_fusion
  13.3 0.0 collective-permute-done.north_ref
  13.3 0.3 collective-permute-done.1.south_ref
  13.6 2.0 %collective-permute-start.2 = (bf16[5,32,128]{2,1,0:T(8,128)(2,1)S(1)}, bf16[5,32,128]{2,1,0:T(8,128)(2,1)S(1)}, u32[]{:S(2)}, u32[]{:S(2)}) collective-permute-start(bf16[5,32,128]{2,1,0:T(8,128)(2,1)S(1)} %pad_maximum_fusion.1), channel_id=1, source_target_pairs={{0,1},{1,2},{2,3},{3,4},{4,5},{5,6},{6,7},{7,8},{8,9},{9,10},{10,1... | collective-permute-start | bytes 122888 | tf_op jit(solution)/shard_map/ppermute | solution.py:307
  15.6 1.3 %collective-permute-start.3 = (bf16[5,32,128]{2,1,0:T(8,128)(2,1)S(1)}, bf16[5,32,128]{2,1,0:T(8,128)(2,1)S(1)}, u32[]{:S(2)}, u32[]{:S(2)}) collective-permute-start(bf16[5,32,128]{2,1,0:T(8,128)(2,1)S(1)} %pad_maximum_fusion.2), channel_id=1, source_target_pairs={{1,0},{2,1},{3,2},{4,3},{5,4},{6,5},{7,6},{8,7},{9,8},{10,9},{11,1... | collective-permute-start | bytes 122888 | tf_op jit(solution)/shard_map/ppermute | solution.py:307
  16.9 0.0 copy-done.2
  17.0 0.0 copy-done.3
  17.0 0.0 copy-done.4
  17.0 0.0 copy-done.5
  17.0 0.0 copy-done.6
  17.0 0.0 copy-done.7
  17.0 0.0 copy-done.8
  17.0 0.0 copy-done.9
  17.0 0.0 copy-done.10
  17.0 0.0 copy-start
  17.1 0.0 copy-start.1
  17.1 1.0 %shard_map.121 = (s32[3,4,9]{2,1,0:T(4,128)S(1)}, bf16[12,128,128]{2,1,0:T(8,128)(2,1)S(1)}, bf16[12,128,128]{2,1,0:T(8,128)(2,1)S(1)}, f32[12,128,32]{2,1,0:T(8...) custom-call(s32[3,4,9]{2,1,0:T(4,128)S(1)} %copy-done.6, s32[3,4,9]{2,1,0:T(4,128)S(1)} %copy-done.7, ...), custom_call_target="tpu_custom_call" | custom-call | flops 10000000000 | bytes 8000000 | tf_op jit(solution)/shard_map/pallas_call | solution.py:359
  18.1 0.0 collective-permute-done.2.west_ref
  18.1 2.9 %collective-permute-done.3.east_ref = bf16[5,32,128]{2,1,0:T(8,128)(2,1)S(1)} collective-permute-done((bf16[5,32,128]{2,1,0:T(8,128)(2,1)S(1)}, bf16[5,32,128]{2,1,0:T(8,128)(2,1)S(1)}, u32[]{:S(2)}, u32[]{:S(2)}) %collective-permute-start.3) | collective-permute-done | bytes 40992 | tf_op jit(solution)/shard_map/ppermute | solution.py:307
  21.0 0.0 copy-done
  21.1 0.0 copy-done.1
  21.1 2.1 %shard_map.123 = (bf16[12,16,128]{2,1,0:T(8,128)(2,1)S(1)}, bf16[4,16,128]{2,1,0:T(8,128)(2,1)S(1)}, bf16[4,16,128]{2,1,0:T(8,128)(2,1)S(1)}, f32[12,128,32]{2,1,0:T(8,128)S(1)}) custom-call(s32[3,4,9]{2,1,0:T(4,128)S(1)} %get-tuple-element.48.index_ref, bf16[12,32,128]{2,1,0:T(8,128)(2,1)S(1)} %copy-done.1, ...), custom_call_target="tpu_custom_call" | custom-call | flops 113246208 | bytes 5000000 | tf_op jit(solution)/shard_map/pallas_call | solution.py:387
  23.1 2.9 %collective-permute-start.4 = (bf16[4,16,128]{2,1,0:T(8,128)(2,1)S(1)}, bf16[4,16,128]{2,1,0:T(8,128)(2,1)S(1)}, u32[]{:S(2)}, u32[]{:S(2)}) collective-permute-start(bf16[4,16,128]{2,1,0:T(8,128)(2,1)S(1)} %get-tuple-element.56), channel_id=1, source_target_pairs={{0,32},{32,64},{64,96},{96,128},{128,160},{160,192},{192,224},{224... | collective-permute-start | bytes 49160 | tf_op jit(solution)/shard_map/ppermute | solution.py:307
  26.1 1.9 %collective-permute-start.5 = (bf16[4,16,128]{2,1,0:T(8,128)(2,1)S(1)}, bf16[4,16,128]{2,1,0:T(8,128)(2,1)S(1)}, u32[]{:S(2)}, u32[]{:S(2)}) collective-permute-start(bf16[4,16,128]{2,1,0:T(8,128)(2,1)S(1)} %get-tuple-element.57), channel_id=1, source_target_pairs={{32,0},{64,32},{96,64},{128,96},{160,128},{192,160},{224,192},{256... | collective-permute-start | bytes 49160 | tf_op jit(solution)/shard_map/ppermute | solution.py:307
  28.0 0.0 collective-permute-done.4.north_ref
  28.0 3.1 %collective-permute-done.5.south_ref = bf16[4,16,128]{2,1,0:T(8,128)(2,1)S(1)} collective-permute-done((bf16[4,16,128]{2,1,0:T(8,128)(2,1)S(1)}, bf16[4,16,128]{2,1,0:T(8,128)(2,1)S(1)}, u32[]{:S(2)}, u32[]{:S(2)}) %collective-permute-start.5) | collective-permute-done | bytes 16416 | tf_op jit(solution)/shard_map/ppermute | solution.py:307
  31.2 3.1 %collective-permute-start.6 = (bf16[5,16,128]{2,1,0:T(8,128)(2,1)S(1)}, bf16[5,16,128]{2,1,0:T(8,128)(2,1)S(1)}, u32[]{:S(2)}, u32[]{:S(2)}) collective-permute-start(bf16[5,16,128]{2,1,0:T(8,128)(2,1)S(1)} %pad_maximum_fusion.3), channel_id=1, source_target_pairs={{0,1},{1,2},{2,3},{3,4},{4,5},{5,6},{6,7},{7,8},{8,9},{9,10},{10,1... | collective-permute-start | bytes 61448 | tf_op jit(solution)/shard_map/ppermute | solution.py:307
  34.3 1.3 %collective-permute-start.7 = (bf16[5,16,128]{2,1,0:T(8,128)(2,1)S(1)}, bf16[5,16,128]{2,1,0:T(8,128)(2,1)S(1)}, u32[]{:S(2)}, u32[]{:S(2)}) collective-permute-start(bf16[5,16,128]{2,1,0:T(8,128)(2,1)S(1)} %pad_maximum_fusion.4), channel_id=1, source_target_pairs={{1,0},{2,1},{3,2},{4,3},{5,4},{6,5},{7,6},{8,7},{9,8},{10,9},{11,1... | collective-permute-start | bytes 61448 | tf_op jit(solution)/shard_map/ppermute | solution.py:307
  35.6 1.4 %shard_map.124.source_ref = f32[12,128,16]{2,1,0:T(8,128)S(1)} custom-call(f32[12,128,32]{2,1,0:T(8,128)S(1)} %get-tuple-element.58.state_ref, f32[128,16]{1,0:T(8,128)S(1)} %get-tuple-element.59.rate_column_ref, f32[1,16]{1,0:T(1,128)S(1)} %bitcast.50), custom_call_target="tpu_custom_call" | custom-call | flops 100000 | bytes 2000000 | tf_op jit(solution)/shard_map/pallas_call | solution.py:402
  37.0 0.0 collective-permute-done.6.west_ref
  37.1 1.8 %collective-permute-done.7.east_ref = bf16[5,16,128]{2,1,0:T(8,128)(2,1)S(1)} collective-permute-done((bf16[5,16,128]{2,1,0:T(8,128)(2,1)S(1)}, bf16[5,16,128]{2,1,0:T(8,128)(2,1)S(1)}, u32[]{:S(2)}, u32[]{:S(2)}) %collective-permute-start.7) | collective-permute-done | bytes 20512 | tf_op jit(solution)/shard_map/ppermute | solution.py:307
  38.8 2.2 %shard_map.125 = (f32[192,128]{1,0:T(8,128)S(1)}, f32[16,128]{1,0:T(8,128)S(1)}) custom-call(s32[3,4,9]{2,1,0:T(4,128)S(1)} %get-tuple-element.48.index_ref, bf16[12,16,128]{2,1,0:T(8,128)(2,1)S(1)} %get-tuple-element.55.x_ref, bf16[4,16,128]{2,1,0:T(8,128)(2,1)S(1)} %collective-permute-done.4.north_ref, ...), custom_call_target="tpu_custom_call" | custom-call | flops 56623104 | bytes 5000000 | tf_op jit(solution)/shard_map/pallas_call | solution.py:407
  41.1 16.5 %all_to_all.28 = f32[16,1,128]{2,1,0:T(1,128)S(1)} all-to-all(f32[16,1,128]{2,1,0:T(1,128)S(1)} %bitcast.48), channel_id=1, replica_groups=mesh['lat'=16,'lon'=32] {'lat'}, dimensions={0} | all-to-all | bytes 16384 | tf_op jit(solution)/shard_map/all_to_all | solution.py:298
  57.6 25.3 %all_to_all.29 = f32[32,1,128]{2,1,0:T(1,128)S(1)} all-to-all(f32[32,1,128]{2,1,0:T(1,128)S(1)} %broadcast_in_dim.6), channel_id=1, replica_groups=mesh['lat'=16,'lon'=32] {'lon'}, dimensions={0} | all-to-all | bytes 32768 | tf_op jit(solution)/shard_map/all_to_all | solution.py:300
  82.8 1.3 %shard_map.126 = (f32[192,128]{1,0:T(8,128)}, f32[192,128]{1,0:T(8,128)}, f32[5]{0:T(128)S(1)}, s32[1]{0:T(128)}) custom-call(f32[32,128]{1,0:T(8,128)S(1)} %bitcast.47, f32[192,128]{1,0:T(8,128)S(1)} %get-tuple-element.102.product_ref, f32[4,192,128]{2,1,0:T(8,128)S(1)} %bitcast.57), custom_call_target="tpu_custom_call" | custom-call | bytes 700000 | tf_op jit(solution)/shard_map/pallas_call | solution.py:421
  84.2 0.7 while.11
  84.8 0.0 copy-start.11
  84.8 0.5 copy-done.11
  (11 shorter events, 0.1 us)
Async XLA Ops:
  0.6 16.3 %copy-start.2 = (f32[16]{0:T(128)S(1)}, f32[16]{0:T(128)}, u32[]{:S(2)}) copy-start(f32[16]{0:T(128)} %param.20) | copy-start | bytes 196
  0.6 16.3 %copy-start.3 = (f32[3,4,8,16,16]{4,3,2,1,0:T(8,128)S(1)}, f32[3,4,8,16,16]{4,3,2,1,0:T(8,128)}, u32[]{:S(2)}) copy-start(f32[3,4,8,16,16]{4,3,2,1,0:T(8,128)} %inverse_ref.1) | copy-start | bytes 294916
  0.7 16.3 %copy-start.4 = (f32[16,3,4,128]{3,2,1,0:T(4,128)S(1)}, f32[16,3,4,128]{3,2,1,0:T(4,128)}, u32[]{:S(2)}) copy-start(f32[16,3,4,128]{3,2,1,0:T(4,128)} %param.12) | copy-start | bytes 294916
  0.7 16.3 %copy-start.5 = (f32[16,3,4,128]{3,2,1,0:T(4,128)S(1)}, f32[16,3,4,128]{3,2,1,0:T(4,128)}, u32[]{:S(2)}) copy-start(f32[16,3,4,128]{3,2,1,0:T(4,128)} %param.13) | copy-start | bytes 294916
  0.7 16.3 %copy-start.6 = (s32[3,4,9]{2,1,0:T(4,128)S(1)}, s32[3,4,9]{2,1,0:T(4,128)}, u32[]{:S(2)}) copy-start(s32[3,4,9]{2,1,0:T(4,128)} %pattern_ref.1) | copy-start | bytes 1300
  0.7 16.3 %copy-start.7 = (s32[3,4,9]{2,1,0:T(4,128)S(1)}, s32[3,4,9]{2,1,0:T(4,128)}, u32[]{:S(2)}) copy-start(s32[3,4,9]{2,1,0:T(4,128)} %live_ref.1) | copy-start | bytes 1300
  0.7 16.3 %copy-start.8 = (s32[3,4,8]{2,1,0:T(4,128)S(1)}, s32[3,4,8]{2,1,0:T(4,128)}, u32[]{:S(2)}) copy-start(s32[3,4,8]{2,1,0:T(4,128)} %depth_ref.1) | copy-start | bytes 1156
  0.7 16.3 %copy-start.9 = (f32[3,4,128]{2,1,0:T(4,128)S(1)}, f32[3,4,128]{2,1,0:T(4,128)}, u32[]{:S(2)}) copy-start(f32[3,4,128]{2,1,0:T(4,128)} %rate_ref.1) | copy-start | bytes 18436
  0.7 16.3 %copy-start.10 = (f32[4,16,3,4,128]{4,3,2,1,0:T(4,128)S(1)}, f32[4,16,3,4,128]{4,3,2,1,0:T(4,128)}, u32[]{:S(2)}) copy-start(f32[4,16,3,4,128]{4,3,2,1,0:T(4,128)} %param.21) | copy-start | bytes 1179652
  2.4 10.9 %collective-permute-start = (bf16[4,32,128]{2,1,0:T(8,128)(2,1)}, bf16[4,32,128]{2,1,0:T(8,128)(2,1)S(1)}, u32[]{:S(2)}, u32[]{:S(2)}) collective-permute-start(bf16[4,32,128]{2,1,0:T(8,128)(2,1)} %get-tuple-element.50), channel_id=1, source_target_pairs={{0,32},{32,64},{64,96},{96,128},{128,160},{160,192},{192,224},{224... | collective-permute-start | bytes 98312 | tf_op jit(solution)/shard_map/ppermute | solution.py:307
  7.0 6.5 %collective-permute-start.1 = (bf16[4,32,128]{2,1,0:T(8,128)(2,1)}, bf16[4,32,128]{2,1,0:T(8,128)(2,1)S(1)}, u32[]{:S(2)}, u32[]{:S(2)}) collective-permute-start(bf16[4,32,128]{2,1,0:T(8,128)(2,1)} %get-tuple-element.51), channel_id=1, source_target_pairs={{32,0},{64,32},{96,64},{128,96},{160,128},{192,160},{224,192},{256... | collective-permute-start | bytes 98312 | tf_op jit(solution)/shard_map/ppermute | solution.py:307
  13.6 4.5 %collective-permute-start.2 = (bf16[5,32,128]{2,1,0:T(8,128)(2,1)S(1)}, bf16[5,32,128]{2,1,0:T(8,128)(2,1)S(1)}, u32[]{:S(2)}, u32[]{:S(2)}) collective-permute-start(bf16[5,32,128]{2,1,0:T(8,128)(2,1)S(1)} %pad_maximum_fusion.1), channel_id=1, source_target_pairs={{0,1},{1,2},{2,3},{3,4},{4,5},{5,6},{6,7},{7,8},{8,9},{9,10},{10,1... | collective-permute-start | bytes 122888 | tf_op jit(solution)/shard_map/ppermute | solution.py:307
  15.6 5.4 %collective-permute-start.3 = (bf16[5,32,128]{2,1,0:T(8,128)(2,1)S(1)}, bf16[5,32,128]{2,1,0:T(8,128)(2,1)S(1)}, u32[]{:S(2)}, u32[]{:S(2)}) collective-permute-start(bf16[5,32,128]{2,1,0:T(8,128)(2,1)S(1)} %pad_maximum_fusion.2), channel_id=1, source_target_pairs={{1,0},{2,1},{3,2},{4,3},{5,4},{6,5},{7,6},{8,7},{9,8},{10,9},{11,1... | collective-permute-start | bytes 122888 | tf_op jit(solution)/shard_map/ppermute | solution.py:307
  17.0 4.0 %copy-start = (bf16[3,4,9,128,128]{4,3,2,1,0:T(8,128)(2,1)S(1)}, bf16[3,4,9,128,128]{4,3,2,1,0:T(8,128)(2,1)}, u32[]{:S(2)}) copy-start(bf16[3,4,9,128,128]{4,3,2,1,0:T(8,128)(2,1)} %param.14) | copy-start | bytes 10616836
  17.1 4.0 %copy-start.1 = (bf16[12,32,128]{2,1,0:T(8,128)(2,1)S(1)}, bf16[12,32,128]{2,1,0:T(8,128)(2,1)}, u32[]{:S(2)}) copy-start(bf16[12,32,128]{2,1,0:T(8,128)(2,1)} %get-tuple-element.49.x_ref) | copy-start | bytes 294916
  23.1 4.9 %collective-permute-start.4 = (bf16[4,16,128]{2,1,0:T(8,128)(2,1)S(1)}, bf16[4,16,128]{2,1,0:T(8,128)(2,1)S(1)}, u32[]{:S(2)}, u32[]{:S(2)}) collective-permute-start(bf16[4,16,128]{2,1,0:T(8,128)(2,1)S(1)} %get-tuple-element.56), channel_id=1, source_target_pairs={{0,32},{32,64},{64,96},{96,128},{128,160},{160,192},{192,224},{224... | collective-permute-start | bytes 49160 | tf_op jit(solution)/shard_map/ppermute | solution.py:307
  26.1 5.1 %collective-permute-start.5 = (bf16[4,16,128]{2,1,0:T(8,128)(2,1)S(1)}, bf16[4,16,128]{2,1,0:T(8,128)(2,1)S(1)}, u32[]{:S(2)}, u32[]{:S(2)}) collective-permute-start(bf16[4,16,128]{2,1,0:T(8,128)(2,1)S(1)} %get-tuple-element.57), channel_id=1, source_target_pairs={{32,0},{64,32},{96,64},{128,96},{160,128},{192,160},{224,192},{256... | collective-permute-start | bytes 49160 | tf_op jit(solution)/shard_map/ppermute | solution.py:307
  31.2 5.9 %collective-permute-start.6 = (bf16[5,16,128]{2,1,0:T(8,128)(2,1)S(1)}, bf16[5,16,128]{2,1,0:T(8,128)(2,1)S(1)}, u32[]{:S(2)}, u32[]{:S(2)}) collective-permute-start(bf16[5,16,128]{2,1,0:T(8,128)(2,1)S(1)} %pad_maximum_fusion.3), channel_id=1, source_target_pairs={{0,1},{1,2},{2,3},{3,4},{4,5},{5,6},{6,7},{7,8},{8,9},{9,10},{10,1... | collective-permute-start | bytes 61448 | tf_op jit(solution)/shard_map/ppermute | solution.py:307
  34.3 4.5 %collective-permute-start.7 = (bf16[5,16,128]{2,1,0:T(8,128)(2,1)S(1)}, bf16[5,16,128]{2,1,0:T(8,128)(2,1)S(1)}, u32[]{:S(2)}, u32[]{:S(2)}) collective-permute-start(bf16[5,16,128]{2,1,0:T(8,128)(2,1)S(1)} %pad_maximum_fusion.4), channel_id=1, source_target_pairs={{1,0},{2,1},{3,2},{4,3},{5,4},{6,5},{7,6},{8,7},{9,8},{10,9},{11,1... | collective-permute-start | bytes 61448 | tf_op jit(solution)/shard_map/ppermute | solution.py:307
  84.8 0.5 copy-start.11

commit v5 on v4

--- a/solution.py
+++ b/solution.py
@@ -295,25 +295,26 @@
 
 
 def summed(rows):
-    row = jnp.sum(lax.all_to_all(rows, "lat", 0, 0), 0, keepdims=True)
-    rows = jnp.broadcast_to(row, (lax.axis_size("lon"), row.shape[1]))
-    return lax.all_to_all(rows, "lon", 0, 0)
-
-
-def halo(x, first, last, lat, lon):
+    row = jnp.sum(lax.all_to_all(rows, "lon", 0, 0), 0, keepdims=True)
+    rows = jnp.broadcast_to(row, (lax.axis_size("lat"), row.shape[1]))
+    return lax.all_to_all(rows, "lat", 0, 0)
+
+
+def halo(x, first, last, lat, lon, beside=None):
     def moved(a, axis, step):
         size = lax.axis_size(axis)
-        pairs = [(i, i + step) for i in range(size) if 0 <= i + step < size]
-        return lax.ppermute(a, axis, pairs)
+        return lax.ppermute(a, axis, [(i, (i + step) % size) for i in range(size)])
 
     north = moved(last, "lat", 1)
     south = moved(first, "lat", -1)
+    if beside is not None:
+        north, south, beside = lax.optimization_barrier((north, south, beside))
     grid = x.reshape((lat, lon) + x.shape[1:])
     right = jnp.concatenate([north[None, lon - 1], grid[:, lon - 1], south[None, lon - 1]], 0)
     left = jnp.concatenate([north[None, 0], grid[:, 0], south[None, 0]], 0)
     west = moved(right, "lon", 1)
     east = moved(left, "lon", -1)
-    return north, south, west, east
+    return north, south, west, east, beside
 
 
 def body(
@@ -382,7 +383,7 @@
         flat_v,
     )
 
-    north, south, west, east = halo(x, first, last, lat, lon)
+    north, south, west, east, _ = halo(x, first, last, lat, lon)
     work = 2 * 2 * tracers * rows * slots * points * points
     x, first, last, state = call(
         functools.partial(first_kernel, lat, lon),
@@ -403,10 +404,10 @@
         pull_kernel, like((rows, points, tracers)), [VMEM] * 3, VMEM, flops=100000, size=2000000
     )(state, rate_column, share)
 
-    north, south, west, east = halo(x, first, last, lat, lon)
+    north, south, west, east, source = halo(x, first, last, lat, lon, source)
     product, sums = call(
         functools.partial(second_kernel, lat, lon),
-        (like((size, points)), like((lax.axis_size("lat"), points))),
+        (like((size, points)), like((lax.axis_size("lon"), points))),
         [SMEM] + [VMEM] * 11,
         [VMEM] * 2,
         scratch=[
@@ -433,7 +434,7 @@
             "k,ksp->sp", coeffs[:count], flat_basis, precision=lax.Precision.HIGHEST
         )
         part = jnp.pad(jnp.sum(rest * rest).reshape(1, 1), ((0, 0), (0, points - 1)))
-        squared = jnp.sum(summed(jnp.broadcast_to(part, (lax.axis_size("lat"), points))), 0)[0]
+        squared = jnp.sum(summed(jnp.broadcast_to(part, (lax.axis_size("lon"), points))), 0)[0]
         beta = jnp.sqrt(squared + 1e-06)
         return rest / beta, jnp.concatenate([coeffs[:count], beta[None]]), flag * 0
 

time: 85.8 us -> 79.6 us (0.928)
  blocking collectives: 41.7 us -> 33.2 us
  starting transfers between devices: 22.7 us -> 29.3 us
  waiting for transfers between devices: 8.09 us -> 3.07 us
  local copies, waits for them, and re-layouts: 1.35 us -> 2.25 us
    all_to_all x2, blocking collectives: 41.7 us -> 33.2 us  [the longest x1 17.5 us: summed(): return lax.all_to_all(rows, 'lat', 0, 0)]
    ppermute x8, starting transfers between devices: 22.7 us -> 29.3 us  [moved(): return lax.ppermute(a, axis, [(i, (i + step) % size) for i in range(size)])]
    ppermute x8, waiting for transfers between devices: 8.09 us -> 3.07 us  [moved(): return lax.ppermute(a, axis, [(i, (i + step) % size) for i in range(size)])]
    unnamed x24, local copies, waits for them, and re-layouts: 0.56 us -> 1.47 us
where the time goes in v5:
time: 79.6 us; the launch traced here: 79.2 us
  blocking collectives  33.2 us (42%)
  starting transfers between devices  29.3 us (37%)
  Pallas kernels  9.81 us (12%)
  waiting for transfers between devices  3.07 us (4%)
  local copies, waits for them, and re-layouts  2.25 us (3%)
  between operations  0.94 us (1%)
    ppermute x8, starting transfers between devices, moved(): return lax.ppermute(a, axis, [(i, (i + step) % size) for i in range(size)])  29.3 us
    all_to_all x1, blocking collectives, summed(): return lax.all_to_all(rows, 'lat', 0, 0)  17.5 us
    all_to_all x1, blocking collectives, summed(): row = jnp.sum(lax.all_to_all(rows, 'lon', 0, 0), 0, keepdims=True)  15.6 us
    ppermute x8, waiting for transfers between devices, moved(): return lax.ppermute(a, axis, [(i, (i + step) % size) for i in range(size)])  3.07 us
    pallas_call x1, Pallas kernels, body(): call(functools.partial(second_kernel, lat, lon), (like((size, points)), l...  2.23 us
    pallas_call x1, Pallas kernels, body(): call(functools.partial(first_kernel, lat, lon), (like((rows, tracers, poi...  2.08 us
    pallas_call x1, Pallas kernels, body(): call(functools.partial(pack_kernel, lon), (like((rows, 2 * tracers, point...  1.72 us
  transfers between devices with their start and end apart: 8, of which 4 were waited for; matrix products, arithmetic and copies ran while one was open for 1% of the time, Pallas kernels for 3%

profile of v5, /device:TPU:1, one launch (start us, length us, event | category | flops | bytes accessed | tf_op | source)
XLA Modules:
  0.0 79.2 jit_solution(401201679978643729)
XLA Ops:
  0.6 0.0 copy-start.2
  0.6 0.0 copy-start.3
  0.7 0.0 copy-start.4
  0.7 0.0 copy-start.5
  0.7 0.0 copy-start.6
  0.7 0.0 copy-start.7
  0.7 0.0 copy-start.8
  0.7 0.0 copy-start.9
  0.7 0.0 copy-start.10
  0.7 1.7 %shard_map.122 = (bf16[12,32,128]{2,1,0:T(8,128)(2,1)}, bf16[4,32,128]{2,1,0:T(8,128)(2,1)}, bf16[4,32,128]{2,1,0:T(8,128)(2,1)}) custom-call(f32[192,128]{1,0:T(8,128)} %bitcast.51, f32[192,128]{1,0:T(8,128)} %bitcast.53), custom_call_target="tpu_custom_call" | custom-call | flops 20000000000 | bytes 400000 | tf_op jit(solution)/shard_map/pallas_call | solution.py:343
  2.4 2.7 %collective-permute-start = (bf16[4,32,128]{2,1,0:T(8,128)(2,1)}, bf16[4,32,128]{2,1,0:T(8,128)(2,1)S(1)}, u32[]{:S(2)}, u32[]{:S(2)}) collective-permute-start(bf16[4,32,128]{2,1,0:T(8,128)(2,1)} %get-tuple-element.53), channel_id=1, source_target_pairs={{0,32},{32,64},{64,96},{96,128},{128,160},{160,192},{192,224},{224... | collective-permute-start | bytes 98312 | tf_op jit(solution)/shard_map/ppermute | solution.py:306
  5.1 4.2 %collective-permute-start.1 = (bf16[4,32,128]{2,1,0:T(8,128)(2,1)}, bf16[4,32,128]{2,1,0:T(8,128)(2,1)S(1)}, u32[]{:S(2)}, u32[]{:S(2)}) collective-permute-start(bf16[4,32,128]{2,1,0:T(8,128)(2,1)} %get-tuple-element.54), channel_id=1, source_target_pairs={{0,480},{32,0},{64,32},{96,64},{128,96},{160,128},{192,160},{224,1... | collective-permute-start | bytes 98312 | tf_op jit(solution)/shard_map/ppermute | solution.py:306
  9.4 0.8 slice_bitcast_fusion
  10.1 0.1 collective-permute-done.north_ref
  10.3 0.2 collective-permute-done.1.south_ref
  10.4 1.9 %collective-permute-start.2 = (bf16[5,32,128]{2,1,0:T(8,128)(2,1)S(1)}, bf16[5,32,128]{2,1,0:T(8,128)(2,1)S(1)}, u32[]{:S(2)}, u32[]{:S(2)}) collective-permute-start(bf16[5,32,128]{2,1,0:T(8,128)(2,1)S(1)} %pad_maximum_fusion.1), channel_id=1, source_target_pairs={{0,1},{1,2},{2,3},{3,4},{4,5},{5,6},{6,7},{7,8},{8,9},{9,10},{10,1... | collective-permute-start | bytes 122888 | tf_op jit(solution)/shard_map/ppermute | solution.py:306
  12.4 11.1 %collective-permute-start.3 = (bf16[5,32,128]{2,1,0:T(8,128)(2,1)S(1)}, bf16[5,32,128]{2,1,0:T(8,128)(2,1)S(1)}, u32[]{:S(2)}, u32[]{:S(2)}) collective-permute-start(bf16[5,32,128]{2,1,0:T(8,128)(2,1)S(1)} %pad_maximum_fusion.2), channel_id=1, source_target_pairs={{0,31},{1,0},{2,1},{3,2},{4,3},{5,4},{6,5},{7,6},{8,7},{9,8},{10,9... | collective-permute-start | bytes 122888 | tf_op jit(solution)/shard_map/ppermute | solution.py:306
  23.5 0.0 copy-done.2
  23.5 0.0 copy-done.3
  23.5 0.0 copy-done.4
  23.6 0.0 copy-done.5
  23.6 0.0 copy-done.6
  23.6 0.0 copy-done.7
  23.6 0.0 copy-done.8
  23.6 0.0 copy-done.9
  23.6 0.0 copy-done.10
  23.6 0.0 copy-start
  23.6 0.0 copy-start.1
  23.6 1.0 %shard_map.121 = (s32[3,4,9]{2,1,0:T(4,128)S(1)}, bf16[12,128,128]{2,1,0:T(8,128)(2,1)S(1)}, bf16[12,128,128]{2,1,0:T(8,128)(2,1)S(1)}, f32[12,128,32]{2,1,0:T(8...) custom-call(s32[3,4,9]{2,1,0:T(4,128)S(1)} %copy-done.6, s32[3,4,9]{2,1,0:T(4,128)S(1)} %copy-done.7, ...), custom_call_target="tpu_custom_call" | custom-call | flops 10000000000 | bytes 8000000 | tf_op jit(solution)/shard_map/pallas_call | solution.py:360
  24.7 0.0 collective-permute-done.2.west_ref
  24.7 0.0 collective-permute-done.3.east_ref
  24.7 0.9 %copy-done = bf16[3,4,9,128,128]{4,3,2,1,0:T(8,128)(2,1)S(1)} copy-done((bf16[3,4,9,128,128]{4,3,2,1,0:T(8,128)(2,1)S(1)}, bf16[3,4,9,128,128]{4,3,2,1,0:T(8,128)(2,1)}, u32[]{:S(2)}) %copy-start) | copy-done | bytes 3538968
  25.6 0.0 copy-done.1
  25.6 2.1 %shard_map.123 = (bf16[12,16,128]{2,1,0:T(8,128)(2,1)S(1)}, bf16[4,16,128]{2,1,0:T(8,128)(2,1)S(1)}, bf16[4,16,128]{2,1,0:T(8,128)(2,1)S(1)}, f32[12,128,32]{2,1,0:T(8,128)S(1)}) custom-call(s32[3,4,9]{2,1,0:T(4,128)S(1)} %get-tuple-element.51.index_ref, bf16[12,32,128]{2,1,0:T(8,128)(2,1)S(1)} %copy-done.1, ...), custom_call_target="tpu_custom_call" | custom-call | flops 113246208 | bytes 5000000 | tf_op jit(solution)/shard_map/pallas_call | solution.py:388
  27.7 0.4 collective-permute-start.4
  28.1 0.1 collective-permute-start.5
  28.3 1.4 %shard_map.124.source_ref = f32[12,128,16]{2,1,0:T(8,128)S(1)} custom-call(f32[12,128,32]{2,1,0:T(8,128)S(1)} %get-tuple-element.61.state_ref, f32[128,16]{1,0:T(8,128)S(1)} %get-tuple-element.62.rate_column_ref, f32[1,16]{1,0:T(1,128)S(1)} %bitcast.50), custom_call_target="tpu_custom_call" | custom-call | flops 100000 | bytes 2000000 | tf_op jit(solution)/shard_map/pallas_call | solution.py:403
  29.7 0.0 collective-permute-done.4.north_ref
  29.7 1.9 %collective-permute-done.5.south_ref = bf16[4,16,128]{2,1,0:T(8,128)(2,1)S(1)} collective-permute-done((bf16[4,16,128]{2,1,0:T(8,128)(2,1)S(1)}, bf16[4,16,128]{2,1,0:T(8,128)(2,1)S(1)}, u32[]{:S(2)}, u32[]{:S(2)}) %collective-permute-start.5) | collective-permute-done | bytes 16416 | tf_op jit(solution)/shard_map/ppermute | solution.py:306
  31.6 1.9 %collective-permute-start.6 = (bf16[5,16,128]{2,1,0:T(8,128)(2,1)S(1)}, bf16[5,16,128]{2,1,0:T(8,128)(2,1)S(1)}, u32[]{:S(2)}, u32[]{:S(2)}) collective-permute-start(bf16[5,16,128]{2,1,0:T(8,128)(2,1)S(1)} %pad_maximum_fusion.3), channel_id=1, source_target_pairs={{0,1},{1,2},{2,3},{3,4},{4,5},{5,6},{6,7},{7,8},{8,9},{9,10},{10,1... | collective-permute-start | bytes 61448 | tf_op jit(solution)/shard_map/ppermute | solution.py:306
  33.6 6.8 %collective-permute-start.7 = (bf16[5,16,128]{2,1,0:T(8,128)(2,1)S(1)}, bf16[5,16,128]{2,1,0:T(8,128)(2,1)S(1)}, u32[]{:S(2)}, u32[]{:S(2)}) collective-permute-start(bf16[5,16,128]{2,1,0:T(8,128)(2,1)S(1)} %pad_maximum_fusion.4), channel_id=1, source_target_pairs={{0,31},{1,0},{2,1},{3,2},{4,3},{5,4},{6,5},{7,6},{8,7},{9,8},{10,9... | collective-permute-start | bytes 61448 | tf_op jit(solution)/shard_map/ppermute | solution.py:306
  40.4 0.0 collective-permute-done.6.west_ref
  40.4 0.9 %collective-permute-done.7.east_ref = bf16[5,16,128]{2,1,0:T(8,128)(2,1)S(1)} collective-permute-done((bf16[5,16,128]{2,1,0:T(8,128)(2,1)S(1)}, bf16[5,16,128]{2,1,0:T(8,128)(2,1)S(1)}, u32[]{:S(2)}, u32[]{:S(2)}) %collective-permute-start.7) | collective-permute-done | bytes 20512 | tf_op jit(solution)/shard_map/ppermute | solution.py:306
  41.3 2.2 %shard_map.125 = (f32[192,128]{1,0:T(8,128)S(1)}, f32[32,128]{1,0:T(8,128)S(1)}) custom-call(s32[3,4,9]{2,1,0:T(4,128)S(1)} %get-tuple-element.51.index_ref, bf16[12,16,128]{2,1,0:T(8,128)(2,1)S(1)} %get-tuple-element.58.x_ref, bf16[4,16,128]{2,1,0:T(8,128)(2,1)S(1)} %collective-permute-done.4.north_ref, ...), custom_call_target="tpu_custom_call" | custom-call | flops 56623104 | bytes 5000000 | tf_op jit(solution)/shard_map/pallas_call | solution.py:408
  43.5 15.6 %all_to_all.28 = f32[32,1,128]{2,1,0:T(1,128)S(1)} all-to-all(f32[32,1,128]{2,1,0:T(1,128)S(1)} %bitcast.48), channel_id=1, replica_groups=mesh['lat'=16,'lon'=32] {'lon'}, dimensions={0} | all-to-all | bytes 32768 | tf_op jit(solution)/shard_map/all_to_all | solution.py:298
  59.1 0.1 reduce_sum.36
  59.2 17.5 %all_to_all.29 = f32[16,1,128]{2,1,0:T(1,128)S(1)} all-to-all(f32[16,1,128]{2,1,0:T(1,128)S(1)} %broadcast_in_dim.6), channel_id=1, replica_groups=mesh['lat'=16,'lon'=32] {'lat'}, dimensions={0} | all-to-all | bytes 16384 | tf_op jit(solution)/shard_map/all_to_all | solution.py:300
  76.7 1.3 %shard_map.126 = (f32[192,128]{1,0:T(8,128)}, f32[192,128]{1,0:T(8,128)}, f32[5]{0:T(128)S(1)}, s32[1]{0:T(128)}) custom-call(f32[16,128]{1,0:T(8,128)S(1)} %bitcast.47, f32[192,128]{1,0:T(8,128)S(1)} %get-tuple-element.110.product_ref, f32[4,192,128]{2,1,0:T(8,128)S(1)} %bitcast.57), custom_call_target="tpu_custom_call" | custom-call | bytes 700000 | tf_op jit(solution)/shard_map/pallas_call | solution.py:422
  78.1 0.7 while.11
  78.7 0.0 copy-start.11
  78.7 0.5 copy-done.11
  (9 shorter events, 0.0 us)
Async XLA Ops:
  0.6 22.9 %copy-start.2 = (f32[16]{0:T(128)S(1)}, f32[16]{0:T(128)}, u32[]{:S(2)}) copy-start(f32[16]{0:T(128)} %param.20) | copy-start | bytes 196
  0.6 22.9 %copy-start.3 = (f32[3,4,8,16,16]{4,3,2,1,0:T(8,128)S(1)}, f32[3,4,8,16,16]{4,3,2,1,0:T(8,128)}, u32[]{:S(2)}) copy-start(f32[3,4,8,16,16]{4,3,2,1,0:T(8,128)} %inverse_ref.1) | copy-start | bytes 294916
  0.7 22.9 %copy-start.4 = (f32[16,3,4,128]{3,2,1,0:T(4,128)S(1)}, f32[16,3,4,128]{3,2,1,0:T(4,128)}, u32[]{:S(2)}) copy-start(f32[16,3,4,128]{3,2,1,0:T(4,128)} %param.12) | copy-start | bytes 294916
  0.7 22.9 %copy-start.5 = (f32[16,3,4,128]{3,2,1,0:T(4,128)S(1)}, f32[16,3,4,128]{3,2,1,0:T(4,128)}, u32[]{:S(2)}) copy-start(f32[16,3,4,128]{3,2,1,0:T(4,128)} %param.13) | copy-start | bytes 294916
  0.7 22.9 %copy-start.6 = (s32[3,4,9]{2,1,0:T(4,128)S(1)}, s32[3,4,9]{2,1,0:T(4,128)}, u32[]{:S(2)}) copy-start(s32[3,4,9]{2,1,0:T(4,128)} %pattern_ref.1) | copy-start | bytes 1300
  0.7 22.9 %copy-start.7 = (s32[3,4,9]{2,1,0:T(4,128)S(1)}, s32[3,4,9]{2,1,0:T(4,128)}, u32[]{:S(2)}) copy-start(s32[3,4,9]{2,1,0:T(4,128)} %live_ref.1) | copy-start | bytes 1300
  0.7 22.9 %copy-start.8 = (s32[3,4,8]{2,1,0:T(4,128)S(1)}, s32[3,4,8]{2,1,0:T(4,128)}, u32[]{:S(2)}) copy-start(s32[3,4,8]{2,1,0:T(4,128)} %depth_ref.1) | copy-start | bytes 1156
  0.7 22.9 %copy-start.9 = (f32[3,4,128]{2,1,0:T(4,128)S(1)}, f32[3,4,128]{2,1,0:T(4,128)}, u32[]{:S(2)}) copy-start(f32[3,4,128]{2,1,0:T(4,128)} %rate_ref.1) | copy-start | bytes 18436
  0.7 22.9 %copy-start.10 = (f32[4,16,3,4,128]{4,3,2,1,0:T(4,128)S(1)}, f32[4,16,3,4,128]{4,3,2,1,0:T(4,128)}, u32[]{:S(2)}) copy-start(f32[4,16,3,4,128]{4,3,2,1,0:T(4,128)} %param.21) | copy-start | bytes 1179652
  2.4 7.8 %collective-permute-start = (bf16[4,32,128]{2,1,0:T(8,128)(2,1)}, bf16[4,32,128]{2,1,0:T(8,128)(2,1)S(1)}, u32[]{:S(2)}, u32[]{:S(2)}) collective-permute-start(bf16[4,32,128]{2,1,0:T(8,128)(2,1)} %get-tuple-element.53), channel_id=1, source_target_pairs={{0,32},{32,64},{64,96},{96,128},{128,160},{160,192},{192,224},{224... | collective-permute-start | bytes 98312 | tf_op jit(solution)/shard_map/ppermute | solution.py:306
  5.1 5.3 %collective-permute-start.1 = (bf16[4,32,128]{2,1,0:T(8,128)(2,1)}, bf16[4,32,128]{2,1,0:T(8,128)(2,1)S(1)}, u32[]{:S(2)}, u32[]{:S(2)}) collective-permute-start(bf16[4,32,128]{2,1,0:T(8,128)(2,1)} %get-tuple-element.54), channel_id=1, source_target_pairs={{0,480},{32,0},{64,32},{96,64},{128,96},{160,128},{192,160},{224,1... | collective-permute-start | bytes 98312 | tf_op jit(solution)/shard_map/ppermute | solution.py:306
  10.4 14.2 %collective-permute-start.2 = (bf16[5,32,128]{2,1,0:T(8,128)(2,1)S(1)}, bf16[5,32,128]{2,1,0:T(8,128)(2,1)S(1)}, u32[]{:S(2)}, u32[]{:S(2)}) collective-permute-start(bf16[5,32,128]{2,1,0:T(8,128)(2,1)S(1)} %pad_maximum_fusion.1), channel_id=1, source_target_pairs={{0,1},{1,2},{2,3},{3,4},{4,5},{5,6},{6,7},{7,8},{8,9},{9,10},{10,1... | collective-permute-start | bytes 122888 | tf_op jit(solution)/shard_map/ppermute | solution.py:306
  12.4 12.3 %collective-permute-start.3 = (bf16[5,32,128]{2,1,0:T(8,128)(2,1)S(1)}, bf16[5,32,128]{2,1,0:T(8,128)(2,1)S(1)}, u32[]{:S(2)}, u32[]{:S(2)}) collective-permute-start(bf16[5,32,128]{2,1,0:T(8,128)(2,1)S(1)} %pad_maximum_fusion.2), channel_id=1, source_target_pairs={{0,31},{1,0},{2,1},{3,2},{4,3},{5,4},{6,5},{7,6},{8,7},{9,8},{10,9... | collective-permute-start | bytes 122888 | tf_op jit(solution)/shard_map/ppermute | solution.py:306
  23.6 2.0 %copy-start = (bf16[3,4,9,128,128]{4,3,2,1,0:T(8,128)(2,1)S(1)}, bf16[3,4,9,128,128]{4,3,2,1,0:T(8,128)(2,1)}, u32[]{:S(2)}) copy-start(bf16[3,4,9,128,128]{4,3,2,1,0:T(8,128)(2,1)} %param.14) | copy-start | bytes 10616836
  23.6 2.0 %copy-start.1 = (bf16[12,32,128]{2,1,0:T(8,128)(2,1)S(1)}, bf16[12,32,128]{2,1,0:T(8,128)(2,1)}, u32[]{:S(2)}) copy-start(bf16[12,32,128]{2,1,0:T(8,128)(2,1)} %get-tuple-element.52.x_ref) | copy-start | bytes 294916
  27.7 2.0 %collective-permute-start.4 = (bf16[4,16,128]{2,1,0:T(8,128)(2,1)S(1)}, bf16[4,16,128]{2,1,0:T(8,128)(2,1)S(1)}, u32[]{:S(2)}, u32[]{:S(2)}) collective-permute-start(bf16[4,16,128]{2,1,0:T(8,128)(2,1)S(1)} %get-tuple-element.59), channel_id=1, source_target_pairs={{0,32},{32,64},{64,96},{96,128},{128,160},{160,192},{192,224},{224... | collective-permute-start | bytes 49160 | tf_op jit(solution)/shard_map/ppermute | solution.py:306
  28.1 3.5 %collective-permute-start.5 = (bf16[4,16,128]{2,1,0:T(8,128)(2,1)S(1)}, bf16[4,16,128]{2,1,0:T(8,128)(2,1)S(1)}, u32[]{:S(2)}, u32[]{:S(2)}) collective-permute-start(bf16[4,16,128]{2,1,0:T(8,128)(2,1)S(1)} %get-tuple-element.60), channel_id=1, source_target_pairs={{0,480},{32,0},{64,32},{96,64},{128,96},{160,128},{192,160},{224,1... | collective-permute-start | bytes 49160 | tf_op jit(solution)/shard_map/ppermute | solution.py:306
  31.6 8.8 %collective-permute-start.6 = (bf16[5,16,128]{2,1,0:T(8,128)(2,1)S(1)}, bf16[5,16,128]{2,1,0:T(8,128)(2,1)S(1)}, u32[]{:S(2)}, u32[]{:S(2)}) collective-permute-start(bf16[5,16,128]{2,1,0:T(8,128)(2,1)S(1)} %pad_maximum_fusion.3), channel_id=1, source_target_pairs={{0,1},{1,2},{2,3},{3,4},{4,5},{5,6},{6,7},{7,8},{8,9},{9,10},{10,1... | collective-permute-start | bytes 61448 | tf_op jit(solution)/shard_map/ppermute | solution.py:306
  33.6 7.7 %collective-permute-start.7 = (bf16[5,16,128]{2,1,0:T(8,128)(2,1)S(1)}, bf16[5,16,128]{2,1,0:T(8,128)(2,1)S(1)}, u32[]{:S(2)}, u32[]{:S(2)}) collective-permute-start(bf16[5,16,128]{2,1,0:T(8,128)(2,1)S(1)} %pad_maximum_fusion.4), channel_id=1, source_target_pairs={{0,31},{1,0},{2,1},{3,2},{4,3},{5,4},{6,5},{7,6},{8,7},{9,8},{10,9... | collective-permute-start | bytes 61448 | tf_op jit(solution)/shard_map/ppermute | solution.py:306
  78.7 0.5 copy-start.11

commit v6 on v5

--- a/solution.py
+++ b/solution.py
@@ -14,6 +14,7 @@
 HBM = pl.BlockSpec(memory_space=pltpu.HBM)
 PACK = 20000000000
 PREP = 10000000000
+BULK = 2000000000
 NT = (((1,), (1,)), ((), ()))
 
 
@@ -37,7 +38,9 @@
     return lax.broadcasted_iota(jnp.int32, shape, dim)
 
 
-def pack_kernel(lon, c_hbm, v_hbm, x_ref, first_ref, last_ref, c_ref, v_ref, sems):
+def pack_kernel(
+    c_hbm, v_hbm, x_ref, first_ref, last_ref, left_ref, right_ref, c_ref, v_ref, sems
+):
     copies = [
         pltpu.make_async_copy(c_hbm, c_ref, sems.at[0]),
         pltpu.make_async_copy(v_hbm, v_ref, sems.at[1]),
@@ -51,11 +54,7 @@
     for r in range(rows):
         at = pl.ds(r, tracers, stride=rows)
         x = jnp.concatenate([c_ref[at, :], v_ref[at, :]], 0).astype(BF16)
-        x_ref[r] = x
-        if r < lon:
-            first_ref[r] = x
-        if r >= rows - lon:
-            last_ref[r - (rows - lon)] = x
+        share_out(r, x, x_ref, first_ref, last_ref, left_ref, right_ref)
 
 
 def prep_kernel(
@@ -85,8 +84,21 @@
     far_lat = pattern // total_lon - itself // total_lon
     far_lon = pattern % total_lon - itself % total_lon
     shape = pattern.shape
-    place = (iota(shape, 0) + 1 + far_lat) * (lon + 2) + iota(shape, 1) + 1 + far_lon
-    index_ref[...] = jnp.where(live_ref[...] > 0, place, (lat + 2) * (lon + 2))
+    named = jnp.where(live_ref[...] > 0, (far_lat + 1) * 3 + far_lon + 1, -1)
+    slot = iota(shape, 2)
+    place = (iota(shape, 0) + slot // 3) * (lon + 2) + iota(shape, 1) + slot % 3
+    held_at = jnp.zeros(shape, jnp.int32)
+    found_at = jnp.zeros(shape, jnp.int32)
+    for k in range(9):
+        match = named == k
+        held_at = jnp.where(
+            slot == k, jnp.sum(jnp.where(match, slot, 0), 2, keepdims=True), held_at
+        )
+        found_at = jnp.where(
+            slot == k, jnp.sum(jnp.where(match, 1, 0), 2, keepdims=True), found_at
+        )
+    index_ref[0] = held_at
+    index_ref[1] = jnp.where(found_at > 0, place, (lat + 2) * (lon + 2))
 
     lane = iota((rows, points), 1)
     depth = jnp.concatenate([depth_ref[i] for i in range(lat)], 0)
@@ -141,12 +153,18 @@
     return uptake, slope * own_v
 
 
-def pull_kernel(state_ref, rate_column_ref, stoich_ref, source_ref):
+def corners_of(lat, lon):
+    return {0: 0, lon - 1: 2, (lat - 1) * lon: 6, lat * lon - 1: 8}
+
+
+def pull_kernel(lat, lon, state_ref, corner_ref, rate_column_ref, stoich_ref, source_ref):
     rows, _, tracers = source_ref.shape
     share = stoich_ref[...]
+    corners = list(corners_of(lat, lon))
     for r in range(rows):
-        own_c = state_ref[r, :, 0:1]
-        own_v = state_ref[r, :, tracers : tracers + 1]
+        ref, at = (corner_ref, corners.index(r)) if r in corners else (state_ref, r)
+        own_c = ref[at, :, 0:1]
+        own_v = ref[at, :, tracers : tracers + 1]
         source_ref[r] = sources(own_c, own_v, rate_column_ref[:, r : r + 1])[1] * share
 
 
@@ -157,18 +175,18 @@
         pad_ref[(lat + 1) * wide + 1 + j] = south_ref[j]
         for i in range(lat):
             pad_ref[(i + 1) * wide + 1 + j] = x_ref[i * lon + j]
-    for i in range(lat + 2):
-        pad_ref[i * wide] = west_ref[i]
-        pad_ref[i * wide + lon + 1] = east_ref[i]
+    for i in range(lat):
+        pad_ref[(i + 1) * wide] = west_ref[i]
+        pad_ref[(i + 1) * wide + lon + 1] = east_ref[i]
     pad_ref[(lat + 2) * wide] = jnp.zeros(pad_ref.shape[1:], BF16)
 
 
-def transport(r, index_ref, pad_ref, held_ref, source_ref):
-    lon, slots = index_ref.shape[1:]
-    z = source_ref[r]
-    for s in range(slots):
-        x = pad_ref[index_ref[r // lon, r % lon, s]]
-        z = z + lax.dot_general(held_ref[r * slots + s], x, NT, preferred_element_type=F32)
+def transport(r, index_ref, pad_ref, held_ref, z, neighbours):
+    lon, slots = index_ref.shape[2:]
+    for k in neighbours:
+        block = held_ref[r * slots + index_ref[0, r // lon, r % lon, k]]
+        x = pad_ref[index_ref[1, r // lon, r % lon, k]]
+        z = z + lax.dot_general(block, x, NT, preferred_element_type=F32)
     return z
 
 
@@ -177,6 +195,32 @@
     z_low = (z - z_high.astype(F32)).astype(BF16)
     dot = functools.partial(jnp.dot, preferred_element_type=F32)
     return dot(high, z_high) + (dot(low, z_high) + dot(high, z_low))
+
+
+def bulk(lat, lon, index_ref, pad_ref, held_ref, high_ref, low_ref, source_ref, state_ref):
+    corners = corners_of(lat, lon)
+    for r in range(lat * lon):
+        neighbours = [k for k in range(9) if k != corners.get(r)]
+        state_ref[r] = transport(r, index_ref, pad_ref, held_ref, source_ref[r], neighbours)
+    for r in range(lat * lon):
+        if r not in corners:
+            state_ref[r] = mix(state_ref[r], high_ref[r], low_ref[r])
+
+
+def finish(
+    lat, lon, index_ref, north_ref, south_ref, state_ref, held_ref, high_ref, low_ref, pad_ref, out_ref
+):
+    wide = lon + 2
+    pad_ref[0] = north_ref[0]
+    pad_ref[lon + 1] = north_ref[1]
+    pad_ref[(lat + 1) * wide] = south_ref[0]
+    pad_ref[(lat + 1) * wide + lon + 1] = south_ref[1]
+    pad_ref[(lat + 2) * wide] = jnp.zeros(pad_ref.shape[1:], BF16)
+    corners = corners_of(lat, lon)
+    for n, (r, k) in enumerate(corners.items()):
+        out_ref[n] = transport(r, index_ref, pad_ref, held_ref, state_ref[r], [k])
+    for n, r in enumerate(corners):
+        out_ref[n] = mix(out_ref[n], high_ref[r], low_ref[r])
 
 
 def first_kernel(
@@ -193,25 +237,62 @@
     low_ref,
     source_ref,
     y_ref,
+    state_ref,
+    pad_ref,
+):
+    fill(pad_ref, x_ref, north_ref, south_ref, west_ref, east_ref, lat, lon)
+    bulk(lat, lon, index_ref, pad_ref, held_ref, high_ref, low_ref, source_ref, state_ref)
+    tracers = y_ref.shape[1]
+    for r in range(lat * lon):
+        if r in corners_of(lat, lon):
+            y_ref[r] = jnp.zeros(y_ref.shape[1:], BF16)
+        else:
+            y_ref[r] = jnp.transpose(state_ref[r])[tracers:].astype(BF16)
+
+
+def first_end_kernel(
+    lat,
+    lon,
+    index_ref,
+    north_ref,
+    south_ref,
+    state_ref,
+    held_ref,
+    high_ref,
+    low_ref,
+    part_ref,
+    y_ref,
     first_ref,
     last_ref,
-    state_ref,
+    left_ref,
+    right_ref,
+    corner_ref,
     pad_ref,
 ):
-    rows = lat * lon
-    fill(pad_ref, x_ref, north_ref, south_ref, west_ref, east_ref, lat, lon)
+    finish(
+        lat, lon, index_ref, north_ref, south_ref, state_ref, held_ref, high_ref, low_ref, pad_ref, corner_ref
+    )
+    corners = list(corners_of(lat, lon))
     tracers = y_ref.shape[1]
-    for r in range(rows):
-        state_ref[r] = transport(r, index_ref, pad_ref, held_ref, source_ref)
-    for r in range(rows):
-        state_ref[r] = mix(state_ref[r], high_ref[r], low_ref[r])
-    for r in range(rows):
-        y = jnp.transpose(state_ref[r])[tracers:].astype(BF16)
-        y_ref[r] = y
-        if r < lon:
-            first_ref[r] = y
-        if r >= rows - lon:
-            last_ref[r - (rows - lon)] = y
+    for r in range(lat * lon):
+        if r in corners:
+            y = jnp.transpose(corner_ref[corners.index(r)])[tracers:].astype(BF16)
+        else:
+            y = part_ref[r]
+        share_out(r, y, y_ref, first_ref, last_ref, left_ref, right_ref)
+
+
+def share_out(r, x, x_ref, first_ref, last_ref, left_ref, right_ref):
+    rows, lon = x_ref.shape[0], first_ref.shape[0]
+    x_ref[r] = x
+    if r < lon:
+        first_ref[r] = x
+    if r >= rows - lon:
+        last_ref[r - (rows - lon)] = x
+    if r % lon == 0:
+        left_ref[r // lon] = x
+    if r % lon == lon - 1:
+        right_ref[r // lon] = x
 
 
 def second_kernel(
@@ -227,22 +308,48 @@
     high_ref,
     low_ref,
     source_ref,
+    part_ref,
+    state_ref,
+    pad_ref,
+):
+    rows = lat * lon
+    fill(pad_ref, x_ref, north_ref, south_ref, west_ref, east_ref, lat, lon)
+    bulk(lat, lon, index_ref, pad_ref, held_ref, high_ref, low_ref, source_ref, state_ref)
+    tracers = x_ref.shape[1]
+    for r in range(rows):
+        at = pl.ds(r, tracers, stride=rows)
+        if r in corners_of(lat, lon):
+            part_ref[at, :] = jnp.zeros((tracers, part_ref.shape[1]), F32)
+        else:
+            part_ref[at, :] = jnp.transpose(state_ref[r])
+
+
+def second_end_kernel(
+    lat,
+    lon,
+    index_ref,
+    north_ref,
+    south_ref,
+    state_ref,
+    held_ref,
+    high_ref,
+    low_ref,
+    part_ref,
     gram_ref,
     basis_ref,
     product_ref,
     sums_ref,
     pad_ref,
-    state_ref,
-):
+    corner_ref,
+):
+    finish(
+        lat, lon, index_ref, north_ref, south_ref, state_ref, held_ref, high_ref, low_ref, pad_ref, corner_ref
+    )
     rows = lat * lon
-    fill(pad_ref, x_ref, north_ref, south_ref, west_ref, east_ref, lat, lon)
-    tracers = x_ref.shape[1]
-    for r in range(rows):
-        state_ref[r] = transport(r, index_ref, pad_ref, held_ref, source_ref)
-    for r in range(rows):
-        state_ref[r] = mix(state_ref[r], high_ref[r], low_ref[r])
-    for r in range(rows):
-        product_ref[pl.ds(r, tracers, stride=rows), :] = jnp.transpose(state_ref[r])
+    product_ref[...] = part_ref[...]
+    tracers = product_ref.shape[0] // rows
+    for n, r in enumerate(corners_of(lat, lon)):
+        product_ref[pl.ds(r, tracers, stride=rows), :] = jnp.transpose(corner_ref[n])
     product = product_ref[...]
     count = basis_ref.shape[0]
     pairs = count * (count + 1) // 2
@@ -300,21 +407,20 @@
     return lax.all_to_all(rows, "lat", 0, 0)
 
 
-def halo(x, first, last, lat, lon, beside=None):
-    def moved(a, axis, step):
-        size = lax.axis_size(axis)
-        return lax.ppermute(a, axis, [(i, (i + step) % size) for i in range(size)])
-
+def moved(a, axis, step):
+    size = lax.axis_size(axis)
+    return lax.ppermute(a, axis, [(i, (i + step) % size) for i in range(size)])
+
+
+def halo(first, last, left, right, beside):
+    west = moved(right, "lon", 1)
+    east = moved(left, "lon", -1)
     north = moved(last, "lat", 1)
     south = moved(first, "lat", -1)
-    if beside is not None:
-        north, south, beside = lax.optimization_barrier((north, south, beside))
-    grid = x.reshape((lat, lon) + x.shape[1:])
-    right = jnp.concatenate([north[None, lon - 1], grid[:, lon - 1], south[None, lon - 1]], 0)
-    left = jnp.concatenate([north[None, 0], grid[:, 0], south[None, 0]], 0)
-    west = moved(right, "lon", 1)
-    east = moved(left, "lon", -1)
-    return north, south, west, east, beside
+    west, east, beside = lax.optimization_barrier((west, east, beside))
+    above = moved(jnp.stack([west[-1], east[-1]]), "lat", 1)
+    below = moved(jnp.stack([west[0], east[0]]), "lat", -1)
+    return (north, south, west, east), (above, below), beside
 
 
 def body(
@@ -340,15 +446,20 @@
 
     flat_c = base_state.reshape(size, points)
     flat_v = tangent.reshape(size, points)
-    x, first, last = call(
-        functools.partial(pack_kernel, lon),
-        (
-            like((rows, 2 * tracers, points), BF16),
-            like((lon, 2 * tracers, points), BF16),
-            like((lon, 2 * tracers, points), BF16),
-        ),
+    def edges(width):
+        return (
+            like((rows, width, points), BF16),
+            like((lon, width, points), BF16),
+            like((lon, width, points), BF16),
+            like((lat, width, points), BF16),
+            like((lat, width, points), BF16),
+        )
+
+    x, *outer = call(
+        pack_kernel,
+        edges(2 * tracers),
         [HBM] * 2,
-        [VMEM] * 3,
+        [VMEM] * 5,
         scratch=[pltpu.VMEM((size, points), F32)] * 2 + [pltpu.SemaphoreType.DMA((2,))],
         size=400000,
         flops=PACK,
@@ -360,7 +471,7 @@
     index, high, low, source, rate_column, gram = call(
         functools.partial(prep_kernel, total_lon),
         (
-            like((lat, lon, slots), jnp.int32),
+            like((2, lat, lon, slots), jnp.int32),
             like((rows, points, points), BF16),
             like((rows, points, points), BF16),
             like((rows, points, 2 * tracers)),
@@ -383,40 +494,60 @@
         flat_v,
     )
 
-    north, south, west, east, _ = halo(x, first, last, lat, lon)
     work = 2 * 2 * tracers * rows * slots * points * points
-    x, first, last, state = call(
+    ends = len(corners_of(lat, lon))
+
+    near, far, source = halo(*outer, source)
+    part, state = call(
         functools.partial(first_kernel, lat, lon),
-        (
-            like((rows, tracers, points), BF16),
-            like((lon, tracers, points), BF16),
-            like((lon, tracers, points), BF16),
-            like((rows, points, 2 * tracers)),
-        ),
+        (like((rows, tracers, points), BF16), like((rows, points, 2 * tracers))),
         [SMEM] + [VMEM] * 9,
+        [VMEM] * 2,
+        scratch=[pltpu.VMEM((places, 2 * tracers, points), BF16)],
+        flops=BULK,
+        size=5000000,
+    )(index, x, *near, held, high, low, source)
+    x, *outer, corner = call(
+        functools.partial(first_end_kernel, lat, lon),
+        edges(tracers) + (like((ends, points, 2 * tracers)),),
+        [SMEM] + [VMEM] * 7,
+        [VMEM] * 6,
+        scratch=[pltpu.VMEM((places, 2 * tracers, points), BF16)],
+        flops=work // 20,
+        size=500000,
+    )(index, *far, state, held, high, low, part)
+
+    source = call(
+        functools.partial(pull_kernel, lat, lon),
+        like((rows, points, tracers)),
         [VMEM] * 4,
-        scratch=[pltpu.VMEM((places, 2 * tracers, points), BF16)],
-        flops=work,
+        VMEM,
+        flops=100000,
+        size=2000000,
+    )(state, corner, rate_column, share)
+
+    near, far, source = halo(*outer, source)
+    part, state = call(
+        functools.partial(second_kernel, lat, lon),
+        (like((size, points)), like((rows, points, tracers))),
+        [SMEM] + [VMEM] * 9,
+        [VMEM] * 2,
+        scratch=[pltpu.VMEM((places, tracers, points), BF16)],
+        flops=BULK,
         size=5000000,
-    )(index, x, north, south, west, east, held, high, low, source)
-
-    source = call(
-        pull_kernel, like((rows, points, tracers)), [VMEM] * 3, VMEM, flops=100000, size=2000000
-    )(state, rate_column, share)
-
-    north, south, west, east, source = halo(x, first, last, lat, lon, source)
+    )(index, x, *near, held, high, low, source)
     product, sums = call(
-        functools.partial(second_kernel, lat, lon),
+        functools.partial(second_end_kernel, lat, lon),
         (like((size, points)), like((lax.axis_size("lon"), points))),
-        [SMEM] + [VMEM] * 11,
+        [SMEM] + [VMEM] * 9,
         [VMEM] * 2,
         scratch=[
             pltpu.VMEM((places, tracers, points), BF16),
-            pltpu.VMEM((rows, points, tracers), F32),
+            pltpu.VMEM((ends, points, tracers), F32),
         ],
-        flops=work // 2,
-        size=5000000,
-    )(index, x, north, south, west, east, held, high, low, source, gram, flat_basis)
+        flops=work // 20,
+        size=1500000,
+    )(index, *far, state, held, high, low, part, gram, flat_basis)
 
     parts = summed(sums)
     following, written, coeffs, flag = call(

time: 79.6 us -> 80.8 us (1.015)
  starting transfers between devices: 29.3 us -> 33.4 us
  Pallas kernels: 9.81 us -> 12.3 us
  blocking collectives: 33.2 us -> 31.1 us
  waiting for transfers between devices: 3.07 us -> 1.37 us
  local copies, waits for them, and re-layouts: 2.25 us -> 0.58 us
    ppermute x8 -> x12, starting transfers between devices: 29.3 us -> 33.4 us  [moved(): return lax.ppermute(a, axis, [(i, (i + step) % size) for i in range(size)])]
    all_to_all x1, blocking collectives: 15.6 us -> 12.9 us  [summed(): row = jnp.sum(lax.all_to_all(rows, 'lon', 0, 0), 0, keepdims=True)]
    pallas_call x3 -> x5, Pallas kernels: 4.19 us -> 6.87 us  [the longest x1 1.73 us: body(): call(pack_kernel, edges(2 * tracers), [HBM] * 2, [VMEM] * 5, scratch=[plt...]
    ppermute x8 -> x12, waiting for transfers between devices: 3.07 us -> 1.37 us  [moved(): return lax.ppermute(a, axis, [(i, (i + step) % size) for i in range(size)])]
    unnamed x24, local copies, waits for them, and re-layouts: 1.47 us -> 0.56 us
  transfers between devices with their start and end apart: 8 -> 12, of which waited for: 4 -> 2; matrix products, arithmetic and copies ran while one was open for 1% -> 0% of each run, Pallas kernels for 3% -> 8%
where the time goes in v6:
time: 80.8 us; the launch traced here: 80.5 us
  starting transfers between devices  33.4 us (41%)
  blocking collectives  31.1 us (38%)
  Pallas kernels  12.3 us (15%)
  waiting for transfers between devices  1.37 us (2%)
  between operations  0.97 us (1%)
    ppermute x12, starting transfers between devices, moved(): return lax.ppermute(a, axis, [(i, (i + step) % size) for i in range(size)])  33.4 us
    all_to_all x1, blocking collectives, summed(): return lax.all_to_all(rows, 'lat', 0, 0)  18.3 us
    all_to_all x1, blocking collectives, summed(): row = jnp.sum(lax.all_to_all(rows, 'lon', 0, 0), 0, keepdims=True)  12.9 us
    pallas_call x1, Pallas kernels, body(): call(functools.partial(second_kernel, lat, lon), (like((size, points)), l...  2.04 us
    pallas_call x1, Pallas kernels, body(): call(functools.partial(first_kernel, lat, lon), (like((rows, tracers, poi...  2.03 us
    pallas_call x1, Pallas kernels, body(): call(pack_kernel, edges(2 * tracers), [HBM] * 2, [VMEM] * 5, scratch=[plt...  1.73 us
  transfers between devices with their start and end apart: 12, of which 2 were waited for; matrix products, arithmetic and copies ran while one was open for 0% of the time, Pallas kernels for 8%

profile of v6, /device:TPU:1, one launch (start us, length us, event | category | flops | bytes accessed | tf_op | source)
XLA Modules:
  0.0 80.5 jit_solution(3524800144632561149)
XLA Ops:
  0.6 0.0 copy-start.1
  0.6 0.0 copy-start.2
  0.7 0.0 copy-start.3
  0.7 0.0 copy-start.4
  0.7 0.0 copy-start.5
  0.7 0.0 copy-start.6
  0.7 0.0 copy-start.7
  0.7 0.0 copy-start.8
  0.7 0.0 copy-start.10
  0.7 1.7 %shard_map.122 = (bf16[12,32,128]{2,1,0:T(8,128)(2,1)}, bf16[4,32,128]{2,1,0:T(8,128)(2,1)}, bf16[4,32,128]{2,1,0:T(8,128)(2,1)}, bf16[3,32,128]{2,1,0:T(8,128)(2,1)}, bf16[3,32,128]{2,1,0:T(8,128)(2,1)}) custom-call(f32[192,128]{1,0:T(8,128)} %bitcast.33, f32[192,128]{1,0:T(8,128)} %bitcast.35), custom_call_target="tpu_custom_call" | custom-call | flops 20000000000 | bytes 400000 | tf_op jit(solution)/shard_map/pallas_call | solution.py:458
  2.5 3.9 %collective-permute-start = (bf16[3,32,128]{2,1,0:T(8,128)(2,1)}, bf16[3,32,128]{2,1,0:T(8,128)(2,1)S(1)}, u32[]{:S(2)}, u32[]{:S(2)}) collective-permute-start(bf16[3,32,128]{2,1,0:T(8,128)(2,1)} %get-tuple-element.63), channel_id=1, source_target_pairs={{0,1},{1,2},{2,3},{3,4},{4,5},{5,6},{6,7},{7,8},{8,9},{9,10},{10,1... | collective-permute-start | bytes 73736 | tf_op jit(solution)/shard_map/ppermute | solution.py:412
  6.4 11.7 %collective-permute-start.1 = (bf16[3,32,128]{2,1,0:T(8,128)(2,1)}, bf16[3,32,128]{2,1,0:T(8,128)(2,1)S(1)}, u32[]{:S(2)}, u32[]{:S(2)}) collective-permute-start(bf16[3,32,128]{2,1,0:T(8,128)(2,1)} %get-tuple-element.64), channel_id=1, source_target_pairs={{0,31},{1,0},{2,1},{3,2},{4,3},{5,4},{6,5},{7,6},{8,7},{9,8},{10,9... | collective-permute-start | bytes 73736 | tf_op jit(solution)/shard_map/ppermute | solution.py:412
  18.1 2.1 %collective-permute-start.4 = (bf16[4,32,128]{2,1,0:T(8,128)(2,1)}, bf16[4,32,128]{2,1,0:T(8,128)(2,1)S(1)}, u32[]{:S(2)}, u32[]{:S(2)}) collective-permute-start(bf16[4,32,128]{2,1,0:T(8,128)(2,1)} %get-tuple-element.69), channel_id=1, source_target_pairs={{0,32},{32,64},{64,96},{96,128},{128,160},{160,192},{192,224},{224... | collective-permute-start | bytes 98312 | tf_op jit(solution)/shard_map/ppermute | solution.py:412
  20.2 0.0 collective-permute-start.5
  20.2 0.0 copy-done.1
  20.2 0.0 copy-done.2
  20.3 0.0 copy-done.3
  20.3 0.0 copy-done.4
  20.3 0.0 copy-done.5
  20.3 0.0 copy-done.6
  20.3 0.0 copy-done.7
  20.3 0.0 copy-done.8
  20.3 0.0 copy-done.10
  20.3 0.0 copy-start
  20.3 0.0 copy-start.9
  20.3 1.2 %shard_map.121 = (s32[2,3,4,9]{3,2,1,0:T(4,128)S(1)}, bf16[12,128,128]{2,1,0:T(8,128)(2,1)S(1)}, bf16[12,128,128]{2,1,0:T(8,128)(2,1)S(1)}, f32[12,128,32]{2,1,0...) custom-call(s32[3,4,9]{2,1,0:T(4,128)S(1)} %copy-done.5, s32[3,4,9]{2,1,0:T(4,128)S(1)} %copy-done.6, ...), custom_call_target="tpu_custom_call" | custom-call | flops 10000000000 | bytes 8000000 | tf_op jit(solution)/shard_map/pallas_call | solution.py:471
  21.5 0.0 collective-permute-done.west_ref
  21.5 0.0 collective-permute-done.1.east_ref
  21.6 1.7 %collective-permute-start.2 = (bf16[2,32,128]{2,1,0:T(8,128)(2,1)S(1)}, bf16[2,32,128]{2,1,0:T(8,128)(2,1)S(1)}, u32[]{:S(2)}, u32[]{:S(2)}) collective-permute-start(bf16[2,32,128]{2,1,0:T(8,128)(2,1)S(1)} %pad_maximum_fusion.1), channel_id=1, source_target_pairs={{0,32},{32,64},{64,96},{96,128},{128,160},{160,192},{192,224},{224... | collective-permute-start | bytes 49160 | tf_op jit(solution)/shard_map/ppermute | solution.py:412
  23.3 0.1 collective-permute-start.3
  23.4 0.0 collective-permute-done.4.north_ref
  23.4 0.4 collective-permute-done.5.south_ref
  23.8 0.0 copy-done
  23.8 0.0 copy-done.9
  23.8 2.0 %shard_map.123 = (bf16[12,16,128]{2,1,0:T(8,128)(2,1)S(1)}, f32[12,128,32]{2,1,0:T(8,128)S(1)}) custom-call(s32[2,3,4,9]{3,2,1,0:T(4,128)S(1)} %get-tuple-element.62.index_ref, bf16[12,32,128]{2,1,0:T(8,128)(2,1)S(1)} %copy-done.9, bf16[4,32,128]{2,1,0:T(8,128)(2,1)S(1)} %collective-permute-done.4.north_ref, ...), custom_call_target="tpu_custom_call" | custom-call | flops 2000000000 | bytes 5000000 | tf_op jit(solution)/shard_map/pallas_call | solution.py:501
  25.8 0.0 collective-permute-done.2.north_ref
  25.8 0.9 %collective-permute-done.3.south_ref = bf16[2,32,128]{2,1,0:T(8,128)(2,1)S(1)} collective-permute-done((bf16[2,32,128]{2,1,0:T(8,128)(2,1)S(1)}, bf16[2,32,128]{2,1,0:T(8,128)(2,1)S(1)}, u32[]{:S(2)}, u32[]{:S(2)}) %collective-permute-start.3) | collective-permute-done | bytes 16416 | tf_op jit(solution)/shard_map/ppermute | solution.py:412
  26.8 1.2 %shard_map.124 = (bf16[12,16,128]{2,1,0:T(8,128)(2,1)S(1)}, bf16[4,16,128]{2,1,0:T(8,128)(2,1)S(1)}, bf16[4,16,128]{2,1,0:T(8,128)(2,1)S(1)}, bf16[3,16,128]{2,1...) custom-call(s32[2,3,4,9]{3,2,1,0:T(4,128)S(1)} %get-tuple-element.62.index_ref, ...), custom_call_target="tpu_custom_call" | custom-call | flops 5662310 | bytes 500000 | tf_op jit(solution)/shard_map/pallas_call | solution.py:510
  28.0 1.9 %collective-permute-start.6 = (bf16[3,16,128]{2,1,0:T(8,128)(2,1)S(1)}, bf16[3,16,128]{2,1,0:T(8,128)(2,1)S(1)}, u32[]{:S(2)}, u32[]{:S(2)}) collective-permute-start(bf16[3,16,128]{2,1,0:T(8,128)(2,1)S(1)} %get-tuple-element.76), channel_id=1, source_target_pairs={{0,1},{1,2},{2,3},{3,4},{4,5},{5,6},{6,7},{7,8},{8,9},{9,10},{10,1... | collective-permute-start | bytes 36872 | tf_op jit(solution)/shard_map/ppermute | solution.py:412
  29.9 6.7 %collective-permute-start.7 = (bf16[3,16,128]{2,1,0:T(8,128)(2,1)S(1)}, bf16[3,16,128]{2,1,0:T(8,128)(2,1)S(1)}, u32[]{:S(2)}, u32[]{:S(2)}) collective-permute-start(bf16[3,16,128]{2,1,0:T(8,128)(2,1)S(1)} %get-tuple-element.77), channel_id=1, source_target_pairs={{0,31},{1,0},{2,1},{3,2},{4,3},{5,4},{6,5},{7,6},{8,7},{9,8},{10,9... | collective-permute-start | bytes 36872 | tf_op jit(solution)/shard_map/ppermute | solution.py:412
  36.6 1.0 %collective-permute-start.10 = (bf16[4,16,128]{2,1,0:T(8,128)(2,1)S(1)}, bf16[4,16,128]{2,1,0:T(8,128)(2,1)S(1)}, u32[]{:S(2)}, u32[]{:S(2)}) collective-permute-start(bf16[4,16,128]{2,1,0:T(8,128)(2,1)S(1)} %get-tuple-element.83), channel_id=1, source_target_pairs={{0,32},{32,64},{64,96},{96,128},{128,160},{160,192},{192,224},{224... | collective-permute-start | bytes 49160 | tf_op jit(solution)/shard_map/ppermute | solution.py:412
  37.6 1.3 %collective-permute-start.11 = (bf16[4,16,128]{2,1,0:T(8,128)(2,1)S(1)}, bf16[4,16,128]{2,1,0:T(8,128)(2,1)S(1)}, u32[]{:S(2)}, u32[]{:S(2)}) collective-permute-start(bf16[4,16,128]{2,1,0:T(8,128)(2,1)S(1)} %get-tuple-element.84), channel_id=1, source_target_pairs={{0,480},{32,0},{64,32},{96,64},{128,96},{160,128},{192,160},{224,1... | collective-permute-start | bytes 49160 | tf_op jit(solution)/shard_map/ppermute | solution.py:412
  38.9 1.4 %shard_map.125.source_ref = f32[12,128,16]{2,1,0:T(8,128)S(1)} custom-call(f32[12,128,32]{2,1,0:T(8,128)S(1)} %get-tuple-element.74.state_ref, f32[4,128,32]{2,1,0:T(8,128)S(1)} %get-tuple-element.78.corner_ref, f32[128,16]{1,0:T(8,128)S(1)} %get-tuple-element.79.rate_column_ref, f32[1,16]{1,0:T(1,128)S(1)} %bitcast.32), custom_call_target="tpu_custom_call" | custom-call | flops 100000 | bytes 2000000 | tf_op jit(solution)/shard_map/pallas_call | solution.py:520
  40.3 0.0 collective-permute-done.6.west_ref
  40.3 0.0 collective-permute-done.7.east_ref
  40.4 0.5 collective-permute-start.8
  40.9 2.5 %collective-permute-start.9 = (bf16[2,16,128]{2,1,0:T(8,128)(2,1)S(1)}, bf16[2,16,128]{2,1,0:T(8,128)(2,1)S(1)}, u32[]{:S(2)}, u32[]{:S(2)}) collective-permute-start(bf16[2,16,128]{2,1,0:T(8,128)(2,1)S(1)} %pad_maximum_fusion.4), channel_id=1, source_target_pairs={{0,480},{32,0},{64,32},{96,64},{128,96},{160,128},{192,160},{224,1... | collective-permute-start | bytes 24584 | tf_op jit(solution)/shard_map/ppermute | solution.py:412
  43.3 0.0 collective-permute-done.10.north_ref
  43.3 0.0 collective-permute-done.11.south_ref
  43.3 2.0 %shard_map.126 = (f32[192,128]{1,0:T(8,128)S(1)}, f32[12,128,16]{2,1,0:T(8,128)S(1)}) custom-call(s32[2,3,4,9]{3,2,1,0:T(4,128)S(1)} %get-tuple-element.62.index_ref, bf16[12,16,128]{2,1,0:T(8,128)(2,1)S(1)} %get-tuple-element.82.x_ref, bf16[4,16,128]{2,1,0:T(8,128)(2,1)S(1)} %collective-permute-done.10.north_ref, ...), custom_call_target="tpu_custom_call" | custom-call | flops 2000000000 | bytes 5000000 | tf_op jit(solution)/shard_map/pallas_call | solution.py:530
  45.4 0.0 collective-permute-done.8.north_ref
  45.4 0.0 collective-permute-done.9.south_ref
  45.4 1.4 %shard_map.127 = (f32[192,128]{1,0:T(8,128)S(1)}, f32[32,128]{1,0:T(8,128)S(1)}) custom-call(s32[2,3,4,9]{3,2,1,0:T(4,128)S(1)} %get-tuple-element.62.index_ref, bf16[2,16,128]{2,1,0:T(8,128)(2,1)S(1)} %collective-permute-done.8.north_ref, bf16[2,16,128]{2,1,0:T(8,128)(2,1)S(1)} %collective-permute-done.9.south_ref, ...), custom_call_target="tpu_custom_call" | custom-call | flops 5662310 | bytes 1500000 | tf_op jit(solution)/shard_map/pallas_call | solution.py:539
  46.8 12.9 %all_to_all.28 = f32[32,1,128]{2,1,0:T(1,128)S(1)} all-to-all(f32[32,1,128]{2,1,0:T(1,128)S(1)} %bitcast.30), channel_id=1, replica_groups=mesh['lat'=16,'lon'=32] {'lon'}, dimensions={0} | all-to-all | bytes 32768 | tf_op jit(solution)/shard_map/all_to_all | solution.py:405
  59.6 0.1 reduce_sum.36
  59.7 18.3 %all_to_all.29 = f32[16,1,128]{2,1,0:T(1,128)S(1)} all-to-all(f32[16,1,128]{2,1,0:T(1,128)S(1)} %broadcast_in_dim.6), channel_id=1, replica_groups=mesh['lat'=16,'lon'=32] {'lat'}, dimensions={0} | all-to-all | bytes 16384 | tf_op jit(solution)/shard_map/all_to_all | solution.py:407
  78.0 1.3 %shard_map.128 = (f32[192,128]{1,0:T(8,128)}, f32[192,128]{1,0:T(8,128)}, f32[5]{0:T(128)S(1)}, s32[1]{0:T(128)}) custom-call(f32[16,128]{1,0:T(8,128)S(1)} %bitcast.29, f32[192,128]{1,0:T(8,128)S(1)} %get-tuple-element.128.product_ref, f32[4,192,128]{2,1,0:T(8,128)S(1)} %bitcast.39), custom_call_target="tpu_custom_call" | custom-call | bytes 700000 | tf_op jit(solution)/shard_map/pallas_call | solution.py:553
  79.3 0.7 while.11
  79.9 0.0 copy-start.11
  80.0 0.5 copy-done.11
  (8 shorter events, 0.0 us)
Async XLA Ops:
  0.6 19.6 %copy-start.1 = (f32[16]{0:T(128)S(1)}, f32[16]{0:T(128)}, u32[]{:S(2)}) copy-start(f32[16]{0:T(128)} %param.20) | copy-start | bytes 196
  0.6 19.6 %copy-start.2 = (f32[3,4,8,16,16]{4,3,2,1,0:T(8,128)S(1)}, f32[3,4,8,16,16]{4,3,2,1,0:T(8,128)}, u32[]{:S(2)}) copy-start(f32[3,4,8,16,16]{4,3,2,1,0:T(8,128)} %inverse_ref.1) | copy-start | bytes 294916
  0.7 19.6 %copy-start.3 = (f32[16,3,4,128]{3,2,1,0:T(4,128)S(1)}, f32[16,3,4,128]{3,2,1,0:T(4,128)}, u32[]{:S(2)}) copy-start(f32[16,3,4,128]{3,2,1,0:T(4,128)} %param.12) | copy-start | bytes 294916
  0.7 19.6 %copy-start.4 = (f32[16,3,4,128]{3,2,1,0:T(4,128)S(1)}, f32[16,3,4,128]{3,2,1,0:T(4,128)}, u32[]{:S(2)}) copy-start(f32[16,3,4,128]{3,2,1,0:T(4,128)} %param.13) | copy-start | bytes 294916
  0.7 19.6 %copy-start.5 = (s32[3,4,9]{2,1,0:T(4,128)S(1)}, s32[3,4,9]{2,1,0:T(4,128)}, u32[]{:S(2)}) copy-start(s32[3,4,9]{2,1,0:T(4,128)} %pattern_ref.1) | copy-start | bytes 1300
  0.7 19.6 %copy-start.6 = (s32[3,4,9]{2,1,0:T(4,128)S(1)}, s32[3,4,9]{2,1,0:T(4,128)}, u32[]{:S(2)}) copy-start(s32[3,4,9]{2,1,0:T(4,128)} %live_ref.1) | copy-start | bytes 1300
  0.7 19.6 %copy-start.7 = (s32[3,4,8]{2,1,0:T(4,128)S(1)}, s32[3,4,8]{2,1,0:T(4,128)}, u32[]{:S(2)}) copy-start(s32[3,4,8]{2,1,0:T(4,128)} %depth_ref.1) | copy-start | bytes 1156
  0.7 19.6 %copy-start.8 = (f32[3,4,128]{2,1,0:T(4,128)S(1)}, f32[3,4,128]{2,1,0:T(4,128)}, u32[]{:S(2)}) copy-start(f32[3,4,128]{2,1,0:T(4,128)} %rate_ref.1) | copy-start | bytes 18436
  0.7 19.6 %copy-start.10 = (f32[4,16,3,4,128]{4,3,2,1,0:T(4,128)S(1)}, f32[4,16,3,4,128]{4,3,2,1,0:T(4,128)}, u32[]{:S(2)}) copy-start(f32[4,16,3,4,128]{4,3,2,1,0:T(4,128)} %param.21) | copy-start | bytes 1179652
  2.5 19.1 %collective-permute-start = (bf16[3,32,128]{2,1,0:T(8,128)(2,1)}, bf16[3,32,128]{2,1,0:T(8,128)(2,1)S(1)}, u32[]{:S(2)}, u32[]{:S(2)}) collective-permute-start(bf16[3,32,128]{2,1,0:T(8,128)(2,1)} %get-tuple-element.63), channel_id=1, source_target_pairs={{0,1},{1,2},{2,3},{3,4},{4,5},{5,6},{6,7},{7,8},{8,9},{9,10},{10,1... | collective-permute-start | bytes 73736 | tf_op jit(solution)/shard_map/ppermute | solution.py:412
  6.4 15.1 %collective-permute-start.1 = (bf16[3,32,128]{2,1,0:T(8,128)(2,1)}, bf16[3,32,128]{2,1,0:T(8,128)(2,1)S(1)}, u32[]{:S(2)}, u32[]{:S(2)}) collective-permute-start(bf16[3,32,128]{2,1,0:T(8,128)(2,1)} %get-tuple-element.64), channel_id=1, source_target_pairs={{0,31},{1,0},{2,1},{3,2},{4,3},{5,4},{6,5},{7,6},{8,7},{9,8},{10,9... | collective-permute-start | bytes 73736 | tf_op jit(solution)/shard_map/ppermute | solution.py:412
  18.1 5.3 %collective-permute-start.4 = (bf16[4,32,128]{2,1,0:T(8,128)(2,1)}, bf16[4,32,128]{2,1,0:T(8,128)(2,1)S(1)}, u32[]{:S(2)}, u32[]{:S(2)}) collective-permute-start(bf16[4,32,128]{2,1,0:T(8,128)(2,1)} %get-tuple-element.69), channel_id=1, source_target_pairs={{0,32},{32,64},{64,96},{96,128},{128,160},{160,192},{192,224},{224... | collective-permute-start | bytes 98312 | tf_op jit(solution)/shard_map/ppermute | solution.py:412
  20.2 3.6 %collective-permute-start.5 = (bf16[4,32,128]{2,1,0:T(8,128)(2,1)}, bf16[4,32,128]{2,1,0:T(8,128)(2,1)S(1)}, u32[]{:S(2)}, u32[]{:S(2)}) collective-permute-start(bf16[4,32,128]{2,1,0:T(8,128)(2,1)} %get-tuple-element.70), channel_id=1, source_target_pairs={{0,480},{32,0},{64,32},{96,64},{128,96},{160,128},{192,160},{224,1... | collective-permute-start | bytes 98312 | tf_op jit(solution)/shard_map/ppermute | solution.py:412
  20.3 3.5 %copy-start = (bf16[3,4,9,128,128]{4,3,2,1,0:T(8,128)(2,1)S(1)}, bf16[3,4,9,128,128]{4,3,2,1,0:T(8,128)(2,1)}, u32[]{:S(2)}) copy-start(bf16[3,4,9,128,128]{4,3,2,1,0:T(8,128)(2,1)} %param.14) | copy-start | bytes 10616836
  20.3 3.5 %copy-start.9 = (bf16[12,32,128]{2,1,0:T(8,128)(2,1)S(1)}, bf16[12,32,128]{2,1,0:T(8,128)(2,1)}, u32[]{:S(2)}) copy-start(bf16[12,32,128]{2,1,0:T(8,128)(2,1)} %get-tuple-element.68.x_ref) | copy-start | bytes 294916
  21.6 4.3 %collective-permute-start.2 = (bf16[2,32,128]{2,1,0:T(8,128)(2,1)S(1)}, bf16[2,32,128]{2,1,0:T(8,128)(2,1)S(1)}, u32[]{:S(2)}, u32[]{:S(2)}) collective-permute-start(bf16[2,32,128]{2,1,0:T(8,128)(2,1)S(1)} %pad_maximum_fusion.1), channel_id=1, source_target_pairs={{0,32},{32,64},{64,96},{96,128},{128,160},{160,192},{192,224},{224... | collective-permute-start | bytes 49160 | tf_op jit(solution)/shard_map/ppermute | solution.py:412
  23.3 3.5 %collective-permute-start.3 = (bf16[2,32,128]{2,1,0:T(8,128)(2,1)S(1)}, bf16[2,32,128]{2,1,0:T(8,128)(2,1)S(1)}, u32[]{:S(2)}, u32[]{:S(2)}) collective-permute-start(bf16[2,32,128]{2,1,0:T(8,128)(2,1)S(1)} %pad_maximum_fusion.2), channel_id=1, source_target_pairs={{0,480},{32,0},{64,32},{96,64},{128,96},{160,128},{192,160},{224,1... | collective-permute-start | bytes 49160 | tf_op jit(solution)/shard_map/ppermute | solution.py:412
  28.0 12.3 %collective-permute-start.6 = (bf16[3,16,128]{2,1,0:T(8,128)(2,1)S(1)}, bf16[3,16,128]{2,1,0:T(8,128)(2,1)S(1)}, u32[]{:S(2)}, u32[]{:S(2)}) collective-permute-start(bf16[3,16,128]{2,1,0:T(8,128)(2,1)S(1)} %get-tuple-element.76), channel_id=1, source_target_pairs={{0,1},{1,2},{2,3},{3,4},{4,5},{5,6},{6,7},{7,8},{8,9},{9,10},{10,1... | collective-permute-start | bytes 36872 | tf_op jit(solution)/shard_map/ppermute | solution.py:412
  29.9 10.4 %collective-permute-start.7 = (bf16[3,16,128]{2,1,0:T(8,128)(2,1)S(1)}, bf16[3,16,128]{2,1,0:T(8,128)(2,1)S(1)}, u32[]{:S(2)}, u32[]{:S(2)}) collective-permute-start(bf16[3,16,128]{2,1,0:T(8,128)(2,1)S(1)} %get-tuple-element.77), channel_id=1, source_target_pairs={{0,31},{1,0},{2,1},{3,2},{4,3},{5,4},{6,5},{7,6},{8,7},{9,8},{10,9... | collective-permute-start | bytes 36872 | tf_op jit(solution)/shard_map/ppermute | solution.py:412
  36.6 6.7 %collective-permute-start.10 = (bf16[4,16,128]{2,1,0:T(8,128)(2,1)S(1)}, bf16[4,16,128]{2,1,0:T(8,128)(2,1)S(1)}, u32[]{:S(2)}, u32[]{:S(2)}) collective-permute-start(bf16[4,16,128]{2,1,0:T(8,128)(2,1)S(1)} %get-tuple-element.83), channel_id=1, source_target_pairs={{0,32},{32,64},{64,96},{96,128},{128,160},{160,192},{192,224},{224... | collective-permute-start | bytes 49160 | tf_op jit(solution)/shard_map/ppermute | solution.py:412
  37.6 5.8 %collective-permute-start.11 = (bf16[4,16,128]{2,1,0:T(8,128)(2,1)S(1)}, bf16[4,16,128]{2,1,0:T(8,128)(2,1)S(1)}, u32[]{:S(2)}, u32[]{:S(2)}) collective-permute-start(bf16[4,16,128]{2,1,0:T(8,128)(2,1)S(1)} %get-tuple-element.84), channel_id=1, source_target_pairs={{0,480},{32,0},{64,32},{96,64},{128,96},{160,128},{192,160},{224,1... | collective-permute-start | bytes 49160 | tf_op jit(solution)/shard_map/ppermute | solution.py:412
  40.4 5.0 %collective-permute-start.8 = (bf16[2,16,128]{2,1,0:T(8,128)(2,1)S(1)}, bf16[2,16,128]{2,1,0:T(8,128)(2,1)S(1)}, u32[]{:S(2)}, u32[]{:S(2)}) collective-permute-start(bf16[2,16,128]{2,1,0:T(8,128)(2,1)S(1)} %pad_maximum_fusion.3), channel_id=1, source_target_pairs={{0,32},{32,64},{64,96},{96,128},{128,160},{160,192},{192,224},{224... | collective-permute-start | bytes 24584 | tf_op jit(solution)/shard_map/ppermute | solution.py:412
  40.9 4.5 %collective-permute-start.9 = (bf16[2,16,128]{2,1,0:T(8,128)(2,1)S(1)}, bf16[2,16,128]{2,1,0:T(8,128)(2,1)S(1)}, u32[]{:S(2)}, u32[]{:S(2)}) collective-permute-start(bf16[2,16,128]{2,1,0:T(8,128)(2,1)S(1)} %pad_maximum_fusion.4), channel_id=1, source_target_pairs={{0,480},{32,0},{64,32},{96,64},{128,96},{160,128},{192,160},{224,1... | collective-permute-start | bytes 24584 | tf_op jit(solution)/shard_map/ppermute | solution.py:412
  79.9 0.5 copy-start.11

commit v7 on v6

--- a/solution.py
+++ b/solution.py
@@ -153,31 +153,33 @@
     return uptake, slope * own_v
 
 
-def corners_of(lat, lon):
-    return {0: 0, lon - 1: 2, (lat - 1) * lon: 6, lat * lon - 1: 8}
-
-
-def pull_kernel(lat, lon, state_ref, corner_ref, rate_column_ref, stoich_ref, source_ref):
+def beyond(lat, lon):
+    found = {}
+    for r in range(lat * lon):
+        ends = [k for k in range(9) if not 0 <= r % lon + k % 3 - 1 < lon]
+        if ends:
+            found[r] = ends
+    return found
+
+
+def pull_kernel(lat, lon, state_ref, edge_ref, rate_column_ref, stoich_ref, source_ref):
     rows, _, tracers = source_ref.shape
     share = stoich_ref[...]
-    corners = list(corners_of(lat, lon))
+    edges = list(beyond(lat, lon))
     for r in range(rows):
-        ref, at = (corner_ref, corners.index(r)) if r in corners else (state_ref, r)
+        ref, at = (edge_ref, edges.index(r)) if r in edges else (state_ref, r)
         own_c = ref[at, :, 0:1]
         own_v = ref[at, :, tracers : tracers + 1]
         source_ref[r] = sources(own_c, own_v, rate_column_ref[:, r : r + 1])[1] * share
 
 
-def fill(pad_ref, x_ref, north_ref, south_ref, west_ref, east_ref, lat, lon):
+def fill(pad_ref, x_ref, north_ref, south_ref, lat, lon):
     wide = lon + 2
     for j in range(lon):
         pad_ref[1 + j] = north_ref[j]
         pad_ref[(lat + 1) * wide + 1 + j] = south_ref[j]
         for i in range(lat):
             pad_ref[(i + 1) * wide + 1 + j] = x_ref[i * lon + j]
-    for i in range(lat):
-        pad_ref[(i + 1) * wide] = west_ref[i]
-        pad_ref[(i + 1) * wide + lon + 1] = east_ref[i]
     pad_ref[(lat + 2) * wide] = jnp.zeros(pad_ref.shape[1:], BF16)
 
 
@@ -198,28 +200,27 @@
 
 
 def bulk(lat, lon, index_ref, pad_ref, held_ref, high_ref, low_ref, source_ref, state_ref):
-    corners = corners_of(lat, lon)
+    edges = beyond(lat, lon)
     for r in range(lat * lon):
-        neighbours = [k for k in range(9) if k != corners.get(r)]
+        neighbours = [k for k in range(9) if k not in edges.get(r, ())]
         state_ref[r] = transport(r, index_ref, pad_ref, held_ref, source_ref[r], neighbours)
     for r in range(lat * lon):
-        if r not in corners:
+        if r not in edges:
             state_ref[r] = mix(state_ref[r], high_ref[r], low_ref[r])
 
 
 def finish(
-    lat, lon, index_ref, north_ref, south_ref, state_ref, held_ref, high_ref, low_ref, pad_ref, out_ref
+    lat, lon, index_ref, west_ref, east_ref, state_ref, held_ref, high_ref, low_ref, pad_ref, out_ref
 ):
     wide = lon + 2
-    pad_ref[0] = north_ref[0]
-    pad_ref[lon + 1] = north_ref[1]
-    pad_ref[(lat + 1) * wide] = south_ref[0]
-    pad_ref[(lat + 1) * wide + lon + 1] = south_ref[1]
+    for i in range(lat + 2):
+        pad_ref[i * wide] = west_ref[i]
+        pad_ref[i * wide + lon + 1] = east_ref[i]
     pad_ref[(lat + 2) * wide] = jnp.zeros(pad_ref.shape[1:], BF16)
-    corners = corners_of(lat, lon)
-    for n, (r, k) in enumerate(corners.items()):
-        out_ref[n] = transport(r, index_ref, pad_ref, held_ref, state_ref[r], [k])
-    for n, r in enumerate(corners):
+    edges = beyond(lat, lon)
+    for n, (r, neighbours) in enumerate(edges.items()):
+        out_ref[n] = transport(r, index_ref, pad_ref, held_ref, state_ref[r], neighbours)
+    for n, r in enumerate(edges):
         out_ref[n] = mix(out_ref[n], high_ref[r], low_ref[r])
 
 
@@ -230,8 +231,6 @@
     x_ref,
     north_ref,
     south_ref,
-    west_ref,
-    east_ref,
     held_ref,
     high_ref,
     low_ref,
@@ -240,11 +239,11 @@
     state_ref,
     pad_ref,
 ):
-    fill(pad_ref, x_ref, north_ref, south_ref, west_ref, east_ref, lat, lon)
+    fill(pad_ref, x_ref, north_ref, south_ref, lat, lon)
     bulk(lat, lon, index_ref, pad_ref, held_ref, high_ref, low_ref, source_ref, state_ref)
     tracers = y_ref.shape[1]
     for r in range(lat * lon):
-        if r in corners_of(lat, lon):
+        if r in beyond(lat, lon):
             y_ref[r] = jnp.zeros(y_ref.shape[1:], BF16)
         else:
             y_ref[r] = jnp.transpose(state_ref[r])[tracers:].astype(BF16)
@@ -254,8 +253,8 @@
     lat,
     lon,
     index_ref,
-    north_ref,
-    south_ref,
+    west_ref,
+    east_ref,
     state_ref,
     held_ref,
     high_ref,
@@ -266,17 +265,17 @@
     last_ref,
     left_ref,
     right_ref,
-    corner_ref,
+    edge_ref,
     pad_ref,
 ):
     finish(
-        lat, lon, index_ref, north_ref, south_ref, state_ref, held_ref, high_ref, low_ref, pad_ref, corner_ref
+        lat, lon, index_ref, west_ref, east_ref, state_ref, held_ref, high_ref, low_ref, pad_ref, edge_ref
     )
-    corners = list(corners_of(lat, lon))
+    edges = list(beyond(lat, lon))
     tracers = y_ref.shape[1]
     for r in range(lat * lon):
-        if r in corners:
-            y = jnp.transpose(corner_ref[corners.index(r)])[tracers:].astype(BF16)
+        if r in edges:
+            y = jnp.transpose(edge_ref[edges.index(r)])[tracers:].astype(BF16)
         else:
             y = part_ref[r]
         share_out(r, y, y_ref, first_ref, last_ref, left_ref, right_ref)
@@ -302,8 +301,6 @@
     x_ref,
     north_ref,
     south_ref,
-    west_ref,
-    east_ref,
     held_ref,
     high_ref,
     low_ref,
@@ -313,12 +310,12 @@
     pad_ref,
 ):
     rows = lat * lon
-    fill(pad_ref, x_ref, north_ref, south_ref, west_ref, east_ref, lat, lon)
+    fill(pad_ref, x_ref, north_ref, south_ref, lat, lon)
     bulk(lat, lon, index_ref, pad_ref, held_ref, high_ref, low_ref, source_ref, state_ref)
     tracers = x_ref.shape[1]
     for r in range(rows):
         at = pl.ds(r, tracers, stride=rows)
-        if r in corners_of(lat, lon):
+        if r in beyond(lat, lon):
             part_ref[at, :] = jnp.zeros((tracers, part_ref.shape[1]), F32)
         else:
             part_ref[at, :] = jnp.transpose(state_ref[r])
@@ -328,8 +325,8 @@
     lat,
     lon,
     index_ref,
-    north_ref,
-    south_ref,
+    west_ref,
+    east_ref,
     state_ref,
     held_ref,
     high_ref,
@@ -340,16 +337,16 @@
     product_ref,
     sums_ref,
     pad_ref,
-    corner_ref,
+    edge_ref,
 ):
     finish(
-        lat, lon, index_ref, north_ref, south_ref, state_ref, held_ref, high_ref, low_ref, pad_ref, corner_ref
+        lat, lon, index_ref, west_ref, east_ref, state_ref, held_ref, high_ref, low_ref, pad_ref, edge_ref
     )
     rows = lat * lon
     product_ref[...] = part_ref[...]
     tracers = product_ref.shape[0] // rows
-    for n, r in enumerate(corners_of(lat, lon)):
-        product_ref[pl.ds(r, tracers, stride=rows), :] = jnp.transpose(corner_ref[n])
+    for n, r in enumerate(beyond(lat, lon)):
+        product_ref[pl.ds(r, tracers, stride=rows), :] = jnp.transpose(edge_ref[n])
     product = product_ref[...]
     count = basis_ref.shape[0]
     pairs = count * (count + 1) // 2
@@ -412,15 +409,16 @@
     return lax.ppermute(a, axis, [(i, (i + step) % size) for i in range(size)])
 
 
-def halo(first, last, left, right, beside):
-    west = moved(right, "lon", 1)
-    east = moved(left, "lon", -1)
+def rows_around(first, last, beside):
     north = moved(last, "lat", 1)
     south = moved(first, "lat", -1)
-    west, east, beside = lax.optimization_barrier((west, east, beside))
-    above = moved(jnp.stack([west[-1], east[-1]]), "lat", 1)
-    below = moved(jnp.stack([west[0], east[0]]), "lat", -1)
-    return (north, south, west, east), (above, below), beside
+    return lax.optimization_barrier((north, south, beside))
+
+
+def columns_around(left, right, north, south):
+    right = jnp.concatenate([north[-1:], right, south[-1:]], 0)
+    left = jnp.concatenate([north[:1], left, south[:1]], 0)
+    return moved(right, "lon", 1), moved(left, "lon", -1)
 
 
 def body(
@@ -455,7 +453,7 @@
             like((lat, width, points), BF16),
         )
 
-    x, *outer = call(
+    x, first, last, left, right = call(
         pack_kernel,
         edges(2 * tracers),
         [HBM] * 2,
@@ -495,19 +493,22 @@
     )
 
     work = 2 * 2 * tracers * rows * slots * points * points
-    ends = len(corners_of(lat, lon))
-
-    near, far, source = halo(*outer, source)
+    ends = len(beyond(lat, lon))
+
+    prepared = (index, high, low, source, rate_column, gram)
+    north, south, prepared = rows_around(first, last, prepared)
+    index, high, low, source, rate_column, gram = prepared
+    west, east = columns_around(left, right, north, south)
     part, state = call(
         functools.partial(first_kernel, lat, lon),
         (like((rows, tracers, points), BF16), like((rows, points, 2 * tracers))),
-        [SMEM] + [VMEM] * 9,
+        [SMEM] + [VMEM] * 7,
         [VMEM] * 2,
         scratch=[pltpu.VMEM((places, 2 * tracers, points), BF16)],
         flops=BULK,
         size=5000000,
-    )(index, x, *near, held, high, low, source)
-    x, *outer, corner = call(
+    )(index, x, north, south, held, high, low, source)
+    x, first, last, left, right, edge = call(
         functools.partial(first_end_kernel, lat, lon),
         edges(tracers) + (like((ends, points, 2 * tracers)),),
         [SMEM] + [VMEM] * 7,
@@ -515,7 +516,7 @@
         scratch=[pltpu.VMEM((places, 2 * tracers, points), BF16)],
         flops=work // 20,
         size=500000,
-    )(index, *far, state, held, high, low, part)
+    )(index, west, east, state, held, high, low, part)
 
     source = call(
         functools.partial(pull_kernel, lat, lon),
@@ -524,18 +525,19 @@
         VMEM,
         flops=100000,
         size=2000000,
-    )(state, corner, rate_column, share)
-
-    near, far, source = halo(*outer, source)
+    )(state, edge, rate_column, share)
+
+    north, south, source = rows_around(first, last, source)
+    west, east = columns_around(left, right, north, south)
     part, state = call(
         functools.partial(second_kernel, lat, lon),
         (like((size, points)), like((rows, points, tracers))),
-        [SMEM] + [VMEM] * 9,
+        [SMEM] + [VMEM] * 7,
         [VMEM] * 2,
         scratch=[pltpu.VMEM((places, tracers, points), BF16)],
         flops=BULK,
         size=5000000,
-    )(index, x, *near, held, high, low, source)
+    )(index, x, north, south, held, high, low, source)
     product, sums = call(
         functools.partial(second_end_kernel, lat, lon),
         (like((size, points)), like((lax.axis_size("lon"), points))),
@@ -547,7 +549,7 @@
         ],
         flops=work // 20,
         size=1500000,
-    )(index, *far, state, held, high, low, part, gram, flat_basis)
+    )(index, west, east, state, held, high, low, part, gram, flat_basis)
 
     parts = summed(sums)
     following, written, coeffs, flag = call(

time: 80.8 us -> 77.9 us (0.964)
  starting transfers between devices: 33.4 us -> 29.1 us
  blocking collectives: 31.1 us -> 32 us
    ppermute x12 -> x8, starting transfers between devices: 33.4 us -> 29.1 us  [moved(): return lax.ppermute(a, axis, [(i, (i + step) % size) for i in range(size)])]
    all_to_all x1, blocking collectives: 12.9 us -> 14.6 us  [summed(): row = jnp.sum(lax.all_to_all(rows, 'lon', 0, 0), 0, keepdims=True)]
    all_to_all x1, blocking collectives: 18.3 us -> 17.4 us  [summed(): return lax.all_to_all(rows, 'lat', 0, 0)]
    ppermute x12 -> x8, waiting for transfers between devices: 1.37 us -> 1.94 us  [moved(): return lax.ppermute(a, axis, [(i, (i + step) % size) for i in range(size)])]
  transfers between devices with their start and end apart: 12 -> 8, of which waited for: 2 -> 1; matrix products, arithmetic and copies ran while one was open for 0% -> 0% of each run, Pallas kernels for 8% -> 8%
where the time goes in v7:
time: 77.9 us; the launch traced here: 77.6 us
  blocking collectives  32 us (41%)
  starting transfers between devices  29.1 us (37%)
  Pallas kernels  12.2 us (16%)
  waiting for transfers between devices  1.94 us (2%)
  between operations  0.99 us (1%)
    ppermute x8, starting transfers between devices, moved(): return lax.ppermute(a, axis, [(i, (i + step) % size) for i in range(size)])  29.1 us
    all_to_all x1, blocking collectives, summed(): return lax.all_to_all(rows, 'lat', 0, 0)  17.4 us
    all_to_all x1, blocking collectives, summed(): row = jnp.sum(lax.all_to_all(rows, 'lon', 0, 0), 0, keepdims=True)  14.6 us
    ppermute x8, waiting for transfers between devices, moved(): return lax.ppermute(a, axis, [(i, (i + step) % size) for i in range(size)])  1.94 us
    pallas_call x1, Pallas kernels, body(): call(functools.partial(second_kernel, lat, lon), (like((size, points)), l...  1.9 us
    pallas_call x1, Pallas kernels, body(): call(functools.partial(first_kernel, lat, lon), (like((rows, tracers, poi...  1.88 us
    pallas_call x1, Pallas kernels, body(): call(pack_kernel, edges(2 * tracers), [HBM] * 2, [VMEM] * 5, scratch=[plt...  1.74 us
  transfers between devices with their start and end apart: 8, of which 1 were waited for; matrix products, arithmetic and copies ran while one was open for 0% of the time, Pallas kernels for 8%

profile of v7, /device:TPU:1, one launch (start us, length us, event | category | flops | bytes accessed | tf_op | source)
XLA Modules:
  0.0 77.6 jit_solution(17801148047008798896)
XLA Ops:
  0.6 0.0 copy-start.1
  0.6 0.0 copy-start.2
  0.7 0.0 copy-start.3
  0.7 0.0 copy-start.4
  0.7 0.0 copy-start.5
  0.7 0.0 copy-start.6
  0.7 0.0 copy-start.7
  0.7 0.0 copy-start.8
  0.7 0.0 copy-start.10
  0.7 1.7 %shard_map.121 = (bf16[12,32,128]{2,1,0:T(8,128)(2,1)}, bf16[4,32,128]{2,1,0:T(8,128)(2,1)}, bf16[4,32,128]{2,1,0:T(8,128)(2,1)}, bf16[3,32,128]{2,1,0:T(8,128)(2,1)}, bf16[3,32,128]{2,1,0:T(8,128)(2,1)}) custom-call(f32[192,128]{1,0:T(8,128)} %bitcast.33, f32[192,128]{1,0:T(8,128)} %bitcast.35), custom_call_target="tpu_custom_call" | custom-call | flops 20000000000 | bytes 400000 | tf_op jit(solution)/shard_map/pallas_call | solution.py:456
  2.5 2.7 %collective-permute-start = (bf16[4,32,128]{2,1,0:T(8,128)(2,1)}, bf16[4,32,128]{2,1,0:T(8,128)(2,1)S(1)}, u32[]{:S(2)}, u32[]{:S(2)}) collective-permute-start(bf16[4,32,128]{2,1,0:T(8,128)(2,1)} %get-tuple-element.67), channel_id=1, source_target_pairs={{0,32},{32,64},{64,96},{96,128},{128,160},{160,192},{192,224},{224... | collective-permute-start | bytes 98312 | tf_op jit(solution)/shard_map/ppermute | solution.py:409
  5.2 4.2 %collective-permute-start.1 = (bf16[4,32,128]{2,1,0:T(8,128)(2,1)}, bf16[4,32,128]{2,1,0:T(8,128)(2,1)S(1)}, u32[]{:S(2)}, u32[]{:S(2)}) collective-permute-start(bf16[4,32,128]{2,1,0:T(8,128)(2,1)} %get-tuple-element.68), channel_id=1, source_target_pairs={{0,480},{32,0},{64,32},{96,64},{128,96},{160,128},{192,160},{224,1... | collective-permute-start | bytes 98312 | tf_op jit(solution)/shard_map/ppermute | solution.py:409
  9.4 0.0 copy-done.1
  9.4 0.0 copy-done.2
  9.4 0.0 copy-done.3
  9.4 0.0 copy-done.4
  9.4 0.0 copy-done.5
  9.4 0.0 copy-done.6
  9.4 0.0 copy-done.7
  9.4 0.0 copy-done.8
  9.4 0.0 copy-done.10
  9.5 0.0 copy-start.12
  9.5 0.0 copy-start.11
  9.5 0.0 copy-start
  9.5 0.0 copy-start.9
  9.5 1.2 %shard_map.122 = (s32[2,3,4,9]{3,2,1,0:T(4,128)S(1)}, bf16[12,128,128]{2,1,0:T(8,128)(2,1)S(1)}, bf16[12,128,128]{2,1,0:T(8,128)(2,1)S(1)}, f32[12,128,32]{2,1,0...) custom-call(s32[3,4,9]{2,1,0:T(4,128)S(1)} %copy-done.5, s32[3,4,9]{2,1,0:T(4,128)S(1)} %copy-done.6, ...), custom_call_target="tpu_custom_call" | custom-call | flops 10000000000 | bytes 8000000 | tf_op jit(solution)/shard_map/pallas_call | solution.py:469
  10.7 0.0 collective-permute-done.north_ref
  10.7 0.0 collective-permute-done.1.south_ref
  10.7 0.0 copy-done.12
  10.7 1.9 %collective-permute-start.2 = (bf16[5,32,128]{2,1,0:T(8,128)(2,1)S(1)}, bf16[5,32,128]{2,1,0:T(8,128)(2,1)S(1)}, u32[]{:S(2)}, u32[]{:S(2)}) collective-permute-start(bf16[5,32,128]{2,1,0:T(8,128)(2,1)S(1)} %pad_maximum_fusion.1), channel_id=1, source_target_pairs={{0,1},{1,2},{2,3},{3,4},{4,5},{5,6},{6,7},{7,8},{8,9},{9,10},{10,1... | collective-permute-start | bytes 122888 | tf_op jit(solution)/shard_map/ppermute | solution.py:409
  12.7 0.0 copy-done.11
  12.7 10.9 %collective-permute-start.3 = (bf16[5,32,128]{2,1,0:T(8,128)(2,1)S(1)}, bf16[5,32,128]{2,1,0:T(8,128)(2,1)S(1)}, u32[]{:S(2)}, u32[]{:S(2)}) collective-permute-start(bf16[5,32,128]{2,1,0:T(8,128)(2,1)S(1)} %pad_maximum_fusion.2), channel_id=1, source_target_pairs={{0,31},{1,0},{2,1},{3,2},{4,3},{5,4},{6,5},{7,6},{8,7},{9,8},{10,9... | collective-permute-start | bytes 122888 | tf_op jit(solution)/shard_map/ppermute | solution.py:409
  23.6 0.0 copy-done
  23.6 0.0 copy-done.9
  23.6 1.9 %shard_map.123 = (bf16[12,16,128]{2,1,0:T(8,128)(2,1)S(1)}, f32[12,128,32]{2,1,0:T(8,128)S(1)}) custom-call(s32[2,3,4,9]{3,2,1,0:T(4,128)S(1)} %get-tuple-element.75.index_ref, bf16[12,32,128]{2,1,0:T(8,128)(2,1)S(1)} %copy-done.9, bf16[4,32,128]{2,1,0:T(8,128)(2,1)S(1)} %collective-permute-done.north_ref, ...), custom_call_target="tpu_custom_call" | custom-call | flops 2000000000 | bytes 5000000 | tf_op jit(solution)/shard_map/pallas_call | solution.py:502
  25.5 0.0 collective-permute-done.2.west_ref
  25.5 0.0 collective-permute-done.3.east_ref
  25.5 1.3 %shard_map.124 = (bf16[12,16,128]{2,1,0:T(8,128)(2,1)S(1)}, bf16[4,16,128]{2,1,0:T(8,128)(2,1)S(1)}, bf16[4,16,128]{2,1,0:T(8,128)(2,1)S(1)}, bf16[3,16,128]{2,1...) custom-call(s32[2,3,4,9]{3,2,1,0:T(4,128)S(1)} %get-tuple-element.75.index_ref, ...), custom_call_target="tpu_custom_call" | custom-call | flops 5662310 | bytes 500000 | tf_op jit(solution)/shard_map/pallas_call | solution.py:511
  26.8 0.4 collective-permute-start.4
  27.3 0.1 collective-permute-start.5
  27.4 1.4 %shard_map.125.source_ref = f32[12,128,16]{2,1,0:T(8,128)S(1)} custom-call(f32[12,128,32]{2,1,0:T(8,128)S(1)} %get-tuple-element.84.state_ref, f32[6,128,32]{2,1,0:T(8,128)S(1)} %get-tuple-element.88.edge_ref, f32[128,16]{1,0:T(8,128)S(1)} %get-tuple-element.89.rate_column_ref, f32[1,16]{1,0:T(1,128)S(1)} %bitcast.32), custom_call_target="tpu_custom_call" | custom-call | flops 100000 | bytes 2000000 | tf_op jit(solution)/shard_map/pallas_call | solution.py:521
  28.8 0.0 collective-permute-done.4.north_ref
  28.8 1.9 %collective-permute-done.5.south_ref = bf16[4,16,128]{2,1,0:T(8,128)(2,1)S(1)} collective-permute-done((bf16[4,16,128]{2,1,0:T(8,128)(2,1)S(1)}, bf16[4,16,128]{2,1,0:T(8,128)(2,1)S(1)}, u32[]{:S(2)}, u32[]{:S(2)}) %collective-permute-start.5) | collective-permute-done | bytes 16416 | tf_op jit(solution)/shard_map/ppermute | solution.py:409
  30.7 1.9 %collective-permute-start.6 = (bf16[5,16,128]{2,1,0:T(8,128)(2,1)S(1)}, bf16[5,16,128]{2,1,0:T(8,128)(2,1)S(1)}, u32[]{:S(2)}, u32[]{:S(2)}) collective-permute-start(bf16[5,16,128]{2,1,0:T(8,128)(2,1)S(1)} %pad_maximum_fusion.3), channel_id=1, source_target_pairs={{0,1},{1,2},{2,3},{3,4},{4,5},{5,6},{6,7},{7,8},{8,9},{9,10},{10,1... | collective-permute-start | bytes 61448 | tf_op jit(solution)/shard_map/ppermute | solution.py:409
  32.7 7.0 %collective-permute-start.7 = (bf16[5,16,128]{2,1,0:T(8,128)(2,1)S(1)}, bf16[5,16,128]{2,1,0:T(8,128)(2,1)S(1)}, u32[]{:S(2)}, u32[]{:S(2)}) collective-permute-start(bf16[5,16,128]{2,1,0:T(8,128)(2,1)S(1)} %pad_maximum_fusion.4), channel_id=1, source_target_pairs={{0,31},{1,0},{2,1},{3,2},{4,3},{5,4},{6,5},{7,6},{8,7},{9,8},{10,9... | collective-permute-start | bytes 61448 | tf_op jit(solution)/shard_map/ppermute | solution.py:409
  39.6 1.9 %shard_map.126 = (f32[192,128]{1,0:T(8,128)S(1)}, f32[12,128,16]{2,1,0:T(8,128)S(1)}) custom-call(s32[2,3,4,9]{3,2,1,0:T(4,128)S(1)} %get-tuple-element.75.index_ref, bf16[12,16,128]{2,1,0:T(8,128)(2,1)S(1)} %get-tuple-element.94.x_ref, bf16[4,16,128]{2,1,0:T(8,128)(2,1)S(1)} %collective-permute-done.4.north_ref, ...), custom_call_target="tpu_custom_call" | custom-call | flops 2000000000 | bytes 5000000 | tf_op jit(solution)/shard_map/pallas_call | solution.py:532
  41.5 0.0 collective-permute-done.6.west_ref
  41.5 0.0 collective-permute-done.7.east_ref
  41.5 1.5 %shard_map.127 = (f32[192,128]{1,0:T(8,128)S(1)}, f32[32,128]{1,0:T(8,128)S(1)}) custom-call(s32[2,3,4,9]{3,2,1,0:T(4,128)S(1)} %get-tuple-element.75.index_ref, bf16[5,16,128]{2,1,0:T(8,128)(2,1)S(1)} %collective-permute-done.6.west_ref, bf16[5,16,128]{2,1,0:T(8,128)(2,1)S(1)} %collective-permute-done.7.east_ref, ...), custom_call_target="tpu_custom_call" | custom-call | flops 5662310 | bytes 1500000 | tf_op jit(solution)/shard_map/pallas_call | solution.py:541
  43.0 14.6 %all_to_all.28 = f32[32,1,128]{2,1,0:T(1,128)S(1)} all-to-all(f32[32,1,128]{2,1,0:T(1,128)S(1)} %bitcast.30), channel_id=1, replica_groups=mesh['lat'=16,'lon'=32] {'lon'}, dimensions={0} | all-to-all | bytes 32768 | tf_op jit(solution)/shard_map/all_to_all | solution.py:402
  57.6 0.1 reduce_sum.36
  57.7 17.4 %all_to_all.29 = f32[16,1,128]{2,1,0:T(1,128)S(1)} all-to-all(f32[16,1,128]{2,1,0:T(1,128)S(1)} %broadcast_in_dim.6), channel_id=1, replica_groups=mesh['lat'=16,'lon'=32] {'lat'}, dimensions={0} | all-to-all | bytes 16384 | tf_op jit(solution)/shard_map/all_to_all | solution.py:404
  75.1 1.3 %shard_map.128 = (f32[192,128]{1,0:T(8,128)}, f32[192,128]{1,0:T(8,128)}, f32[5]{0:T(128)S(1)}, s32[1]{0:T(128)}) custom-call(f32[16,128]{1,0:T(8,128)S(1)} %bitcast.29, f32[192,128]{1,0:T(8,128)S(1)} %get-tuple-element.138.product_ref, f32[4,192,128]{2,1,0:T(8,128)S(1)} %bitcast.39), custom_call_target="tpu_custom_call" | custom-call | bytes 700000 | tf_op jit(solution)/shard_map/pallas_call | solution.py:555
  76.4 0.7 while.11
  77.1 0.0 copy-start.13
  77.1 0.5 copy-done.13
  (8 shorter events, 0.0 us)
Async XLA Ops:
  0.6 8.8 %copy-start.1 = (f32[16]{0:T(128)S(1)}, f32[16]{0:T(128)}, u32[]{:S(2)}) copy-start(f32[16]{0:T(128)} %param.20) | copy-start | bytes 196
  0.6 8.7 %copy-start.2 = (f32[3,4,8,16,16]{4,3,2,1,0:T(8,128)S(1)}, f32[3,4,8,16,16]{4,3,2,1,0:T(8,128)}, u32[]{:S(2)}) copy-start(f32[3,4,8,16,16]{4,3,2,1,0:T(8,128)} %inverse_ref.1) | copy-start | bytes 294916
  0.7 8.7 %copy-start.3 = (f32[16,3,4,128]{3,2,1,0:T(4,128)S(1)}, f32[16,3,4,128]{3,2,1,0:T(4,128)}, u32[]{:S(2)}) copy-start(f32[16,3,4,128]{3,2,1,0:T(4,128)} %param.12) | copy-start | bytes 294916
  0.7 8.7 %copy-start.4 = (f32[16,3,4,128]{3,2,1,0:T(4,128)S(1)}, f32[16,3,4,128]{3,2,1,0:T(4,128)}, u32[]{:S(2)}) copy-start(f32[16,3,4,128]{3,2,1,0:T(4,128)} %param.13) | copy-start | bytes 294916
  0.7 8.7 %copy-start.5 = (s32[3,4,9]{2,1,0:T(4,128)S(1)}, s32[3,4,9]{2,1,0:T(4,128)}, u32[]{:S(2)}) copy-start(s32[3,4,9]{2,1,0:T(4,128)} %pattern_ref.1) | copy-start | bytes 1300
  0.7 8.7 %copy-start.6 = (s32[3,4,9]{2,1,0:T(4,128)S(1)}, s32[3,4,9]{2,1,0:T(4,128)}, u32[]{:S(2)}) copy-start(s32[3,4,9]{2,1,0:T(4,128)} %live_ref.1) | copy-start | bytes 1300
  0.7 8.7 %copy-start.7 = (s32[3,4,8]{2,1,0:T(4,128)S(1)}, s32[3,4,8]{2,1,0:T(4,128)}, u32[]{:S(2)}) copy-start(s32[3,4,8]{2,1,0:T(4,128)} %depth_ref.1) | copy-start | bytes 1156
  0.7 8.7 %copy-start.8 = (f32[3,4,128]{2,1,0:T(4,128)S(1)}, f32[3,4,128]{2,1,0:T(4,128)}, u32[]{:S(2)}) copy-start(f32[3,4,128]{2,1,0:T(4,128)} %rate_ref.1) | copy-start | bytes 18436
  0.7 8.7 %copy-start.10 = (f32[4,16,3,4,128]{4,3,2,1,0:T(4,128)S(1)}, f32[4,16,3,4,128]{4,3,2,1,0:T(4,128)}, u32[]{:S(2)}) copy-start(f32[4,16,3,4,128]{4,3,2,1,0:T(4,128)} %param.21) | copy-start | bytes 1179652
  2.5 8.2 %collective-permute-start = (bf16[4,32,128]{2,1,0:T(8,128)(2,1)}, bf16[4,32,128]{2,1,0:T(8,128)(2,1)S(1)}, u32[]{:S(2)}, u32[]{:S(2)}) collective-permute-start(bf16[4,32,128]{2,1,0:T(8,128)(2,1)} %get-tuple-element.67), channel_id=1, source_target_pairs={{0,32},{32,64},{64,96},{96,128},{128,160},{160,192},{192,224},{224... | collective-permute-start | bytes 98312 | tf_op jit(solution)/shard_map/ppermute | solution.py:409
  5.2 5.5 %collective-permute-start.1 = (bf16[4,32,128]{2,1,0:T(8,128)(2,1)}, bf16[4,32,128]{2,1,0:T(8,128)(2,1)S(1)}, u32[]{:S(2)}, u32[]{:S(2)}) collective-permute-start(bf16[4,32,128]{2,1,0:T(8,128)(2,1)} %get-tuple-element.68), channel_id=1, source_target_pairs={{0,480},{32,0},{64,32},{96,64},{128,96},{160,128},{192,160},{224,1... | collective-permute-start | bytes 98312 | tf_op jit(solution)/shard_map/ppermute | solution.py:409
  9.5 1.3 %copy-start.12 = (bf16[3,32,128]{2,1,0:T(8,128)(2,1)S(1)}, bf16[3,32,128]{2,1,0:T(8,128)(2,1)}, u32[]{:S(2)}) copy-start(bf16[3,32,128]{2,1,0:T(8,128)(2,1)} %get-tuple-element.77) | copy-start | bytes 73732
  9.5 3.2 %copy-start.11 = (bf16[3,32,128]{2,1,0:T(8,128)(2,1)S(1)}, bf16[3,32,128]{2,1,0:T(8,128)(2,1)}, u32[]{:S(2)}) copy-start(bf16[3,32,128]{2,1,0:T(8,128)(2,1)} %get-tuple-element.79) | copy-start | bytes 73732
  9.5 14.1 %copy-start = (bf16[3,4,9,128,128]{4,3,2,1,0:T(8,128)(2,1)S(1)}, bf16[3,4,9,128,128]{4,3,2,1,0:T(8,128)(2,1)}, u32[]{:S(2)}) copy-start(bf16[3,4,9,128,128]{4,3,2,1,0:T(8,128)(2,1)} %param.14) | copy-start | bytes 10616836
  9.5 14.1 %copy-start.9 = (bf16[12,32,128]{2,1,0:T(8,128)(2,1)S(1)}, bf16[12,32,128]{2,1,0:T(8,128)(2,1)}, u32[]{:S(2)}) copy-start(bf16[12,32,128]{2,1,0:T(8,128)(2,1)} %get-tuple-element.80.x_ref) | copy-start | bytes 294916
  10.7 14.7 %collective-permute-start.2 = (bf16[5,32,128]{2,1,0:T(8,128)(2,1)S(1)}, bf16[5,32,128]{2,1,0:T(8,128)(2,1)S(1)}, u32[]{:S(2)}, u32[]{:S(2)}) collective-permute-start(bf16[5,32,128]{2,1,0:T(8,128)(2,1)S(1)} %pad_maximum_fusion.1), channel_id=1, source_target_pairs={{0,1},{1,2},{2,3},{3,4},{4,5},{5,6},{6,7},{7,8},{8,9},{9,10},{10,1... | collective-permute-start | bytes 122888 | tf_op jit(solution)/shard_map/ppermute | solution.py:409
  12.7 12.8 %collective-permute-start.3 = (bf16[5,32,128]{2,1,0:T(8,128)(2,1)S(1)}, bf16[5,32,128]{2,1,0:T(8,128)(2,1)S(1)}, u32[]{:S(2)}, u32[]{:S(2)}) collective-permute-start(bf16[5,32,128]{2,1,0:T(8,128)(2,1)S(1)} %pad_maximum_fusion.2), channel_id=1, source_target_pairs={{0,31},{1,0},{2,1},{3,2},{4,3},{5,4},{6,5},{7,6},{8,7},{9,8},{10,9... | collective-permute-start | bytes 122888 | tf_op jit(solution)/shard_map/ppermute | solution.py:409
  26.8 2.0 %collective-permute-start.4 = (bf16[4,16,128]{2,1,0:T(8,128)(2,1)S(1)}, bf16[4,16,128]{2,1,0:T(8,128)(2,1)S(1)}, u32[]{:S(2)}, u32[]{:S(2)}) collective-permute-start(bf16[4,16,128]{2,1,0:T(8,128)(2,1)S(1)} %get-tuple-element.86), channel_id=1, source_target_pairs={{0,32},{32,64},{64,96},{96,128},{128,160},{160,192},{192,224},{224... | collective-permute-start | bytes 49160 | tf_op jit(solution)/shard_map/ppermute | solution.py:409
  27.3 3.5 %collective-permute-start.5 = (bf16[4,16,128]{2,1,0:T(8,128)(2,1)S(1)}, bf16[4,16,128]{2,1,0:T(8,128)(2,1)S(1)}, u32[]{:S(2)}, u32[]{:S(2)}) collective-permute-start(bf16[4,16,128]{2,1,0:T(8,128)(2,1)S(1)} %get-tuple-element.87), channel_id=1, source_target_pairs={{0,480},{32,0},{64,32},{96,64},{128,96},{160,128},{192,160},{224,1... | collective-permute-start | bytes 49160 | tf_op jit(solution)/shard_map/ppermute | solution.py:409
  30.7 10.8 %collective-permute-start.6 = (bf16[5,16,128]{2,1,0:T(8,128)(2,1)S(1)}, bf16[5,16,128]{2,1,0:T(8,128)(2,1)S(1)}, u32[]{:S(2)}, u32[]{:S(2)}) collective-permute-start(bf16[5,16,128]{2,1,0:T(8,128)(2,1)S(1)} %pad_maximum_fusion.3), channel_id=1, source_target_pairs={{0,1},{1,2},{2,3},{3,4},{4,5},{5,6},{6,7},{7,8},{8,9},{9,10},{10,1... | collective-permute-start | bytes 61448 | tf_op jit(solution)/shard_map/ppermute | solution.py:409
  32.7 8.9 %collective-permute-start.7 = (bf16[5,16,128]{2,1,0:T(8,128)(2,1)S(1)}, bf16[5,16,128]{2,1,0:T(8,128)(2,1)S(1)}, u32[]{:S(2)}, u32[]{:S(2)}) collective-permute-start(bf16[5,16,128]{2,1,0:T(8,128)(2,1)S(1)} %pad_maximum_fusion.4), channel_id=1, source_target_pairs={{0,31},{1,0},{2,1},{3,2},{4,3},{5,4},{6,5},{7,6},{8,7},{9,8},{10,9... | collective-permute-start | bytes 61448 | tf_op jit(solution)/shard_map/ppermute | solution.py:409
  77.1 0.5 copy-start.13

commit v8 on v7

--- a/solution.py
+++ b/solution.py
@@ -38,17 +38,13 @@
     return lax.broadcasted_iota(jnp.int32, shape, dim)
 
 
+def begin_kernel(out_ref):
+    out_ref[...] = jnp.zeros(out_ref.shape, F32)
+
+
 def pack_kernel(
-    c_hbm, v_hbm, x_ref, first_ref, last_ref, left_ref, right_ref, c_ref, v_ref, sems
-):
-    copies = [
-        pltpu.make_async_copy(c_hbm, c_ref, sems.at[0]),
-        pltpu.make_async_copy(v_hbm, v_ref, sems.at[1]),
-    ]
-    for copy in copies:
-        copy.start()
-    for copy in copies:
-        copy.wait()
+    begun_ref, c_ref, v_ref, x_ref, first_ref, last_ref, left_ref, right_ref
+):
     rows = x_ref.shape[0]
     tracers = c_ref.shape[0] // rows
     for r in range(rows):
@@ -199,8 +195,19 @@
     return dot(high, z_high) + (dot(low, z_high) + dot(high, z_low))
 
 
-def bulk(lat, lon, index_ref, pad_ref, held_ref, high_ref, low_ref, source_ref, state_ref):
+def bulk(
+    lat, lon, index_ref, pad_ref, held_ref, high_ref, low_ref, source_ref, state_ref, later_ref
+):
     edges = beyond(lat, lon)
+    slots = index_ref.shape[3]
+    n = 0
+    for r, neighbours in edges.items():
+        for k in neighbours:
+            at = (r // lon, r % lon, k)
+            block = held_ref[r * slots + index_ref[0, *at]]
+            named = index_ref[1, *at] < (lat + 2) * (lon + 2)
+            later_ref[n] = jnp.where(named, block, jnp.zeros_like(block))
+            n += 1
     for r in range(lat * lon):
         neighbours = [k for k in range(9) if k not in edges.get(r, ())]
         state_ref[r] = transport(r, index_ref, pad_ref, held_ref, source_ref[r], neighbours)
@@ -209,17 +216,16 @@
             state_ref[r] = mix(state_ref[r], high_ref[r], low_ref[r])
 
 
-def finish(
-    lat, lon, index_ref, west_ref, east_ref, state_ref, held_ref, high_ref, low_ref, pad_ref, out_ref
-):
-    wide = lon + 2
-    for i in range(lat + 2):
-        pad_ref[i * wide] = west_ref[i]
-        pad_ref[i * wide + lon + 1] = east_ref[i]
-    pad_ref[(lat + 2) * wide] = jnp.zeros(pad_ref.shape[1:], BF16)
+def finish(lat, lon, west_ref, east_ref, state_ref, later_ref, high_ref, low_ref, out_ref):
     edges = beyond(lat, lon)
+    at = 0
     for n, (r, neighbours) in enumerate(edges.items()):
-        out_ref[n] = transport(r, index_ref, pad_ref, held_ref, state_ref[r], neighbours)
+        z = state_ref[r]
+        for k in neighbours:
+            x = (west_ref if r % lon + k % 3 == 0 else east_ref)[r // lon + k // 3]
+            z = z + lax.dot_general(later_ref[at], x, NT, preferred_element_type=F32)
+            at += 1
+        out_ref[n] = z
     for n, r in enumerate(edges):
         out_ref[n] = mix(out_ref[n], high_ref[r], low_ref[r])
 
@@ -237,10 +243,13 @@
     source_ref,
     y_ref,
     state_ref,
+    later_ref,
     pad_ref,
 ):
     fill(pad_ref, x_ref, north_ref, south_ref, lat, lon)
-    bulk(lat, lon, index_ref, pad_ref, held_ref, high_ref, low_ref, source_ref, state_ref)
+    bulk(
+        lat, lon, index_ref, pad_ref, held_ref, high_ref, low_ref, source_ref, state_ref, later_ref
+    )
     tracers = y_ref.shape[1]
     for r in range(lat * lon):
         if r in beyond(lat, lon):
@@ -252,11 +261,10 @@
 def first_end_kernel(
     lat,
     lon,
-    index_ref,
     west_ref,
     east_ref,
     state_ref,
-    held_ref,
+    later_ref,
     high_ref,
     low_ref,
     part_ref,
@@ -266,11 +274,8 @@
     left_ref,
     right_ref,
     edge_ref,
-    pad_ref,
-):
-    finish(
-        lat, lon, index_ref, west_ref, east_ref, state_ref, held_ref, high_ref, low_ref, pad_ref, edge_ref
-    )
+):
+    finish(lat, lon, west_ref, east_ref, state_ref, later_ref, high_ref, low_ref, edge_ref)
     edges = list(beyond(lat, lon))
     tracers = y_ref.shape[1]
     for r in range(lat * lon):
@@ -307,11 +312,14 @@
     source_ref,
     part_ref,
     state_ref,
+    later_ref,
     pad_ref,
 ):
     rows = lat * lon
     fill(pad_ref, x_ref, north_ref, south_ref, lat, lon)
-    bulk(lat, lon, index_ref, pad_ref, held_ref, high_ref, low_ref, source_ref, state_ref)
+    bulk(
+        lat, lon, index_ref, pad_ref, held_ref, high_ref, low_ref, source_ref, state_ref, later_ref
+    )
     tracers = x_ref.shape[1]
     for r in range(rows):
         at = pl.ds(r, tracers, stride=rows)
@@ -324,29 +332,29 @@
 def second_end_kernel(
     lat,
     lon,
-    index_ref,
     west_ref,
     east_ref,
     state_ref,
-    held_ref,
+    later_ref,
     high_ref,
     low_ref,
     part_ref,
     gram_ref,
     basis_ref,
     product_ref,
+    out_hbm,
     sums_ref,
-    pad_ref,
     edge_ref,
-):
-    finish(
-        lat, lon, index_ref, west_ref, east_ref, state_ref, held_ref, high_ref, low_ref, pad_ref, edge_ref
-    )
+    sem,
+):
+    finish(lat, lon, west_ref, east_ref, state_ref, later_ref, high_ref, low_ref, edge_ref)
     rows = lat * lon
     product_ref[...] = part_ref[...]
     tracers = product_ref.shape[0] // rows
     for n, r in enumerate(beyond(lat, lon)):
         product_ref[pl.ds(r, tracers, stride=rows), :] = jnp.transpose(edge_ref[n])
+    copy = pltpu.make_async_copy(product_ref, out_hbm, sem)
+    copy.start()
     product = product_ref[...]
     count = basis_ref.shape[0]
     pairs = count * (count + 1) // 2
@@ -359,13 +367,10 @@
     column = jnp.sum(all_sums, 1, keepdims=True)
     row = jnp.sum(jnp.where(spot == iota(spot.shape, 1), column, 0.0), 0, keepdims=True)
     sums_ref[...] = jnp.broadcast_to(row, sums_ref.shape)
-
-
-def last_kernel(
-    parts_ref, product_ref, basis_ref, next_ref, out_hbm, coeffs_ref, flag_ref, sem
-):
-    copy = pltpu.make_async_copy(product_ref, out_hbm, sem)
-    copy.start()
+    copy.wait()
+
+
+def last_kernel(parts_ref, product_ref, basis_ref, next_ref, coeffs_ref, flag_ref):
     count = basis_ref.shape[0]
     row = jnp.sum(parts_ref[...], 0, keepdims=True)
     lane = iota(row.shape, 1)
@@ -395,7 +400,6 @@
         coeffs_ref[k] = heights[k][0, 0]
     coeffs_ref[count] = beta[0, 0]
     flag_ref[0] = jnp.where(short < 0.01 * size, 1, 0)[0, 0]
-    copy.wait()
 
 
 def summed(rows):
@@ -453,16 +457,10 @@
             like((lat, width, points), BF16),
         )
 
+    begun = call(begin_kernel, like((8, points)), [], VMEM, flops=PACK)()
     x, first, last, left, right = call(
-        pack_kernel,
-        edges(2 * tracers),
-        [HBM] * 2,
-        [VMEM] * 5,
-        scratch=[pltpu.VMEM((size, points), F32)] * 2 + [pltpu.SemaphoreType.DMA((2,))],
-        size=400000,
-        flops=PACK,
-        limit=59,
-    )(flat_c, flat_v)
+        pack_kernel, edges(2 * tracers), [VMEM] * 3, [VMEM] * 5, flops=PACK, size=400000
+    )(begun, flat_c, flat_v)
 
     flat_basis = basis.reshape(count, size, points)
     held = blocks.reshape(rows * slots, points, points)
@@ -494,16 +492,17 @@
 
     work = 2 * 2 * tracers * rows * slots * points * points
     ends = len(beyond(lat, lon))
+    later = like((sum(map(len, beyond(lat, lon).values())), points, points), BF16)
 
     prepared = (index, high, low, source, rate_column, gram)
     north, south, prepared = rows_around(first, last, prepared)
     index, high, low, source, rate_column, gram = prepared
     west, east = columns_around(left, right, north, south)
-    part, state = call(
+    part, state, blocks_later = call(
         functools.partial(first_kernel, lat, lon),
-        (like((rows, tracers, points), BF16), like((rows, points, 2 * tracers))),
+        (like((rows, tracers, points), BF16), like((rows, points, 2 * tracers)), later),
         [SMEM] + [VMEM] * 7,
-        [VMEM] * 2,
+        [VMEM] * 3,
         scratch=[pltpu.VMEM((places, 2 * tracers, points), BF16)],
         flops=BULK,
         size=5000000,
@@ -511,12 +510,11 @@
     x, first, last, left, right, edge = call(
         functools.partial(first_end_kernel, lat, lon),
         edges(tracers) + (like((ends, points, 2 * tracers)),),
-        [SMEM] + [VMEM] * 7,
+        [VMEM] * 7,
         [VMEM] * 6,
-        scratch=[pltpu.VMEM((places, 2 * tracers, points), BF16)],
         flops=work // 20,
         size=500000,
-    )(index, west, east, state, held, high, low, part)
+    )(west, east, state, blocks_later, high, low, part)
 
     source = call(
         functools.partial(pull_kernel, lat, lon),
@@ -529,47 +527,44 @@
 
     north, south, source = rows_around(first, last, source)
     west, east = columns_around(left, right, north, south)
-    part, state = call(
+    part, state, blocks_later = call(
         functools.partial(second_kernel, lat, lon),
-        (like((size, points)), like((rows, points, tracers))),
+        (like((size, points)), like((rows, points, tracers)), later),
         [SMEM] + [VMEM] * 7,
-        [VMEM] * 2,
+        [VMEM] * 3,
         scratch=[pltpu.VMEM((places, tracers, points), BF16)],
         flops=BULK,
         size=5000000,
     )(index, x, north, south, held, high, low, source)
-    product, sums = call(
+    product, written, sums = call(
         functools.partial(second_end_kernel, lat, lon),
-        (like((size, points)), like((lax.axis_size("lon"), points))),
-        [SMEM] + [VMEM] * 9,
-        [VMEM] * 2,
-        scratch=[
-            pltpu.VMEM((places, tracers, points), BF16),
-            pltpu.VMEM((ends, points, tracers), F32),
-        ],
+        (like((size, points)), like((size, points)), like((lax.axis_size("lon"), points))),
+        [VMEM] * 9,
+        [VMEM, HBM, VMEM],
+        scratch=[pltpu.VMEM((ends, points, tracers), F32), pltpu.SemaphoreType.DMA],
         flops=work // 20,
         size=1500000,
-    )(index, west, east, state, held, high, low, part, gram, flat_basis)
+    )(west, east, state, blocks_later, high, low, part, gram, flat_basis)
 
     parts = summed(sums)
-    following, written, coeffs, flag = call(
+    following, coeffs, flag = call(
         last_kernel,
-        (like((size, points)), like((size, points)), like((count + 1,)), like((1,), jnp.int32)),
+        (like((size, points)), like((count + 1,)), like((1,), jnp.int32)),
         [VMEM] * 3,
-        [VMEM, HBM, SMEM, SMEM],
-        scratch=[pltpu.SemaphoreType.DMA],
+        [VMEM, SMEM, SMEM],
         size=700000,
     )(parts, product, flat_basis)
 
     def again(carry):
-        following, coeffs, flag = carry
+        pairs = count * (count + 1) // 2
+        heights = jnp.sum(parts, 0)[pairs : pairs + count]
         rest = product - jnp.einsum(
-            "k,ksp->sp", coeffs[:count], flat_basis, precision=lax.Precision.HIGHEST
+            "k,ksp->sp", heights, flat_basis, precision=lax.Precision.HIGHEST
         )
         part = jnp.pad(jnp.sum(rest * rest).reshape(1, 1), ((0, 0), (0, points - 1)))
         squared = jnp.sum(summed(jnp.broadcast_to(part, (lax.axis_size("lon"), points))), 0)[0]
         beta = jnp.sqrt(squared + 1e-06)
-        return rest / beta, jnp.concatenate([coeffs[:count], beta[None]]), flag * 0
+        return rest / beta, jnp.concatenate([heights, beta[None]]), carry[2] * 0
 
     following, coeffs, flag = lax.while_loop(
         lambda carry: carry[2][0] > 0, again, (following, coeffs, flag)

time: 77.9 us -> 76 us (0.976)
  waiting for transfers between devices: 1.94 us -> 8.53 us
  blocking collectives: 32 us -> 28.9 us
  Pallas kernels: 12.2 us -> 9.22 us
  starting transfers between devices: 29.1 us -> 26.3 us
    ppermute x8, waiting for transfers between devices: 1.94 us -> 8.53 us  [moved(): return lax.ppermute(a, axis, [(i, (i + step) % size) for i in range(size)])]
    all_to_all x1, blocking collectives: 14.6 us -> 11.6 us  [summed(): row = jnp.sum(lax.all_to_all(rows, 'lon', 0, 0), 0, keepdims=True)]
    ppermute x8, starting transfers between devices: 29.1 us -> 26.3 us  [moved(): return lax.ppermute(a, axis, [(i, (i + step) % size) for i in range(size)])]
    pallas_call x2 -> x3, Pallas kernels: 3.05 us -> 0.81 us  [the longest x1 0.79 us: body(): call(last_kernel, (like((size, points)), like((count + 1,)), like((1,), j...]
  transfers between devices with their start and end apart: 8 -> 8, of which waited for: 1 -> 3; matrix products, arithmetic and copies ran while one was open for 0% -> 0% of each run, Pallas kernels for 8% -> 9%
where the time goes in v8:
time: 76 us; the launch traced here: 75.6 us
  blocking collectives  28.9 us (38%)
  starting transfers between devices  26.3 us (35%)
  Pallas kernels  9.22 us (12%)
  waiting for transfers between devices  8.53 us (11%)
  local copies, waits for them, and re-layouts  0.97 us (1%)
  between operations  0.88 us (1%)
    ppermute x8, starting transfers between devices, moved(): return lax.ppermute(a, axis, [(i, (i + step) % size) for i in range(size)])  26.3 us
    all_to_all x1, blocking collectives, summed(): return lax.all_to_all(rows, 'lat', 0, 0)  17.4 us
    all_to_all x1, blocking collectives, summed(): row = jnp.sum(lax.all_to_all(rows, 'lon', 0, 0), 0, keepdims=True)  11.6 us
    ppermute x8, waiting for transfers between devices, moved(): return lax.ppermute(a, axis, [(i, (i + step) % size) for i in range(size)])  8.53 us
    pallas_call x1, Pallas kernels, body(): call(functools.partial(second_kernel, lat, lon), (like((size, points)), l...  2.02 us
    pallas_call x1, Pallas kernels, body(): call(functools.partial(first_kernel, lat, lon), (like((rows, tracers, poi...  2.01 us
  transfers between devices with their start and end apart: 8, of which 3 were waited for; matrix products, arithmetic and copies ran while one was open for 0% of the time, Pallas kernels for 9%

profile of v8, /device:TPU:1, one launch (start us, length us, event | category | flops | bytes accessed | tf_op | source)
XLA Modules:
  0.0 75.6 jit_solution(5107716930741676708)
XLA Ops:
  0.6 0.0 copy-start.4
  0.6 0.0 copy-start.3
  0.7 0.9 %copy-done.4 = f32[16,3,4,128]{3,2,1,0:T(4,128)S(1)} copy-done((f32[16,3,4,128]{3,2,1,0:T(4,128)S(1)}, f32[16,3,4,128]{3,2,1,0:T(4,128)}, u32[]{:S(2)}) %copy-start.4) | copy-done | bytes 98328
  1.5 0.0 copy-done.3
  1.6 0.0 copy-start
  1.6 0.0 copy-start.2
  1.6 0.0 copy-start.5
  1.6 0.0 copy-start.6
  1.6 0.0 copy-start.7
  1.6 0.0 copy-start.8
  1.6 0.0 copy-start.9
  1.6 2.7 %collective-permute-start = (bf16[4,32,128]{2,1,0:T(8,128)(2,1)S(1)}, bf16[4,32,128]{2,1,0:T(8,128)(2,1)S(1)}, u32[]{:S(2)}, u32[]{:S(2)}) collective-permute-start(bf16[4,32,128]{2,1,0:T(8,128)(2,1)S(1)} %get-tuple-element.73), channel_id=1, source_target_pairs={{0,32},{32,64},{64,96},{96,128},{128,160},{160,192},{192,224},{224... | collective-permute-start | bytes 98312 | tf_op jit(solution)/shard_map/ppermute | solution.py:413
  4.3 4.2 %collective-permute-start.1 = (bf16[4,32,128]{2,1,0:T(8,128)(2,1)S(1)}, bf16[4,32,128]{2,1,0:T(8,128)(2,1)S(1)}, u32[]{:S(2)}, u32[]{:S(2)}) collective-permute-start(bf16[4,32,128]{2,1,0:T(8,128)(2,1)S(1)} %get-tuple-element.74), channel_id=1, source_target_pairs={{0,480},{32,0},{64,32},{96,64},{128,96},{160,128},{192,160},{224,1... | collective-permute-start | bytes 98312 | tf_op jit(solution)/shard_map/ppermute | solution.py:413
  8.6 0.0 copy-done
  8.6 0.0 copy-done.2
  8.6 0.0 copy-done.5
  8.6 0.0 copy-done.6
  8.6 0.0 copy-done.7
  8.6 0.0 copy-done.8
  8.6 0.0 copy-done.9
  8.6 0.0 copy-start.1
  8.6 1.2 %shard_map.123 = (s32[2,3,4,9]{3,2,1,0:T(4,128)S(1)}, bf16[12,128,128]{2,1,0:T(8,128)(2,1)S(1)}, bf16[12,128,128]{2,1,0:T(8,128)(2,1)S(1)}, f32[12,128,32]{2,1,0...) custom-call(s32[3,4,9]{2,1,0:T(4,128)S(1)} %copy-done.5, s32[3,4,9]{2,1,0:T(4,128)S(1)} %copy-done.6, ...), custom_call_target="tpu_custom_call" | custom-call | flops 10000000000 | bytes 8000000 | tf_op jit(solution)/shard_map/pallas_call | solution.py:467
  9.8 0.0 collective-permute-done.north_ref
  9.8 0.0 collective-permute-done.1.south_ref
  9.9 10.7 %collective-permute-start.3 = (bf16[5,32,128]{2,1,0:T(8,128)(2,1)S(1)}, bf16[5,32,128]{2,1,0:T(8,128)(2,1)S(1)}, u32[]{:S(2)}, u32[]{:S(2)}) collective-permute-start(bf16[5,32,128]{2,1,0:T(8,128)(2,1)S(1)} %pad_maximum_fusion.2), channel_id=1, source_target_pairs={{0,31},{1,0},{2,1},{3,2},{4,3},{5,4},{6,5},{7,6},{8,7},{9,8},{10,9... | collective-permute-start | bytes 122888 | tf_op jit(solution)/shard_map/ppermute | solution.py:413
  20.6 1.9 %collective-permute-start.2 = (bf16[5,32,128]{2,1,0:T(8,128)(2,1)S(1)}, bf16[5,32,128]{2,1,0:T(8,128)(2,1)S(1)}, u32[]{:S(2)}, u32[]{:S(2)}) collective-permute-start(bf16[5,32,128]{2,1,0:T(8,128)(2,1)S(1)} %pad_maximum_fusion.1), channel_id=1, source_target_pairs={{0,1},{1,2},{2,3},{3,4},{4,5},{5,6},{6,7},{7,8},{8,9},{9,10},{10,1... | collective-permute-start | bytes 122888 | tf_op jit(solution)/shard_map/ppermute | solution.py:413
  22.5 0.0 copy-done.1
  22.5 2.0 %shard_map.124 = (bf16[12,16,128]{2,1,0:T(8,128)(2,1)S(1)}, f32[12,128,32]{2,1,0:T(8,128)S(1)}, bf16[18,128,128]{2,1,0:T(8,128)(2,1)S(1)}) custom-call(s32[2,3,4,9]{3,2,1,0:T(4,128)S(1)} %get-tuple-element.85.index_ref, bf16[12,32,128]{2,1,0:T(8,128)(2,1)S(1)} %get-tuple-element.86.x_ref, bf16[4,32,128]{2,1,0:T(8,128)(2,1)S(1)} %collective-permute-done.north_ref, ...), custom_call_target="tpu_custom_call" | custom-call | flops 2000000000 | bytes 5000000 | tf_op jit(solution)/shard_map/pallas_call | solution.py:501
  24.5 0.0 collective-permute-done.3.east_ref
  24.6 4.1 %collective-permute-done.2.west_ref = bf16[5,32,128]{2,1,0:T(8,128)(2,1)S(1)} collective-permute-done((bf16[5,32,128]{2,1,0:T(8,128)(2,1)S(1)}, bf16[5,32,128]{2,1,0:T(8,128)(2,1)S(1)}, u32[]{:S(2)}, u32[]{:S(2)}) %collective-permute-start.2) | collective-permute-done | bytes 40992 | tf_op jit(solution)/shard_map/ppermute | solution.py:413
  28.7 0.5 shard_map.125
  29.2 1.5 %collective-permute-start.4 = (bf16[4,16,128]{2,1,0:T(8,128)(2,1)S(1)}, bf16[4,16,128]{2,1,0:T(8,128)(2,1)S(1)}, u32[]{:S(2)}, u32[]{:S(2)}) collective-permute-start(bf16[4,16,128]{2,1,0:T(8,128)(2,1)S(1)} %get-tuple-element.93), channel_id=1, source_target_pairs={{0,32},{32,64},{64,96},{96,128},{128,160},{160,192},{192,224},{224... | collective-permute-start | bytes 49160 | tf_op jit(solution)/shard_map/ppermute | solution.py:413
  30.7 0.0 collective-permute-start.5
  30.7 1.4 %shard_map.126.source_ref = f32[12,128,16]{2,1,0:T(8,128)S(1)} custom-call(f32[12,128,32]{2,1,0:T(8,128)S(1)} %get-tuple-element.90.state_ref, f32[6,128,32]{2,1,0:T(8,128)S(1)} %get-tuple-element.95.edge_ref, f32[128,16]{1,0:T(8,128)S(1)} %get-tuple-element.96.rate_column_ref, f32[1,16]{1,0:T(1,128)S(1)} %bitcast.26), custom_call_target="tpu_custom_call" | custom-call | flops 100000 | bytes 2000000 | tf_op jit(solution)/shard_map/pallas_call | solution.py:519
  32.2 0.0 collective-permute-done.4.north_ref
  32.2 2.0 %collective-permute-done.5.south_ref = bf16[4,16,128]{2,1,0:T(8,128)(2,1)S(1)} collective-permute-done((bf16[4,16,128]{2,1,0:T(8,128)(2,1)S(1)}, bf16[4,16,128]{2,1,0:T(8,128)(2,1)S(1)}, u32[]{:S(2)}, u32[]{:S(2)}) %collective-permute-start.5) | collective-permute-done | bytes 16416 | tf_op jit(solution)/shard_map/ppermute | solution.py:413
  34.1 1.9 %collective-permute-start.7 = (bf16[5,16,128]{2,1,0:T(8,128)(2,1)S(1)}, bf16[5,16,128]{2,1,0:T(8,128)(2,1)S(1)}, u32[]{:S(2)}, u32[]{:S(2)}) collective-permute-start(bf16[5,16,128]{2,1,0:T(8,128)(2,1)S(1)} %pad_maximum_fusion.4), channel_id=1, source_target_pairs={{0,31},{1,0},{2,1},{3,2},{4,3},{5,4},{6,5},{7,6},{8,7},{9,8},{10,9... | collective-permute-start | bytes 61448 | tf_op jit(solution)/shard_map/ppermute | solution.py:413
  36.1 3.4 %collective-permute-start.6 = (bf16[5,16,128]{2,1,0:T(8,128)(2,1)S(1)}, bf16[5,16,128]{2,1,0:T(8,128)(2,1)S(1)}, u32[]{:S(2)}, u32[]{:S(2)}) collective-permute-start(bf16[5,16,128]{2,1,0:T(8,128)(2,1)S(1)} %pad_maximum_fusion.3), channel_id=1, source_target_pairs={{0,1},{1,2},{2,3},{3,4},{4,5},{5,6},{6,7},{7,8},{8,9},{9,10},{10,1... | collective-permute-start | bytes 61448 | tf_op jit(solution)/shard_map/ppermute | solution.py:413
  39.5 2.0 %shard_map.127 = (f32[192,128]{1,0:T(8,128)S(1)}, f32[12,128,16]{2,1,0:T(8,128)S(1)}, bf16[18,128,128]{2,1,0:T(8,128)(2,1)S(1)}) custom-call(s32[2,3,4,9]{3,2,1,0:T(4,128)S(1)} %get-tuple-element.85.index_ref, bf16[12,16,128]{2,1,0:T(8,128)(2,1)S(1)} %get-tuple-element.101.x_ref, bf16[4,16,128]{2,1,0:T(8,128)(2,1)S(1)} %collective-permute-done.4.north_ref, ...), custom_call_target="tpu_custom_call" | custom-call | flops 2000000000 | bytes 5000000 | tf_op jit(solution)/shard_map/pallas_call | solution.py:530
  41.5 0.0 collective-permute-done.7.east_ref
  41.5 2.4 %collective-permute-done.6.west_ref = bf16[5,16,128]{2,1,0:T(8,128)(2,1)S(1)} collective-permute-done((bf16[5,16,128]{2,1,0:T(8,128)(2,1)S(1)}, bf16[5,16,128]{2,1,0:T(8,128)(2,1)S(1)}, u32[]{:S(2)}, u32[]{:S(2)}) %collective-permute-start.6) | collective-permute-done | bytes 20512 | tf_op jit(solution)/shard_map/ppermute | solution.py:413
  43.9 1.2 %shard_map.128 = (f32[192,128]{1,0:T(8,128)S(1)}, f32[192,128]{1,0:T(8,128)}, f32[32,128]{1,0:T(8,128)S(1)}) custom-call(bf16[5,16,128]{2,1,0:T(8,128)(2,1)S(1)} %collective-permute-done.6.west_ref, bf16[5,16,128]{2,1,0:T(8,128)(2,1)S(1)} %collective-permute-done.7.east_ref, f32[12,128,16]{2,1,0:T(8,128)S(1)} %get-tuple-element.103.state_ref, ...), custom_call_target="tpu_custom_call" | custom-call | flops 5662310 | bytes 1500000 | tf_op jit(solution)/shard_map/pallas_call | solution.py:539
  45.2 11.6 %all_to_all.28 = f32[32,1,128]{2,1,0:T(1,128)S(1)} all-to-all(f32[32,1,128]{2,1,0:T(1,128)S(1)} %bitcast.24), channel_id=1, replica_groups=mesh['lat'=16,'lon'=32] {'lon'}, dimensions={0} | all-to-all | bytes 32768 | tf_op jit(solution)/shard_map/all_to_all | solution.py:406
  56.7 0.1 reduce_sum.45
  56.8 17.4 %all_to_all.29 = f32[16,1,128]{2,1,0:T(1,128)S(1)} all-to-all(f32[16,1,128]{2,1,0:T(1,128)S(1)} %broadcast_in_dim.6), channel_id=1, replica_groups=mesh['lat'=16,'lon'=32] {'lat'}, dimensions={0} | all-to-all | bytes 16384 | tf_op jit(solution)/shard_map/all_to_all | solution.py:408
  74.1 0.8 %shard_map.129 = (f32[192,128]{1,0:T(8,128)}, f32[5]{0:T(128)}, s32[1]{0:T(128)}) custom-call(f32[16,128]{1,0:T(8,128)S(1)} %bitcast.40, f32[192,128]{1,0:T(8,128)S(1)} %get-tuple-element.150.product_ref, f32[4,192,128]{2,1,0:T(8,128)S(1)} %bitcast.35), custom_call_target="tpu_custom_call" | custom-call | bytes 700000 | tf_op jit(solution)/shard_map/pallas_call | solution.py:550
  74.9 0.7 while.11
  (10 shorter events, 0.1 us)
Async XLA Ops:
  0.6 0.9 %copy-start.4 = (f32[16,3,4,128]{3,2,1,0:T(4,128)S(1)}, f32[16,3,4,128]{3,2,1,0:T(4,128)}, u32[]{:S(2)}) copy-start(f32[16,3,4,128]{3,2,1,0:T(4,128)} %param.13) | copy-start | bytes 294916
  0.6 0.9 %copy-start.3 = (f32[16,3,4,128]{3,2,1,0:T(4,128)S(1)}, f32[16,3,4,128]{3,2,1,0:T(4,128)}, u32[]{:S(2)}) copy-start(f32[16,3,4,128]{3,2,1,0:T(4,128)} %param.12) | copy-start | bytes 294916
  1.6 7.0 %copy-start = (f32[16]{0:T(128)S(1)}, f32[16]{0:T(128)}, u32[]{:S(2)}) copy-start(f32[16]{0:T(128)} %param.20) | copy-start | bytes 196
  1.6 7.0 %copy-start.2 = (f32[3,4,8,16,16]{4,3,2,1,0:T(8,128)S(1)}, f32[3,4,8,16,16]{4,3,2,1,0:T(8,128)}, u32[]{:S(2)}) copy-start(f32[3,4,8,16,16]{4,3,2,1,0:T(8,128)} %inverse_ref.1) | copy-start | bytes 294916
  1.6 7.0 %copy-start.5 = (s32[3,4,9]{2,1,0:T(4,128)S(1)}, s32[3,4,9]{2,1,0:T(4,128)}, u32[]{:S(2)}) copy-start(s32[3,4,9]{2,1,0:T(4,128)} %pattern_ref.1) | copy-start | bytes 1300
  1.6 7.0 %copy-start.6 = (s32[3,4,9]{2,1,0:T(4,128)S(1)}, s32[3,4,9]{2,1,0:T(4,128)}, u32[]{:S(2)}) copy-start(s32[3,4,9]{2,1,0:T(4,128)} %live_ref.1) | copy-start | bytes 1300
  1.6 7.0 %copy-start.7 = (s32[3,4,8]{2,1,0:T(4,128)S(1)}, s32[3,4,8]{2,1,0:T(4,128)}, u32[]{:S(2)}) copy-start(s32[3,4,8]{2,1,0:T(4,128)} %depth_ref.1) | copy-start | bytes 1156
  1.6 7.0 %copy-start.8 = (f32[3,4,128]{2,1,0:T(4,128)S(1)}, f32[3,4,128]{2,1,0:T(4,128)}, u32[]{:S(2)}) copy-start(f32[3,4,128]{2,1,0:T(4,128)} %rate_ref.1) | copy-start | bytes 18436
  1.6 7.0 %copy-start.9 = (f32[4,16,3,4,128]{4,3,2,1,0:T(4,128)S(1)}, f32[4,16,3,4,128]{4,3,2,1,0:T(4,128)}, u32[]{:S(2)}) copy-start(f32[4,16,3,4,128]{4,3,2,1,0:T(4,128)} %param.21) | copy-start | bytes 1179652
  1.6 8.2 %collective-permute-start = (bf16[4,32,128]{2,1,0:T(8,128)(2,1)S(1)}, bf16[4,32,128]{2,1,0:T(8,128)(2,1)S(1)}, u32[]{:S(2)}, u32[]{:S(2)}) collective-permute-start(bf16[4,32,128]{2,1,0:T(8,128)(2,1)S(1)} %get-tuple-element.73), channel_id=1, source_target_pairs={{0,32},{32,64},{64,96},{96,128},{128,160},{160,192},{192,224},{224... | collective-permute-start | bytes 98312 | tf_op jit(solution)/shard_map/ppermute | solution.py:413
  4.3 5.5 %collective-permute-start.1 = (bf16[4,32,128]{2,1,0:T(8,128)(2,1)S(1)}, bf16[4,32,128]{2,1,0:T(8,128)(2,1)S(1)}, u32[]{:S(2)}, u32[]{:S(2)}) collective-permute-start(bf16[4,32,128]{2,1,0:T(8,128)(2,1)S(1)} %get-tuple-element.74), channel_id=1, source_target_pairs={{0,480},{32,0},{64,32},{96,64},{128,96},{160,128},{192,160},{224,1... | collective-permute-start | bytes 98312 | tf_op jit(solution)/shard_map/ppermute | solution.py:413
  8.6 13.9 %copy-start.1 = (bf16[3,4,9,128,128]{4,3,2,1,0:T(8,128)(2,1)S(1)}, bf16[3,4,9,128,128]{4,3,2,1,0:T(8,128)(2,1)}, u32[]{:S(2)}) copy-start(bf16[3,4,9,128,128]{4,3,2,1,0:T(8,128)(2,1)} %param.14) | copy-start | bytes 10616836
  9.9 14.7 %collective-permute-start.3 = (bf16[5,32,128]{2,1,0:T(8,128)(2,1)S(1)}, bf16[5,32,128]{2,1,0:T(8,128)(2,1)S(1)}, u32[]{:S(2)}, u32[]{:S(2)}) collective-permute-start(bf16[5,32,128]{2,1,0:T(8,128)(2,1)S(1)} %pad_maximum_fusion.2), channel_id=1, source_target_pairs={{0,31},{1,0},{2,1},{3,2},{4,3},{5,4},{6,5},{7,6},{8,7},{9,8},{10,9... | collective-permute-start | bytes 122888 | tf_op jit(solution)/shard_map/ppermute | solution.py:413
  20.6 8.1 %collective-permute-start.2 = (bf16[5,32,128]{2,1,0:T(8,128)(2,1)S(1)}, bf16[5,32,128]{2,1,0:T(8,128)(2,1)S(1)}, u32[]{:S(2)}, u32[]{:S(2)}) collective-permute-start(bf16[5,32,128]{2,1,0:T(8,128)(2,1)S(1)} %pad_maximum_fusion.1), channel_id=1, source_target_pairs={{0,1},{1,2},{2,3},{3,4},{4,5},{5,6},{6,7},{7,8},{8,9},{9,10},{10,1... | collective-permute-start | bytes 122888 | tf_op jit(solution)/shard_map/ppermute | solution.py:413
  29.2 3.0 %collective-permute-start.4 = (bf16[4,16,128]{2,1,0:T(8,128)(2,1)S(1)}, bf16[4,16,128]{2,1,0:T(8,128)(2,1)S(1)}, u32[]{:S(2)}, u32[]{:S(2)}) collective-permute-start(bf16[4,16,128]{2,1,0:T(8,128)(2,1)S(1)} %get-tuple-element.93), channel_id=1, source_target_pairs={{0,32},{32,64},{64,96},{96,128},{128,160},{160,192},{192,224},{224... | collective-permute-start | bytes 49160 | tf_op jit(solution)/shard_map/ppermute | solution.py:413
  30.7 3.5 %collective-permute-start.5 = (bf16[4,16,128]{2,1,0:T(8,128)(2,1)S(1)}, bf16[4,16,128]{2,1,0:T(8,128)(2,1)S(1)}, u32[]{:S(2)}, u32[]{:S(2)}) collective-permute-start(bf16[4,16,128]{2,1,0:T(8,128)(2,1)S(1)} %get-tuple-element.94), channel_id=1, source_target_pairs={{0,480},{32,0},{64,32},{96,64},{128,96},{160,128},{192,160},{224,1... | collective-permute-start | bytes 49160 | tf_op jit(solution)/shard_map/ppermute | solution.py:413
  34.1 7.3 %collective-permute-start.7 = (bf16[5,16,128]{2,1,0:T(8,128)(2,1)S(1)}, bf16[5,16,128]{2,1,0:T(8,128)(2,1)S(1)}, u32[]{:S(2)}, u32[]{:S(2)}) collective-permute-start(bf16[5,16,128]{2,1,0:T(8,128)(2,1)S(1)} %pad_maximum_fusion.4), channel_id=1, source_target_pairs={{0,31},{1,0},{2,1},{3,2},{4,3},{5,4},{6,5},{7,6},{8,7},{9,8},{10,9... | collective-permute-start | bytes 61448 | tf_op jit(solution)/shard_map/ppermute | solution.py:413
  36.1 7.8 %collective-permute-start.6 = (bf16[5,16,128]{2,1,0:T(8,128)(2,1)S(1)}, bf16[5,16,128]{2,1,0:T(8,128)(2,1)S(1)}, u32[]{:S(2)}, u32[]{:S(2)}) collective-permute-start(bf16[5,16,128]{2,1,0:T(8,128)(2,1)S(1)} %pad_maximum_fusion.3), channel_id=1, source_target_pairs={{0,1},{1,2},{2,3},{3,4},{4,5},{5,6},{6,7},{7,8},{8,9},{9,10},{10,1... | collective-permute-start | bytes 61448 | tf_op jit(solution)/shard_map/ppermute | solution.py:413

commit v9 on v8

--- a/solution.py
+++ b/solution.py
@@ -408,21 +408,22 @@
     return lax.all_to_all(rows, "lat", 0, 0)
 
 
-def moved(a, axis, step):
+def moved(a, axis, step, around):
     size = lax.axis_size(axis)
-    return lax.ppermute(a, axis, [(i, (i + step) % size) for i in range(size)])
+    pairs = [(i, (i + step) % size) for i in range(size) if around or 0 <= i + step < size]
+    return lax.ppermute(a, axis, pairs)
 
 
 def rows_around(first, last, beside):
-    north = moved(last, "lat", 1)
-    south = moved(first, "lat", -1)
+    north = moved(last, "lat", 1, True)
+    south = moved(first, "lat", -1, True)
     return lax.optimization_barrier((north, south, beside))
 
 
 def columns_around(left, right, north, south):
     right = jnp.concatenate([north[-1:], right, south[-1:]], 0)
     left = jnp.concatenate([north[:1], left, south[:1]], 0)
-    return moved(right, "lon", 1), moved(left, "lon", -1)
+    return moved(right, "lon", 1, False), moved(left, "lon", -1, False)
 
 
 def body(

time: 76 us -> 74.1 us (0.975)
  blocking collectives: 28.9 us -> 40.3 us
  waiting for transfers between devices: 8.53 us -> 0.06 us
  starting transfers between devices: 26.3 us -> 21.5 us
    all_to_all x1, blocking collectives: 11.6 us -> 22.6 us  [summed(): row = jnp.sum(lax.all_to_all(rows, 'lon', 0, 0), 0, keepdims=True)]
    ppermute x8, waiting for transfers between devices: 8.53 us -> 0.06 us  [moved(): return lax.ppermute(a, axis, pairs)]
    ppermute x8, starting transfers between devices: 26.3 us -> 21.5 us  [moved(): return lax.ppermute(a, axis, pairs)]
  transfers between devices with their start and end apart: 8 -> 8, of which waited for: 3 -> 0; matrix products, arithmetic and copies ran while one was open for 0% -> 0% of each run, Pallas kernels for 9% -> 9%
where the time goes in v9:
time: 74.1 us; the launch traced here: 73.7 us
  blocking collectives  40.3 us (54%)
  starting transfers between devices  21.5 us (29%)
  Pallas kernels  9.24 us (12%)
  local copies, waits for them, and re-layouts  0.98 us (1%)
  between operations  0.93 us (1%)
    all_to_all x1, blocking collectives, summed(): row = jnp.sum(lax.all_to_all(rows, 'lon', 0, 0), 0, keepdims=True)  22.6 us
    ppermute x8, starting transfers between devices, moved(): return lax.ppermute(a, axis, pairs)  21.5 us
    all_to_all x1, blocking collectives, summed(): return lax.all_to_all(rows, 'lat', 0, 0)  17.6 us
    pallas_call x1, Pallas kernels, body(): call(functools.partial(second_kernel, lat, lon), (like((size, points)), l...  2.03 us
    pallas_call x1, Pallas kernels, body(): call(functools.partial(first_kernel, lat, lon), (like((rows, tracers, poi...  2.01 us
  transfers between devices with their start and end apart: 8, of which 0 were waited for; matrix products, arithmetic and copies ran while one was open for 0% of the time, Pallas kernels for 9%

profile of v9, /device:TPU:1, one launch (start us, length us, event | category | flops | bytes accessed | tf_op | source)
XLA Modules:
  0.0 73.7 jit_solution(16253807800242603585)
XLA Ops:
  0.6 0.0 copy-start.4
  0.6 0.0 copy-start.3
  0.7 0.9 %copy-done.4 = f32[16,3,4,128]{3,2,1,0:T(4,128)S(1)} copy-done((f32[16,3,4,128]{3,2,1,0:T(4,128)S(1)}, f32[16,3,4,128]{3,2,1,0:T(4,128)}, u32[]{:S(2)}) %copy-start.4) | copy-done | bytes 98328
  1.5 0.0 copy-done.3
  1.6 0.0 copy-start
  1.6 0.0 copy-start.2
  1.6 0.0 copy-start.5
  1.6 0.0 copy-start.6
  1.6 0.0 copy-start.7
  1.6 0.0 copy-start.8
  1.6 0.0 copy-start.9
  1.6 2.7 %collective-permute-start = (bf16[4,32,128]{2,1,0:T(8,128)(2,1)S(1)}, bf16[4,32,128]{2,1,0:T(8,128)(2,1)S(1)}, u32[]{:S(2)}, u32[]{:S(2)}) collective-permute-start(bf16[4,32,128]{2,1,0:T(8,128)(2,1)S(1)} %get-tuple-element.73), channel_id=1, source_target_pairs={{0,32},{32,64},{64,96},{96,128},{128,160},{160,192},{192,224},{224... | collective-permute-start | bytes 98312 | tf_op jit(solution)/shard_map/ppermute | solution.py:414
  4.3 4.2 %collective-permute-start.1 = (bf16[4,32,128]{2,1,0:T(8,128)(2,1)S(1)}, bf16[4,32,128]{2,1,0:T(8,128)(2,1)S(1)}, u32[]{:S(2)}, u32[]{:S(2)}) collective-permute-start(bf16[4,32,128]{2,1,0:T(8,128)(2,1)S(1)} %get-tuple-element.74), channel_id=1, source_target_pairs={{0,480},{32,0},{64,32},{96,64},{128,96},{160,128},{192,160},{224,1... | collective-permute-start | bytes 98312 | tf_op jit(solution)/shard_map/ppermute | solution.py:414
  8.6 0.0 copy-done
  8.6 0.0 copy-done.2
  8.6 0.0 copy-done.5
  8.6 0.0 copy-done.6
  8.6 0.0 copy-done.7
  8.6 0.0 copy-done.8
  8.6 0.0 copy-done.9
  8.6 0.0 copy-start.1
  8.6 1.2 %shard_map.123 = (s32[2,3,4,9]{3,2,1,0:T(4,128)S(1)}, bf16[12,128,128]{2,1,0:T(8,128)(2,1)S(1)}, bf16[12,128,128]{2,1,0:T(8,128)(2,1)S(1)}, f32[12,128,32]{2,1,0...) custom-call(s32[3,4,9]{2,1,0:T(4,128)S(1)} %copy-done.5, s32[3,4,9]{2,1,0:T(4,128)S(1)} %copy-done.6, ...), custom_call_target="tpu_custom_call" | custom-call | flops 10000000000 | bytes 8000000 | tf_op jit(solution)/shard_map/pallas_call | solution.py:468
  9.8 0.0 collective-permute-done.north_ref
  9.8 0.0 collective-permute-done.1.south_ref
  9.9 1.3 %collective-permute-start.3 = (bf16[5,32,128]{2,1,0:T(8,128)(2,1)S(1)}, bf16[5,32,128]{2,1,0:T(8,128)(2,1)S(1)}, u32[]{:S(2)}, u32[]{:S(2)}) collective-permute-start(bf16[5,32,128]{2,1,0:T(8,128)(2,1)S(1)} %pad_maximum_fusion.2), channel_id=1, source_target_pairs={{1,0},{2,1},{3,2},{4,3},{5,4},{6,5},{7,6},{8,7},{9,8},{10,9},{11,1... | collective-permute-start | bytes 122888 | tf_op jit(solution)/shard_map/ppermute | solution.py:414
  11.2 4.0 %collective-permute-start.2 = (bf16[5,32,128]{2,1,0:T(8,128)(2,1)S(1)}, bf16[5,32,128]{2,1,0:T(8,128)(2,1)S(1)}, u32[]{:S(2)}, u32[]{:S(2)}) collective-permute-start(bf16[5,32,128]{2,1,0:T(8,128)(2,1)S(1)} %pad_maximum_fusion.1), channel_id=1, source_target_pairs={{0,1},{1,2},{2,3},{3,4},{4,5},{5,6},{6,7},{7,8},{8,9},{9,10},{10,1... | collective-permute-start | bytes 122888 | tf_op jit(solution)/shard_map/ppermute | solution.py:414
  15.2 0.0 copy-done.1
  15.2 2.0 %shard_map.124 = (bf16[12,16,128]{2,1,0:T(8,128)(2,1)S(1)}, f32[12,128,32]{2,1,0:T(8,128)S(1)}, bf16[18,128,128]{2,1,0:T(8,128)(2,1)S(1)}) custom-call(s32[2,3,4,9]{3,2,1,0:T(4,128)S(1)} %get-tuple-element.85.index_ref, bf16[12,32,128]{2,1,0:T(8,128)(2,1)S(1)} %get-tuple-element.86.x_ref, bf16[4,32,128]{2,1,0:T(8,128)(2,1)S(1)} %collective-permute-done.north_ref, ...), custom_call_target="tpu_custom_call" | custom-call | flops 2000000000 | bytes 5000000 | tf_op jit(solution)/shard_map/pallas_call | solution.py:502
  17.2 0.0 collective-permute-done.3.east_ref
  17.2 0.0 collective-permute-done.2.west_ref
  17.2 0.5 shard_map.125
  17.8 0.0 collective-permute-start.4
  17.8 3.8 %collective-permute-start.5 = (bf16[4,16,128]{2,1,0:T(8,128)(2,1)S(1)}, bf16[4,16,128]{2,1,0:T(8,128)(2,1)S(1)}, u32[]{:S(2)}, u32[]{:S(2)}) collective-permute-start(bf16[4,16,128]{2,1,0:T(8,128)(2,1)S(1)} %get-tuple-element.94), channel_id=1, source_target_pairs={{0,480},{32,0},{64,32},{96,64},{128,96},{160,128},{192,160},{224,1... | collective-permute-start | bytes 49160 | tf_op jit(solution)/shard_map/ppermute | solution.py:414
  21.7 1.4 %shard_map.126.source_ref = f32[12,128,16]{2,1,0:T(8,128)S(1)} custom-call(f32[12,128,32]{2,1,0:T(8,128)S(1)} %get-tuple-element.90.state_ref, f32[6,128,32]{2,1,0:T(8,128)S(1)} %get-tuple-element.95.edge_ref, f32[128,16]{1,0:T(8,128)S(1)} %get-tuple-element.96.rate_column_ref, f32[1,16]{1,0:T(1,128)S(1)} %bitcast.26), custom_call_target="tpu_custom_call" | custom-call | flops 100000 | bytes 2000000 | tf_op jit(solution)/shard_map/pallas_call | solution.py:520
  23.1 0.0 collective-permute-done.4.north_ref
  23.1 0.0 collective-permute-done.5.south_ref
  23.2 1.3 %collective-permute-start.7 = (bf16[5,16,128]{2,1,0:T(8,128)(2,1)S(1)}, bf16[5,16,128]{2,1,0:T(8,128)(2,1)S(1)}, u32[]{:S(2)}, u32[]{:S(2)}) collective-permute-start(bf16[5,16,128]{2,1,0:T(8,128)(2,1)S(1)} %pad_maximum_fusion.4), channel_id=1, source_target_pairs={{1,0},{2,1},{3,2},{4,3},{5,4},{6,5},{7,6},{8,7},{9,8},{10,9},{11,1... | collective-permute-start | bytes 61448 | tf_op jit(solution)/shard_map/ppermute | solution.py:414
  24.5 4.2 %collective-permute-start.6 = (bf16[5,16,128]{2,1,0:T(8,128)(2,1)S(1)}, bf16[5,16,128]{2,1,0:T(8,128)(2,1)S(1)}, u32[]{:S(2)}, u32[]{:S(2)}) collective-permute-start(bf16[5,16,128]{2,1,0:T(8,128)(2,1)S(1)} %pad_maximum_fusion.3), channel_id=1, source_target_pairs={{0,1},{1,2},{2,3},{3,4},{4,5},{5,6},{6,7},{7,8},{8,9},{9,10},{10,1... | collective-permute-start | bytes 61448 | tf_op jit(solution)/shard_map/ppermute | solution.py:414
  28.6 2.0 %shard_map.127 = (f32[192,128]{1,0:T(8,128)S(1)}, f32[12,128,16]{2,1,0:T(8,128)S(1)}, bf16[18,128,128]{2,1,0:T(8,128)(2,1)S(1)}) custom-call(s32[2,3,4,9]{3,2,1,0:T(4,128)S(1)} %get-tuple-element.85.index_ref, bf16[12,16,128]{2,1,0:T(8,128)(2,1)S(1)} %get-tuple-element.101.x_ref, bf16[4,16,128]{2,1,0:T(8,128)(2,1)S(1)} %collective-permute-done.4.north_ref, ...), custom_call_target="tpu_custom_call" | custom-call | flops 2000000000 | bytes 5000000 | tf_op jit(solution)/shard_map/pallas_call | solution.py:531
  30.7 0.0 collective-permute-done.7.east_ref
  30.7 0.0 collective-permute-done.6.west_ref
  30.7 1.2 %shard_map.128 = (f32[192,128]{1,0:T(8,128)S(1)}, f32[192,128]{1,0:T(8,128)}, f32[32,128]{1,0:T(8,128)S(1)}) custom-call(bf16[5,16,128]{2,1,0:T(8,128)(2,1)S(1)} %collective-permute-done.6.west_ref, bf16[5,16,128]{2,1,0:T(8,128)(2,1)S(1)} %collective-permute-done.7.east_ref, f32[12,128,16]{2,1,0:T(8,128)S(1)} %get-tuple-element.103.state_ref, ...), custom_call_target="tpu_custom_call" | custom-call | flops 5662310 | bytes 1500000 | tf_op jit(solution)/shard_map/pallas_call | solution.py:540
  31.9 22.6 %all_to_all.28 = f32[32,1,128]{2,1,0:T(1,128)S(1)} all-to-all(f32[32,1,128]{2,1,0:T(1,128)S(1)} %bitcast.24), channel_id=1, replica_groups=mesh['lat'=16,'lon'=32] {'lon'}, dimensions={0} | all-to-all | bytes 32768 | tf_op jit(solution)/shard_map/all_to_all | solution.py:406
  54.6 0.1 reduce_sum.45
  54.6 17.6 %all_to_all.29 = f32[16,1,128]{2,1,0:T(1,128)S(1)} all-to-all(f32[16,1,128]{2,1,0:T(1,128)S(1)} %broadcast_in_dim.6), channel_id=1, replica_groups=mesh['lat'=16,'lon'=32] {'lat'}, dimensions={0} | all-to-all | bytes 16384 | tf_op jit(solution)/shard_map/all_to_all | solution.py:408
  72.3 0.8 %shard_map.129 = (f32[192,128]{1,0:T(8,128)}, f32[5]{0:T(128)}, s32[1]{0:T(128)}) custom-call(f32[16,128]{1,0:T(8,128)S(1)} %bitcast.40, f32[192,128]{1,0:T(8,128)S(1)} %get-tuple-element.150.product_ref, f32[4,192,128]{2,1,0:T(8,128)S(1)} %bitcast.35), custom_call_target="tpu_custom_call" | custom-call | bytes 700000 | tf_op jit(solution)/shard_map/pallas_call | solution.py:551
  73.1 0.7 while.11
  (10 shorter events, 0.1 us)
Async XLA Ops:
  0.6 0.9 %copy-start.4 = (f32[16,3,4,128]{3,2,1,0:T(4,128)S(1)}, f32[16,3,4,128]{3,2,1,0:T(4,128)}, u32[]{:S(2)}) copy-start(f32[16,3,4,128]{3,2,1,0:T(4,128)} %param.13) | copy-start | bytes 294916
  0.6 0.9 %copy-start.3 = (f32[16,3,4,128]{3,2,1,0:T(4,128)S(1)}, f32[16,3,4,128]{3,2,1,0:T(4,128)}, u32[]{:S(2)}) copy-start(f32[16,3,4,128]{3,2,1,0:T(4,128)} %param.12) | copy-start | bytes 294916
  1.6 7.0 %copy-start = (f32[16]{0:T(128)S(1)}, f32[16]{0:T(128)}, u32[]{:S(2)}) copy-start(f32[16]{0:T(128)} %param.20) | copy-start | bytes 196
  1.6 7.0 %copy-start.2 = (f32[3,4,8,16,16]{4,3,2,1,0:T(8,128)S(1)}, f32[3,4,8,16,16]{4,3,2,1,0:T(8,128)}, u32[]{:S(2)}) copy-start(f32[3,4,8,16,16]{4,3,2,1,0:T(8,128)} %inverse_ref.1) | copy-start | bytes 294916
  1.6 7.0 %copy-start.5 = (s32[3,4,9]{2,1,0:T(4,128)S(1)}, s32[3,4,9]{2,1,0:T(4,128)}, u32[]{:S(2)}) copy-start(s32[3,4,9]{2,1,0:T(4,128)} %pattern_ref.1) | copy-start | bytes 1300
  1.6 7.0 %copy-start.6 = (s32[3,4,9]{2,1,0:T(4,128)S(1)}, s32[3,4,9]{2,1,0:T(4,128)}, u32[]{:S(2)}) copy-start(s32[3,4,9]{2,1,0:T(4,128)} %live_ref.1) | copy-start | bytes 1300
  1.6 7.0 %copy-start.7 = (s32[3,4,8]{2,1,0:T(4,128)S(1)}, s32[3,4,8]{2,1,0:T(4,128)}, u32[]{:S(2)}) copy-start(s32[3,4,8]{2,1,0:T(4,128)} %depth_ref.1) | copy-start | bytes 1156
  1.6 7.0 %copy-start.8 = (f32[3,4,128]{2,1,0:T(4,128)S(1)}, f32[3,4,128]{2,1,0:T(4,128)}, u32[]{:S(2)}) copy-start(f32[3,4,128]{2,1,0:T(4,128)} %rate_ref.1) | copy-start | bytes 18436
  1.6 7.0 %copy-start.9 = (f32[4,16,3,4,128]{4,3,2,1,0:T(4,128)S(1)}, f32[4,16,3,4,128]{4,3,2,1,0:T(4,128)}, u32[]{:S(2)}) copy-start(f32[4,16,3,4,128]{4,3,2,1,0:T(4,128)} %param.21) | copy-start | bytes 1179652
  1.6 8.2 %collective-permute-start = (bf16[4,32,128]{2,1,0:T(8,128)(2,1)S(1)}, bf16[4,32,128]{2,1,0:T(8,128)(2,1)S(1)}, u32[]{:S(2)}, u32[]{:S(2)}) collective-permute-start(bf16[4,32,128]{2,1,0:T(8,128)(2,1)S(1)} %get-tuple-element.73), channel_id=1, source_target_pairs={{0,32},{32,64},{64,96},{96,128},{128,160},{160,192},{192,224},{224... | collective-permute-start | bytes 98312 | tf_op jit(solution)/shard_map/ppermute | solution.py:414
  4.3 5.5 %collective-permute-start.1 = (bf16[4,32,128]{2,1,0:T(8,128)(2,1)S(1)}, bf16[4,32,128]{2,1,0:T(8,128)(2,1)S(1)}, u32[]{:S(2)}, u32[]{:S(2)}) collective-permute-start(bf16[4,32,128]{2,1,0:T(8,128)(2,1)S(1)} %get-tuple-element.74), channel_id=1, source_target_pairs={{0,480},{32,0},{64,32},{96,64},{128,96},{160,128},{192,160},{224,1... | collective-permute-start | bytes 98312 | tf_op jit(solution)/shard_map/ppermute | solution.py:414
  8.6 6.6 %copy-start.1 = (bf16[3,4,9,128,128]{4,3,2,1,0:T(8,128)(2,1)S(1)}, bf16[3,4,9,128,128]{4,3,2,1,0:T(8,128)(2,1)}, u32[]{:S(2)}) copy-start(bf16[3,4,9,128,128]{4,3,2,1,0:T(8,128)(2,1)} %param.14) | copy-start | bytes 10616836
  9.9 7.3 %collective-permute-start.3 = (bf16[5,32,128]{2,1,0:T(8,128)(2,1)S(1)}, bf16[5,32,128]{2,1,0:T(8,128)(2,1)S(1)}, u32[]{:S(2)}, u32[]{:S(2)}) collective-permute-start(bf16[5,32,128]{2,1,0:T(8,128)(2,1)S(1)} %pad_maximum_fusion.2), channel_id=1, source_target_pairs={{1,0},{2,1},{3,2},{4,3},{5,4},{6,5},{7,6},{8,7},{9,8},{10,9},{11,1... | collective-permute-start | bytes 122888 | tf_op jit(solution)/shard_map/ppermute | solution.py:414
  11.2 6.1 %collective-permute-start.2 = (bf16[5,32,128]{2,1,0:T(8,128)(2,1)S(1)}, bf16[5,32,128]{2,1,0:T(8,128)(2,1)S(1)}, u32[]{:S(2)}, u32[]{:S(2)}) collective-permute-start(bf16[5,32,128]{2,1,0:T(8,128)(2,1)S(1)} %pad_maximum_fusion.1), channel_id=1, source_target_pairs={{0,1},{1,2},{2,3},{3,4},{4,5},{5,6},{6,7},{7,8},{8,9},{9,10},{10,1... | collective-permute-start | bytes 122888 | tf_op jit(solution)/shard_map/ppermute | solution.py:414
  17.8 5.3 %collective-permute-start.4 = (bf16[4,16,128]{2,1,0:T(8,128)(2,1)S(1)}, bf16[4,16,128]{2,1,0:T(8,128)(2,1)S(1)}, u32[]{:S(2)}, u32[]{:S(2)}) collective-permute-start(bf16[4,16,128]{2,1,0:T(8,128)(2,1)S(1)} %get-tuple-element.93), channel_id=1, source_target_pairs={{0,32},{32,64},{64,96},{96,128},{128,160},{160,192},{192,224},{224... | collective-permute-start | bytes 49160 | tf_op jit(solution)/shard_map/ppermute | solution.py:414
  17.8 5.3 %collective-permute-start.5 = (bf16[4,16,128]{2,1,0:T(8,128)(2,1)S(1)}, bf16[4,16,128]{2,1,0:T(8,128)(2,1)S(1)}, u32[]{:S(2)}, u32[]{:S(2)}) collective-permute-start(bf16[4,16,128]{2,1,0:T(8,128)(2,1)S(1)} %get-tuple-element.94), channel_id=1, source_target_pairs={{0,480},{32,0},{64,32},{96,64},{128,96},{160,128},{192,160},{224,1... | collective-permute-start | bytes 49160 | tf_op jit(solution)/shard_map/ppermute | solution.py:414
  23.2 7.5 %collective-permute-start.7 = (bf16[5,16,128]{2,1,0:T(8,128)(2,1)S(1)}, bf16[5,16,128]{2,1,0:T(8,128)(2,1)S(1)}, u32[]{:S(2)}, u32[]{:S(2)}) collective-permute-start(bf16[5,16,128]{2,1,0:T(8,128)(2,1)S(1)} %pad_maximum_fusion.4), channel_id=1, source_target_pairs={{1,0},{2,1},{3,2},{4,3},{5,4},{6,5},{7,6},{8,7},{9,8},{10,9},{11,1... | collective-permute-start | bytes 61448 | tf_op jit(solution)/shard_map/ppermute | solution.py:414
  24.5 6.2 %collective-permute-start.6 = (bf16[5,16,128]{2,1,0:T(8,128)(2,1)S(1)}, bf16[5,16,128]{2,1,0:T(8,128)(2,1)S(1)}, u32[]{:S(2)}, u32[]{:S(2)}) collective-permute-start(bf16[5,16,128]{2,1,0:T(8,128)(2,1)S(1)} %pad_maximum_fusion.3), channel_id=1, source_target_pairs={{0,1},{1,2},{2,3},{3,4},{4,5},{5,6},{6,7},{7,8},{8,9},{9,10},{10,1... | collective-permute-start | bytes 61448 | tf_op jit(solution)/shard_map/ppermute | solution.py:414

commit v10 on v8

--- a/solution.py
+++ b/solution.py
@@ -408,21 +408,27 @@
     return lax.all_to_all(rows, "lat", 0, 0)
 
 
-def moved(a, axis, step):
-    size = lax.axis_size(axis)
-    return lax.ppermute(a, axis, [(i, (i + step) % size) for i in range(size)])
-
-
 def rows_around(first, last, beside):
-    north = moved(last, "lat", 1)
-    south = moved(first, "lat", -1)
+    size = lax.axis_size("lat")
+    north = lax.ppermute(last, "lat", [(i, (i + 1) % size) for i in range(size)])
+    south = lax.ppermute(first, "lat", [((i + 1) % size, i) for i in range(size)])
     return lax.optimization_barrier((north, south, beside))
 
 
 def columns_around(left, right, north, south):
+    size = lax.axis_size("lon")
+    odd = lax.axis_index("lon") % 2 == 1
     right = jnp.concatenate([north[-1:], right, south[-1:]], 0)
     left = jnp.concatenate([north[:1], left, south[:1]], 0)
-    return moved(right, "lon", 1), moved(left, "lon", -1)
+
+    def swapped(a, start):
+        pairs = [(i, i + 1) for i in range(start, size - 1, 2)]
+        return lax.ppermute(a, "lon", pairs + [(j, i) for i, j in pairs])
+
+    near = swapped(jnp.where(odd, left, right), 0)
+    far = swapped(jnp.where(odd, right, left), 1)
+    far, near = lax.optimization_barrier((far, near))
+    return jnp.where(odd, near, far), jnp.where(odd, far, near)
 
 
 def body(

time: 76 us -> 72.1 us (0.949)
  blocking collectives: 28.9 us -> 37.5 us
  waiting for transfers between devices: 8.53 us -> 0.57 us
  starting transfers between devices: 26.3 us -> 19.8 us
  local copies, waits for them, and re-layouts: 0.97 us -> 2.97 us
    all_to_all x1, blocking collectives: 11.6 us -> 20.4 us  [summed(): row = jnp.sum(lax.all_to_all(rows, 'lon', 0, 0), 0, keepdims=True)]
    ppermute x8, waiting for transfers between devices: 8.53 us -> 0.57 us  [the longest x2 0.52 us: rows_around(): lax.ppermute(first, 'lat', [((i + 1) % size, i) for i in range(size)])]
    ppermute x8, starting transfers between devices: 26.3 us -> 19.8 us  [the longest x4 11.1 us: swapped(): return lax.ppermute(a, 'lon', pairs + [(j, i) for i, j in pairs])]
    unnamed x20 -> x22, local copies, waits for them, and re-layouts: 0.96 us -> 2.95 us
  transfers between devices with their start and end apart: 8 -> 8, of which waited for: 3 -> 1; matrix products, arithmetic and copies ran while one was open for 0% -> 0% of each run, Pallas kernels for 9% -> 9%
where the time goes in v10:
time: 72.1 us; the launch traced here: 71.8 us
  blocking collectives  37.5 us (52%)
  starting transfers between devices  19.8 us (27%)
  Pallas kernels  9.22 us (13%)
  local copies, waits for them, and re-layouts  2.97 us (4%)
  between operations  0.91 us (1%)
    all_to_all x1, blocking collectives, summed(): row = jnp.sum(lax.all_to_all(rows, 'lon', 0, 0), 0, keepdims=True)  20.4 us
    all_to_all x1, blocking collectives, summed(): return lax.all_to_all(rows, 'lat', 0, 0)  17.2 us
    ppermute x4, starting transfers between devices, swapped(): return lax.ppermute(a, 'lon', pairs + [(j, i) for i, j in pairs])  11.1 us
    ppermute x2, starting transfers between devices, rows_around(): lax.ppermute(first, 'lat', [((i + 1) % size, i) for i in range(size)])  5.41 us
    ppermute x2, starting transfers between devices, rows_around(): lax.ppermute(last, 'lat', [(i, (i + 1) % size) for i in range(size)])  3.3 us
    unnamed x22, local copies, waits for them, and re-layouts  2.95 us
    pallas_call x1, Pallas kernels, body(): call(functools.partial(second_kernel, lat, lon), (like((size, points)), l...  2.02 us
    pallas_call x1, Pallas kernels, body(): call(functools.partial(first_kernel, lat, lon), (like((rows, tracers, poi...  2 us
  transfers between devices with their start and end apart: 8, of which 1 were waited for; matrix products, arithmetic and copies ran while one was open for 0% of the time, Pallas kernels for 9%

profile of v10, /device:TPU:1, one launch (start us, length us, event | category | flops | bytes accessed | tf_op | source)
XLA Modules:
  0.0 71.8 jit_solution(7536114441115958768)
XLA Ops:
  0.6 0.0 copy-start.5
  0.6 0.0 copy-start.4
  0.7 0.9 %copy-done.5 = f32[16,3,4,128]{3,2,1,0:T(4,128)S(1)} copy-done((f32[16,3,4,128]{3,2,1,0:T(4,128)S(1)}, f32[16,3,4,128]{3,2,1,0:T(4,128)}, u32[]{:S(2)}) %copy-start.5) | copy-done | bytes 98328
  1.5 0.0 copy-done.4
  1.6 0.0 copy-start
  1.6 0.0 copy-start.3
  1.6 0.0 copy-start.6
  1.6 0.0 copy-start.7
  1.6 0.0 copy-start.8
  1.6 0.0 copy-start.9
  1.6 0.0 copy-start.10
  1.6 2.7 %collective-permute-start = (bf16[4,32,128]{2,1,0:T(8,128)(2,1)S(1)}, bf16[4,32,128]{2,1,0:T(8,128)(2,1)S(1)}, u32[]{:S(2)}, u32[]{:S(2)}) collective-permute-start(bf16[4,32,128]{2,1,0:T(8,128)(2,1)S(1)} %get-tuple-element.77), channel_id=1, source_target_pairs={{0,32},{32,64},{64,96},{96,128},{128,160},{160,192},{192,224},{224... | collective-permute-start | bytes 98312 | tf_op jit(solution)/shard_map/ppermute | solution.py:413
  4.3 4.2 %collective-permute-start.1 = (bf16[4,32,128]{2,1,0:T(8,128)(2,1)S(1)}, bf16[4,32,128]{2,1,0:T(8,128)(2,1)S(1)}, u32[]{:S(2)}, u32[]{:S(2)}) collective-permute-start(bf16[4,32,128]{2,1,0:T(8,128)(2,1)S(1)} %get-tuple-element.78), channel_id=1, source_target_pairs={{32,0},{64,32},{96,64},{128,96},{160,128},{192,160},{224,192},{256... | collective-permute-start | bytes 98312 | tf_op jit(solution)/shard_map/ppermute | solution.py:414
  8.6 0.0 copy-done
  8.6 0.0 copy-done.3
  8.6 0.0 copy-done.6
  8.6 0.0 copy-done.7
  8.6 0.0 copy-done.8
  8.6 0.0 copy-done.9
  8.6 0.0 copy-done.10
  8.6 1.2 %shard_map.123 = (s32[2,3,4,9]{3,2,1,0:T(4,128)S(1)}, bf16[12,128,128]{2,1,0:T(8,128)(2,1)S(1)}, bf16[12,128,128]{2,1,0:T(8,128)(2,1)S(1)}, f32[12,128,32]{2,1,0...) custom-call(s32[3,4,9]{2,1,0:T(4,128)S(1)} %copy-done.6, s32[3,4,9]{2,1,0:T(4,128)S(1)} %copy-done.7, ...), custom_call_target="tpu_custom_call" | custom-call | flops 10000000000 | bytes 8000000 | tf_op jit(solution)/shard_map/pallas_call | solution.py:473
  9.8 0.0 collective-permute-done.north_ref
  9.8 0.0 collective-permute-done.1.south_ref
  9.9 0.7 collective-permute-start.2
  10.5 3.4 %collective-permute-start.3 = (bf16[5,32,128]{2,1,0:T(8,128)(2,1)S(1)}, bf16[5,32,128]{2,1,0:T(8,128)(2,1)S(1)}, u32[]{:S(2)}, u32[]{:S(2)}) collective-permute-start(bf16[5,32,128]{2,1,0:T(8,128)(2,1)S(1)} %get-tuple-element.139), channel_id=1, source_target_pairs={{0,1},{2,3},{4,5},{6,7},{8,9},{10,11},{12,13},{14,15},{16,17},{18,... | collective-permute-start | bytes 122888 | tf_op jit(solution)/shard_map/ppermute | solution.py:426
  14.0 0.0 copy-start.1
  14.0 2.0 %copy-done.1 = bf16[3,4,9,128,128]{4,3,2,1,0:T(8,128)(2,1)S(1)} copy-done((bf16[3,4,9,128,128]{4,3,2,1,0:T(8,128)(2,1)S(1)}, bf16[3,4,9,128,128]{4,3,2,1,0:T(8,128)(2,1)}, u32[]{:S(2)}) %copy-start.1) | copy-done | bytes 3538968
  16.0 2.0 %shard_map.124 = (bf16[12,16,128]{2,1,0:T(8,128)(2,1)S(1)}, f32[12,128,32]{2,1,0:T(8,128)S(1)}, bf16[18,128,128]{2,1,0:T(8,128)(2,1)S(1)}) custom-call(s32[2,3,4,9]{3,2,1,0:T(4,128)S(1)} %get-tuple-element.91.index_ref, bf16[12,32,128]{2,1,0:T(8,128)(2,1)S(1)} %get-tuple-element.92.x_ref, bf16[4,32,128]{2,1,0:T(8,128)(2,1)S(1)} %collective-permute-done.north_ref, ...), custom_call_target="tpu_custom_call" | custom-call | flops 2000000000 | bytes 5000000 | tf_op jit(solution)/shard_map/pallas_call | solution.py:507
  18.0 0.0 copy-start.2
  18.0 0.0 collective-permute-done.2
  18.0 0.0 collective-permute-done.3
  18.1 0.5 shard_map.125
  18.6 0.6 collective-permute-start.4
  19.2 1.2 %collective-permute-start.5 = (bf16[4,16,128]{2,1,0:T(8,128)(2,1)S(1)}, bf16[4,16,128]{2,1,0:T(8,128)(2,1)S(1)}, u32[]{:S(2)}, u32[]{:S(2)}) collective-permute-start(bf16[4,16,128]{2,1,0:T(8,128)(2,1)S(1)} %get-tuple-element.100), channel_id=1, source_target_pairs={{32,0},{64,32},{96,64},{128,96},{160,128},{192,160},{224,192},{256... | collective-permute-start | bytes 49160 | tf_op jit(solution)/shard_map/ppermute | solution.py:414
  20.4 1.4 %shard_map.126.source_ref = f32[12,128,16]{2,1,0:T(8,128)S(1)} custom-call(f32[12,128,32]{2,1,0:T(8,128)S(1)} %get-tuple-element.96.state_ref, f32[6,128,32]{2,1,0:T(8,128)S(1)} %get-tuple-element.101.edge_ref, f32[128,16]{1,0:T(8,128)S(1)} %get-tuple-element.102.rate_column_ref, f32[1,16]{1,0:T(1,128)S(1)} %bitcast.26), custom_call_target="tpu_custom_call" | custom-call | flops 100000 | bytes 2000000 | tf_op jit(solution)/shard_map/pallas_call | solution.py:525
  21.9 0.0 collective-permute-done.4.north_ref
  21.9 0.5 collective-permute-done.5.south_ref
  22.4 0.7 collective-permute-start.6
  23.1 6.4 %collective-permute-start.7 = (bf16[5,16,128]{2,1,0:T(8,128)(2,1)S(1)}, bf16[5,16,128]{2,1,0:T(8,128)(2,1)S(1)}, u32[]{:S(2)}, u32[]{:S(2)}) collective-permute-start(bf16[5,16,128]{2,1,0:T(8,128)(2,1)S(1)} %get-tuple-element.143), channel_id=1, source_target_pairs={{0,1},{2,3},{4,5},{6,7},{8,9},{10,11},{12,13},{14,15},{16,17},{18,... | collective-permute-start | bytes 61448 | tf_op jit(solution)/shard_map/ppermute | solution.py:426
  29.5 0.0 copy-done.2
  29.5 2.0 %shard_map.127 = (f32[192,128]{1,0:T(8,128)S(1)}, f32[12,128,16]{2,1,0:T(8,128)S(1)}, bf16[18,128,128]{2,1,0:T(8,128)(2,1)S(1)}) custom-call(s32[2,3,4,9]{3,2,1,0:T(4,128)S(1)} %get-tuple-element.91.index_ref, bf16[12,16,128]{2,1,0:T(8,128)(2,1)S(1)} %get-tuple-element.109.x_ref, bf16[4,16,128]{2,1,0:T(8,128)(2,1)S(1)} %collective-permute-done.4.north_ref, ...), custom_call_target="tpu_custom_call" | custom-call | flops 2000000000 | bytes 5000000 | tf_op jit(solution)/shard_map/pallas_call | solution.py:536
  31.5 0.0 collective-permute-done.6
  31.5 0.0 collective-permute-done.7
  31.5 1.2 %shard_map.128 = (f32[192,128]{1,0:T(8,128)S(1)}, f32[192,128]{1,0:T(8,128)}, f32[32,128]{1,0:T(8,128)S(1)}) custom-call(bf16[5,16,128]{2,1,0:T(8,128)(2,1)S(1)} %get-tuple-element.142.west_ref, bf16[5,16,128]{2,1,0:T(8,128)(2,1)S(1)} %get-tuple-element.141.east_ref, f32[12,128,16]{2,1,0:T(8,128)S(1)} %get-tuple-element.111.state_ref, ...), custom_call_target="tpu_custom_call" | custom-call | flops 5662310 | bytes 1500000 | tf_op jit(solution)/shard_map/pallas_call | solution.py:545
  32.8 20.4 %all_to_all.28 = f32[32,1,128]{2,1,0:T(1,128)S(1)} all-to-all(f32[32,1,128]{2,1,0:T(1,128)S(1)} %bitcast.24), channel_id=1, replica_groups=mesh['lat'=16,'lon'=32] {'lon'}, dimensions={0} | all-to-all | bytes 32768 | tf_op jit(solution)/shard_map/all_to_all | solution.py:406
  53.1 0.1 reduce_sum.45
  53.2 17.2 %all_to_all.29 = f32[16,1,128]{2,1,0:T(1,128)S(1)} all-to-all(f32[16,1,128]{2,1,0:T(1,128)S(1)} %broadcast_in_dim.6), channel_id=1, replica_groups=mesh['lat'=16,'lon'=32] {'lat'}, dimensions={0} | all-to-all | bytes 16384 | tf_op jit(solution)/shard_map/all_to_all | solution.py:408
  70.3 0.8 %shard_map.129 = (f32[192,128]{1,0:T(8,128)}, f32[5]{0:T(128)}, s32[1]{0:T(128)}) custom-call(f32[16,128]{1,0:T(8,128)S(1)} %bitcast.40, f32[192,128]{1,0:T(8,128)S(1)} %get-tuple-element.166.product_ref, f32[4,192,128]{2,1,0:T(8,128)S(1)} %bitcast.35), custom_call_target="tpu_custom_call" | custom-call | bytes 700000 | tf_op jit(solution)/shard_map/pallas_call | solution.py:556
  71.1 0.6 while.11
  (10 shorter events, 0.1 us)
Async XLA Ops:
  0.6 0.9 %copy-start.5 = (f32[16,3,4,128]{3,2,1,0:T(4,128)S(1)}, f32[16,3,4,128]{3,2,1,0:T(4,128)}, u32[]{:S(2)}) copy-start(f32[16,3,4,128]{3,2,1,0:T(4,128)} %param.13) | copy-start | bytes 294916
  0.6 0.9 %copy-start.4 = (f32[16,3,4,128]{3,2,1,0:T(4,128)S(1)}, f32[16,3,4,128]{3,2,1,0:T(4,128)}, u32[]{:S(2)}) copy-start(f32[16,3,4,128]{3,2,1,0:T(4,128)} %param.12) | copy-start | bytes 294916
  1.6 7.0 %copy-start = (f32[16]{0:T(128)S(1)}, f32[16]{0:T(128)}, u32[]{:S(2)}) copy-start(f32[16]{0:T(128)} %param.20) | copy-start | bytes 196
  1.6 7.0 %copy-start.3 = (f32[3,4,8,16,16]{4,3,2,1,0:T(8,128)S(1)}, f32[3,4,8,16,16]{4,3,2,1,0:T(8,128)}, u32[]{:S(2)}) copy-start(f32[3,4,8,16,16]{4,3,2,1,0:T(8,128)} %inverse_ref.1) | copy-start | bytes 294916
  1.6 7.0 %copy-start.6 = (s32[3,4,9]{2,1,0:T(4,128)S(1)}, s32[3,4,9]{2,1,0:T(4,128)}, u32[]{:S(2)}) copy-start(s32[3,4,9]{2,1,0:T(4,128)} %pattern_ref.1) | copy-start | bytes 1300
  1.6 7.0 %copy-start.7 = (s32[3,4,9]{2,1,0:T(4,128)S(1)}, s32[3,4,9]{2,1,0:T(4,128)}, u32[]{:S(2)}) copy-start(s32[3,4,9]{2,1,0:T(4,128)} %live_ref.1) | copy-start | bytes 1300
  1.6 7.0 %copy-start.8 = (s32[3,4,8]{2,1,0:T(4,128)S(1)}, s32[3,4,8]{2,1,0:T(4,128)}, u32[]{:S(2)}) copy-start(s32[3,4,8]{2,1,0:T(4,128)} %depth_ref.1) | copy-start | bytes 1156
  1.6 7.0 %copy-start.9 = (f32[3,4,128]{2,1,0:T(4,128)S(1)}, f32[3,4,128]{2,1,0:T(4,128)}, u32[]{:S(2)}) copy-start(f32[3,4,128]{2,1,0:T(4,128)} %rate_ref.1) | copy-start | bytes 18436
  1.6 7.0 %copy-start.10 = (f32[4,16,3,4,128]{4,3,2,1,0:T(4,128)S(1)}, f32[4,16,3,4,128]{4,3,2,1,0:T(4,128)}, u32[]{:S(2)}) copy-start(f32[4,16,3,4,128]{4,3,2,1,0:T(4,128)} %param.21) | copy-start | bytes 1179652
  1.6 8.2 %collective-permute-start = (bf16[4,32,128]{2,1,0:T(8,128)(2,1)S(1)}, bf16[4,32,128]{2,1,0:T(8,128)(2,1)S(1)}, u32[]{:S(2)}, u32[]{:S(2)}) collective-permute-start(bf16[4,32,128]{2,1,0:T(8,128)(2,1)S(1)} %get-tuple-element.77), channel_id=1, source_target_pairs={{0,32},{32,64},{64,96},{96,128},{128,160},{160,192},{192,224},{224... | collective-permute-start | bytes 98312 | tf_op jit(solution)/shard_map/ppermute | solution.py:413
  4.3 5.5 %collective-permute-start.1 = (bf16[4,32,128]{2,1,0:T(8,128)(2,1)S(1)}, bf16[4,32,128]{2,1,0:T(8,128)(2,1)S(1)}, u32[]{:S(2)}, u32[]{:S(2)}) collective-permute-start(bf16[4,32,128]{2,1,0:T(8,128)(2,1)S(1)} %get-tuple-element.78), channel_id=1, source_target_pairs={{32,0},{64,32},{96,64},{128,96},{160,128},{192,160},{224,192},{256... | collective-permute-start | bytes 98312 | tf_op jit(solution)/shard_map/ppermute | solution.py:414
  9.9 8.2 %collective-permute-start.2 = (bf16[5,32,128]{2,1,0:T(8,128)(2,1)S(1)}, bf16[5,32,128]{2,1,0:T(8,128)(2,1)S(1)}, u32[]{:S(2)}, u32[]{:S(2)}) collective-permute-start(bf16[5,32,128]{2,1,0:T(8,128)(2,1)S(1)} %get-tuple-element.140), channel_id=1, source_target_pairs={{1,2},{3,4},{5,6},{7,8},{9,10},{11,12},{13,14},{15,16},{17,18},{19... | collective-permute-start | bytes 122888 | tf_op jit(solution)/shard_map/ppermute | solution.py:426
  10.5 7.5 %collective-permute-start.3 = (bf16[5,32,128]{2,1,0:T(8,128)(2,1)S(1)}, bf16[5,32,128]{2,1,0:T(8,128)(2,1)S(1)}, u32[]{:S(2)}, u32[]{:S(2)}) collective-permute-start(bf16[5,32,128]{2,1,0:T(8,128)(2,1)S(1)} %get-tuple-element.139), channel_id=1, source_target_pairs={{0,1},{2,3},{4,5},{6,7},{8,9},{10,11},{12,13},{14,15},{16,17},{18,... | collective-permute-start | bytes 122888 | tf_op jit(solution)/shard_map/ppermute | solution.py:426
  14.0 2.0 %copy-start.1 = (bf16[3,4,9,128,128]{4,3,2,1,0:T(8,128)(2,1)S(1)}, bf16[3,4,9,128,128]{4,3,2,1,0:T(8,128)(2,1)}, u32[]{:S(2)}) copy-start(bf16[3,4,9,128,128]{4,3,2,1,0:T(8,128)(2,1)} %param.14) | copy-start | bytes 10616836
  18.0 11.5 %copy-start.2 = (bf16[3,4,9,128,128]{4,3,2,1,0:T(8,128)(2,1)S(1)}, bf16[3,4,9,128,128]{4,3,2,1,0:T(8,128)(2,1)}, u32[]{:S(2)}) copy-start(bf16[3,4,9,128,128]{4,3,2,1,0:T(8,128)(2,1)} %param.14) | copy-start | bytes 10616836
  18.6 3.2 %collective-permute-start.4 = (bf16[4,16,128]{2,1,0:T(8,128)(2,1)S(1)}, bf16[4,16,128]{2,1,0:T(8,128)(2,1)S(1)}, u32[]{:S(2)}, u32[]{:S(2)}) collective-permute-start(bf16[4,16,128]{2,1,0:T(8,128)(2,1)S(1)} %get-tuple-element.99), channel_id=1, source_target_pairs={{0,32},{32,64},{64,96},{96,128},{128,160},{160,192},{192,224},{224... | collective-permute-start | bytes 49160 | tf_op jit(solution)/shard_map/ppermute | solution.py:413
  19.2 3.2 %collective-permute-start.5 = (bf16[4,16,128]{2,1,0:T(8,128)(2,1)S(1)}, bf16[4,16,128]{2,1,0:T(8,128)(2,1)S(1)}, u32[]{:S(2)}, u32[]{:S(2)}) collective-permute-start(bf16[4,16,128]{2,1,0:T(8,128)(2,1)S(1)} %get-tuple-element.100), channel_id=1, source_target_pairs={{32,0},{64,32},{96,64},{128,96},{160,128},{192,160},{224,192},{256... | collective-permute-start | bytes 49160 | tf_op jit(solution)/shard_map/ppermute | solution.py:414
  22.4 9.1 %collective-permute-start.6 = (bf16[5,16,128]{2,1,0:T(8,128)(2,1)S(1)}, bf16[5,16,128]{2,1,0:T(8,128)(2,1)S(1)}, u32[]{:S(2)}, u32[]{:S(2)}) collective-permute-start(bf16[5,16,128]{2,1,0:T(8,128)(2,1)S(1)} %get-tuple-element.144), channel_id=1, source_target_pairs={{1,2},{3,4},{5,6},{7,8},{9,10},{11,12},{13,14},{15,16},{17,18},{19... | collective-permute-start | bytes 61448 | tf_op jit(solution)/shard_map/ppermute | solution.py:426
  23.1 8.4 %collective-permute-start.7 = (bf16[5,16,128]{2,1,0:T(8,128)(2,1)S(1)}, bf16[5,16,128]{2,1,0:T(8,128)(2,1)S(1)}, u32[]{:S(2)}, u32[]{:S(2)}) collective-permute-start(bf16[5,16,128]{2,1,0:T(8,128)(2,1)S(1)} %get-tuple-element.143), channel_id=1, source_target_pairs={{0,1},{2,3},{4,5},{6,7},{8,9},{10,11},{12,13},{14,15},{16,17},{18,... | collective-permute-start | bytes 61448 | tf_op jit(solution)/shard_map/ppermute | solution.py:426

commit v11 on v10

--- a/solution.py
+++ b/solution.py
@@ -38,12 +38,13 @@
     return lax.broadcasted_iota(jnp.int32, shape, dim)
 
 
-def begin_kernel(out_ref):
-    out_ref[...] = jnp.zeros(out_ref.shape, F32)
+def begin_kernel(odd_ref):
+    odd = lax.axis_index("lon") % 2
+    odd_ref[...] = jnp.full(odd_ref.shape, odd, jnp.int32).astype(F32)
 
 
 def pack_kernel(
-    begun_ref, c_ref, v_ref, x_ref, first_ref, last_ref, left_ref, right_ref
+    odd_ref, c_ref, v_ref, x_ref, first_ref, last_ref, left_ref, right_ref
 ):
     rows = x_ref.shape[0]
     tracers = c_ref.shape[0] // rows
@@ -415,9 +416,9 @@
     return lax.optimization_barrier((north, south, beside))
 
 
-def columns_around(left, right, north, south):
+def columns_around(left, right, north, south, odd):
     size = lax.axis_size("lon")
-    odd = lax.axis_index("lon") % 2 == 1
+    odd = odd[None, : left.shape[1]] > 0.5
     right = jnp.concatenate([north[-1:], right, south[-1:]], 0)
     left = jnp.concatenate([north[:1], left, south[:1]], 0)
 
@@ -463,10 +464,10 @@
             like((lat, width, points), BF16),
         )
 
-    begun = call(begin_kernel, like((8, points)), [], VMEM, flops=PACK)()
+    odd = call(begin_kernel, like((2 * tracers, points)), [], VMEM, flops=PACK)()
     x, first, last, left, right = call(
         pack_kernel, edges(2 * tracers), [VMEM] * 3, [VMEM] * 5, flops=PACK, size=400000
-    )(begun, flat_c, flat_v)
+    )(odd, flat_c, flat_v)
 
     flat_basis = basis.reshape(count, size, points)
     held = blocks.reshape(rows * slots, points, points)
@@ -503,7 +504,7 @@
     prepared = (index, high, low, source, rate_column, gram)
     north, south, prepared = rows_around(first, last, prepared)
     index, high, low, source, rate_column, gram = prepared
-    west, east = columns_around(left, right, north, south)
+    west, east = columns_around(left, right, north, south, odd)
     part, state, blocks_later = call(
         functools.partial(first_kernel, lat, lon),
         (like((rows, tracers, points), BF16), like((rows, points, 2 * tracers)), later),
@@ -532,7 +533,7 @@
     )(state, edge, rate_column, share)
 
     north, south, source = rows_around(first, last, source)
-    west, east = columns_around(left, right, north, south)
+    west, east = columns_around(left, right, north, south, odd)
     part, state, blocks_later = call(
         functools.partial(second_kernel, lat, lon),
         (like((size, points)), like((rows, points, tracers)), later),

time: 72.1 us -> 71.8 us (level)
  local copies, waits for them, and re-layouts: 2.97 us -> 0.97 us
  blocking collectives: 37.5 us -> 39.2 us
    unnamed x22 -> x20, local copies, waits for them, and re-layouts: 2.95 us -> 0.94 us
    ppermute x2, starting transfers between devices: 5.41 us -> 7.28 us  [rows_around(): lax.ppermute(first, 'lat', [((i + 1) % size, i) for i in range(size)])]
    all_to_all x1, blocking collectives: 20.4 us -> 22 us  [summed(): row = jnp.sum(lax.all_to_all(rows, 'lon', 0, 0), 0, keepdims=True)]
    ppermute x4, starting transfers between devices: 11.1 us -> 9.71 us  [swapped(): return lax.ppermute(a, 'lon', pairs + [(j, i) for i, j in pairs])]
  transfers between devices with their start and end apart: 8 -> 8, of which waited for: 1 -> 0; matrix products, arithmetic and copies ran while one was open for 0% -> 0% of each run, Pallas kernels for 9% -> 9%
where the time goes in v11:
time: 71.8 us; the launch traced here: 71.4 us
  blocking collectives  39.2 us (55%)
  starting transfers between devices  20.3 us (28%)
  Pallas kernels  9.24 us (13%)
  local copies, waits for them, and re-layouts  0.97 us (1%)
  between operations  0.93 us (1%)
    all_to_all x1, blocking collectives, summed(): row = jnp.sum(lax.all_to_all(rows, 'lon', 0, 0), 0, keepdims=True)  22 us
    all_to_all x1, blocking collectives, summed(): return lax.all_to_all(rows, 'lat', 0, 0)  17.2 us
    ppermute x4, starting transfers between devices, swapped(): return lax.ppermute(a, 'lon', pairs + [(j, i) for i, j in pairs])  9.71 us
    ppermute x2, starting transfers between devices, rows_around(): lax.ppermute(first, 'lat', [((i + 1) % size, i) for i in range(size)])  7.28 us
    ppermute x2, starting transfers between devices, rows_around(): lax.ppermute(last, 'lat', [(i, (i + 1) % size) for i in range(size)])  3.31 us
    pallas_call x1, Pallas kernels, body(): call(functools.partial(second_kernel, lat, lon), (like((size, points)), l...  2.02 us
    pallas_call x1, Pallas kernels, body(): call(functools.partial(first_kernel, lat, lon), (like((rows, tracers, poi...  2.01 us
    pallas_call x1, Pallas kernels, body(): call(functools.partial(pull_kernel, lat, lon), like((rows, points, tracer...  1.44 us
  transfers between devices with their start and end apart: 8, of which 0 were waited for; matrix products, arithmetic and copies ran while one was open for 0% of the time, Pallas kernels for 9%

profile of v11, /device:TPU:1, one launch (start us, length us, event | category | flops | bytes accessed | tf_op | source)
XLA Modules:
  0.0 71.4 jit_solution(7087389810215107812)
XLA Ops:
  0.6 0.0 copy-start.4
  0.6 0.0 copy-start.3
  0.7 0.9 %copy-done.4 = f32[16,3,4,128]{3,2,1,0:T(4,128)S(1)} copy-done((f32[16,3,4,128]{3,2,1,0:T(4,128)S(1)}, f32[16,3,4,128]{3,2,1,0:T(4,128)}, u32[]{:S(2)}) %copy-start.4) | copy-done | bytes 98328
  1.5 0.0 copy-done.3
  1.6 0.0 copy-start
  1.6 0.0 copy-start.2
  1.6 0.0 copy-start.5
  1.6 0.0 copy-start.6
  1.6 0.0 copy-start.7
  1.6 0.0 copy-start.8
  1.6 0.0 copy-start.9
  1.6 2.7 %collective-permute-start = (bf16[4,32,128]{2,1,0:T(8,128)(2,1)S(1)}, bf16[4,32,128]{2,1,0:T(8,128)(2,1)S(1)}, u32[]{:S(2)}, u32[]{:S(2)}) collective-permute-start(bf16[4,32,128]{2,1,0:T(8,128)(2,1)S(1)} %get-tuple-element.77), channel_id=1, source_target_pairs={{0,32},{32,64},{64,96},{96,128},{128,160},{160,192},{192,224},{224... | collective-permute-start | bytes 98312 | tf_op jit(solution)/shard_map/ppermute | solution.py:414
  4.3 4.2 %collective-permute-start.1 = (bf16[4,32,128]{2,1,0:T(8,128)(2,1)S(1)}, bf16[4,32,128]{2,1,0:T(8,128)(2,1)S(1)}, u32[]{:S(2)}, u32[]{:S(2)}) collective-permute-start(bf16[4,32,128]{2,1,0:T(8,128)(2,1)S(1)} %get-tuple-element.78), channel_id=1, source_target_pairs={{32,0},{64,32},{96,64},{128,96},{160,128},{192,160},{224,192},{256... | collective-permute-start | bytes 98312 | tf_op jit(solution)/shard_map/ppermute | solution.py:415
  8.6 0.0 copy-done
  8.6 0.0 copy-done.2
  8.6 0.0 copy-done.5
  8.6 0.0 copy-done.6
  8.6 0.0 copy-done.7
  8.6 0.0 copy-done.8
  8.6 0.0 copy-done.9
  8.6 0.0 copy-start.1
  8.6 1.2 %shard_map.123 = (s32[2,3,4,9]{3,2,1,0:T(4,128)S(1)}, bf16[12,128,128]{2,1,0:T(8,128)(2,1)S(1)}, bf16[12,128,128]{2,1,0:T(8,128)(2,1)S(1)}, f32[12,128,32]{2,1,0...) custom-call(s32[3,4,9]{2,1,0:T(4,128)S(1)} %copy-done.5, s32[3,4,9]{2,1,0:T(4,128)S(1)} %copy-done.6, ...), custom_call_target="tpu_custom_call" | custom-call | flops 10000000000 | bytes 8000000 | tf_op jit(solution)/shard_map/pallas_call | solution.py:474
  9.8 0.0 collective-permute-done.north_ref
  9.8 0.0 collective-permute-done.1.south_ref
  9.9 0.7 collective-permute-start.2
  10.5 3.4 %collective-permute-start.3 = (bf16[5,32,128]{2,1,0:T(8,128)(2,1)S(1)}, bf16[5,32,128]{2,1,0:T(8,128)(2,1)S(1)}, u32[]{:S(2)}, u32[]{:S(2)}) collective-permute-start(bf16[5,32,128]{2,1,0:T(8,128)(2,1)S(1)} %get-tuple-element.139), channel_id=1, source_target_pairs={{0,1},{2,3},{4,5},{6,7},{8,9},{10,11},{12,13},{14,15},{16,17},{18,... | collective-permute-start | bytes 122888 | tf_op jit(solution)/shard_map/ppermute | solution.py:427
  14.0 0.0 copy-done.1
  14.0 2.0 %shard_map.124 = (bf16[12,16,128]{2,1,0:T(8,128)(2,1)S(1)}, f32[12,128,32]{2,1,0:T(8,128)S(1)}, bf16[18,128,128]{2,1,0:T(8,128)(2,1)S(1)}) custom-call(s32[2,3,4,9]{3,2,1,0:T(4,128)S(1)} %get-tuple-element.91.index_ref, bf16[12,32,128]{2,1,0:T(8,128)(2,1)S(1)} %get-tuple-element.92.x_ref, bf16[4,32,128]{2,1,0:T(8,128)(2,1)S(1)} %collective-permute-done.north_ref, ...), custom_call_target="tpu_custom_call" | custom-call | flops 2000000000 | bytes 5000000 | tf_op jit(solution)/shard_map/pallas_call | solution.py:508
  16.0 0.0 collective-permute-done.2
  16.0 0.0 collective-permute-done.3
  16.1 0.5 shard_map.125
  16.6 0.6 collective-permute-start.4
  17.2 3.1 %collective-permute-start.5 = (bf16[4,16,128]{2,1,0:T(8,128)(2,1)S(1)}, bf16[4,16,128]{2,1,0:T(8,128)(2,1)S(1)}, u32[]{:S(2)}, u32[]{:S(2)}) collective-permute-start(bf16[4,16,128]{2,1,0:T(8,128)(2,1)S(1)} %get-tuple-element.100), channel_id=1, source_target_pairs={{32,0},{64,32},{96,64},{128,96},{160,128},{192,160},{224,192},{256... | collective-permute-start | bytes 49160 | tf_op jit(solution)/shard_map/ppermute | solution.py:415
  20.3 1.4 %shard_map.126.source_ref = f32[12,128,16]{2,1,0:T(8,128)S(1)} custom-call(f32[12,128,32]{2,1,0:T(8,128)S(1)} %get-tuple-element.96.state_ref, f32[6,128,32]{2,1,0:T(8,128)S(1)} %get-tuple-element.101.edge_ref, f32[128,16]{1,0:T(8,128)S(1)} %get-tuple-element.102.rate_column_ref, f32[1,16]{1,0:T(1,128)S(1)} %bitcast.26), custom_call_target="tpu_custom_call" | custom-call | flops 100000 | bytes 2000000 | tf_op jit(solution)/shard_map/pallas_call | solution.py:526
  21.7 0.0 collective-permute-done.4.north_ref
  21.8 0.0 collective-permute-done.5.south_ref
  21.8 0.7 collective-permute-start.6
  22.5 5.0 %collective-permute-start.7 = (bf16[5,16,128]{2,1,0:T(8,128)(2,1)S(1)}, bf16[5,16,128]{2,1,0:T(8,128)(2,1)S(1)}, u32[]{:S(2)}, u32[]{:S(2)}) collective-permute-start(bf16[5,16,128]{2,1,0:T(8,128)(2,1)S(1)} %get-tuple-element.143), channel_id=1, source_target_pairs={{0,1},{2,3},{4,5},{6,7},{8,9},{10,11},{12,13},{14,15},{16,17},{18,... | collective-permute-start | bytes 61448 | tf_op jit(solution)/shard_map/ppermute | solution.py:427
  27.5 2.0 %shard_map.127 = (f32[192,128]{1,0:T(8,128)S(1)}, f32[12,128,16]{2,1,0:T(8,128)S(1)}, bf16[18,128,128]{2,1,0:T(8,128)(2,1)S(1)}) custom-call(s32[2,3,4,9]{3,2,1,0:T(4,128)S(1)} %get-tuple-element.91.index_ref, bf16[12,16,128]{2,1,0:T(8,128)(2,1)S(1)} %get-tuple-element.109.x_ref, bf16[4,16,128]{2,1,0:T(8,128)(2,1)S(1)} %collective-permute-done.4.north_ref, ...), custom_call_target="tpu_custom_call" | custom-call | flops 2000000000 | bytes 5000000 | tf_op jit(solution)/shard_map/pallas_call | solution.py:537
  29.5 0.0 collective-permute-done.6
  29.5 0.0 collective-permute-done.7
  29.5 1.2 %shard_map.128 = (f32[192,128]{1,0:T(8,128)S(1)}, f32[192,128]{1,0:T(8,128)}, f32[32,128]{1,0:T(8,128)S(1)}) custom-call(bf16[5,16,128]{2,1,0:T(8,128)(2,1)S(1)} %get-tuple-element.142.west_ref, bf16[5,16,128]{2,1,0:T(8,128)(2,1)S(1)} %get-tuple-element.141.east_ref, f32[12,128,16]{2,1,0:T(8,128)S(1)} %get-tuple-element.111.state_ref, ...), custom_call_target="tpu_custom_call" | custom-call | flops 5662310 | bytes 1500000 | tf_op jit(solution)/shard_map/pallas_call | solution.py:546
  30.8 22.0 %all_to_all.28 = f32[32,1,128]{2,1,0:T(1,128)S(1)} all-to-all(f32[32,1,128]{2,1,0:T(1,128)S(1)} %bitcast.24), channel_id=1, replica_groups=mesh['lat'=16,'lon'=32] {'lon'}, dimensions={0} | all-to-all | bytes 32768 | tf_op jit(solution)/shard_map/all_to_all | solution.py:407
  52.8 0.1 reduce_sum.45
  52.8 17.2 %all_to_all.29 = f32[16,1,128]{2,1,0:T(1,128)S(1)} all-to-all(f32[16,1,128]{2,1,0:T(1,128)S(1)} %broadcast_in_dim.56), channel_id=1, replica_groups=mesh['lat'=16,'lon'=32] {'lat'}, dimensions={0} | all-to-all | bytes 16384 | tf_op jit(solution)/shard_map/all_to_all | solution.py:409
  70.0 0.8 %shard_map.129 = (f32[192,128]{1,0:T(8,128)}, f32[5]{0:T(128)}, s32[1]{0:T(128)}) custom-call(f32[16,128]{1,0:T(8,128)S(1)} %bitcast.40, f32[192,128]{1,0:T(8,128)S(1)} %get-tuple-element.166.product_ref, f32[4,192,128]{2,1,0:T(8,128)S(1)} %bitcast.35), custom_call_target="tpu_custom_call" | custom-call | bytes 700000 | tf_op jit(solution)/shard_map/pallas_call | solution.py:557
  70.8 0.6 while.11
  (12 shorter events, 0.1 us)
Async XLA Ops:
  0.6 0.9 %copy-start.4 = (f32[16,3,4,128]{3,2,1,0:T(4,128)S(1)}, f32[16,3,4,128]{3,2,1,0:T(4,128)}, u32[]{:S(2)}) copy-start(f32[16,3,4,128]{3,2,1,0:T(4,128)} %param.13) | copy-start | bytes 294916
  0.6 0.9 %copy-start.3 = (f32[16,3,4,128]{3,2,1,0:T(4,128)S(1)}, f32[16,3,4,128]{3,2,1,0:T(4,128)}, u32[]{:S(2)}) copy-start(f32[16,3,4,128]{3,2,1,0:T(4,128)} %param.12) | copy-start | bytes 294916
  1.6 7.0 %copy-start = (f32[16]{0:T(128)S(1)}, f32[16]{0:T(128)}, u32[]{:S(2)}) copy-start(f32[16]{0:T(128)} %param.20) | copy-start | bytes 196
  1.6 7.0 %copy-start.2 = (f32[3,4,8,16,16]{4,3,2,1,0:T(8,128)S(1)}, f32[3,4,8,16,16]{4,3,2,1,0:T(8,128)}, u32[]{:S(2)}) copy-start(f32[3,4,8,16,16]{4,3,2,1,0:T(8,128)} %inverse_ref.1) | copy-start | bytes 294916
  1.6 7.0 %copy-start.5 = (s32[3,4,9]{2,1,0:T(4,128)S(1)}, s32[3,4,9]{2,1,0:T(4,128)}, u32[]{:S(2)}) copy-start(s32[3,4,9]{2,1,0:T(4,128)} %pattern_ref.1) | copy-start | bytes 1300
  1.6 7.0 %copy-start.6 = (s32[3,4,9]{2,1,0:T(4,128)S(1)}, s32[3,4,9]{2,1,0:T(4,128)}, u32[]{:S(2)}) copy-start(s32[3,4,9]{2,1,0:T(4,128)} %live_ref.1) | copy-start | bytes 1300
  1.6 7.0 %copy-start.7 = (s32[3,4,8]{2,1,0:T(4,128)S(1)}, s32[3,4,8]{2,1,0:T(4,128)}, u32[]{:S(2)}) copy-start(s32[3,4,8]{2,1,0:T(4,128)} %depth_ref.1) | copy-start | bytes 1156
  1.6 7.0 %copy-start.8 = (f32[3,4,128]{2,1,0:T(4,128)S(1)}, f32[3,4,128]{2,1,0:T(4,128)}, u32[]{:S(2)}) copy-start(f32[3,4,128]{2,1,0:T(4,128)} %rate_ref.1) | copy-start | bytes 18436
  1.6 7.0 %copy-start.9 = (f32[4,16,3,4,128]{4,3,2,1,0:T(4,128)S(1)}, f32[4,16,3,4,128]{4,3,2,1,0:T(4,128)}, u32[]{:S(2)}) copy-start(f32[4,16,3,4,128]{4,3,2,1,0:T(4,128)} %param.21) | copy-start | bytes 1179652
  1.6 8.2 %collective-permute-start = (bf16[4,32,128]{2,1,0:T(8,128)(2,1)S(1)}, bf16[4,32,128]{2,1,0:T(8,128)(2,1)S(1)}, u32[]{:S(2)}, u32[]{:S(2)}) collective-permute-start(bf16[4,32,128]{2,1,0:T(8,128)(2,1)S(1)} %get-tuple-element.77), channel_id=1, source_target_pairs={{0,32},{32,64},{64,96},{96,128},{128,160},{160,192},{192,224},{224... | collective-permute-start | bytes 98312 | tf_op jit(solution)/shard_map/ppermute | solution.py:414
  4.3 5.5 %collective-permute-start.1 = (bf16[4,32,128]{2,1,0:T(8,128)(2,1)S(1)}, bf16[4,32,128]{2,1,0:T(8,128)(2,1)S(1)}, u32[]{:S(2)}, u32[]{:S(2)}) collective-permute-start(bf16[4,32,128]{2,1,0:T(8,128)(2,1)S(1)} %get-tuple-element.78), channel_id=1, source_target_pairs={{32,0},{64,32},{96,64},{128,96},{160,128},{192,160},{224,192},{256... | collective-permute-start | bytes 98312 | tf_op jit(solution)/shard_map/ppermute | solution.py:415
  8.6 5.4 %copy-start.1 = (bf16[3,4,9,128,128]{4,3,2,1,0:T(8,128)(2,1)S(1)}, bf16[3,4,9,128,128]{4,3,2,1,0:T(8,128)(2,1)}, u32[]{:S(2)}) copy-start(bf16[3,4,9,128,128]{4,3,2,1,0:T(8,128)(2,1)} %param.14) | copy-start | bytes 10616836
  9.9 6.1 %collective-permute-start.2 = (bf16[5,32,128]{2,1,0:T(8,128)(2,1)S(1)}, bf16[5,32,128]{2,1,0:T(8,128)(2,1)S(1)}, u32[]{:S(2)}, u32[]{:S(2)}) collective-permute-start(bf16[5,32,128]{2,1,0:T(8,128)(2,1)S(1)} %get-tuple-element.140), channel_id=1, source_target_pairs={{1,2},{3,4},{5,6},{7,8},{9,10},{11,12},{13,14},{15,16},{17,18},{19... | collective-permute-start | bytes 122888 | tf_op jit(solution)/shard_map/ppermute | solution.py:427
  10.5 5.5 %collective-permute-start.3 = (bf16[5,32,128]{2,1,0:T(8,128)(2,1)S(1)}, bf16[5,32,128]{2,1,0:T(8,128)(2,1)S(1)}, u32[]{:S(2)}, u32[]{:S(2)}) collective-permute-start(bf16[5,32,128]{2,1,0:T(8,128)(2,1)S(1)} %get-tuple-element.139), channel_id=1, source_target_pairs={{0,1},{2,3},{4,5},{6,7},{8,9},{10,11},{12,13},{14,15},{16,17},{18,... | collective-permute-start | bytes 122888 | tf_op jit(solution)/shard_map/ppermute | solution.py:427
  16.6 5.1 %collective-permute-start.4 = (bf16[4,16,128]{2,1,0:T(8,128)(2,1)S(1)}, bf16[4,16,128]{2,1,0:T(8,128)(2,1)S(1)}, u32[]{:S(2)}, u32[]{:S(2)}) collective-permute-start(bf16[4,16,128]{2,1,0:T(8,128)(2,1)S(1)} %get-tuple-element.99), channel_id=1, source_target_pairs={{0,32},{32,64},{64,96},{96,128},{128,160},{160,192},{192,224},{224... | collective-permute-start | bytes 49160 | tf_op jit(solution)/shard_map/ppermute | solution.py:414
  17.2 4.5 %collective-permute-start.5 = (bf16[4,16,128]{2,1,0:T(8,128)(2,1)S(1)}, bf16[4,16,128]{2,1,0:T(8,128)(2,1)S(1)}, u32[]{:S(2)}, u32[]{:S(2)}) collective-permute-start(bf16[4,16,128]{2,1,0:T(8,128)(2,1)S(1)} %get-tuple-element.100), channel_id=1, source_target_pairs={{32,0},{64,32},{96,64},{128,96},{160,128},{192,160},{224,192},{256... | collective-permute-start | bytes 49160 | tf_op jit(solution)/shard_map/ppermute | solution.py:415
  21.8 7.7 %collective-permute-start.6 = (bf16[5,16,128]{2,1,0:T(8,128)(2,1)S(1)}, bf16[5,16,128]{2,1,0:T(8,128)(2,1)S(1)}, u32[]{:S(2)}, u32[]{:S(2)}) collective-permute-start(bf16[5,16,128]{2,1,0:T(8,128)(2,1)S(1)} %get-tuple-element.144), channel_id=1, source_target_pairs={{1,2},{3,4},{5,6},{7,8},{9,10},{11,12},{13,14},{15,16},{17,18},{19... | collective-permute-start | bytes 61448 | tf_op jit(solution)/shard_map/ppermute | solution.py:427
  22.5 7.0 %collective-permute-start.7 = (bf16[5,16,128]{2,1,0:T(8,128)(2,1)S(1)}, bf16[5,16,128]{2,1,0:T(8,128)(2,1)S(1)}, u32[]{:S(2)}, u32[]{:S(2)}) collective-permute-start(bf16[5,16,128]{2,1,0:T(8,128)(2,1)S(1)} %get-tuple-element.143), channel_id=1, source_target_pairs={{0,1},{2,3},{4,5},{6,7},{8,9},{10,11},{12,13},{14,15},{16,17},{18,... | collective-permute-start | bytes 61448 | tf_op jit(solution)/shard_map/ppermute | solution.py:427

commit v12 on v11

--- a/solution.py
+++ b/solution.py
@@ -404,9 +404,9 @@
 
 
 def summed(rows):
-    row = jnp.sum(lax.all_to_all(rows, "lon", 0, 0), 0, keepdims=True)
-    rows = jnp.broadcast_to(row, (lax.axis_size("lat"), row.shape[1]))
-    return lax.all_to_all(rows, "lat", 0, 0)
+    row = jnp.sum(lax.all_to_all(rows, "lat", 0, 0), 0, keepdims=True)
+    rows = jnp.broadcast_to(row, (lax.axis_size("lon"), row.shape[1]))
+    return lax.all_to_all(rows, "lon", 0, 0)
 
 
 def rows_around(first, last, beside):
@@ -545,7 +545,7 @@
     )(index, x, north, south, held, high, low, source)
     product, written, sums = call(
         functools.partial(second_end_kernel, lat, lon),
-        (like((size, points)), like((size, points)), like((lax.axis_size("lon"), points))),
+        (like((size, points)), like((size, points)), like((lax.axis_size("lat"), points))),
         [VMEM] * 9,
         [VMEM, HBM, VMEM],
         scratch=[pltpu.VMEM((ends, points, tracers), F32), pltpu.SemaphoreType.DMA],
@@ -569,7 +569,7 @@
             "k,ksp->sp", heights, flat_basis, precision=lax.Precision.HIGHEST
         )
         part = jnp.pad(jnp.sum(rest * rest).reshape(1, 1), ((0, 0), (0, points - 1)))
-        squared = jnp.sum(summed(jnp.broadcast_to(part, (lax.axis_size("lon"), points))), 0)[0]
+        squared = jnp.sum(summed(jnp.broadcast_to(part, (lax.axis_size("lat"), points))), 0)[0]
         beta = jnp.sqrt(squared + 1e-06)
         return rest / beta, jnp.concatenate([heights, beta[None]]), carry[2] * 0
 

time: 71.8 us -> 70.3 us (0.979)
  blocking collectives: 39.2 us -> 37.8 us
    all_to_all x2, blocking collectives: 39.2 us -> 37.8 us  [the longest x1 22.3 us: summed(): return lax.all_to_all(rows, 'lon', 0, 0)]
  transfers between devices with their start and end apart: 8 -> 8, of which waited for: 0 -> 0; matrix products, arithmetic and copies ran while one was open for 0% -> 0% of each run, Pallas kernels for 9% -> 10%
where the time goes in v12:
time: 70.3 us; the launch traced here: 70 us
  blocking collectives  37.8 us (54%)
  starting transfers between devices  20.3 us (29%)
  Pallas kernels  9.25 us (13%)
  local copies, waits for them, and re-layouts  0.97 us (1%)
  between operations  0.93 us (1%)
    all_to_all x1, blocking collectives, summed(): return lax.all_to_all(rows, 'lon', 0, 0)  22.3 us
    all_to_all x1, blocking collectives, summed(): row = jnp.sum(lax.all_to_all(rows, 'lat', 0, 0), 0, keepdims=True)  15.5 us
    ppermute x4, starting transfers between devices, swapped(): return lax.ppermute(a, 'lon', pairs + [(j, i) for i, j in pairs])  9.71 us
    ppermute x2, starting transfers between devices, rows_around(): lax.ppermute(first, 'lat', [((i + 1) % size, i) for i in range(size)])  7.28 us
    ppermute x2, starting transfers between devices, rows_around(): lax.ppermute(last, 'lat', [(i, (i + 1) % size) for i in range(size)])  3.31 us
    pallas_call x1, Pallas kernels, body(): call(functools.partial(second_kernel, lat, lon), (like((size, points)), l...  2.03 us
    pallas_call x1, Pallas kernels, body(): call(functools.partial(first_kernel, lat, lon), (like((rows, tracers, poi...  2.01 us
    pallas_call x1, Pallas kernels, body(): call(functools.partial(pull_kernel, lat, lon), like((rows, points, tracer...  1.44 us
  transfers between devices with their start and end apart: 8, of which 0 were waited for; matrix products, arithmetic and copies ran while one was open for 0% of the time, Pallas kernels for 10%

profile of v12, /device:TPU:1, one launch (start us, length us, event | category | flops | bytes accessed | tf_op | source)
XLA Modules:
  0.0 70.0 jit_solution(11362308874112408389)
XLA Ops:
  0.6 0.0 copy-start.4
  0.6 0.0 copy-start.3
  0.7 0.9 %copy-done.4 = f32[16,3,4,128]{3,2,1,0:T(4,128)S(1)} copy-done((f32[16,3,4,128]{3,2,1,0:T(4,128)S(1)}, f32[16,3,4,128]{3,2,1,0:T(4,128)}, u32[]{:S(2)}) %copy-start.4) | copy-done | bytes 98328
  1.5 0.0 copy-done.3
  1.6 0.0 copy-start
  1.6 0.0 copy-start.2
  1.6 0.0 copy-start.5
  1.6 0.0 copy-start.6
  1.6 0.0 copy-start.7
  1.6 0.0 copy-start.8
  1.6 0.0 copy-start.9
  1.6 2.7 %collective-permute-start = (bf16[4,32,128]{2,1,0:T(8,128)(2,1)S(1)}, bf16[4,32,128]{2,1,0:T(8,128)(2,1)S(1)}, u32[]{:S(2)}, u32[]{:S(2)}) collective-permute-start(bf16[4,32,128]{2,1,0:T(8,128)(2,1)S(1)} %get-tuple-element.77), channel_id=1, source_target_pairs={{0,32},{32,64},{64,96},{96,128},{128,160},{160,192},{192,224},{224... | collective-permute-start | bytes 98312 | tf_op jit(solution)/shard_map/ppermute | solution.py:414
  4.3 4.2 %collective-permute-start.1 = (bf16[4,32,128]{2,1,0:T(8,128)(2,1)S(1)}, bf16[4,32,128]{2,1,0:T(8,128)(2,1)S(1)}, u32[]{:S(2)}, u32[]{:S(2)}) collective-permute-start(bf16[4,32,128]{2,1,0:T(8,128)(2,1)S(1)} %get-tuple-element.78), channel_id=1, source_target_pairs={{32,0},{64,32},{96,64},{128,96},{160,128},{192,160},{224,192},{256... | collective-permute-start | bytes 98312 | tf_op jit(solution)/shard_map/ppermute | solution.py:415
  8.6 0.0 copy-done
  8.6 0.0 copy-done.2
  8.6 0.0 copy-done.5
  8.6 0.0 copy-done.6
  8.6 0.0 copy-done.7
  8.6 0.0 copy-done.8
  8.6 0.0 copy-done.9
  8.6 0.0 copy-start.1
  8.6 1.2 %shard_map.123 = (s32[2,3,4,9]{3,2,1,0:T(4,128)S(1)}, bf16[12,128,128]{2,1,0:T(8,128)(2,1)S(1)}, bf16[12,128,128]{2,1,0:T(8,128)(2,1)S(1)}, f32[12,128,32]{2,1,0...) custom-call(s32[3,4,9]{2,1,0:T(4,128)S(1)} %copy-done.5, s32[3,4,9]{2,1,0:T(4,128)S(1)} %copy-done.6, ...), custom_call_target="tpu_custom_call" | custom-call | flops 10000000000 | bytes 8000000 | tf_op jit(solution)/shard_map/pallas_call | solution.py:474
  9.8 0.0 collective-permute-done.north_ref
  9.8 0.0 collective-permute-done.1.south_ref
  9.9 0.7 collective-permute-start.2
  10.5 3.4 %collective-permute-start.3 = (bf16[5,32,128]{2,1,0:T(8,128)(2,1)S(1)}, bf16[5,32,128]{2,1,0:T(8,128)(2,1)S(1)}, u32[]{:S(2)}, u32[]{:S(2)}) collective-permute-start(bf16[5,32,128]{2,1,0:T(8,128)(2,1)S(1)} %get-tuple-element.139), channel_id=1, source_target_pairs={{0,1},{2,3},{4,5},{6,7},{8,9},{10,11},{12,13},{14,15},{16,17},{18,... | collective-permute-start | bytes 122888 | tf_op jit(solution)/shard_map/ppermute | solution.py:427
  14.0 0.0 copy-done.1
  14.0 2.0 %shard_map.124 = (bf16[12,16,128]{2,1,0:T(8,128)(2,1)S(1)}, f32[12,128,32]{2,1,0:T(8,128)S(1)}, bf16[18,128,128]{2,1,0:T(8,128)(2,1)S(1)}) custom-call(s32[2,3,4,9]{3,2,1,0:T(4,128)S(1)} %get-tuple-element.91.index_ref, bf16[12,32,128]{2,1,0:T(8,128)(2,1)S(1)} %get-tuple-element.92.x_ref, bf16[4,32,128]{2,1,0:T(8,128)(2,1)S(1)} %collective-permute-done.north_ref, ...), custom_call_target="tpu_custom_call" | custom-call | flops 2000000000 | bytes 5000000 | tf_op jit(solution)/shard_map/pallas_call | solution.py:508
  16.0 0.0 collective-permute-done.2
  16.0 0.0 collective-permute-done.3
  16.1 0.5 shard_map.125
  16.6 0.6 collective-permute-start.4
  17.2 3.1 %collective-permute-start.5 = (bf16[4,16,128]{2,1,0:T(8,128)(2,1)S(1)}, bf16[4,16,128]{2,1,0:T(8,128)(2,1)S(1)}, u32[]{:S(2)}, u32[]{:S(2)}) collective-permute-start(bf16[4,16,128]{2,1,0:T(8,128)(2,1)S(1)} %get-tuple-element.100), channel_id=1, source_target_pairs={{32,0},{64,32},{96,64},{128,96},{160,128},{192,160},{224,192},{256... | collective-permute-start | bytes 49160 | tf_op jit(solution)/shard_map/ppermute | solution.py:415
  20.3 1.4 %shard_map.126.source_ref = f32[12,128,16]{2,1,0:T(8,128)S(1)} custom-call(f32[12,128,32]{2,1,0:T(8,128)S(1)} %get-tuple-element.96.state_ref, f32[6,128,32]{2,1,0:T(8,128)S(1)} %get-tuple-element.101.edge_ref, f32[128,16]{1,0:T(8,128)S(1)} %get-tuple-element.102.rate_column_ref, f32[1,16]{1,0:T(1,128)S(1)} %bitcast.26), custom_call_target="tpu_custom_call" | custom-call | flops 100000 | bytes 2000000 | tf_op jit(solution)/shard_map/pallas_call | solution.py:526
  21.7 0.0 collective-permute-done.4.north_ref
  21.8 0.0 collective-permute-done.5.south_ref
  21.8 0.7 collective-permute-start.6
  22.5 5.0 %collective-permute-start.7 = (bf16[5,16,128]{2,1,0:T(8,128)(2,1)S(1)}, bf16[5,16,128]{2,1,0:T(8,128)(2,1)S(1)}, u32[]{:S(2)}, u32[]{:S(2)}) collective-permute-start(bf16[5,16,128]{2,1,0:T(8,128)(2,1)S(1)} %get-tuple-element.143), channel_id=1, source_target_pairs={{0,1},{2,3},{4,5},{6,7},{8,9},{10,11},{12,13},{14,15},{16,17},{18,... | collective-permute-start | bytes 61448 | tf_op jit(solution)/shard_map/ppermute | solution.py:427
  27.5 2.0 %shard_map.127 = (f32[192,128]{1,0:T(8,128)S(1)}, f32[12,128,16]{2,1,0:T(8,128)S(1)}, bf16[18,128,128]{2,1,0:T(8,128)(2,1)S(1)}) custom-call(s32[2,3,4,9]{3,2,1,0:T(4,128)S(1)} %get-tuple-element.91.index_ref, bf16[12,16,128]{2,1,0:T(8,128)(2,1)S(1)} %get-tuple-element.109.x_ref, bf16[4,16,128]{2,1,0:T(8,128)(2,1)S(1)} %collective-permute-done.4.north_ref, ...), custom_call_target="tpu_custom_call" | custom-call | flops 2000000000 | bytes 5000000 | tf_op jit(solution)/shard_map/pallas_call | solution.py:537
  29.5 0.0 collective-permute-done.6
  29.5 0.0 collective-permute-done.7
  29.5 1.2 %shard_map.128 = (f32[192,128]{1,0:T(8,128)S(1)}, f32[192,128]{1,0:T(8,128)}, f32[16,128]{1,0:T(8,128)S(1)}) custom-call(bf16[5,16,128]{2,1,0:T(8,128)(2,1)S(1)} %get-tuple-element.142.west_ref, bf16[5,16,128]{2,1,0:T(8,128)(2,1)S(1)} %get-tuple-element.141.east_ref, f32[12,128,16]{2,1,0:T(8,128)S(1)} %get-tuple-element.111.state_ref, ...), custom_call_target="tpu_custom_call" | custom-call | flops 5662310 | bytes 1500000 | tf_op jit(solution)/shard_map/pallas_call | solution.py:546
  30.8 15.5 %all_to_all.28 = f32[16,1,128]{2,1,0:T(1,128)S(1)} all-to-all(f32[16,1,128]{2,1,0:T(1,128)S(1)} %bitcast.24), channel_id=1, replica_groups=mesh['lat'=16,'lon'=32] {'lat'}, dimensions={0} | all-to-all | bytes 16384 | tf_op jit(solution)/shard_map/all_to_all | solution.py:407
  46.3 22.3 %all_to_all.29 = f32[32,1,128]{2,1,0:T(1,128)S(1)} all-to-all(f32[32,1,128]{2,1,0:T(1,128)S(1)} %broadcast_in_dim.56), channel_id=1, replica_groups=mesh['lat'=16,'lon'=32] {'lon'}, dimensions={0} | all-to-all | bytes 32768 | tf_op jit(solution)/shard_map/all_to_all | solution.py:409
  68.6 0.8 %shard_map.129 = (f32[192,128]{1,0:T(8,128)}, f32[5]{0:T(128)}, s32[1]{0:T(128)}) custom-call(f32[32,128]{1,0:T(8,128)S(1)} %bitcast.40, f32[192,128]{1,0:T(8,128)S(1)} %get-tuple-element.166.product_ref, f32[4,192,128]{2,1,0:T(8,128)S(1)} %bitcast.35), custom_call_target="tpu_custom_call" | custom-call | bytes 700000 | tf_op jit(solution)/shard_map/pallas_call | solution.py:557
  69.4 0.6 while.11
  (13 shorter events, 0.2 us)
Async XLA Ops:
  0.6 0.9 %copy-start.4 = (f32[16,3,4,128]{3,2,1,0:T(4,128)S(1)}, f32[16,3,4,128]{3,2,1,0:T(4,128)}, u32[]{:S(2)}) copy-start(f32[16,3,4,128]{3,2,1,0:T(4,128)} %param.13) | copy-start | bytes 294916
  0.6 0.9 %copy-start.3 = (f32[16,3,4,128]{3,2,1,0:T(4,128)S(1)}, f32[16,3,4,128]{3,2,1,0:T(4,128)}, u32[]{:S(2)}) copy-start(f32[16,3,4,128]{3,2,1,0:T(4,128)} %param.12) | copy-start | bytes 294916
  1.6 7.0 %copy-start = (f32[16]{0:T(128)S(1)}, f32[16]{0:T(128)}, u32[]{:S(2)}) copy-start(f32[16]{0:T(128)} %param.20) | copy-start | bytes 196
  1.6 7.0 %copy-start.2 = (f32[3,4,8,16,16]{4,3,2,1,0:T(8,128)S(1)}, f32[3,4,8,16,16]{4,3,2,1,0:T(8,128)}, u32[]{:S(2)}) copy-start(f32[3,4,8,16,16]{4,3,2,1,0:T(8,128)} %inverse_ref.1) | copy-start | bytes 294916
  1.6 7.0 %copy-start.5 = (s32[3,4,9]{2,1,0:T(4,128)S(1)}, s32[3,4,9]{2,1,0:T(4,128)}, u32[]{:S(2)}) copy-start(s32[3,4,9]{2,1,0:T(4,128)} %pattern_ref.1) | copy-start | bytes 1300
  1.6 7.0 %copy-start.6 = (s32[3,4,9]{2,1,0:T(4,128)S(1)}, s32[3,4,9]{2,1,0:T(4,128)}, u32[]{:S(2)}) copy-start(s32[3,4,9]{2,1,0:T(4,128)} %live_ref.1) | copy-start | bytes 1300
  1.6 7.0 %copy-start.7 = (s32[3,4,8]{2,1,0:T(4,128)S(1)}, s32[3,4,8]{2,1,0:T(4,128)}, u32[]{:S(2)}) copy-start(s32[3,4,8]{2,1,0:T(4,128)} %depth_ref.1) | copy-start | bytes 1156
  1.6 7.0 %copy-start.8 = (f32[3,4,128]{2,1,0:T(4,128)S(1)}, f32[3,4,128]{2,1,0:T(4,128)}, u32[]{:S(2)}) copy-start(f32[3,4,128]{2,1,0:T(4,128)} %rate_ref.1) | copy-start | bytes 18436
  1.6 7.0 %copy-start.9 = (f32[4,16,3,4,128]{4,3,2,1,0:T(4,128)S(1)}, f32[4,16,3,4,128]{4,3,2,1,0:T(4,128)}, u32[]{:S(2)}) copy-start(f32[4,16,3,4,128]{4,3,2,1,0:T(4,128)} %param.21) | copy-start | bytes 1179652
  1.6 8.2 %collective-permute-start = (bf16[4,32,128]{2,1,0:T(8,128)(2,1)S(1)}, bf16[4,32,128]{2,1,0:T(8,128)(2,1)S(1)}, u32[]{:S(2)}, u32[]{:S(2)}) collective-permute-start(bf16[4,32,128]{2,1,0:T(8,128)(2,1)S(1)} %get-tuple-element.77), channel_id=1, source_target_pairs={{0,32},{32,64},{64,96},{96,128},{128,160},{160,192},{192,224},{224... | collective-permute-start | bytes 98312 | tf_op jit(solution)/shard_map/ppermute | solution.py:414
  4.3 5.5 %collective-permute-start.1 = (bf16[4,32,128]{2,1,0:T(8,128)(2,1)S(1)}, bf16[4,32,128]{2,1,0:T(8,128)(2,1)S(1)}, u32[]{:S(2)}, u32[]{:S(2)}) collective-permute-start(bf16[4,32,128]{2,1,0:T(8,128)(2,1)S(1)} %get-tuple-element.78), channel_id=1, source_target_pairs={{32,0},{64,32},{96,64},{128,96},{160,128},{192,160},{224,192},{256... | collective-permute-start | bytes 98312 | tf_op jit(solution)/shard_map/ppermute | solution.py:415
  8.6 5.4 %copy-start.1 = (bf16[3,4,9,128,128]{4,3,2,1,0:T(8,128)(2,1)S(1)}, bf16[3,4,9,128,128]{4,3,2,1,0:T(8,128)(2,1)}, u32[]{:S(2)}) copy-start(bf16[3,4,9,128,128]{4,3,2,1,0:T(8,128)(2,1)} %param.14) | copy-start | bytes 10616836
  9.9 6.1 %collective-permute-start.2 = (bf16[5,32,128]{2,1,0:T(8,128)(2,1)S(1)}, bf16[5,32,128]{2,1,0:T(8,128)(2,1)S(1)}, u32[]{:S(2)}, u32[]{:S(2)}) collective-permute-start(bf16[5,32,128]{2,1,0:T(8,128)(2,1)S(1)} %get-tuple-element.140), channel_id=1, source_target_pairs={{1,2},{3,4},{5,6},{7,8},{9,10},{11,12},{13,14},{15,16},{17,18},{19... | collective-permute-start | bytes 122888 | tf_op jit(solution)/shard_map/ppermute | solution.py:427
  10.5 5.5 %collective-permute-start.3 = (bf16[5,32,128]{2,1,0:T(8,128)(2,1)S(1)}, bf16[5,32,128]{2,1,0:T(8,128)(2,1)S(1)}, u32[]{:S(2)}, u32[]{:S(2)}) collective-permute-start(bf16[5,32,128]{2,1,0:T(8,128)(2,1)S(1)} %get-tuple-element.139), channel_id=1, source_target_pairs={{0,1},{2,3},{4,5},{6,7},{8,9},{10,11},{12,13},{14,15},{16,17},{18,... | collective-permute-start | bytes 122888 | tf_op jit(solution)/shard_map/ppermute | solution.py:427
  16.6 5.1 %collective-permute-start.4 = (bf16[4,16,128]{2,1,0:T(8,128)(2,1)S(1)}, bf16[4,16,128]{2,1,0:T(8,128)(2,1)S(1)}, u32[]{:S(2)}, u32[]{:S(2)}) collective-permute-start(bf16[4,16,128]{2,1,0:T(8,128)(2,1)S(1)} %get-tuple-element.99), channel_id=1, source_target_pairs={{0,32},{32,64},{64,96},{96,128},{128,160},{160,192},{192,224},{224... | collective-permute-start | bytes 49160 | tf_op jit(solution)/shard_map/ppermute | solution.py:414
  17.2 4.5 %collective-permute-start.5 = (bf16[4,16,128]{2,1,0:T(8,128)(2,1)S(1)}, bf16[4,16,128]{2,1,0:T(8,128)(2,1)S(1)}, u32[]{:S(2)}, u32[]{:S(2)}) collective-permute-start(bf16[4,16,128]{2,1,0:T(8,128)(2,1)S(1)} %get-tuple-element.100), channel_id=1, source_target_pairs={{32,0},{64,32},{96,64},{128,96},{160,128},{192,160},{224,192},{256... | collective-permute-start | bytes 49160 | tf_op jit(solution)/shard_map/ppermute | solution.py:415
  21.8 7.7 %collective-permute-start.6 = (bf16[5,16,128]{2,1,0:T(8,128)(2,1)S(1)}, bf16[5,16,128]{2,1,0:T(8,128)(2,1)S(1)}, u32[]{:S(2)}, u32[]{:S(2)}) collective-permute-start(bf16[5,16,128]{2,1,0:T(8,128)(2,1)S(1)} %get-tuple-element.144), channel_id=1, source_target_pairs={{1,2},{3,4},{5,6},{7,8},{9,10},{11,12},{13,14},{15,16},{17,18},{19... | collective-permute-start | bytes 61448 | tf_op jit(solution)/shard_map/ppermute | solution.py:427
  22.5 7.0 %collective-permute-start.7 = (bf16[5,16,128]{2,1,0:T(8,128)(2,1)S(1)}, bf16[5,16,128]{2,1,0:T(8,128)(2,1)S(1)}, u32[]{:S(2)}, u32[]{:S(2)}) collective-permute-start(bf16[5,16,128]{2,1,0:T(8,128)(2,1)S(1)} %get-tuple-element.143), channel_id=1, source_target_pairs={{0,1},{2,3},{4,5},{6,7},{8,9},{10,11},{12,13},{14,15},{16,17},{18,... | collective-permute-start | bytes 61448 | tf_op jit(solution)/shard_map/ppermute | solution.py:427
